TPU v7x, 32 devices: a whole 2x2x4 slice. The times are simulated.
32 devices in a mesh: fsdp: 8 (over z, x), layer: 4 (over y, core).
Axes of the slice: x: 2, y: 2, z: 4, core: 2. Of those that a mesh axis runs over, the one named last changes fastest.
Arguments:
- gradients: bfloat16 [4, 64, 256, 256], P('layer', 'fsdp'), may hold values from -8 to 8
- second_moment: float32 [4, 64, 256, 256], P('layer', 'fsdp'), may hold values from 0.0001 to 0.01
- owners: int32 [4, 64, 1], P('layer'), may hold values from 0 to 7, as said below
- left_stats: float32 [4, 64, 256, 256], P('layer', 'fsdp'), may hold values from -0.3 to 4.3, as said below
- right_stats: float32 [4, 64, 256, 256], P('layer', 'fsdp'), may hold values from -0.3 to 4.3, as said below
- left_root: bfloat16 [4, 64, 256, 256], P('layer', 'fsdp'), may hold values from -0.3 to 1.8
- right_root: bfloat16 [4, 64, 256, 256], P('layer', 'fsdp'), may hold values from -0.3 to 1.8
Outputs:
- update: bfloat16 [4, 64, 256, 256], P('layer', 'fsdp')
- new_left_stats: float32 [4, 64, 256, 256], P('layer', 'fsdp')
- new_right_stats: float32 [4, 64, 256, 256], P('layer', 'fsdp')
Inputs may be any that keep to these rules, and one draw needn't show every extreme that they name: In the list of one matrix, the 8 blocks of one index of fsdp (blocks i * 8 to (i + 1) * 8 - 1) name distinct owners, and no owner is named more than 8 times; every owner keeps the statistics and roots of its k-th owned block (in list order) in its slot k, and slots past its count are unused. `left_stats`: Symmetric. `right_stats`: Symmetric.
All inputs are finite; a program needn't handle non-finite values.
Results may differ from a plain program's by a relative error of at most 0.0057.
Values may be sent and summed in bfloat16 or wider, within the bound.
No kernel may reach another device: no remote copies, remote signals or barrier semaphores. Data moves between devices by JAX's collectives and lax.ppermute only.
A program may use at most 192 MiB of HBM per device.

v0:
```python
import jax
import jax.numpy as jnp
from jax import lax
from jax.sharding import PartitionSpec as P

ADAM_EPS = 1e-08
DECAY_RATE = 0.95
UPDATE_RMS = 1.0
NORM_FLOOR = 1e-06


def selection_tables(owner_list, owner_count, blocks, slots_here, my_index):
    total_blocks = owner_list.shape[0]
    owner_hot = (owner_list[:, None] == lax.iota(jnp.int32, owner_count)[None, :]).astype(
        jnp.float32
    )
    row_ids = lax.iota(jnp.int32, total_blocks)
    strict_lower = (row_ids[:, None] > row_ids[None, :]).astype(jnp.float32)
    before_all = jnp.dot(strict_lower, owner_hot, precision=lax.Precision.HIGHEST)
    slot_number = jnp.sum(before_all * owner_hot, axis=1)
    mine_mask = (owner_list == my_index).astype(jnp.float32)
    slot_hot = (slot_number[:, None] == lax.iota(jnp.float32, slots_here)[None, :]).astype(
        jnp.float32
    ) * mine_mask[:, None]
    home_hot = ((row_ids // blocks)[:, None] == lax.iota(jnp.int32, owner_count)[None, :]).astype(
        jnp.float32
    )
    return (owner_hot, home_hot, slot_hot)


def owner_work(gathered, left_stats, right_stats, left_root, right_root):
    gram_left = jnp.einsum("sij,skj->sik", gathered, gathered, preferred_element_type=jnp.float32)
    gram_right = jnp.einsum("sji,sjk->sik", gathered, gathered, preferred_element_type=jnp.float32)
    new_left = DECAY_RATE * left_stats[0] + (1.0 - DECAY_RATE) * gram_left
    new_right = DECAY_RATE * right_stats[0] + (1.0 - DECAY_RATE) * gram_right
    half_done = jnp.einsum(
        "sij,sjk->sik", left_root[0], gathered, preferred_element_type=jnp.float32
    ).astype(jnp.bfloat16)
    preconditioned = jnp.einsum(
        "sij,sjk->sik", half_done, right_root[0], preferred_element_type=jnp.float32
    ).astype(jnp.bfloat16)
    return (preconditioned, new_left[None], new_right[None])


def per_device(gradients, second_moment, owners, left_stats, right_stats, left_root, right_root):
    owner_count = lax.axis_size("fsdp")
    my_index = lax.axis_index("fsdp")
    blocks = gradients.shape[1]
    block_side = gradients.shape[3]
    slots_here = left_stats.shape[1]
    grad_local = gradients[0]
    owner_list = owners[0, :, 0]
    total_blocks = owner_list.shape[0]
    adam_dir = grad_local.astype(jnp.float32) / (jnp.sqrt(second_moment[0]) + ADAM_EPS)
    block_sq = jnp.sum(adam_dir * adam_dir, axis=(1, 2))
    global_sq = lax.psum(jnp.sum(block_sq), ("fsdp", "layer"))
    entry_count = float(total_blocks * lax.axis_size("layer") * block_side * block_side)
    clip_factor = jnp.minimum(1.0, UPDATE_RMS / jnp.sqrt(global_sq / entry_count))
    owner_hot, home_hot, slot_hot = selection_tables(
        owner_list, owner_count, blocks, slots_here, my_index
    )
    first_row = my_index * blocks
    my_owner_hot = lax.dynamic_slice_in_dim(owner_hot, first_row, blocks, 0).astype(jnp.bfloat16)
    outgoing = jnp.einsum(
        "jo,jxy->oxy", my_owner_hot, grad_local, preferred_element_type=jnp.float32
    ).astype(jnp.bfloat16)
    received = lax.all_to_all(outgoing, "fsdp", split_axis=0, concat_axis=0, tiled=True)
    pick_table = jnp.einsum("bs,bh->sh", slot_hot, home_hot).astype(jnp.bfloat16)
    gathered = jnp.einsum(
        "sh,hxy->sxy", pick_table, received, preferred_element_type=jnp.float32
    ).astype(jnp.bfloat16)
    preconditioned, new_left, new_right = owner_work(
        gathered, left_stats, right_stats, left_root, right_root
    )
    answers = jnp.einsum(
        "sh,sxy->hxy", pick_table, preconditioned, preferred_element_type=jnp.float32
    ).astype(jnp.bfloat16)
    returned = lax.all_to_all(answers, "fsdp", split_axis=0, concat_axis=0, tiled=True)
    home_blocks = jnp.einsum(
        "jo,oxy->jxy", my_owner_hot, returned, preferred_element_type=jnp.float32
    )
    pre_float = home_blocks.astype(jnp.bfloat16).astype(jnp.float32)
    graft_ratio = jnp.sqrt(block_sq / float(block_side * block_side)) / jnp.sqrt(
        jnp.sum(pre_float * pre_float, axis=(1, 2)) / float(block_side * block_side) + NORM_FLOOR
    )
    update = (pre_float * (graft_ratio * clip_factor)[:, None, None]).astype(jnp.bfloat16)
    return (update[None], new_left, new_right)


def solution(mesh):
    return jax.shard_map(
        per_device,
        mesh=mesh,
        in_specs=(
            P("layer", "fsdp", None, None),
            P("layer", "fsdp", None, None),
            P("layer", None, None),
            P("layer", "fsdp", None, None),
            P("layer", "fsdp", None, None),
            P("layer", "fsdp", None, None),
            P("layer", "fsdp", None, None),
        ),
        out_specs=(
            P("layer", "fsdp", None, None),
            P("layer", "fsdp", None, None),
            P("layer", "fsdp", None, None),
        ),
        check_vma=False,
    )
```

profile of v0, /device:TPU:0, one launch (start us, length us, event | category | flops | bytes accessed | tf_op | source)
XLA Modules:
  0.0 105.8 jit_solution(2701510871258278394)
XLA Ops:
  0.6 0.0 copy-start
  0.7 0.8 iota_compare_fusion.3
  1.5 2.0 %fusion.13 = bf16[8,256,256]{2,0,1:T(8,128)(2,1)S(1)} fusion(bf16[8,256,256]{2,1,0:T(8,128)(2,1)} %bitcast.49, pred[64,8]{1,0:T(8,128)(4,1)S(1)} %iota_compare_fusion.3, s32[]{:T(128)S(6)} %select_n.12), kind=kOutput, calls=%fused_computation.25 | convolution fusion | flops 8388736 | bytes 2098180 | tf_op jit(solution)/shard_map/jo,jxy->oxy/dot_general | solution.py:64
  3.4 0.0 copy-start.2
  3.5 1.2 %copy.41 = bf16[8,256,256]{2,1,0:T(8,128)(2,1)} copy(bf16[8,256,256]{2,0,1:T(8,128)(2,1)S(1)} %fusion.13) | data formatting | bytes 2097152 | tf_op jit(solution)/shard_map/jo,jxy->oxy/dot_general | solution.py:64
  4.6 7.3 %all-to-all-start = ((bf16[8,256,256]{2,1,0:T(8,128)(2,1)}), bf16[8,256,256]{2,1,0:T(8,128)(2,1)S(1)}, u32[]{:S(2)}, u32[]{:S(2)}) async-start(bf16[8,256,256]{2,1,0:T(8,128)(2,1)} %copy.41), calls=%async_computation | async-start | bytes 2097152 | tf_op jit(solution)/shard_map/all_to_all | solution.py:67
  11.9 0.0 copy-done.2
  11.9 0.3 fusion.5
  12.2 0.2 fusion.6
  12.5 25.2 %all-to-all-done = bf16[8,256,256]{2,1,0:T(8,128)(2,1)S(1)} async-done(((bf16[8,256,256]{2,1,0:T(8,128)(2,1)}), bf16[8,256,256]{2,1,0:T(8,128)(2,1)S(1)}, u32[]{:S(2)}, u32[]{:S(2)}) %all-to-all-start) | async-done | bytes 1048608 | tf_op jit(solution)/shard_map/all_to_all | solution.py:67
  37.6 0.7 convolution_convert_fusion.3
  38.3 0.8 copy.19
  39.1 0.0 copy-done
  39.2 2.9 %convolution_convert_fusion.1 = bf16[8,256,256]{2,1,0:T(8,128)(2,1)} fusion(bf16[8,256,256]{1,2,0:T(8,128)(2,1)S(1)} %copy.19, bf16[1,8,256,256]{3,2,1,0:T(8,128)(2,1)S(1)} %copy-done, bf16[1,8,256,256]{3,2,1,0:T(8,128)(2,1)} %param.12), kind=kOutput, calls=%fused_computation.13 | convolution fusion | flops 537919488 | bytes 4194304 | tf_op jit(solution)/shard_map/sij,sjk->sik/dot_general | solution.py:39
  42.1 1.9 %fusion.11 = bf16[8,256,256]{2,0,1:T(8,128)(2,1)S(1)} fusion(bf16[8,8,1]{1,0,2:T(8,128)(2,1)S(1)} %fusion.6, bf16[8,256,256]{2,1,0:T(8,128)(2,1)} %convolution_convert_fusion.1), kind=kOutput, calls=%fused_computation.23 | convolution fusion | flops 8388608 | bytes 2097280 | tf_op jit(solution)/shard_map/sh,sxy->hxy/dot_general | solution.py:75
  44.0 1.2 %copy.40 = bf16[8,256,256]{2,1,0:T(8,128)(2,1)} copy(bf16[8,256,256]{2,0,1:T(8,128)(2,1)S(1)} %fusion.11) | data formatting | bytes 2097152 | tf_op jit(solution)/shard_map/sh,sxy->hxy/dot_general | solution.py:75
  45.2 4.2 %all-to-all-start.1 = ((bf16[8,256,256]{2,1,0:T(8,128)(2,1)}), bf16[8,256,256]{2,1,0:T(8,128)(2,1)}, u32[]{:S(2)}, u32[]{:S(2)}) async-start(bf16[8,256,256]{2,1,0:T(8,128)(2,1)} %copy.40), calls=%async_computation.1 | async-start | bytes 2097152 | tf_op jit(solution)/shard_map/all_to_all | solution.py:78
  49.5 3.9 %fusion.30 = (f32[]{:T(128)}, f32[8]{0:T(128)S(1)}) fusion(f32[1,8,256,256]{3,2,1,0:T(8,128)} %param.8, bf16[1,8,256,256]{3,2,1,0:T(8,128)(2,1)} %param.7), kind=kLoop, calls=%fused_computation.51 | loop fusion | flops 3145719 | bytes 3145764 | tf_op jit(solution)/shard_map/reduce_sum | solution.py:56
  53.4 42.4 %psum.7 = f32[]{:T(128)} all-reduce(f32[]{:T(128)} %get-tuple-element.9), channel_id=1, replica_groups=mesh['fsdp'=8,'layer'=4] {'fsdp','layer'}, use_global_device_ids=true, to_apply=%region_4.5 | all-reduce | flops 1 | bytes 8 | tf_op jit(solution)/shard_map/psum | solution.py:56
  96.5 0.0 copy-start.1
  96.5 3.7 %fusion.3 = f32[1,8,256,256]{3,2,1,0:T(8,128)} fusion(f32[1,8,256,256]{3,2,1,0:T(8,128)} %param.10, bf16[8,256,256]{2,0,1:T(8,128)(2,1)S(1)} %convolution_convert_fusion.3), kind=kOutput, calls=%fused_computation.7 | convolution fusion | flops 270008320 | bytes 5242880 | tf_op jit(solution)/shard_map/sij,skj->sik/dot_general | solution.py:32
  100.2 0.0 copy-done.1
  100.2 1.9 %fusion.2 = f32[1,8,256,256]{3,2,1,0:T(8,128)} fusion(f32[1,8,256,256]{3,2,1,0:T(8,128)S(1)} %copy-done.1, bf16[8,256,256]{1,2,0:T(8,128)(2,1)S(1)} %copy.19, bf16[8,256,256]{2,0,1:T(8,128)(2,1)S(1)} %convolution_convert_fusion.3), kind=kOutput, calls=%fused_computation.5 | convolution fusion | flops 270008320 | bytes 6291456 | tf_op jit(solution)/shard_map/sji,sjk->sik/dot_general | solution.py:33
  102.1 0.0 all-to-all-done.1
  102.1 2.1 %fusion = (f32[8]{0:T(128)S(1)}, bf16[8,256,256]{2,0,1:T(8,128)(2,1)S(1)}) fusion(bf16[8,256,256]{2,1,0:T(8,128)(2,1)} %all-to-all-done.1, pred[64,8]{1,0:T(8,128)(4,1)S(1)} %iota_compare_fusion.3, s32[]{:T(128)S(6)} %select_n.12), kind=kOutput, calls=%fused_computation.2 | convolution fusion | flops 10485880 | bytes 2098212 | tf_op jit(solution)/shard_map/jo,oxy->jxy/dot_general | solution.py:79
  104.2 0.5 fusion.7
  104.7 1.2 %copy.21 = bf16[1,8,256,256]{3,2,1,0:T(8,128)(2,1)} copy(bf16[1,8,256,256]{3,1,2,0:T(8,128)(2,1)S(1)} %fusion.7) | data formatting | bytes 2097152
  (3 shorter events, 0.0 us)
Async XLA Ops:
  0.6 38.5 %copy-start = (bf16[1,8,256,256]{3,2,1,0:T(8,128)(2,1)S(1)}, bf16[1,8,256,256]{3,2,1,0:T(8,128)(2,1)}, u32[]{:S(2)}) copy-start(bf16[1,8,256,256]{3,2,1,0:T(8,128)(2,1)} %param.13) | copy-start | bytes 3145732
  3.4 8.4 %copy-start.2 = (s32[1,64,1]{1,2,0:T(1,128)S(1)}, s32[1,64,1]{1,2,0:T(1,128)}, u32[]{:S(2)}) copy-start(s32[1,64,1]{1,2,0:T(1,128)} %param.9) | copy-start | bytes 772
  4.6 33.0 %all-to-all-start = ((bf16[8,256,256]{2,1,0:T(8,128)(2,1)}), bf16[8,256,256]{2,1,0:T(8,128)(2,1)S(1)}, u32[]{:S(2)}, u32[]{:S(2)}) async-start(bf16[8,256,256]{2,1,0:T(8,128)(2,1)} %copy.41), calls=%async_computation | async-start | bytes 2097152 | tf_op jit(solution)/shard_map/all_to_all | solution.py:67
  45.2 56.9 %all-to-all-start.1 = ((bf16[8,256,256]{2,1,0:T(8,128)(2,1)}), bf16[8,256,256]{2,1,0:T(8,128)(2,1)}, u32[]{:S(2)}, u32[]{:S(2)}) async-start(bf16[8,256,256]{2,1,0:T(8,128)(2,1)} %copy.40), calls=%async_computation.1 | async-start | bytes 2097152 | tf_op jit(solution)/shard_map/all_to_all | solution.py:78
  96.5 3.7 %copy-start.1 = (f32[1,8,256,256]{3,2,1,0:T(8,128)S(1)}, f32[1,8,256,256]{3,2,1,0:T(8,128)}, u32[]{:S(2)}) copy-start(f32[1,8,256,256]{3,2,1,0:T(8,128)} %param.11) | copy-start | bytes 6291460
where the time goes:
time: 106 us
  blocking collectives  42.4 us (40%)
  waiting for transfers between devices  25.2 us (24%)
  matrix products  15.7 us (15%)
  starting transfers between devices  11.5 us (11%)
  other arithmetic  5.24 us (5%)
  local copies, waits for them, and re-layouts  4.35 us (4%)
  between operations  1.45 us (1%)
    psum x1, blocking collectives, per_device(): global_sq = lax.psum(jnp.sum(block_sq), ('fsdp', 'layer'))  42.4 us
    all_to_all x1, waiting for transfers between devices, per_device(): lax.all_to_all(outgoing, 'fsdp', split_axis=0, concat_axis=0, tiled=True)  25.2 us
    all_to_all x1, starting transfers between devices, per_device(): lax.all_to_all(outgoing, 'fsdp', split_axis=0, concat_axis=0, tiled=True)  7.25 us
    all_to_all x1, starting transfers between devices, per_device(): lax.all_to_all(answers, 'fsdp', split_axis=0, concat_axis=0, tiled=True)  4.23 us
    reduce_sum x1, other arithmetic, per_device(): global_sq = lax.psum(jnp.sum(block_sq), ('fsdp', 'layer'))  3.92 us
    dot_general x1, matrix products, owner_work(): jnp.einsum('sij,skj->sik', gathered, gathered, preferred_element_type=jnp...  3.71 us
    dot_general x1, matrix products, owner_work(): jnp.einsum('sij,sjk->sik', half_done, right_root[0], preferred_element_ty...  2.94 us
  transfers between devices with their start and end apart: 2, of which 1 were waited for; matrix products, arithmetic and copies ran while one was open for 10% of the time, Pallas kernels for 0%

commit v1 on v0

--- a/solution.py
+++ b/solution.py
@@ -1,6 +1,10 @@
+import functools
+
 import jax
 import jax.numpy as jnp
 from jax import lax
+from jax.experimental import pallas as pl
+from jax.experimental.pallas import tpu as pltpu
 from jax.sharding import PartitionSpec as P
 
 ADAM_EPS = 1e-08
@@ -42,7 +46,7 @@
     return (preconditioned, new_left[None], new_right[None])
 
 
-def per_device(gradients, second_moment, owners, left_stats, right_stats, left_root, right_root):
+def per_device_general(gradients, second_moment, owners, left_stats, right_stats, left_root, right_root):
     owner_count = lax.axis_size("fsdp")
     my_index = lax.axis_index("fsdp")
     blocks = gradients.shape[1]
@@ -87,6 +91,306 @@
     return (update[None], new_left, new_right)
 
 
+TAIL = 16
+
+
+def kernel_params(mebibytes):
+    return pltpu.CompilerParams(vmem_limit_bytes=mebibytes * 2**20)
+
+
+def home_slot(named, target):
+    block = jnp.int32(0)
+    for j in range(1, len(named)):
+        block = jnp.where(named[j] == target, jnp.int32(j), block)
+    return block
+
+
+def route_kernel(order, owners_hbm, me_ref, grad_hbm, *refs):
+    outs, (owners_ref, held, owner_sem, grad_sem) = refs[:-4], refs[-4:]
+    count = held.shape[0]
+    me = me_ref[0]
+    fetch_owners = pltpu.make_async_copy(owners_hbm, owners_ref, owner_sem)
+    fetch_grads = pltpu.make_async_copy(grad_hbm.at[0], held, grad_sem)
+    fetch_owners.start()
+    fetch_grads.start()
+    fetch_owners.wait()
+    named = [owners_ref[me * count + j] for j in range(count)]
+    blocks = [home_slot(named, me ^ m) for m in order]
+    fetch_grads.wait()
+    for block, out in zip(blocks, outs):
+        out[...] = held[block]
+
+
+def route(order, owner_list, me, gradients):
+    count, side = gradients.shape[1], gradients.shape[3]
+    hbm = pl.BlockSpec(memory_space=pltpu.HBM)
+    piece = jax.ShapeDtypeStruct((side, side), gradients.dtype)
+    return pl.pallas_call(
+        functools.partial(route_kernel, order),
+        in_specs=[hbm, pl.BlockSpec(memory_space=pltpu.SMEM), hbm],
+        out_specs=[pl.BlockSpec(memory_space=pltpu.VMEM)] * count,
+        scratch_shapes=[
+            pltpu.SMEM(owner_list.shape, jnp.int32),
+            pltpu.VMEM((count, side, side), gradients.dtype),
+            pltpu.SemaphoreType.DMA,
+            pltpu.SemaphoreType.DMA,
+        ],
+        out_shape=[piece] * count,
+        compiler_params=kernel_params(6),
+        cost_estimate=pl.CostEstimate(
+            flops=0, bytes_accessed=4 * count * side * side, transcendentals=0
+        ),
+    )(
+        pltpu.with_memory_space_constraint(owner_list, pltpu.HBM),
+        me,
+        pltpu.with_memory_space_constraint(gradients, pltpu.HBM),
+    )
+
+
+def adam_kernel(grad_hbm, moment_hbm, out_ref, total_ref, grads, moments, sems):
+    count, side = grads.shape[0], grads.shape[2]
+    lanes = out_ref.shape[1]
+    copies = []
+    for b in range(count):
+        pair = (
+            pltpu.make_async_copy(grad_hbm.at[0, b], grads.at[b], sems.at[0, b]),
+            pltpu.make_async_copy(moment_hbm.at[0, b], moments.at[b], sems.at[1, b]),
+        )
+        for copy in pair:
+            copy.start()
+        copies.append(pair)
+    total = jnp.zeros((1, lanes), jnp.float32)
+    for b, pair in enumerate(copies):
+        for copy in pair:
+            copy.wait()
+        adam_dir = grads[b].astype(jnp.float32) / (jnp.sqrt(moments[b]) + ADAM_EPS)
+        squares = jnp.sum(adam_dir * adam_dir, axis=0, keepdims=True)
+        row = squares[:, 0:lanes]
+        for k in range(lanes, side, lanes):
+            row = row + squares[:, k : k + lanes]
+        out_ref[b : b + 1, :] = row
+        total = total + row
+    total_ref[...] = jnp.broadcast_to(total, total_ref.shape)
+
+
+def adam_squares(gradients, second_moment):
+    count, side = gradients.shape[1], gradients.shape[3]
+    hbm = pl.BlockSpec(memory_space=pltpu.HBM)
+    return pl.pallas_call(
+        adam_kernel,
+        in_specs=[hbm, hbm],
+        out_specs=[pl.BlockSpec(memory_space=pltpu.VMEM)] * 2,
+        out_shape=[
+            jax.ShapeDtypeStruct((count, 128), jnp.float32),
+            jax.ShapeDtypeStruct((8, 128), jnp.float32),
+        ],
+        scratch_shapes=[
+            pltpu.VMEM((count, side, side), gradients.dtype),
+            pltpu.VMEM((count, side, side), second_moment.dtype),
+            pltpu.SemaphoreType.DMA((2, count)),
+        ],
+        compiler_params=kernel_params(8),
+        cost_estimate=pl.CostEstimate(
+            flops=8 * count * side * side,
+            bytes_accessed=6 * count * side * side,
+            transcendentals=2 * count * side * side,
+        ),
+    )(
+        pltpu.with_memory_space_constraint(gradients, pltpu.HBM),
+        pltpu.with_memory_space_constraint(second_moment, pltpu.HBM),
+    )
+
+
+def tail_kernel(total_ref, out_ref):
+    total = jnp.sum(total_ref[0:1, :], keepdims=True)
+    high = total.astype(jnp.bfloat16).astype(jnp.float32)
+    rest = total - high
+    middle = rest.astype(jnp.bfloat16).astype(jnp.float32)
+    low = rest - middle
+    row = lax.broadcasted_iota(jnp.int32, out_ref.shape, 0)
+    value = jnp.where(row == 0, high, jnp.where(row == 1, middle, jnp.where(row == 2, low, 0.0)))
+    out_ref[...] = value.astype(jnp.bfloat16)
+
+
+def sum_tail(total, side):
+    return pl.pallas_call(
+        tail_kernel,
+        in_specs=[pl.BlockSpec(memory_space=pltpu.VMEM)],
+        out_specs=pl.BlockSpec(memory_space=pltpu.VMEM),
+        out_shape=jax.ShapeDtypeStruct((TAIL, side), jnp.bfloat16),
+        compiler_params=kernel_params(2),
+        cost_estimate=pl.CostEstimate(flops=4096, bytes_accessed=32768, transcendentals=0),
+    )(total)
+
+
+def precondition_kernel(m, me_ref, grad_ref, left_ref, right_ref, tail_ref, out_ref):
+    side = grad_ref.shape[0]
+    slot = me_ref[0] ^ m
+    half_done = jnp.dot(
+        left_ref[0, slot], grad_ref[...], preferred_element_type=jnp.float32
+    ).astype(jnp.bfloat16)
+    out_ref[0:side, :] = jnp.dot(
+        half_done, right_ref[0, slot], preferred_element_type=jnp.float32
+    ).astype(jnp.bfloat16)
+    out_ref[side:, :] = tail_ref[...]
+
+
+def precondition(m, me, block, left_root, right_root, tail):
+    side = block.shape[0]
+    return pl.pallas_call(
+        functools.partial(precondition_kernel, m),
+        grid_spec=pltpu.PrefetchScalarGridSpec(
+            num_scalar_prefetch=1,
+            grid=(),
+            in_specs=[pl.BlockSpec(memory_space=pltpu.VMEM)] * 4,
+            out_specs=pl.BlockSpec(memory_space=pltpu.VMEM),
+        ),
+        out_shape=jax.ShapeDtypeStruct((side + TAIL, side), jnp.bfloat16),
+        compiler_params=kernel_params(6),
+        cost_estimate=pl.CostEstimate(
+            flops=4 * side**3, bytes_accessed=8 * side * side, transcendentals=0
+        ),
+    )(me, block, left_root, right_root, tail)
+
+
+def gram_kernel(order, me_ref, *refs):
+    count = len(refs) - 4
+    grads = refs[:count]
+    left_ref, right_ref, new_left_ref, new_right_ref = refs[count:]
+    step = pl.program_id(0)
+    for k, m in enumerate(order):
+
+        @pl.when(step == m)
+        def _():
+            block = grads[k][...]
+            gram_left = lax.dot_general(
+                block, block, (((1,), (1,)), ((), ())), preferred_element_type=jnp.float32
+            )
+            gram_right = lax.dot_general(
+                block, block, (((0,), (0,)), ((), ())), preferred_element_type=jnp.float32
+            )
+            new_left_ref[0, 0] = DECAY_RATE * left_ref[0, 0] + (1.0 - DECAY_RATE) * gram_left
+            new_right_ref[0, 0] = DECAY_RATE * right_ref[0, 0] + (1.0 - DECAY_RATE) * gram_right
+
+
+def gram_update(order, me, blocks, left_stats, right_stats):
+    count, side = len(blocks), blocks[0].shape[0]
+    stat = pl.BlockSpec((1, 1, side, side), lambda i, me_ref: (0, me_ref[0] ^ i, 0, 0))
+    whole = pl.BlockSpec(memory_space=pltpu.VMEM)
+    return pl.pallas_call(
+        functools.partial(gram_kernel, order),
+        grid_spec=pltpu.PrefetchScalarGridSpec(
+            num_scalar_prefetch=1,
+            grid=(count,),
+            in_specs=[whole] * count + [stat, stat],
+            out_specs=[stat, stat],
+        ),
+        out_shape=[
+            jax.ShapeDtypeStruct(left_stats.shape, left_stats.dtype),
+            jax.ShapeDtypeStruct(right_stats.shape, right_stats.dtype),
+        ],
+        compiler_params=kernel_params(12),
+        cost_estimate=pl.CostEstimate(
+            flops=4 * count * side**3, bytes_accessed=18 * count * side * side, transcendentals=0
+        ),
+    )(me, *blocks, left_stats, right_stats)
+
+
+def finish_kernel(order, entries, owners_ref, me_ref, *refs):
+    count = len(order)
+    pieces = refs[:count]
+    squares_ref, out_ref, held, sems = refs[count:]
+    side = out_ref.shape[3]
+    me = me_ref[0]
+    named = [owners_ref[me * count + j] for j in range(count)]
+    global_sq = jnp.zeros((1, 1), jnp.float32)
+    for piece in pieces:
+        terms = piece[side:, 0:1].astype(jnp.float32)
+        global_sq = global_sq + jnp.sum(terms, axis=0, keepdims=True)
+    clip_factor = jnp.minimum(1.0, UPDATE_RMS / jnp.sqrt(global_sq / entries))
+    area = float(side * side)
+    copies = []
+    for k, m in enumerate(order):
+        block = home_slot(named, me ^ m)
+        pre_float = pieces[k][0:side, :].astype(jnp.float32)
+        pre_sq = jnp.sum(pre_float * pre_float, keepdims=True)
+        block_sq = jnp.sum(squares_ref[pl.ds(block, 1), :], axis=1, keepdims=True)
+        graft_ratio = jnp.sqrt(block_sq / area) / jnp.sqrt(pre_sq / area + NORM_FLOOR)
+        held[k] = (pre_float * (graft_ratio * clip_factor)).astype(jnp.bfloat16)
+        copy = pltpu.make_async_copy(held.at[k], out_ref.at[0, block], sems.at[k])
+        copy.start()
+        copies.append(copy)
+    for copy in copies:
+        copy.wait()
+
+
+def finish(order, owner_list, me, pieces, squares, entries):
+    count, side = len(pieces), pieces[0].shape[1]
+    return pl.pallas_call(
+        functools.partial(finish_kernel, order, entries),
+        grid_spec=pltpu.PrefetchScalarGridSpec(
+            num_scalar_prefetch=2,
+            grid=(),
+            in_specs=[pl.BlockSpec(memory_space=pltpu.VMEM)] * (count + 1),
+            out_specs=pl.BlockSpec(memory_space=pl.ANY),
+            scratch_shapes=[
+                pltpu.VMEM((count, side, side), jnp.bfloat16),
+                pltpu.SemaphoreType.DMA((count,)),
+            ],
+        ),
+        out_shape=jax.ShapeDtypeStruct((1, count, side, side), jnp.bfloat16),
+        compiler_params=kernel_params(8),
+        cost_estimate=pl.CostEstimate(
+            flops=6 * count * side * side, bytes_accessed=4 * count * side * side, transcendentals=0
+        ),
+    )(owner_list, me, *pieces, squares)
+
+
+def per_device_exchange(
+    gradients, second_moment, owners, left_stats, right_stats, left_root, right_root
+):
+    count = lax.axis_size("fsdp")
+    layers = lax.axis_size("layer")
+    side = gradients.shape[3]
+    me = lax.axis_index("fsdp").astype(jnp.int32).reshape(1)
+    owner_list = owners[0, :, 0]
+    order = list(range(count))
+
+    def swap(value, m):
+        if m == 0:
+            return value
+        return lax.ppermute(value, "fsdp", [(i, i ^ m) for i in range(count)])
+
+    outgoing = route(order, owner_list, me, gradients)
+    received = {m: swap(outgoing[m], m) for m in order}
+    squares, total = adam_squares(gradients, second_moment)
+    k = 1
+    while k < layers:
+        total = total + lax.ppermute(total, "layer", [(i, i ^ k) for i in range(layers)])
+        k *= 2
+    tail = sum_tail(total, side)
+    returned = {
+        m: swap(precondition(m, me, received[m], left_root, right_root, tail), m) for m in order
+    }
+    new_left, new_right = gram_update(
+        order, me, [received[m] for m in order], left_stats, right_stats
+    )
+    entries = float(owner_list.shape[0] * layers * side * side)
+    update = finish(order, owner_list, me, [returned[m] for m in order], squares, entries)
+    return (update, new_left, new_right)
+
+
+def per_device(gradients, second_moment, owners, left_stats, right_stats, left_root, right_root):
+    owner_count, blocks, slots = lax.axis_size("fsdp"), gradients.shape[1], left_stats.shape[1]
+    layers = lax.axis_size("layer")
+    paired = owner_count == blocks == slots
+    paired = paired and owner_count & (owner_count - 1) == 0 and layers & (layers - 1) == 0
+    body = per_device_exchange if paired else per_device_general
+    return body(
+        gradients, second_moment, owners, left_stats, right_stats, left_root, right_root
+    )
+
+
 def solution(mesh):
     return jax.shard_map(
         per_device,

time: 106 us -> 56.6 us (0.53)
  blocking collectives: 42.4 us -> 0 us
  starting transfers between devices: 11.5 us -> 27.6 us
  matrix products: 15.7 us -> 0 us
  Pallas kernels: 0 us -> 13.4 us
  waiting for transfers between devices: 25.2 us -> 14.6 us
  other arithmetic: 5.24 us -> 0.01 us
  local copies, waits for them, and re-layouts: 4.35 us -> 0.03 us
    psum x1 -> x0, blocking collectives: 42.4 us -> none  [per_device(): global_sq = lax.psum(jnp.sum(block_sq), ('fsdp', 'layer'))]
    ppermute x0 -> x16, starting transfers between devices: none -> 27.6 us  [the longest x14 26 us: swap(): return lax.ppermute(value, 'fsdp', [(i, i ^ m) for i in range(count)])]
    all_to_all x2 -> x0, waiting for transfers between devices: 25.2 us -> none  [the longest x1 25.2 us: per_device(): lax.all_to_all(outgoing, 'fsdp', split_axis=0, concat_axis=0, tiled=True)]
    dot_general x9 -> x0, matrix products: 15.7 us -> none  [the longest x1 3.71 us: owner_work(): jnp.einsum('sij,skj->sik', gathered, gathered, preferred_element_type=jnp...]
    ppermute x0 -> x16, waiting for transfers between devices: none -> 14.6 us  [the longest x14 11.3 us: swap(): return lax.ppermute(value, 'fsdp', [(i, i ^ m) for i in range(count)])]
    pallas_call x0 -> x13, Pallas kernels: none -> 13.4 us  [the longest x1 4.68 us: gram_update(): pl.pallas_call(functools.partial(gram_kernel, order), grid_spec=pltpu.Pre...]
    all_to_all x2 -> x0, starting transfers between devices: 11.5 us -> none  [the longest x1 7.25 us: per_device(): lax.all_to_all(outgoing, 'fsdp', split_axis=0, concat_axis=0, tiled=True)]
    reduce_sum x1 -> x0, other arithmetic: 3.92 us -> none  [per_device(): global_sq = lax.psum(jnp.sum(block_sq), ('fsdp', 'layer'))]
  transfers between devices with their start and end apart: 2 -> 16, of which waited for: 1 -> 5; matrix products, arithmetic and copies ran while one was open for 10% -> 0% of each run, Pallas kernels for 0% -> 18%
where the time goes in v1:
time: 56.6 us; the launch traced here: 56.5 us
  starting transfers between devices  27.6 us (49%)
  waiting for transfers between devices  14.6 us (26%)
  Pallas kernels  13.4 us (24%)
  between operations  0.84 us (1%)
    ppermute x14, starting transfers between devices, swap(): return lax.ppermute(value, 'fsdp', [(i, i ^ m) for i in range(count)])  26 us
    ppermute x14, waiting for transfers between devices, swap(): return lax.ppermute(value, 'fsdp', [(i, i ^ m) for i in range(count)])  11.3 us
    pallas_call x1, Pallas kernels, gram_update(): pl.pallas_call(functools.partial(gram_kernel, order), grid_spec=pltpu.Pre...  4.68 us
    ppermute x2, waiting for transfers between devices, per_device_exchange(): lax.ppermute(total, 'layer', [(i, i ^ k) for i in range(layers)])  3.24 us
    pallas_call x8, Pallas kernels, precondition(): pl.pallas_call(functools.partial(precondition_kernel, m), grid_spec=pltpu...  2.63 us
    pallas_call x1, Pallas kernels, adam_squares(): pl.pallas_call(adam_kernel, in_specs=[hbm, hbm], out_specs=[pl.BlockSpec(...  2.53 us
    pallas_call x1, Pallas kernels, finish(): pl.pallas_call(functools.partial(finish_kernel, order, entries), grid_spe...  1.97 us
    ppermute x2, starting transfers between devices, per_device_exchange(): lax.ppermute(total, 'layer', [(i, i ^ k) for i in range(layers)])  1.59 us
  transfers between devices with their start and end apart: 16, of which 5 were waited for; matrix products, arithmetic and copies ran while one was open for 0% of the time, Pallas kernels for 18%

profile of v1, /device:TPU:0, one launch (start us, length us, event | category | flops | bytes accessed | tf_op | source)
XLA Modules:
  0.0 56.5 jit_solution(2917969703848577685)
XLA Ops:
  0.7 1.5 %shard_map.94 = (bf16[256,256]{1,0:T(8,128)(2,1)S(1)}, bf16[256,256]{1,0:T(8,128)(2,1)S(1)}, bf16[256,256]{1,0:T(8,128)(2,1)S(1)}, bf16[256,256]{1,0:T(8,128)(2,...) custom-call(s32[64]{0:T(128)} %bitcast.2, ...), custom_call_target="tpu_custom_call" | custom-call | bytes 2097152 | tf_op jit(solution)/shard_map/pallas_call | solution.py:128
  2.1 6.0 %collective-permute-start.14 = (bf16[256,256]{1,0:T(8,128)(2,1)S(1)}, bf16[256,256]{1,0:T(8,128)(2,1)S(1)}, u32[]{:S(2)}, u32[]{:S(2)}) collective-permute-start(bf16[256,256]{1,0:T(8,128)(2,1)S(1)} %get-tuple-element.23), channel_id=1, source_target_pairs={{0,28},{4,24},{8,20},{12,16},{16,12},{20,8},{24,4},{28,0},{1,29},{... | collective-permute-start | bytes 393224 | tf_op jit(solution)/shard_map/ppermute | solution.py:362
  8.2 0.2 collective-permute-start.12
  8.4 0.4 collective-permute-start.2
  8.8 1.8 %collective-permute-start.10 = (bf16[256,256]{1,0:T(8,128)(2,1)S(1)}, bf16[256,256]{1,0:T(8,128)(2,1)S(1)}, u32[]{:S(2)}, u32[]{:S(2)}) collective-permute-start(bf16[256,256]{1,0:T(8,128)(2,1)S(1)} %get-tuple-element.21), channel_id=1, source_target_pairs={{0,20},{4,16},{8,28},{12,24},{16,4},{20,0},{24,12},{28,8},{1,21},{... | collective-permute-start | bytes 393224 | tf_op jit(solution)/shard_map/ppermute | solution.py:362
  10.6 2.5 %shard_map.95 = (f32[8,128]{1,0:T(8,128)S(1)}, f32[8,128]{1,0:T(8,128)S(1)}) custom-call(bf16[1,8,256,256]{3,2,1,0:T(8,128)(2,1)} %grad_hbm.3, f32[1,8,256,256]{3,2,1,0:T(8,128)} %moment_hbm.1), custom_call_target="tpu_custom_call" | custom-call | flops 4194304 | bytes 3145728 | tf_op jit(solution)/shard_map/pallas_call | solution.py:179
  13.2 0.1 collective-permute-start
  13.3 1.2 %collective-permute-done = f32[8,128]{1,0:T(8,128)S(1)} collective-permute-done((f32[8,128]{1,0:T(8,128)S(1)}, f32[8,128]{1,0:T(8,128)S(1)}, u32[]{:S(2)}, u32[]{:S(2)}) %collective-permute-start) | collective-permute-done | bytes 4128 | tf_op jit(solution)/shard_map/ppermute | solution.py:369
  14.4 1.5 %collective-permute-start.1 = (f32[8,128]{1,0:T(8,128)S(1)}, f32[8,128]{1,0:T(8,128)S(1)}, u32[]{:S(2)}, u32[]{:S(2)}) collective-permute-start(f32[8,128]{1,0:T(8,128)S(1)} %add.6), channel_id=1, source_target_pairs={{0,2},{1,3},{2,0},{3,1},{4,6},{5,7},{6,4},{7,5},{8,10},{9,11},{10,... | collective-permute-start | bytes 12296 | tf_op jit(solution)/shard_map/ppermute | solution.py:369
  15.9 2.1 %collective-permute-done.1 = f32[8,128]{1,0:T(8,128)S(1)} collective-permute-done((f32[8,128]{1,0:T(8,128)S(1)}, f32[8,128]{1,0:T(8,128)S(1)}, u32[]{:S(2)}, u32[]{:S(2)}) %collective-permute-start.1) | collective-permute-done | bytes 4128 | tf_op jit(solution)/shard_map/ppermute | solution.py:369
  18.0 3.3 %collective-permute-start.6 = (bf16[256,256]{1,0:T(8,128)(2,1)S(1)}, bf16[256,256]{1,0:T(8,128)(2,1)S(1)}, u32[]{:S(2)}, u32[]{:S(2)}) collective-permute-start(bf16[256,256]{1,0:T(8,128)(2,1)S(1)} %get-tuple-element.19), channel_id=1, source_target_pairs={{0,12},{4,8},{8,4},{12,0},{16,28},{20,24},{24,20},{28,16},{1,13},{... | collective-permute-start | bytes 393224 | tf_op jit(solution)/shard_map/ppermute | solution.py:362
  21.4 0.1 shard_map.96.tail_ref
  21.5 0.0 collective-permute-done.14.grad_ref.refs_7_
  21.5 0.4 collective-permute-start.8
  21.9 0.3 shard_map.104
  22.3 0.0 collective-permute-done.12.grad_ref.refs_6_
  22.3 2.1 %collective-permute-start.15 = (bf16[272,256]{1,0:T(8,128)(2,1)S(1)}, bf16[272,256]{1,0:T(8,128)(2,1)S(1)}, u32[]{:S(2)}, u32[]{:S(2)}) collective-permute-start(bf16[272,256]{1,0:T(8,128)(2,1)S(1)} %shard_map.104), channel_id=1, source_target_pairs={{0,28},{4,24},{8,20},{12,16},{16,12},{20,8},{24,4},{28,0},{1,29},{... | collective-permute-start | bytes 417800 | tf_op jit(solution)/shard_map/ppermute | solution.py:362
  24.4 0.3 shard_map.103
  24.7 0.0 collective-permute-done.2.grad_ref.refs_1_
  24.7 2.8 %collective-permute-start.13 = (bf16[272,256]{1,0:T(8,128)(2,1)S(1)}, bf16[272,256]{1,0:T(8,128)(2,1)S(1)}, u32[]{:S(2)}, u32[]{:S(2)}) collective-permute-start(bf16[272,256]{1,0:T(8,128)(2,1)S(1)} %shard_map.103), channel_id=1, source_target_pairs={{0,24},{4,28},{8,16},{12,20},{16,8},{20,12},{24,0},{28,4},{1,25},{... | collective-permute-start | bytes 417800 | tf_op jit(solution)/shard_map/ppermute | solution.py:362
  27.5 5.0 %collective-permute-done.10.grad_ref.refs_5_ = bf16[256,256]{1,0:T(8,128)(2,1)S(1)} collective-permute-done((bf16[256,256]{1,0:T(8,128)(2,1)S(1)}, bf16[256,256]{1,0:T(8,128)(2,1)S(1)}, u32[]{:S(2)}, u32[]{:S(2)}) %collective-permute-start.10) | collective-permute-done | bytes 131104 | tf_op jit(solution)/shard_map/ppermute | solution.py:362
  32.5 0.3 collective-permute-start.4
  32.8 0.3 shard_map.98
  33.1 0.3 shard_map.102
  33.5 3.8 %collective-permute-done.8.grad_ref.refs_4_ = bf16[256,256]{1,0:T(8,128)(2,1)S(1)} collective-permute-done((bf16[256,256]{1,0:T(8,128)(2,1)S(1)}, bf16[256,256]{1,0:T(8,128)(2,1)S(1)}, u32[]{:S(2)}, u32[]{:S(2)}) %collective-permute-start.8) | collective-permute-done | bytes 131104 | tf_op jit(solution)/shard_map/ppermute | solution.py:362
  37.3 1.1 %collective-permute-start.11 = (bf16[272,256]{1,0:T(8,128)(2,1)S(1)}, bf16[272,256]{1,0:T(8,128)(2,1)S(1)}, u32[]{:S(2)}, u32[]{:S(2)}) collective-permute-start(bf16[272,256]{1,0:T(8,128)(2,1)S(1)} %shard_map.102), channel_id=1, source_target_pairs={{0,20},{4,16},{8,28},{12,24},{16,4},{20,0},{24,12},{28,8},{1,21},{... | collective-permute-start | bytes 417800 | tf_op jit(solution)/shard_map/ppermute | solution.py:362
  38.4 0.3 shard_map.101
  38.7 0.0 collective-permute-done.6.grad_ref.refs_3_
  38.7 1.5 %collective-permute-start.9 = (bf16[272,256]{1,0:T(8,128)(2,1)S(1)}, bf16[272,256]{1,0:T(8,128)(2,1)S(1)}, u32[]{:S(2)}, u32[]{:S(2)}) collective-permute-start(bf16[272,256]{1,0:T(8,128)(2,1)S(1)} %shard_map.101), channel_id=1, source_target_pairs={{0,16},{4,20},{8,24},{12,28},{16,0},{20,4},{24,8},{28,12},{1,17},{... | collective-permute-start | bytes 417800 | tf_op jit(solution)/shard_map/ppermute | solution.py:362
  40.2 0.3 shard_map.100
  40.5 0.0 copy-start.2
  40.5 0.0 copy-start.3
  40.6 0.0 collective-permute-done.4.grad_ref.refs_2_
  40.6 1.8 %collective-permute-start.7 = (bf16[272,256]{1,0:T(8,128)(2,1)S(1)}, bf16[272,256]{1,0:T(8,128)(2,1)S(1)}, u32[]{:S(2)}, u32[]{:S(2)}) collective-permute-start(bf16[272,256]{1,0:T(8,128)(2,1)S(1)} %shard_map.100), channel_id=1, source_target_pairs={{0,12},{4,8},{8,4},{12,0},{16,28},{20,24},{24,20},{28,16},{1,13},{... | collective-permute-start | bytes 417800 | tf_op jit(solution)/shard_map/ppermute | solution.py:362
  42.4 0.3 shard_map.99
  42.7 0.0 collective-permute-done.15.refs_7_
  42.7 2.2 %collective-permute-start.5 = (bf16[272,256]{1,0:T(8,128)(2,1)S(1)}, bf16[272,256]{1,0:T(8,128)(2,1)S(1)}, u32[]{:S(2)}, u32[]{:S(2)}) collective-permute-start(bf16[272,256]{1,0:T(8,128)(2,1)S(1)} %shard_map.99), channel_id=1, source_target_pairs={{0,8},{4,12},{8,0},{12,4},{16,24},{20,28},{24,16},{28,20},{1,9},{5... | collective-permute-start | bytes 417800 | tf_op jit(solution)/shard_map/ppermute | solution.py:362
  45.0 0.0 collective-permute-done.13.refs_6_
  45.0 1.9 %collective-permute-start.3 = (bf16[272,256]{1,0:T(8,128)(2,1)S(1)}, bf16[272,256]{1,0:T(8,128)(2,1)S(1)}, u32[]{:S(2)}, u32[]{:S(2)}) collective-permute-start(bf16[272,256]{1,0:T(8,128)(2,1)S(1)} %shard_map.98), channel_id=1, source_target_pairs={{0,4},{4,0},{8,12},{12,8},{16,20},{20,16},{24,28},{28,24},{1,5},{5... | collective-permute-start | bytes 417800 | tf_op jit(solution)/shard_map/ppermute | solution.py:362
  46.9 0.3 shard_map.97.refs_0_
  47.2 0.0 copy-start.4
  47.2 4.7 %shard_map.106 = (f32[1,8,256,256]{3,2,1,0:T(8,128)}, f32[1,8,256,256]{3,2,1,0:T(8,128)}) custom-call(s32[1]{0:T(128)} %bitcast.1.me_ref, bf16[256,256]{1,0:T(8,128)(2,1)S(1)} %get-tuple-element.15.grad_ref.refs_0_, bf16[256,256]{1,0:T(8,128)(2,1)S(1)} %collective-permute-done.2.grad_ref.refs_1_, ...), custom_call_target="tpu_custom_call" | custom-call | flops 536870912 | bytes 9437184 | tf_op jit(solution)/shard_map/pallas_call | solution.py:280
  51.9 0.0 collective-permute-done.11.refs_5_
  51.9 2.5 %collective-permute-done.9.refs_4_ = bf16[272,256]{1,0:T(8,128)(2,1)S(1)} collective-permute-done((bf16[272,256]{1,0:T(8,128)(2,1)S(1)}, bf16[272,256]{1,0:T(8,128)(2,1)S(1)}, u32[]{:S(2)}, u32[]{:S(2)}) %collective-permute-start.9) | collective-permute-done | bytes 139296 | tf_op jit(solution)/shard_map/ppermute | solution.py:362
  54.5 0.0 collective-permute-done.7.refs_3_
  54.5 0.0 collective-permute-done.5.refs_2_
  54.5 0.0 collective-permute-done.3.refs_1_
  54.5 2.0 %shard_map.105 = bf16[1,8,256,256]{3,2,1,0:T(8,128)(2,1)} custom-call(s32[64]{0:T(128)S(1)} %bitcast.3, s32[1]{0:T(128)} %bitcast.1.me_ref, bf16[272,256]{1,0:T(8,128)(2,1)S(1)} %shard_map.97.refs_0_, bf16[272,256]{1,0:T(8,128)(2,1)S(1)} %collective-permute-done.3.refs_1_, bf16[272,256]{1,0:T(8,128)(2,1)S(1)} %collective-permute-done.5.refs_2_, ...), custom_call_target="tpu_custom_call" | custom-call | flops 3145728 | bytes 2097152 | tf_op jit(solution)/shard_map/pallas_call | solution.py:329
  (9 shorter events, 0.0 us)
Async XLA Ops:
  0.6 21.3 %copy-start = (bf16[1,8,256,256]{3,2,1,0:T(8,128)(2,1)S(1)}, bf16[1,8,256,256]{3,2,1,0:T(8,128)(2,1)}, u32[]{:S(2)}) copy-start(bf16[1,8,256,256]{3,2,1,0:T(8,128)(2,1)} %left_ref.15) | copy-start | bytes 3145732
  0.6 21.3 %copy-start.1 = (bf16[1,8,256,256]{3,2,1,0:T(8,128)(2,1)S(1)}, bf16[1,8,256,256]{3,2,1,0:T(8,128)(2,1)}, u32[]{:S(2)}) copy-start(bf16[1,8,256,256]{3,2,1,0:T(8,128)(2,1)} %right_ref.15) | copy-start | bytes 3145732
  2.1 19.4 %collective-permute-start.14 = (bf16[256,256]{1,0:T(8,128)(2,1)S(1)}, bf16[256,256]{1,0:T(8,128)(2,1)S(1)}, u32[]{:S(2)}, u32[]{:S(2)}) collective-permute-start(bf16[256,256]{1,0:T(8,128)(2,1)S(1)} %get-tuple-element.23), channel_id=1, source_target_pairs={{0,28},{4,24},{8,20},{12,16},{16,12},{20,8},{24,4},{28,0},{1,29},{... | collective-permute-start | bytes 393224 | tf_op jit(solution)/shard_map/ppermute | solution.py:362
  8.2 14.1 %collective-permute-start.12 = (bf16[256,256]{1,0:T(8,128)(2,1)S(1)}, bf16[256,256]{1,0:T(8,128)(2,1)S(1)}, u32[]{:S(2)}, u32[]{:S(2)}) collective-permute-start(bf16[256,256]{1,0:T(8,128)(2,1)S(1)} %get-tuple-element.22), channel_id=1, source_target_pairs={{0,24},{4,28},{8,16},{12,20},{16,8},{20,12},{24,0},{28,4},{1,25},{... | collective-permute-start | bytes 393224 | tf_op jit(solution)/shard_map/ppermute | solution.py:362
  8.4 16.3 %collective-permute-start.2 = (bf16[256,256]{1,0:T(8,128)(2,1)S(1)}, bf16[256,256]{1,0:T(8,128)(2,1)S(1)}, u32[]{:S(2)}, u32[]{:S(2)}) collective-permute-start(bf16[256,256]{1,0:T(8,128)(2,1)S(1)} %get-tuple-element.17), channel_id=1, source_target_pairs={{0,4},{4,0},{8,12},{12,8},{16,20},{20,16},{24,28},{28,24},{1,5},{5... | collective-permute-start | bytes 393224 | tf_op jit(solution)/shard_map/ppermute | solution.py:362
  8.8 23.7 %collective-permute-start.10 = (bf16[256,256]{1,0:T(8,128)(2,1)S(1)}, bf16[256,256]{1,0:T(8,128)(2,1)S(1)}, u32[]{:S(2)}, u32[]{:S(2)}) collective-permute-start(bf16[256,256]{1,0:T(8,128)(2,1)S(1)} %get-tuple-element.21), channel_id=1, source_target_pairs={{0,20},{4,16},{8,28},{12,24},{16,4},{20,0},{24,12},{28,8},{1,21},{... | collective-permute-start | bytes 393224 | tf_op jit(solution)/shard_map/ppermute | solution.py:362
  13.2 1.2 %collective-permute-start = (f32[8,128]{1,0:T(8,128)S(1)}, f32[8,128]{1,0:T(8,128)S(1)}, u32[]{:S(2)}, u32[]{:S(2)}) collective-permute-start(f32[8,128]{1,0:T(8,128)S(1)} %get-tuple-element.16), channel_id=1, source_target_pairs={{0,1},{1,0},{2,3},{3,2},{4,5},{5,4},{6,7},{7,6},{8,9},{9,8},{10,11... | collective-permute-start | bytes 12296 | tf_op jit(solution)/shard_map/ppermute | solution.py:369
  14.4 3.6 %collective-permute-start.1 = (f32[8,128]{1,0:T(8,128)S(1)}, f32[8,128]{1,0:T(8,128)S(1)}, u32[]{:S(2)}, u32[]{:S(2)}) collective-permute-start(f32[8,128]{1,0:T(8,128)S(1)} %add.6), channel_id=1, source_target_pairs={{0,2},{1,3},{2,0},{3,1},{4,6},{5,7},{6,4},{7,5},{8,10},{9,11},{10,... | collective-permute-start | bytes 12296 | tf_op jit(solution)/shard_map/ppermute | solution.py:369
  18.0 20.7 %collective-permute-start.6 = (bf16[256,256]{1,0:T(8,128)(2,1)S(1)}, bf16[256,256]{1,0:T(8,128)(2,1)S(1)}, u32[]{:S(2)}, u32[]{:S(2)}) collective-permute-start(bf16[256,256]{1,0:T(8,128)(2,1)S(1)} %get-tuple-element.19), channel_id=1, source_target_pairs={{0,12},{4,8},{8,4},{12,0},{16,28},{20,24},{24,20},{28,16},{1,13},{... | collective-permute-start | bytes 393224 | tf_op jit(solution)/shard_map/ppermute | solution.py:362
  21.5 15.7 %collective-permute-start.8 = (bf16[256,256]{1,0:T(8,128)(2,1)S(1)}, bf16[256,256]{1,0:T(8,128)(2,1)S(1)}, u32[]{:S(2)}, u32[]{:S(2)}) collective-permute-start(bf16[256,256]{1,0:T(8,128)(2,1)S(1)} %get-tuple-element.20), channel_id=1, source_target_pairs={{0,16},{4,20},{8,24},{12,28},{16,0},{20,4},{24,8},{28,12},{1,17},{... | collective-permute-start | bytes 393224 | tf_op jit(solution)/shard_map/ppermute | solution.py:362
  22.3 20.4 %collective-permute-start.15 = (bf16[272,256]{1,0:T(8,128)(2,1)S(1)}, bf16[272,256]{1,0:T(8,128)(2,1)S(1)}, u32[]{:S(2)}, u32[]{:S(2)}) collective-permute-start(bf16[272,256]{1,0:T(8,128)(2,1)S(1)} %shard_map.104), channel_id=1, source_target_pairs={{0,28},{4,24},{8,20},{12,16},{16,12},{20,8},{24,4},{28,0},{1,29},{... | collective-permute-start | bytes 417800 | tf_op jit(solution)/shard_map/ppermute | solution.py:362
  24.7 20.3 %collective-permute-start.13 = (bf16[272,256]{1,0:T(8,128)(2,1)S(1)}, bf16[272,256]{1,0:T(8,128)(2,1)S(1)}, u32[]{:S(2)}, u32[]{:S(2)}) collective-permute-start(bf16[272,256]{1,0:T(8,128)(2,1)S(1)} %shard_map.103), channel_id=1, source_target_pairs={{0,24},{4,28},{8,16},{12,20},{16,8},{20,12},{24,0},{28,4},{1,25},{... | collective-permute-start | bytes 417800 | tf_op jit(solution)/shard_map/ppermute | solution.py:362
  32.5 8.1 %collective-permute-start.4 = (bf16[256,256]{1,0:T(8,128)(2,1)S(1)}, bf16[256,256]{1,0:T(8,128)(2,1)S(1)}, u32[]{:S(2)}, u32[]{:S(2)}) collective-permute-start(bf16[256,256]{1,0:T(8,128)(2,1)S(1)} %get-tuple-element.18), channel_id=1, source_target_pairs={{0,8},{4,12},{8,0},{12,4},{16,24},{20,28},{24,16},{28,20},{1,9},{5... | collective-permute-start | bytes 393224 | tf_op jit(solution)/shard_map/ppermute | solution.py:362
  37.3 14.7 %collective-permute-start.11 = (bf16[272,256]{1,0:T(8,128)(2,1)S(1)}, bf16[272,256]{1,0:T(8,128)(2,1)S(1)}, u32[]{:S(2)}, u32[]{:S(2)}) collective-permute-start(bf16[272,256]{1,0:T(8,128)(2,1)S(1)} %shard_map.102), channel_id=1, source_target_pairs={{0,20},{4,16},{8,28},{12,24},{16,4},{20,0},{24,12},{28,8},{1,21},{... | collective-permute-start | bytes 417800 | tf_op jit(solution)/shard_map/ppermute | solution.py:362
  38.7 15.7 %collective-permute-start.9 = (bf16[272,256]{1,0:T(8,128)(2,1)S(1)}, bf16[272,256]{1,0:T(8,128)(2,1)S(1)}, u32[]{:S(2)}, u32[]{:S(2)}) collective-permute-start(bf16[272,256]{1,0:T(8,128)(2,1)S(1)} %shard_map.101), channel_id=1, source_target_pairs={{0,16},{4,20},{8,24},{12,28},{16,0},{20,4},{24,8},{28,12},{1,17},{... | collective-permute-start | bytes 417800 | tf_op jit(solution)/shard_map/ppermute | solution.py:362
  40.5 6.7 %copy-start.2 = (f32[1,8,256,256]{3,2,1,0:T(8,128)S(1)}, f32[1,8,256,256]{3,2,1,0:T(8,128)}, u32[]{:S(2)}) copy-start(f32[1,8,256,256]{3,2,1,0:T(8,128)} %refs_8_.1) | copy-start | bytes 6291460
  40.5 6.7 %copy-start.3 = (f32[1,8,256,256]{3,2,1,0:T(8,128)S(1)}, f32[1,8,256,256]{3,2,1,0:T(8,128)}, u32[]{:S(2)}) copy-start(f32[1,8,256,256]{3,2,1,0:T(8,128)} %refs_9_.1) | copy-start | bytes 6291460
  40.6 13.9 %collective-permute-start.7 = (bf16[272,256]{1,0:T(8,128)(2,1)S(1)}, bf16[272,256]{1,0:T(8,128)(2,1)S(1)}, u32[]{:S(2)}, u32[]{:S(2)}) collective-permute-start(bf16[272,256]{1,0:T(8,128)(2,1)S(1)} %shard_map.100), channel_id=1, source_target_pairs={{0,12},{4,8},{8,4},{12,0},{16,28},{20,24},{24,20},{28,16},{1,13},{... | collective-permute-start | bytes 417800 | tf_op jit(solution)/shard_map/ppermute | solution.py:362
  42.7 11.8 %collective-permute-start.5 = (bf16[272,256]{1,0:T(8,128)(2,1)S(1)}, bf16[272,256]{1,0:T(8,128)(2,1)S(1)}, u32[]{:S(2)}, u32[]{:S(2)}) collective-permute-start(bf16[272,256]{1,0:T(8,128)(2,1)S(1)} %shard_map.99), channel_id=1, source_target_pairs={{0,8},{4,12},{8,0},{12,4},{16,24},{20,28},{24,16},{28,20},{1,9},{5... | collective-permute-start | bytes 417800 | tf_op jit(solution)/shard_map/ppermute | solution.py:362
  45.0 9.5 %collective-permute-start.3 = (bf16[272,256]{1,0:T(8,128)(2,1)S(1)}, bf16[272,256]{1,0:T(8,128)(2,1)S(1)}, u32[]{:S(2)}, u32[]{:S(2)}) collective-permute-start(bf16[272,256]{1,0:T(8,128)(2,1)S(1)} %shard_map.98), channel_id=1, source_target_pairs={{0,4},{4,0},{8,12},{12,8},{16,20},{20,16},{24,28},{28,24},{1,5},{5... | collective-permute-start | bytes 417800 | tf_op jit(solution)/shard_map/ppermute | solution.py:362
  47.2 7.3 %copy-start.4 = (s32[1,64,1]{1,2,0:T(1,128)S(1)}, s32[1,64,1]{1,2,0:T(1,128)}, u32[]{:S(2)}) copy-start(s32[1,64,1]{1,2,0:T(1,128)} %param.9) | copy-start | bytes 772

commit v2 on v1

--- a/solution.py
+++ b/solution.py
@@ -223,7 +223,7 @@
     )(total)
 
 
-def precondition_kernel(m, me_ref, grad_ref, left_ref, right_ref, tail_ref, out_ref):
+def precondition_kernel(m, rows, me_ref, grad_ref, left_ref, right_ref, tail_ref, out_ref):
     side = grad_ref.shape[0]
     slot = me_ref[0] ^ m
     half_done = jnp.dot(
@@ -232,20 +232,21 @@
     out_ref[0:side, :] = jnp.dot(
         half_done, right_ref[0, slot], preferred_element_type=jnp.float32
     ).astype(jnp.bfloat16)
-    out_ref[side:, :] = tail_ref[...]
-
-
-def precondition(m, me, block, left_root, right_root, tail):
+    if rows:
+        out_ref[side:, :] = tail_ref[...]
+
+
+def precondition(m, rows, me, block, left_root, right_root, tail):
     side = block.shape[0]
     return pl.pallas_call(
-        functools.partial(precondition_kernel, m),
+        functools.partial(precondition_kernel, m, rows),
         grid_spec=pltpu.PrefetchScalarGridSpec(
             num_scalar_prefetch=1,
             grid=(),
             in_specs=[pl.BlockSpec(memory_space=pltpu.VMEM)] * 4,
             out_specs=pl.BlockSpec(memory_space=pltpu.VMEM),
         ),
-        out_shape=jax.ShapeDtypeStruct((side + TAIL, side), jnp.bfloat16),
+        out_shape=jax.ShapeDtypeStruct((side + rows, side), jnp.bfloat16),
         compiler_params=kernel_params(6),
         cost_estimate=pl.CostEstimate(
             flops=4 * side**3, bytes_accessed=8 * side * side, transcendentals=0
@@ -299,42 +300,50 @@
 def finish_kernel(order, entries, owners_ref, me_ref, *refs):
     count = len(order)
     pieces = refs[:count]
-    squares_ref, out_ref, held, sems = refs[count:]
-    side = out_ref.shape[3]
+    squares_ref, tail_ref, out_ref, held, sums, sems = refs[count:]
+    side, lanes = out_ref.shape[3], squares_ref.shape[1]
     me = me_ref[0]
     named = [owners_ref[me * count + j] for j in range(count)]
+    blocks = [home_slot(named, me ^ m) for m in order]
     global_sq = jnp.zeros((1, 1), jnp.float32)
-    for piece in pieces:
-        terms = piece[side:, 0:1].astype(jnp.float32)
+    for rows in [tail_ref[...]] + [piece[side:, :] for piece in pieces if piece.shape[0] > side]:
+        terms = rows[:, 0:1].astype(jnp.float32)
         global_sq = global_sq + jnp.sum(terms, axis=0, keepdims=True)
+    for k, piece in enumerate(pieces):
+        pre_float = piece[0:side, :].astype(jnp.float32)
+        row = jnp.sum(pre_float * pre_float, axis=0, keepdims=True)
+        parts = [row[:, i : i + lanes] for i in range(0, side, lanes)]
+        sums[0, k : k + 1, :] = functools.reduce(jnp.add, parts)
+        sums[1, k : k + 1, :] = squares_ref[pl.ds(blocks[k], 1), :]
+    area = float(side * side)
+    pre_sq = jnp.sum(sums[0], axis=1, keepdims=True)
+    block_sq = jnp.sum(sums[1], axis=1, keepdims=True)
     clip_factor = jnp.minimum(1.0, UPDATE_RMS / jnp.sqrt(global_sq / entries))
-    area = float(side * side)
+    graft_ratio = jnp.sqrt(block_sq / area) / jnp.sqrt(pre_sq / area + NORM_FLOOR)
+    scale = graft_ratio * clip_factor
     copies = []
-    for k, m in enumerate(order):
-        block = home_slot(named, me ^ m)
-        pre_float = pieces[k][0:side, :].astype(jnp.float32)
-        pre_sq = jnp.sum(pre_float * pre_float, keepdims=True)
-        block_sq = jnp.sum(squares_ref[pl.ds(block, 1), :], axis=1, keepdims=True)
-        graft_ratio = jnp.sqrt(block_sq / area) / jnp.sqrt(pre_sq / area + NORM_FLOOR)
-        held[k] = (pre_float * (graft_ratio * clip_factor)).astype(jnp.bfloat16)
-        copy = pltpu.make_async_copy(held.at[k], out_ref.at[0, block], sems.at[k])
+    for k, piece in enumerate(pieces):
+        pre_float = piece[0:side, :].astype(jnp.float32)
+        held[k] = (pre_float * scale[k : k + 1, :]).astype(jnp.bfloat16)
+        copy = pltpu.make_async_copy(held.at[k], out_ref.at[0, blocks[k]], sems.at[k])
         copy.start()
         copies.append(copy)
     for copy in copies:
         copy.wait()
 
 
-def finish(order, owner_list, me, pieces, squares, entries):
+def finish(order, owner_list, me, pieces, squares, tail, entries):
     count, side = len(pieces), pieces[0].shape[1]
     return pl.pallas_call(
         functools.partial(finish_kernel, order, entries),
         grid_spec=pltpu.PrefetchScalarGridSpec(
             num_scalar_prefetch=2,
             grid=(),
-            in_specs=[pl.BlockSpec(memory_space=pltpu.VMEM)] * (count + 1),
+            in_specs=[pl.BlockSpec(memory_space=pltpu.VMEM)] * (count + 2),
             out_specs=pl.BlockSpec(memory_space=pl.ANY),
             scratch_shapes=[
                 pltpu.VMEM((count, side, side), jnp.bfloat16),
+                pltpu.VMEM((2, count, squares.shape[1]), jnp.float32),
                 pltpu.SemaphoreType.DMA((count,)),
             ],
         ),
@@ -343,7 +352,11 @@
         cost_estimate=pl.CostEstimate(
             flops=6 * count * side * side, bytes_accessed=4 * count * side * side, transcendentals=0
         ),
-    )(owner_list, me, *pieces, squares)
+    )(owner_list, me, *pieces, squares, tail)
+
+
+def doublings(size):
+    return [2**k for k in range(size.bit_length() - 1)]
 
 
 def per_device_exchange(
@@ -354,29 +367,28 @@
     side = gradients.shape[3]
     me = lax.axis_index("fsdp").astype(jnp.int32).reshape(1)
     owner_list = owners[0, :, 0]
-    order = list(range(count))
-
-    def swap(value, m):
+    half = count // 2
+    order = [0, half, *range(1, half), *range(half + 1, count)]
+
+    def swap(value, m, axis="fsdp"):
         if m == 0:
             return value
-        return lax.ppermute(value, "fsdp", [(i, i ^ m) for i in range(count)])
+        return lax.ppermute(value, axis, [(i, i ^ m) for i in range(lax.axis_size(axis))])
 
     outgoing = route(order, owner_list, me, gradients)
-    received = {m: swap(outgoing[m], m) for m in order}
+    received = [swap(block, m) for m, block in zip(order, outgoing)]
     squares, total = adam_squares(gradients, second_moment)
-    k = 1
-    while k < layers:
-        total = total + lax.ppermute(total, "layer", [(i, i ^ k) for i in range(layers)])
-        k *= 2
+    for k in doublings(layers):
+        total = total + swap(total, k, "layer")
     tail = sum_tail(total, side)
-    returned = {
-        m: swap(precondition(m, me, received[m], left_root, right_root, tail), m) for m in order
-    }
-    new_left, new_right = gram_update(
-        order, me, [received[m] for m in order], left_stats, right_stats
-    )
+    returned = []
+    for m, block in zip(order, received):
+        rows = TAIL if m else 0
+        done = precondition(m, rows, me, block, left_root, right_root, tail)
+        returned.append(swap(done, m))
+    new_left, new_right = gram_update(order, me, received, left_stats, right_stats)
     entries = float(owner_list.shape[0] * layers * side * side)
-    update = finish(order, owner_list, me, [returned[m] for m in order], squares, entries)
+    update = finish(order, owner_list, me, returned, squares, tail, entries)
     return (update, new_left, new_right)
 
 

time: 56.6 us -> 56.4 us (level)
  waiting for transfers between devices: 14.6 us -> 11.3 us
  starting transfers between devices: 27.6 us -> 30.8 us
    ppermute x16, waiting for transfers between devices: 14.6 us -> 11.3 us  [swap(): lax.ppermute(value, axis, [(i, i ^ m) for i in range(lax.axis_size(axis))])]
    ppermute x16, starting transfers between devices: 27.6 us -> 30.8 us  [swap(): lax.ppermute(value, axis, [(i, i ^ m) for i in range(lax.axis_size(axis))])]
where the time goes in v2:
time: 56.4 us; the launch traced here: 56.2 us
  starting transfers between devices  30.8 us (55%)
  Pallas kernels  13.2 us (23%)
  waiting for transfers between devices  11.3 us (20%)
  between operations  0.85 us (2%)
    ppermute x16, starting transfers between devices, swap(): lax.ppermute(value, axis, [(i, i ^ m) for i in range(lax.axis_size(axis))])  30.8 us
    ppermute x16, waiting for transfers between devices, swap(): lax.ppermute(value, axis, [(i, i ^ m) for i in range(lax.axis_size(axis))])  11.3 us
    pallas_call x1, Pallas kernels, gram_update(): pl.pallas_call(functools.partial(gram_kernel, order), grid_spec=pltpu.Pre...  4.69 us
    pallas_call x8, Pallas kernels, precondition(): pl.pallas_call(functools.partial(precondition_kernel, m, rows), grid_spec...  2.64 us
    pallas_call x1, Pallas kernels, adam_squares(): pl.pallas_call(adam_kernel, in_specs=[hbm, hbm], out_specs=[pl.BlockSpec(...  2.53 us
    pallas_call x1, Pallas kernels, finish(): pl.pallas_call(functools.partial(finish_kernel, order, entries), grid_spe...  1.8 us
    pallas_call x1, Pallas kernels, route(): pl.pallas_call(functools.partial(route_kernel, order), in_specs=[hbm, pl....  1.46 us
  transfers between devices with their start and end apart: 16, of which 5 were waited for; matrix products, arithmetic and copies ran while one was open for 0% of the time, Pallas kernels for 18%

profile of v2, /device:TPU:0, one launch (start us, length us, event | category | flops | bytes accessed | tf_op | source)
XLA Modules:
  0.0 56.2 jit_solution(14997058139421716921)
XLA Ops:
  0.7 1.5 %shard_map.94 = (bf16[256,256]{1,0:T(8,128)(2,1)S(1)}, bf16[256,256]{1,0:T(8,128)(2,1)S(1)}, bf16[256,256]{1,0:T(8,128)(2,1)S(1)}, bf16[256,256]{1,0:T(8,128)(2,...) custom-call(s32[64]{0:T(128)} %bitcast.2, ...), custom_call_target="tpu_custom_call" | custom-call | bytes 2097152 | tf_op jit(solution)/shard_map/pallas_call | solution.py:128
  2.1 6.0 %collective-permute-start.14 = (bf16[256,256]{1,0:T(8,128)(2,1)S(1)}, bf16[256,256]{1,0:T(8,128)(2,1)S(1)}, u32[]{:S(2)}, u32[]{:S(2)}) collective-permute-start(bf16[256,256]{1,0:T(8,128)(2,1)S(1)} %get-tuple-element.23), channel_id=1, source_target_pairs={{0,28},{4,24},{8,20},{12,16},{16,12},{20,8},{24,4},{28,0},{1,29},{... | collective-permute-start | bytes 393224 | tf_op jit(solution)/shard_map/ppermute | solution.py:376
  8.2 0.2 collective-permute-start.12
  8.4 0.8 %collective-permute-start.2 = (bf16[256,256]{1,0:T(8,128)(2,1)S(1)}, bf16[256,256]{1,0:T(8,128)(2,1)S(1)}, u32[]{:S(2)}, u32[]{:S(2)}) collective-permute-start(bf16[256,256]{1,0:T(8,128)(2,1)S(1)} %get-tuple-element.17), channel_id=1, source_target_pairs={{0,16},{4,20},{8,24},{12,28},{16,0},{20,4},{24,8},{28,12},{1,17},{... | collective-permute-start | bytes 393224 | tf_op jit(solution)/shard_map/ppermute | solution.py:376
  9.2 2.0 %collective-permute-start.10 = (bf16[256,256]{1,0:T(8,128)(2,1)S(1)}, bf16[256,256]{1,0:T(8,128)(2,1)S(1)}, u32[]{:S(2)}, u32[]{:S(2)}) collective-permute-start(bf16[256,256]{1,0:T(8,128)(2,1)S(1)} %get-tuple-element.21), channel_id=1, source_target_pairs={{0,20},{4,16},{8,28},{12,24},{16,4},{20,0},{24,12},{28,8},{1,21},{... | collective-permute-start | bytes 393224 | tf_op jit(solution)/shard_map/ppermute | solution.py:376
  11.2 2.5 %shard_map.95 = (f32[8,128]{1,0:T(8,128)S(1)}, f32[8,128]{1,0:T(8,128)S(1)}) custom-call(bf16[1,8,256,256]{3,2,1,0:T(8,128)(2,1)} %grad_hbm.3, f32[1,8,256,256]{3,2,1,0:T(8,128)} %moment_hbm.1), custom_call_target="tpu_custom_call" | custom-call | flops 4194304 | bytes 3145728 | tf_op jit(solution)/shard_map/pallas_call | solution.py:179
  13.7 0.1 collective-permute-start
  13.8 1.2 %collective-permute-done = f32[8,128]{1,0:T(8,128)S(1)} collective-permute-done((f32[8,128]{1,0:T(8,128)S(1)}, f32[8,128]{1,0:T(8,128)S(1)}, u32[]{:S(2)}, u32[]{:S(2)}) %collective-permute-start) | collective-permute-done | bytes 4128 | tf_op jit(solution)/shard_map/ppermute | solution.py:376
  14.9 1.6 %collective-permute-start.1 = (f32[8,128]{1,0:T(8,128)S(1)}, f32[8,128]{1,0:T(8,128)S(1)}, u32[]{:S(2)}, u32[]{:S(2)}) collective-permute-start(f32[8,128]{1,0:T(8,128)S(1)} %add.6), channel_id=1, source_target_pairs={{0,2},{1,3},{2,0},{3,1},{4,6},{5,7},{6,4},{7,5},{8,10},{9,11},{10,... | collective-permute-start | bytes 12296 | tf_op jit(solution)/shard_map/ppermute | solution.py:376
  16.6 2.0 %collective-permute-done.1 = f32[8,128]{1,0:T(8,128)S(1)} collective-permute-done((f32[8,128]{1,0:T(8,128)S(1)}, f32[8,128]{1,0:T(8,128)S(1)}, u32[]{:S(2)}, u32[]{:S(2)}) %collective-permute-start.1) | collective-permute-done | bytes 4128 | tf_op jit(solution)/shard_map/ppermute | solution.py:376
  18.6 1.4 %collective-permute-start.6 = (bf16[256,256]{1,0:T(8,128)(2,1)S(1)}, bf16[256,256]{1,0:T(8,128)(2,1)S(1)}, u32[]{:S(2)}, u32[]{:S(2)}) collective-permute-start(bf16[256,256]{1,0:T(8,128)(2,1)S(1)} %get-tuple-element.19), channel_id=1, source_target_pairs={{0,8},{4,12},{8,0},{12,4},{16,24},{20,28},{24,16},{28,20},{1,9},{5... | collective-permute-start | bytes 393224 | tf_op jit(solution)/shard_map/ppermute | solution.py:376
  19.9 0.1 shard_map.96.tail_ref.refs_9_
  20.1 0.0 collective-permute-done.14.grad_ref.refs_7_
  20.1 4.3 %collective-permute-start.8 = (bf16[256,256]{1,0:T(8,128)(2,1)S(1)}, bf16[256,256]{1,0:T(8,128)(2,1)S(1)}, u32[]{:S(2)}, u32[]{:S(2)}) collective-permute-start(bf16[256,256]{1,0:T(8,128)(2,1)S(1)} %get-tuple-element.20), channel_id=1, source_target_pairs={{0,12},{4,8},{8,4},{12,0},{16,28},{20,24},{24,20},{28,16},{1,13},{... | collective-permute-start | bytes 393224 | tf_op jit(solution)/shard_map/ppermute | solution.py:376
  24.4 0.3 shard_map.104
  24.8 0.0 collective-permute-done.12.grad_ref.refs_6_
  24.8 2.8 %collective-permute-start.15 = (bf16[272,256]{1,0:T(8,128)(2,1)S(1)}, bf16[272,256]{1,0:T(8,128)(2,1)S(1)}, u32[]{:S(2)}, u32[]{:S(2)}) collective-permute-start(bf16[272,256]{1,0:T(8,128)(2,1)S(1)} %shard_map.104), channel_id=1, source_target_pairs={{0,28},{4,24},{8,20},{12,16},{16,12},{20,8},{24,4},{28,0},{1,29},{... | collective-permute-start | bytes 417800 | tf_op jit(solution)/shard_map/ppermute | solution.py:376
  27.5 0.3 shard_map.103
  27.9 2.3 %collective-permute-done.2.grad_ref.refs_1_ = bf16[256,256]{1,0:T(8,128)(2,1)S(1)} collective-permute-done((bf16[256,256]{1,0:T(8,128)(2,1)S(1)}, bf16[256,256]{1,0:T(8,128)(2,1)S(1)}, u32[]{:S(2)}, u32[]{:S(2)}) %collective-permute-start.2) | collective-permute-done | bytes 131104 | tf_op jit(solution)/shard_map/ppermute | solution.py:376
  30.2 2.7 %collective-permute-start.13 = (bf16[272,256]{1,0:T(8,128)(2,1)S(1)}, bf16[272,256]{1,0:T(8,128)(2,1)S(1)}, u32[]{:S(2)}, u32[]{:S(2)}) collective-permute-start(bf16[272,256]{1,0:T(8,128)(2,1)S(1)} %shard_map.103), channel_id=1, source_target_pairs={{0,24},{4,28},{8,16},{12,20},{16,8},{20,12},{24,0},{28,4},{1,25},{... | collective-permute-start | bytes 417800 | tf_op jit(solution)/shard_map/ppermute | solution.py:376
  32.9 4.6 %collective-permute-done.10.grad_ref.refs_5_ = bf16[256,256]{1,0:T(8,128)(2,1)S(1)} collective-permute-done((bf16[256,256]{1,0:T(8,128)(2,1)S(1)}, bf16[256,256]{1,0:T(8,128)(2,1)S(1)}, u32[]{:S(2)}, u32[]{:S(2)}) %collective-permute-start.10) | collective-permute-done | bytes 131104 | tf_op jit(solution)/shard_map/ppermute | solution.py:376
  37.5 1.5 %collective-permute-start.4 = (bf16[256,256]{1,0:T(8,128)(2,1)S(1)}, bf16[256,256]{1,0:T(8,128)(2,1)S(1)}, u32[]{:S(2)}, u32[]{:S(2)}) collective-permute-start(bf16[256,256]{1,0:T(8,128)(2,1)S(1)} %get-tuple-element.18), channel_id=1, source_target_pairs={{0,4},{4,0},{8,12},{12,8},{16,20},{20,16},{24,28},{28,24},{1,5},{5... | collective-permute-start | bytes 393224 | tf_op jit(solution)/shard_map/ppermute | solution.py:376
  39.0 0.3 shard_map.98
  39.3 0.3 shard_map.102
  39.6 0.0 collective-permute-done.8.grad_ref.refs_4_
  39.6 0.5 collective-permute-start.11
  40.1 0.3 shard_map.101
  40.4 0.0 collective-permute-done.6.grad_ref.refs_3_
  40.4 3.8 %collective-permute-start.9 = (bf16[272,256]{1,0:T(8,128)(2,1)S(1)}, bf16[272,256]{1,0:T(8,128)(2,1)S(1)}, u32[]{:S(2)}, u32[]{:S(2)}) collective-permute-start(bf16[272,256]{1,0:T(8,128)(2,1)S(1)} %shard_map.101), channel_id=1, source_target_pairs={{0,12},{4,8},{8,4},{12,0},{16,28},{20,24},{24,20},{28,16},{1,13},{... | collective-permute-start | bytes 417800 | tf_op jit(solution)/shard_map/ppermute | solution.py:376
  44.2 0.3 shard_map.100
  44.5 0.0 copy-start.2
  44.6 0.0 copy-start.3
  44.6 0.0 collective-permute-done.4.grad_ref.refs_2_
  44.6 0.1 collective-permute-start.7
  44.7 0.3 shard_map.99
  45.0 0.0 collective-permute-done.15.refs_7_
  45.0 0.6 %collective-permute-start.5 = (bf16[272,256]{1,0:T(8,128)(2,1)S(1)}, bf16[272,256]{1,0:T(8,128)(2,1)S(1)}, u32[]{:S(2)}, u32[]{:S(2)}) collective-permute-start(bf16[272,256]{1,0:T(8,128)(2,1)S(1)} %shard_map.99), channel_id=1, source_target_pairs={{0,4},{4,0},{8,12},{12,8},{16,20},{20,16},{24,28},{28,24},{1,5},{5... | collective-permute-start | bytes 417800 | tf_op jit(solution)/shard_map/ppermute | solution.py:376
  45.6 0.0 collective-permute-done.13.refs_6_
  45.6 2.5 %collective-permute-start.3 = (bf16[272,256]{1,0:T(8,128)(2,1)S(1)}, bf16[272,256]{1,0:T(8,128)(2,1)S(1)}, u32[]{:S(2)}, u32[]{:S(2)}) collective-permute-start(bf16[272,256]{1,0:T(8,128)(2,1)S(1)} %shard_map.98), channel_id=1, source_target_pairs={{0,16},{4,20},{8,24},{12,28},{16,0},{20,4},{24,8},{28,12},{1,17},{... | collective-permute-start | bytes 417800 | tf_op jit(solution)/shard_map/ppermute | solution.py:376
  48.2 0.3 shard_map.97.refs_0_
  48.5 0.0 copy-start.4
  48.5 4.7 %shard_map.106 = (f32[1,8,256,256]{3,2,1,0:T(8,128)}, f32[1,8,256,256]{3,2,1,0:T(8,128)}) custom-call(s32[1]{0:T(128)} %bitcast.1.me_ref, bf16[256,256]{1,0:T(8,128)(2,1)S(1)} %get-tuple-element.15.grad_ref.refs_0_, bf16[256,256]{1,0:T(8,128)(2,1)S(1)} %collective-permute-done.2.grad_ref.refs_1_, ...), custom_call_target="tpu_custom_call" | custom-call | flops 536870912 | bytes 9437184 | tf_op jit(solution)/shard_map/pallas_call | solution.py:281
  53.2 0.0 collective-permute-done.11.refs_5_
  53.2 0.0 collective-permute-done.9.refs_4_
  53.2 1.2 %collective-permute-done.7.refs_3_ = bf16[272,256]{1,0:T(8,128)(2,1)S(1)} collective-permute-done((bf16[272,256]{1,0:T(8,128)(2,1)S(1)}, bf16[272,256]{1,0:T(8,128)(2,1)S(1)}, u32[]{:S(2)}, u32[]{:S(2)}) %collective-permute-start.7) | collective-permute-done | bytes 139296 | tf_op jit(solution)/shard_map/ppermute | solution.py:376
  54.4 0.0 collective-permute-done.5.refs_2_
  54.4 0.0 collective-permute-done.3.refs_1_
  54.4 1.8 %shard_map.105 = bf16[1,8,256,256]{3,2,1,0:T(8,128)(2,1)} custom-call(s32[64]{0:T(128)S(1)} %bitcast.3, s32[1]{0:T(128)} %bitcast.1.me_ref, bf16[256,256]{1,0:T(8,128)(2,1)S(1)} %shard_map.97.refs_0_, bf16[272,256]{1,0:T(8,128)(2,1)S(1)} %collective-permute-done.3.refs_1_, bf16[272,256]{1,0:T(8,128)(2,1)S(1)} %collective-permute-done.5.refs_2_, ...), custom_call_target="tpu_custom_call" | custom-call | flops 3145728 | bytes 2097152 | tf_op jit(solution)/shard_map/pallas_call | solution.py:337
  (9 shorter events, 0.0 us)
Async XLA Ops:
  0.6 23.8 %copy-start = (bf16[1,8,256,256]{3,2,1,0:T(8,128)(2,1)S(1)}, bf16[1,8,256,256]{3,2,1,0:T(8,128)(2,1)}, u32[]{:S(2)}) copy-start(bf16[1,8,256,256]{3,2,1,0:T(8,128)(2,1)} %left_ref.15) | copy-start | bytes 3145732
  0.6 23.8 %copy-start.1 = (bf16[1,8,256,256]{3,2,1,0:T(8,128)(2,1)S(1)}, bf16[1,8,256,256]{3,2,1,0:T(8,128)(2,1)}, u32[]{:S(2)}) copy-start(bf16[1,8,256,256]{3,2,1,0:T(8,128)(2,1)} %right_ref.15) | copy-start | bytes 3145732
  2.1 18.0 %collective-permute-start.14 = (bf16[256,256]{1,0:T(8,128)(2,1)S(1)}, bf16[256,256]{1,0:T(8,128)(2,1)S(1)}, u32[]{:S(2)}, u32[]{:S(2)}) collective-permute-start(bf16[256,256]{1,0:T(8,128)(2,1)S(1)} %get-tuple-element.23), channel_id=1, source_target_pairs={{0,28},{4,24},{8,20},{12,16},{16,12},{20,8},{24,4},{28,0},{1,29},{... | collective-permute-start | bytes 393224 | tf_op jit(solution)/shard_map/ppermute | solution.py:376
  8.2 16.6 %collective-permute-start.12 = (bf16[256,256]{1,0:T(8,128)(2,1)S(1)}, bf16[256,256]{1,0:T(8,128)(2,1)S(1)}, u32[]{:S(2)}, u32[]{:S(2)}) collective-permute-start(bf16[256,256]{1,0:T(8,128)(2,1)S(1)} %get-tuple-element.22), channel_id=1, source_target_pairs={{0,24},{4,28},{8,16},{12,20},{16,8},{20,12},{24,0},{28,4},{1,25},{... | collective-permute-start | bytes 393224 | tf_op jit(solution)/shard_map/ppermute | solution.py:376
  8.4 21.8 %collective-permute-start.2 = (bf16[256,256]{1,0:T(8,128)(2,1)S(1)}, bf16[256,256]{1,0:T(8,128)(2,1)S(1)}, u32[]{:S(2)}, u32[]{:S(2)}) collective-permute-start(bf16[256,256]{1,0:T(8,128)(2,1)S(1)} %get-tuple-element.17), channel_id=1, source_target_pairs={{0,16},{4,20},{8,24},{12,28},{16,0},{20,4},{24,8},{28,12},{1,17},{... | collective-permute-start | bytes 393224 | tf_op jit(solution)/shard_map/ppermute | solution.py:376
  9.2 28.3 %collective-permute-start.10 = (bf16[256,256]{1,0:T(8,128)(2,1)S(1)}, bf16[256,256]{1,0:T(8,128)(2,1)S(1)}, u32[]{:S(2)}, u32[]{:S(2)}) collective-permute-start(bf16[256,256]{1,0:T(8,128)(2,1)S(1)} %get-tuple-element.21), channel_id=1, source_target_pairs={{0,20},{4,16},{8,28},{12,24},{16,4},{20,0},{24,12},{28,8},{1,21},{... | collective-permute-start | bytes 393224 | tf_op jit(solution)/shard_map/ppermute | solution.py:376
  13.7 1.2 %collective-permute-start = (f32[8,128]{1,0:T(8,128)S(1)}, f32[8,128]{1,0:T(8,128)S(1)}, u32[]{:S(2)}, u32[]{:S(2)}) collective-permute-start(f32[8,128]{1,0:T(8,128)S(1)} %get-tuple-element.16), channel_id=1, source_target_pairs={{0,1},{1,0},{2,3},{3,2},{4,5},{5,4},{6,7},{7,6},{8,9},{9,8},{10,11... | collective-permute-start | bytes 12296 | tf_op jit(solution)/shard_map/ppermute | solution.py:376
  14.9 3.6 %collective-permute-start.1 = (f32[8,128]{1,0:T(8,128)S(1)}, f32[8,128]{1,0:T(8,128)S(1)}, u32[]{:S(2)}, u32[]{:S(2)}) collective-permute-start(f32[8,128]{1,0:T(8,128)S(1)} %add.6), channel_id=1, source_target_pairs={{0,2},{1,3},{2,0},{3,1},{4,6},{5,7},{6,4},{7,5},{8,10},{9,11},{10,... | collective-permute-start | bytes 12296 | tf_op jit(solution)/shard_map/ppermute | solution.py:376
  18.6 21.9 %collective-permute-start.6 = (bf16[256,256]{1,0:T(8,128)(2,1)S(1)}, bf16[256,256]{1,0:T(8,128)(2,1)S(1)}, u32[]{:S(2)}, u32[]{:S(2)}) collective-permute-start(bf16[256,256]{1,0:T(8,128)(2,1)S(1)} %get-tuple-element.19), channel_id=1, source_target_pairs={{0,8},{4,12},{8,0},{12,4},{16,24},{20,28},{24,16},{28,20},{1,9},{5... | collective-permute-start | bytes 393224 | tf_op jit(solution)/shard_map/ppermute | solution.py:376
  20.1 19.5 %collective-permute-start.8 = (bf16[256,256]{1,0:T(8,128)(2,1)S(1)}, bf16[256,256]{1,0:T(8,128)(2,1)S(1)}, u32[]{:S(2)}, u32[]{:S(2)}) collective-permute-start(bf16[256,256]{1,0:T(8,128)(2,1)S(1)} %get-tuple-element.20), channel_id=1, source_target_pairs={{0,12},{4,8},{8,4},{12,0},{16,28},{20,24},{24,20},{28,16},{1,13},{... | collective-permute-start | bytes 393224 | tf_op jit(solution)/shard_map/ppermute | solution.py:376
  24.8 20.2 %collective-permute-start.15 = (bf16[272,256]{1,0:T(8,128)(2,1)S(1)}, bf16[272,256]{1,0:T(8,128)(2,1)S(1)}, u32[]{:S(2)}, u32[]{:S(2)}) collective-permute-start(bf16[272,256]{1,0:T(8,128)(2,1)S(1)} %shard_map.104), channel_id=1, source_target_pairs={{0,28},{4,24},{8,20},{12,16},{16,12},{20,8},{24,4},{28,0},{1,29},{... | collective-permute-start | bytes 417800 | tf_op jit(solution)/shard_map/ppermute | solution.py:376
  30.2 15.5 %collective-permute-start.13 = (bf16[272,256]{1,0:T(8,128)(2,1)S(1)}, bf16[272,256]{1,0:T(8,128)(2,1)S(1)}, u32[]{:S(2)}, u32[]{:S(2)}) collective-permute-start(bf16[272,256]{1,0:T(8,128)(2,1)S(1)} %shard_map.103), channel_id=1, source_target_pairs={{0,24},{4,28},{8,16},{12,20},{16,8},{20,12},{24,0},{28,4},{1,25},{... | collective-permute-start | bytes 417800 | tf_op jit(solution)/shard_map/ppermute | solution.py:376
  37.5 7.1 %collective-permute-start.4 = (bf16[256,256]{1,0:T(8,128)(2,1)S(1)}, bf16[256,256]{1,0:T(8,128)(2,1)S(1)}, u32[]{:S(2)}, u32[]{:S(2)}) collective-permute-start(bf16[256,256]{1,0:T(8,128)(2,1)S(1)} %get-tuple-element.18), channel_id=1, source_target_pairs={{0,4},{4,0},{8,12},{12,8},{16,20},{20,16},{24,28},{28,24},{1,5},{5... | collective-permute-start | bytes 393224 | tf_op jit(solution)/shard_map/ppermute | solution.py:376
  39.6 13.6 %collective-permute-start.11 = (bf16[272,256]{1,0:T(8,128)(2,1)S(1)}, bf16[272,256]{1,0:T(8,128)(2,1)S(1)}, u32[]{:S(2)}, u32[]{:S(2)}) collective-permute-start(bf16[272,256]{1,0:T(8,128)(2,1)S(1)} %shard_map.102), channel_id=1, source_target_pairs={{0,20},{4,16},{8,28},{12,24},{16,4},{20,0},{24,12},{28,8},{1,21},{... | collective-permute-start | bytes 417800 | tf_op jit(solution)/shard_map/ppermute | solution.py:376
  40.4 12.8 %collective-permute-start.9 = (bf16[272,256]{1,0:T(8,128)(2,1)S(1)}, bf16[272,256]{1,0:T(8,128)(2,1)S(1)}, u32[]{:S(2)}, u32[]{:S(2)}) collective-permute-start(bf16[272,256]{1,0:T(8,128)(2,1)S(1)} %shard_map.101), channel_id=1, source_target_pairs={{0,12},{4,8},{8,4},{12,0},{16,28},{20,24},{24,20},{28,16},{1,13},{... | collective-permute-start | bytes 417800 | tf_op jit(solution)/shard_map/ppermute | solution.py:376
  44.5 4.0 %copy-start.2 = (f32[1,8,256,256]{3,2,1,0:T(8,128)S(1)}, f32[1,8,256,256]{3,2,1,0:T(8,128)}, u32[]{:S(2)}) copy-start(f32[1,8,256,256]{3,2,1,0:T(8,128)} %refs_8_.1) | copy-start | bytes 6291460
  44.6 4.0 %copy-start.3 = (f32[1,8,256,256]{3,2,1,0:T(8,128)S(1)}, f32[1,8,256,256]{3,2,1,0:T(8,128)}, u32[]{:S(2)}) copy-start(f32[1,8,256,256]{3,2,1,0:T(8,128)} %refs_9_.1) | copy-start | bytes 6291460
  44.6 9.8 %collective-permute-start.7 = (bf16[272,256]{1,0:T(8,128)(2,1)S(1)}, bf16[272,256]{1,0:T(8,128)(2,1)S(1)}, u32[]{:S(2)}, u32[]{:S(2)}) collective-permute-start(bf16[272,256]{1,0:T(8,128)(2,1)S(1)} %shard_map.100), channel_id=1, source_target_pairs={{0,8},{4,12},{8,0},{12,4},{16,24},{20,28},{24,16},{28,20},{1,9},{5... | collective-permute-start | bytes 417800 | tf_op jit(solution)/shard_map/ppermute | solution.py:376
  45.0 9.4 %collective-permute-start.5 = (bf16[272,256]{1,0:T(8,128)(2,1)S(1)}, bf16[272,256]{1,0:T(8,128)(2,1)S(1)}, u32[]{:S(2)}, u32[]{:S(2)}) collective-permute-start(bf16[272,256]{1,0:T(8,128)(2,1)S(1)} %shard_map.99), channel_id=1, source_target_pairs={{0,4},{4,0},{8,12},{12,8},{16,20},{20,16},{24,28},{28,24},{1,5},{5... | collective-permute-start | bytes 417800 | tf_op jit(solution)/shard_map/ppermute | solution.py:376
  45.6 8.8 %collective-permute-start.3 = (bf16[272,256]{1,0:T(8,128)(2,1)S(1)}, bf16[272,256]{1,0:T(8,128)(2,1)S(1)}, u32[]{:S(2)}, u32[]{:S(2)}) collective-permute-start(bf16[272,256]{1,0:T(8,128)(2,1)S(1)} %shard_map.98), channel_id=1, source_target_pairs={{0,16},{4,20},{8,24},{12,28},{16,0},{20,4},{24,8},{28,12},{1,17},{... | collective-permute-start | bytes 417800 | tf_op jit(solution)/shard_map/ppermute | solution.py:376
  48.5 5.9 %copy-start.4 = (s32[1,64,1]{1,2,0:T(1,128)S(1)}, s32[1,64,1]{1,2,0:T(1,128)}, u32[]{:S(2)}) copy-start(s32[1,64,1]{1,2,0:T(1,128)} %param.9) | copy-start | bytes 772

commit v3 on v2

--- a/solution.py
+++ b/solution.py
@@ -201,57 +201,95 @@
     )
 
 
-def tail_kernel(total_ref, out_ref):
-    total = jnp.sum(total_ref[0:1, :], keepdims=True)
+def as_rows(total, shape):
     high = total.astype(jnp.bfloat16).astype(jnp.float32)
     rest = total - high
     middle = rest.astype(jnp.bfloat16).astype(jnp.float32)
     low = rest - middle
-    row = lax.broadcasted_iota(jnp.int32, out_ref.shape, 0)
+    row = lax.broadcasted_iota(jnp.int32, shape, 0)
     value = jnp.where(row == 0, high, jnp.where(row == 1, middle, jnp.where(row == 2, low, 0.0)))
-    out_ref[...] = value.astype(jnp.bfloat16)
-
-
-def sum_tail(total, side):
-    return pl.pallas_call(
-        tail_kernel,
-        in_specs=[pl.BlockSpec(memory_space=pltpu.VMEM)],
-        out_specs=pl.BlockSpec(memory_space=pltpu.VMEM),
-        out_shape=jax.ShapeDtypeStruct((TAIL, side), jnp.bfloat16),
-        compiler_params=kernel_params(2),
+    return value.astype(jnp.bfloat16)
+
+
+def from_rows(rows):
+    return jnp.sum(rows[:, 0:1].astype(jnp.float32), axis=0, keepdims=True)
+
+
+def attach_kernel(total_ref, *refs):
+    count = len(refs) // 2
+    side = refs[0].shape[0]
+    rows = as_rows(jnp.sum(total_ref[0:1, :], keepdims=True), (TAIL, side))
+    for block, out in zip(refs[:count], refs[count:]):
+        out[0:side, :] = block[...]
+        out[side:, :] = rows
+
+
+def attach(total, blocks):
+    side, other = blocks[0].shape
+    vmem = pl.BlockSpec(memory_space=pltpu.VMEM)
+    longer = jax.ShapeDtypeStruct((side + TAIL, other), jnp.bfloat16)
+    return pl.pallas_call(
+        attach_kernel,
+        in_specs=[vmem] * (1 + len(blocks)),
+        out_specs=[vmem] * len(blocks),
+        out_shape=[longer] * len(blocks),
+        compiler_params=kernel_params(4),
+        cost_estimate=pl.CostEstimate(
+            flops=0, bytes_accessed=4 * len(blocks) * side * side, transcendentals=0
+        ),
+    )(total, *blocks)
+
+
+def half_sum_kernel(total_ref, *refs):
+    out_ref = refs[-1]
+    total = jnp.sum(total_ref[0:1, :], keepdims=True)
+    for block in refs[:-1]:
+        total = total + from_rows(block[block.shape[1] :, :])
+    out_ref[...] = as_rows(total, out_ref.shape)
+
+
+def half_sum(total, blocks):
+    vmem = pl.BlockSpec(memory_space=pltpu.VMEM)
+    return pl.pallas_call(
+        half_sum_kernel,
+        in_specs=[vmem] * (1 + len(blocks)),
+        out_specs=vmem,
+        out_shape=jax.ShapeDtypeStruct((TAIL, blocks[0].shape[1]), jnp.bfloat16),
+        compiler_params=kernel_params(4),
         cost_estimate=pl.CostEstimate(flops=4096, bytes_accessed=32768, transcendentals=0),
-    )(total)
-
-
-def precondition_kernel(m, rows, me_ref, grad_ref, left_ref, right_ref, tail_ref, out_ref):
-    side = grad_ref.shape[0]
+    )(total, *blocks)
+
+
+def precondition_kernel(m, me_ref, grad_ref, left_ref, right_ref, *refs):
+    tails, out_ref = refs[:-1], refs[-1]
+    side = grad_ref.shape[1]
     slot = me_ref[0] ^ m
     half_done = jnp.dot(
-        left_ref[0, slot], grad_ref[...], preferred_element_type=jnp.float32
+        left_ref[0, slot], grad_ref[0:side, :], preferred_element_type=jnp.float32
     ).astype(jnp.bfloat16)
     out_ref[0:side, :] = jnp.dot(
         half_done, right_ref[0, slot], preferred_element_type=jnp.float32
     ).astype(jnp.bfloat16)
-    if rows:
+    for tail_ref in tails:
         out_ref[side:, :] = tail_ref[...]
 
 
-def precondition(m, rows, me, block, left_root, right_root, tail):
-    side = block.shape[0]
-    return pl.pallas_call(
-        functools.partial(precondition_kernel, m, rows),
+def precondition(m, me, block, left_root, right_root, *tails):
+    side = block.shape[1]
+    return pl.pallas_call(
+        functools.partial(precondition_kernel, m),
         grid_spec=pltpu.PrefetchScalarGridSpec(
             num_scalar_prefetch=1,
             grid=(),
-            in_specs=[pl.BlockSpec(memory_space=pltpu.VMEM)] * 4,
+            in_specs=[pl.BlockSpec(memory_space=pltpu.VMEM)] * (3 + len(tails)),
             out_specs=pl.BlockSpec(memory_space=pltpu.VMEM),
         ),
-        out_shape=jax.ShapeDtypeStruct((side + rows, side), jnp.bfloat16),
+        out_shape=jax.ShapeDtypeStruct((side + TAIL * len(tails), side), jnp.bfloat16),
         compiler_params=kernel_params(6),
         cost_estimate=pl.CostEstimate(
             flops=4 * side**3, bytes_accessed=8 * side * side, transcendentals=0
         ),
-    )(me, block, left_root, right_root, tail)
+    )(me, block, left_root, right_root, *tails)
 
 
 def gram_kernel(order, me_ref, *refs):
@@ -263,7 +301,7 @@
 
         @pl.when(step == m)
         def _():
-            block = grads[k][...]
+            block = grads[k][0 : grads[k].shape[1], :]
             gram_left = lax.dot_general(
                 block, block, (((1,), (1,)), ((), ())), preferred_element_type=jnp.float32
             )
@@ -275,7 +313,7 @@
 
 
 def gram_update(order, me, blocks, left_stats, right_stats):
-    count, side = len(blocks), blocks[0].shape[0]
+    count, side = len(blocks), blocks[0].shape[1]
     stat = pl.BlockSpec((1, 1, side, side), lambda i, me_ref: (0, me_ref[0] ^ i, 0, 0))
     whole = pl.BlockSpec(memory_space=pltpu.VMEM)
     return pl.pallas_call(
@@ -305,10 +343,10 @@
     me = me_ref[0]
     named = [owners_ref[me * count + j] for j in range(count)]
     blocks = [home_slot(named, me ^ m) for m in order]
-    global_sq = jnp.zeros((1, 1), jnp.float32)
-    for rows in [tail_ref[...]] + [piece[side:, :] for piece in pieces if piece.shape[0] > side]:
-        terms = rows[:, 0:1].astype(jnp.float32)
-        global_sq = global_sq + jnp.sum(terms, axis=0, keepdims=True)
+    global_sq = from_rows(tail_ref[...])
+    for piece in pieces:
+        if piece.shape[0] > side:
+            global_sq = global_sq + from_rows(piece[side:, :])
     for k, piece in enumerate(pieces):
         pre_float = piece[0:side, :].astype(jnp.float32)
         row = jnp.sum(pre_float * pre_float, axis=0, keepdims=True)
@@ -368,25 +406,29 @@
     me = lax.axis_index("fsdp").astype(jnp.int32).reshape(1)
     owner_list = owners[0, :, 0]
     half = count // 2
-    order = [0, half, *range(1, half), *range(half + 1, count)]
+    order = [0, half, *range(1, half), *range(count - 1, half, -1)]
+    near = [m for m in order if 0 < m < half]
 
     def swap(value, m, axis="fsdp"):
         if m == 0:
             return value
         return lax.ppermute(value, axis, [(i, i ^ m) for i in range(lax.axis_size(axis))])
 
-    outgoing = route(order, owner_list, me, gradients)
-    received = [swap(block, m) for m, block in zip(order, outgoing)]
+    outgoing = dict(zip(order, route(order, owner_list, me, gradients)))
     squares, total = adam_squares(gradients, second_moment)
     for k in doublings(layers):
         total = total + swap(total, k, "layer")
-    tail = sum_tail(total, side)
+    outgoing.update(zip(near, attach(total, [outgoing[m] for m in near])))
+    received = {m: swap(outgoing[m], m) for m in order}
+    tail = half_sum(total, [received[m] for m in near])
     returned = []
-    for m, block in zip(order, received):
-        rows = TAIL if m else 0
-        done = precondition(m, rows, me, block, left_root, right_root, tail)
+    for m in order:
+        tails = (tail,) if m == half else ()
+        done = precondition(m, me, received[m], left_root, right_root, *tails)
         returned.append(swap(done, m))
-    new_left, new_right = gram_update(order, me, received, left_stats, right_stats)
+    new_left, new_right = gram_update(
+        order, me, [received[m] for m in order], left_stats, right_stats
+    )
     entries = float(owner_list.shape[0] * layers * side * side)
     update = finish(order, owner_list, me, returned, squares, tail, entries)
     return (update, new_left, new_right)
@@ -395,7 +437,7 @@
 def per_device(gradients, second_moment, owners, left_stats, right_stats, left_root, right_root):
     owner_count, blocks, slots = lax.axis_size("fsdp"), gradients.shape[1], left_stats.shape[1]
     layers = lax.axis_size("layer")
-    paired = owner_count == blocks == slots
+    paired = owner_count == blocks == slots and owner_count >= 4
     paired = paired and owner_count & (owner_count - 1) == 0 and layers & (layers - 1) == 0
     body = per_device_exchange if paired else per_device_general
     return body(

time: 56.4 us -> 58.5 us (1.037)
  waiting for transfers between devices: 11.3 us -> 17.8 us
  starting transfers between devices: 30.8 us -> 26.2 us
    ppermute x16, waiting for transfers between devices: 11.3 us -> 17.8 us  [swap(): lax.ppermute(value, axis, [(i, i ^ m) for i in range(lax.axis_size(axis))])]
    ppermute x16, starting transfers between devices: 30.8 us -> 26.2 us  [swap(): lax.ppermute(value, axis, [(i, i ^ m) for i in range(lax.axis_size(axis))])]
    pallas_call x9 -> x10, Pallas kernels: 2.76 us -> 2.98 us  [the longest x8 2.64 us: precondition(): pl.pallas_call(functools.partial(precondition_kernel, m), grid_spec=pltpu...]
  transfers between devices with their start and end apart: 16 -> 16, of which waited for: 5 -> 6; matrix products, arithmetic and copies ran while one was open for 0% -> 0% of each run, Pallas kernels for 18% -> 17%
where the time goes in v3:
time: 58.5 us; the launch traced here: 58.4 us
  starting transfers between devices  26.2 us (45%)
  waiting for transfers between devices  17.8 us (30%)
  Pallas kernels  13.5 us (23%)
  between operations  0.83 us (1%)
    ppermute x16, starting transfers between devices, swap(): lax.ppermute(value, axis, [(i, i ^ m) for i in range(lax.axis_size(axis))])  26.2 us
    ppermute x16, waiting for transfers between devices, swap(): lax.ppermute(value, axis, [(i, i ^ m) for i in range(lax.axis_size(axis))])  17.8 us
    pallas_call x1, Pallas kernels, gram_update(): pl.pallas_call(functools.partial(gram_kernel, order), grid_spec=pltpu.Pre...  4.69 us
    pallas_call x8, Pallas kernels, precondition(): pl.pallas_call(functools.partial(precondition_kernel, m), grid_spec=pltpu...  2.64 us
    pallas_call x1, Pallas kernels, adam_squares(): pl.pallas_call(adam_kernel, in_specs=[hbm, hbm], out_specs=[pl.BlockSpec(...  2.53 us
    pallas_call x1, Pallas kernels, finish(): pl.pallas_call(functools.partial(finish_kernel, order, entries), grid_spe...  1.79 us
    pallas_call x1, Pallas kernels, route(): pl.pallas_call(functools.partial(route_kernel, order), in_specs=[hbm, pl....  1.46 us
  transfers between devices with their start and end apart: 16, of which 6 were waited for; matrix products, arithmetic and copies ran while one was open for 0% of the time, Pallas kernels for 17%

profile of v3, /device:TPU:0, one launch (start us, length us, event | category | flops | bytes accessed | tf_op | source)
XLA Modules:
  0.0 58.4 jit_solution(6176470902728001040)
XLA Ops:
  0.7 1.5 %shard_map.94 = (bf16[256,256]{1,0:T(8,128)(2,1)S(1)}, bf16[256,256]{1,0:T(8,128)(2,1)S(1)}, bf16[256,256]{1,0:T(8,128)(2,1)S(1)}, bf16[256,256]{1,0:T(8,128)(2,...) custom-call(s32[64]{0:T(128)} %bitcast.2, ...), custom_call_target="tpu_custom_call" | custom-call | bytes 2097152 | tf_op jit(solution)/shard_map/pallas_call | solution.py:128
  2.1 6.0 %collective-permute-start.10 = (bf16[256,256]{1,0:T(8,128)(2,1)S(1)}, bf16[256,256]{1,0:T(8,128)(2,1)S(1)}, u32[]{:S(2)}, u32[]{:S(2)}) collective-permute-start(bf16[256,256]{1,0:T(8,128)(2,1)S(1)} %get-tuple-element.27), channel_id=1, source_target_pairs={{0,28},{4,24},{8,20},{12,16},{16,12},{20,8},{24,4},{28,0},{1,29},{... | collective-permute-start | bytes 393224 | tf_op jit(solution)/shard_map/ppermute | solution.py:415
  8.2 0.2 collective-permute-start.12
  8.4 2.5 %shard_map.96 = (f32[8,128]{1,0:T(8,128)S(1)}, f32[8,128]{1,0:T(8,128)S(1)}) custom-call(bf16[1,8,256,256]{3,2,1,0:T(8,128)(2,1)} %grad_hbm.3, f32[1,8,256,256]{3,2,1,0:T(8,128)} %moment_hbm.1), custom_call_target="tpu_custom_call" | custom-call | flops 4194304 | bytes 3145728 | tf_op jit(solution)/shard_map/pallas_call | solution.py:179
  10.9 0.1 collective-permute-start.1
  11.0 1.2 %collective-permute-done.1 = f32[8,128]{1,0:T(8,128)S(1)} collective-permute-done((f32[8,128]{1,0:T(8,128)S(1)}, f32[8,128]{1,0:T(8,128)S(1)}, u32[]{:S(2)}, u32[]{:S(2)}) %collective-permute-start.1) | collective-permute-done | bytes 4128 | tf_op jit(solution)/shard_map/ppermute | solution.py:415
  12.2 1.5 %collective-permute-start.2 = (f32[8,128]{1,0:T(8,128)S(1)}, f32[8,128]{1,0:T(8,128)S(1)}, u32[]{:S(2)}, u32[]{:S(2)}) collective-permute-start(f32[8,128]{1,0:T(8,128)S(1)} %add.6), channel_id=1, source_target_pairs={{0,2},{1,3},{2,0},{3,1},{4,6},{5,7},{6,4},{7,5},{8,10},{9,11},{10,... | collective-permute-start | bytes 12296 | tf_op jit(solution)/shard_map/ppermute | solution.py:415
  13.7 2.1 %collective-permute-done.2 = f32[8,128]{1,0:T(8,128)S(1)} collective-permute-done((f32[8,128]{1,0:T(8,128)S(1)}, f32[8,128]{1,0:T(8,128)S(1)}, u32[]{:S(2)}, u32[]{:S(2)}) %collective-permute-start.2) | collective-permute-done | bytes 4128 | tf_op jit(solution)/shard_map/ppermute | solution.py:415
  15.8 0.1 shard_map.97
  15.9 0.5 collective-permute-start.3
  16.4 1.8 %collective-permute-start.14 = (bf16[256,256]{1,0:T(8,128)(2,1)S(1)}, bf16[256,256]{1,0:T(8,128)(2,1)S(1)}, u32[]{:S(2)}, u32[]{:S(2)}) collective-permute-start(bf16[256,256]{1,0:T(8,128)(2,1)S(1)} %get-tuple-element.29), channel_id=1, source_target_pairs={{0,20},{4,16},{8,28},{12,24},{16,4},{20,0},{24,12},{28,8},{1,21},{... | collective-permute-start | bytes 393224 | tf_op jit(solution)/shard_map/ppermute | solution.py:415
  18.2 3.4 %collective-permute-start.4 = (bf16[272,256]{1,0:T(8,128)(2,1)S(1)}, bf16[272,256]{1,0:T(8,128)(2,1)S(1)}, u32[]{:S(2)}, u32[]{:S(2)}) collective-permute-start(bf16[272,256]{1,0:T(8,128)(2,1)S(1)} %get-tuple-element.25), channel_id=1, source_target_pairs={{0,8},{4,12},{8,0},{12,4},{16,24},{20,28},{24,16},{28,20},{1,9},{5... | collective-permute-start | bytes 417800 | tf_op jit(solution)/shard_map/ppermute | solution.py:415
  21.6 0.0 collective-permute-done.10.grad_ref.refs_5_
  21.6 0.0 collective-permute-start.5
  21.6 0.0 collective-permute-done.12.grad_ref.refs_6_
  21.6 0.6 %collective-permute-start = (bf16[256,256]{1,0:T(8,128)(2,1)S(1)}, bf16[256,256]{1,0:T(8,128)(2,1)S(1)}, u32[]{:S(2)}, u32[]{:S(2)}) collective-permute-start(bf16[256,256]{1,0:T(8,128)(2,1)S(1)} %get-tuple-element.19), channel_id=1, source_target_pairs={{0,16},{4,20},{8,24},{12,28},{16,0},{20,4},{24,8},{28,12},{1,17},{... | collective-permute-start | bytes 393224 | tf_op jit(solution)/shard_map/ppermute | solution.py:415
  22.3 0.3 shard_map.103
  22.6 0.3 shard_map.104
  22.9 3.1 %collective-permute-done.14.grad_ref.refs_7_ = bf16[256,256]{1,0:T(8,128)(2,1)S(1)} collective-permute-done((bf16[256,256]{1,0:T(8,128)(2,1)S(1)}, bf16[256,256]{1,0:T(8,128)(2,1)S(1)}, u32[]{:S(2)}, u32[]{:S(2)}) %collective-permute-start.14) | collective-permute-done | bytes 131104 | tf_op jit(solution)/shard_map/ppermute | solution.py:415
  26.0 3.4 %collective-permute-start.11 = (bf16[256,256]{1,0:T(8,128)(2,1)S(1)}, bf16[256,256]{1,0:T(8,128)(2,1)S(1)}, u32[]{:S(2)}, u32[]{:S(2)}) collective-permute-start(bf16[256,256]{1,0:T(8,128)(2,1)S(1)} %shard_map.103), channel_id=1, source_target_pairs={{0,28},{4,24},{8,20},{12,16},{16,12},{20,8},{24,4},{28,0},{1,29},{... | collective-permute-start | bytes 393224 | tf_op jit(solution)/shard_map/ppermute | solution.py:415
  29.4 0.0 collective-permute-done.3.refs_0_.grad_ref.refs_2_
  29.4 1.4 %collective-permute-start.13 = (bf16[256,256]{1,0:T(8,128)(2,1)S(1)}, bf16[256,256]{1,0:T(8,128)(2,1)S(1)}, u32[]{:S(2)}, u32[]{:S(2)}) collective-permute-start(bf16[256,256]{1,0:T(8,128)(2,1)S(1)} %shard_map.104), channel_id=1, source_target_pairs={{0,24},{4,28},{8,16},{12,20},{16,8},{20,12},{24,0},{28,4},{1,25},{... | collective-permute-start | bytes 393224 | tf_op jit(solution)/shard_map/ppermute | solution.py:415
  30.8 0.3 shard_map.105
  31.2 0.0 collective-permute-done.4.refs_1_.grad_ref.refs_3_
  31.2 0.1 collective-permute-start.15
  31.2 1.2 %collective-permute-done.5.refs_2_.grad_ref.refs_4_ = bf16[272,256]{1,0:T(8,128)(2,1)S(1)} collective-permute-done((bf16[272,256]{1,0:T(8,128)(2,1)S(1)}, bf16[272,256]{1,0:T(8,128)(2,1)S(1)}, u32[]{:S(2)}, u32[]{:S(2)}) %collective-permute-start.5) | collective-permute-done | bytes 139296 | tf_op jit(solution)/shard_map/ppermute | solution.py:415
  32.4 0.2 shard_map.98.refs_0_.refs_9_
  32.6 9.1 %collective-permute-done.grad_ref.refs_1_ = bf16[256,256]{1,0:T(8,128)(2,1)S(1)} collective-permute-done((bf16[256,256]{1,0:T(8,128)(2,1)S(1)}, bf16[256,256]{1,0:T(8,128)(2,1)S(1)}, u32[]{:S(2)}, u32[]{:S(2)}) %collective-permute-start) | collective-permute-done | bytes 131104 | tf_op jit(solution)/shard_map/ppermute | solution.py:415
  41.7 0.3 shard_map.99
  42.1 0.1 collective-permute-start.6
  42.2 0.3 shard_map.100
  42.5 1.5 %collective-permute-start.7 = (bf16[256,256]{1,0:T(8,128)(2,1)S(1)}, bf16[256,256]{1,0:T(8,128)(2,1)S(1)}, u32[]{:S(2)}, u32[]{:S(2)}) collective-permute-start(bf16[256,256]{1,0:T(8,128)(2,1)S(1)} %shard_map.100), channel_id=1, source_target_pairs={{0,4},{4,0},{8,12},{12,8},{16,20},{20,16},{24,28},{28,24},{1,5},{5... | collective-permute-start | bytes 393224 | tf_op jit(solution)/shard_map/ppermute | solution.py:415
  44.0 0.3 shard_map.101
  44.3 0.0 copy-start.2
  44.3 0.0 copy-start.3
  44.3 0.3 shard_map.102
  44.7 0.0 collective-permute-done.11.refs_5_
  44.7 2.1 %collective-permute-start.8 = (bf16[256,256]{1,0:T(8,128)(2,1)S(1)}, bf16[256,256]{1,0:T(8,128)(2,1)S(1)}, u32[]{:S(2)}, u32[]{:S(2)}) collective-permute-start(bf16[256,256]{1,0:T(8,128)(2,1)S(1)} %shard_map.101), channel_id=1, source_target_pairs={{0,8},{4,12},{8,0},{12,4},{16,24},{20,28},{24,16},{28,20},{1,9},{5... | collective-permute-start | bytes 393224 | tf_op jit(solution)/shard_map/ppermute | solution.py:415
  46.8 3.5 %collective-permute-start.9 = (bf16[256,256]{1,0:T(8,128)(2,1)S(1)}, bf16[256,256]{1,0:T(8,128)(2,1)S(1)}, u32[]{:S(2)}, u32[]{:S(2)}) collective-permute-start(bf16[256,256]{1,0:T(8,128)(2,1)S(1)} %shard_map.102), channel_id=1, source_target_pairs={{0,12},{4,8},{8,4},{12,0},{16,28},{20,24},{24,20},{28,16},{1,13},{... | collective-permute-start | bytes 393224 | tf_op jit(solution)/shard_map/ppermute | solution.py:415
  50.3 0.3 shard_map.95.refs_0_
  50.6 0.0 copy-start.4
  50.6 4.7 %shard_map.107 = (f32[1,8,256,256]{3,2,1,0:T(8,128)}, f32[1,8,256,256]{3,2,1,0:T(8,128)}) custom-call(s32[1]{0:T(128)} %bitcast.1.me_ref, bf16[256,256]{1,0:T(8,128)(2,1)S(1)} %get-tuple-element.18.grad_ref.refs_0_, bf16[256,256]{1,0:T(8,128)(2,1)S(1)} %collective-permute-done.grad_ref.refs_1_, ...), custom_call_target="tpu_custom_call" | custom-call | flops 536870912 | bytes 9437184 | tf_op jit(solution)/shard_map/pallas_call | solution.py:319
  55.3 0.0 collective-permute-done.15.refs_7_
  55.3 0.0 collective-permute-done.7.refs_2_
  55.3 0.0 collective-permute-done.8.refs_3_
  55.3 1.2 %collective-permute-done.9.refs_4_ = bf16[256,256]{1,0:T(8,128)(2,1)S(1)} collective-permute-done((bf16[256,256]{1,0:T(8,128)(2,1)S(1)}, bf16[256,256]{1,0:T(8,128)(2,1)S(1)}, u32[]{:S(2)}, u32[]{:S(2)}) %collective-permute-start.9) | collective-permute-done | bytes 131104 | tf_op jit(solution)/shard_map/ppermute | solution.py:415
  56.6 0.0 collective-permute-done.6.refs_1_
  56.6 1.8 %shard_map.106 = bf16[1,8,256,256]{3,2,1,0:T(8,128)(2,1)} custom-call(s32[64]{0:T(128)S(1)} %bitcast.3, s32[1]{0:T(128)} %bitcast.1.me_ref, bf16[256,256]{1,0:T(8,128)(2,1)S(1)} %shard_map.95.refs_0_, bf16[272,256]{1,0:T(8,128)(2,1)S(1)} %collective-permute-done.6.refs_1_, bf16[256,256]{1,0:T(8,128)(2,1)S(1)} %collective-permute-done.7.refs_2_, ...), custom_call_target="tpu_custom_call" | custom-call | flops 3145728 | bytes 2097152 | tf_op jit(solution)/shard_map/pallas_call | solution.py:375
  (10 shorter events, 0.0 us)
Async XLA Ops:
  0.6 21.6 %copy-start = (bf16[1,8,256,256]{3,2,1,0:T(8,128)(2,1)S(1)}, bf16[1,8,256,256]{3,2,1,0:T(8,128)(2,1)}, u32[]{:S(2)}) copy-start(bf16[1,8,256,256]{3,2,1,0:T(8,128)(2,1)} %left_ref.15) | copy-start | bytes 3145732
  0.6 21.6 %copy-start.1 = (bf16[1,8,256,256]{3,2,1,0:T(8,128)(2,1)S(1)}, bf16[1,8,256,256]{3,2,1,0:T(8,128)(2,1)}, u32[]{:S(2)}) copy-start(bf16[1,8,256,256]{3,2,1,0:T(8,128)(2,1)} %right_ref.15) | copy-start | bytes 3145732
  2.1 19.5 %collective-permute-start.10 = (bf16[256,256]{1,0:T(8,128)(2,1)S(1)}, bf16[256,256]{1,0:T(8,128)(2,1)S(1)}, u32[]{:S(2)}, u32[]{:S(2)}) collective-permute-start(bf16[256,256]{1,0:T(8,128)(2,1)S(1)} %get-tuple-element.27), channel_id=1, source_target_pairs={{0,28},{4,24},{8,20},{12,16},{16,12},{20,8},{24,4},{28,0},{1,29},{... | collective-permute-start | bytes 393224 | tf_op jit(solution)/shard_map/ppermute | solution.py:415
  8.2 13.4 %collective-permute-start.12 = (bf16[256,256]{1,0:T(8,128)(2,1)S(1)}, bf16[256,256]{1,0:T(8,128)(2,1)S(1)}, u32[]{:S(2)}, u32[]{:S(2)}) collective-permute-start(bf16[256,256]{1,0:T(8,128)(2,1)S(1)} %get-tuple-element.28), channel_id=1, source_target_pairs={{0,24},{4,28},{8,16},{12,20},{16,8},{20,12},{24,0},{28,4},{1,25},{... | collective-permute-start | bytes 393224 | tf_op jit(solution)/shard_map/ppermute | solution.py:415
  10.9 1.2 %collective-permute-start.1 = (f32[8,128]{1,0:T(8,128)S(1)}, f32[8,128]{1,0:T(8,128)S(1)}, u32[]{:S(2)}, u32[]{:S(2)}) collective-permute-start(f32[8,128]{1,0:T(8,128)S(1)} %get-tuple-element.20), channel_id=1, source_target_pairs={{0,1},{1,0},{2,3},{3,2},{4,5},{5,4},{6,7},{7,6},{8,9},{9,8},{10,11... | collective-permute-start | bytes 12296 | tf_op jit(solution)/shard_map/ppermute | solution.py:415
  12.2 3.6 %collective-permute-start.2 = (f32[8,128]{1,0:T(8,128)S(1)}, f32[8,128]{1,0:T(8,128)S(1)}, u32[]{:S(2)}, u32[]{:S(2)}) collective-permute-start(f32[8,128]{1,0:T(8,128)S(1)} %add.6), channel_id=1, source_target_pairs={{0,2},{1,3},{2,0},{3,1},{4,6},{5,7},{6,4},{7,5},{8,10},{9,11},{10,... | collective-permute-start | bytes 12296 | tf_op jit(solution)/shard_map/ppermute | solution.py:415
  15.9 13.5 %collective-permute-start.3 = (bf16[272,256]{1,0:T(8,128)(2,1)S(1)}, bf16[272,256]{1,0:T(8,128)(2,1)S(1)}, u32[]{:S(2)}, u32[]{:S(2)}) collective-permute-start(bf16[272,256]{1,0:T(8,128)(2,1)S(1)} %get-tuple-element.24), channel_id=1, source_target_pairs={{0,4},{4,0},{8,12},{12,8},{16,20},{20,16},{24,28},{28,24},{1,5},{5... | collective-permute-start | bytes 417800 | tf_op jit(solution)/shard_map/ppermute | solution.py:415
  16.4 9.6 %collective-permute-start.14 = (bf16[256,256]{1,0:T(8,128)(2,1)S(1)}, bf16[256,256]{1,0:T(8,128)(2,1)S(1)}, u32[]{:S(2)}, u32[]{:S(2)}) collective-permute-start(bf16[256,256]{1,0:T(8,128)(2,1)S(1)} %get-tuple-element.29), channel_id=1, source_target_pairs={{0,20},{4,16},{8,28},{12,24},{16,4},{20,0},{24,12},{28,8},{1,21},{... | collective-permute-start | bytes 393224 | tf_op jit(solution)/shard_map/ppermute | solution.py:415
  18.2 12.9 %collective-permute-start.4 = (bf16[272,256]{1,0:T(8,128)(2,1)S(1)}, bf16[272,256]{1,0:T(8,128)(2,1)S(1)}, u32[]{:S(2)}, u32[]{:S(2)}) collective-permute-start(bf16[272,256]{1,0:T(8,128)(2,1)S(1)} %get-tuple-element.25), channel_id=1, source_target_pairs={{0,8},{4,12},{8,0},{12,4},{16,24},{20,28},{24,16},{28,20},{1,9},{5... | collective-permute-start | bytes 417800 | tf_op jit(solution)/shard_map/ppermute | solution.py:415
  21.6 10.8 %collective-permute-start.5 = (bf16[272,256]{1,0:T(8,128)(2,1)S(1)}, bf16[272,256]{1,0:T(8,128)(2,1)S(1)}, u32[]{:S(2)}, u32[]{:S(2)}) collective-permute-start(bf16[272,256]{1,0:T(8,128)(2,1)S(1)} %get-tuple-element.26), channel_id=1, source_target_pairs={{0,12},{4,8},{8,4},{12,0},{16,28},{20,24},{24,20},{28,16},{1,13},{... | collective-permute-start | bytes 417800 | tf_op jit(solution)/shard_map/ppermute | solution.py:415
  21.6 20.1 %collective-permute-start = (bf16[256,256]{1,0:T(8,128)(2,1)S(1)}, bf16[256,256]{1,0:T(8,128)(2,1)S(1)}, u32[]{:S(2)}, u32[]{:S(2)}) collective-permute-start(bf16[256,256]{1,0:T(8,128)(2,1)S(1)} %get-tuple-element.19), channel_id=1, source_target_pairs={{0,16},{4,20},{8,24},{12,28},{16,0},{20,4},{24,8},{28,12},{1,17},{... | collective-permute-start | bytes 393224 | tf_op jit(solution)/shard_map/ppermute | solution.py:415
  26.0 18.7 %collective-permute-start.11 = (bf16[256,256]{1,0:T(8,128)(2,1)S(1)}, bf16[256,256]{1,0:T(8,128)(2,1)S(1)}, u32[]{:S(2)}, u32[]{:S(2)}) collective-permute-start(bf16[256,256]{1,0:T(8,128)(2,1)S(1)} %shard_map.103), channel_id=1, source_target_pairs={{0,28},{4,24},{8,20},{12,16},{16,12},{20,8},{24,4},{28,0},{1,29},{... | collective-permute-start | bytes 393224 | tf_op jit(solution)/shard_map/ppermute | solution.py:415
  29.4 17.3 %collective-permute-start.13 = (bf16[256,256]{1,0:T(8,128)(2,1)S(1)}, bf16[256,256]{1,0:T(8,128)(2,1)S(1)}, u32[]{:S(2)}, u32[]{:S(2)}) collective-permute-start(bf16[256,256]{1,0:T(8,128)(2,1)S(1)} %shard_map.104), channel_id=1, source_target_pairs={{0,24},{4,28},{8,16},{12,20},{16,8},{20,12},{24,0},{28,4},{1,25},{... | collective-permute-start | bytes 393224 | tf_op jit(solution)/shard_map/ppermute | solution.py:415
  31.2 24.2 %collective-permute-start.15 = (bf16[256,256]{1,0:T(8,128)(2,1)S(1)}, bf16[256,256]{1,0:T(8,128)(2,1)S(1)}, u32[]{:S(2)}, u32[]{:S(2)}) collective-permute-start(bf16[256,256]{1,0:T(8,128)(2,1)S(1)} %shard_map.105), channel_id=1, source_target_pairs={{0,20},{4,16},{8,28},{12,24},{16,4},{20,0},{24,12},{28,8},{1,21},{... | collective-permute-start | bytes 393224 | tf_op jit(solution)/shard_map/ppermute | solution.py:415
  42.1 14.5 %collective-permute-start.6 = (bf16[272,256]{1,0:T(8,128)(2,1)S(1)}, bf16[272,256]{1,0:T(8,128)(2,1)S(1)}, u32[]{:S(2)}, u32[]{:S(2)}) collective-permute-start(bf16[272,256]{1,0:T(8,128)(2,1)S(1)} %shard_map.99), channel_id=1, source_target_pairs={{0,16},{4,20},{8,24},{12,28},{16,0},{20,4},{24,8},{28,12},{1,17},{... | collective-permute-start | bytes 417800 | tf_op jit(solution)/shard_map/ppermute | solution.py:415
  42.5 12.8 %collective-permute-start.7 = (bf16[256,256]{1,0:T(8,128)(2,1)S(1)}, bf16[256,256]{1,0:T(8,128)(2,1)S(1)}, u32[]{:S(2)}, u32[]{:S(2)}) collective-permute-start(bf16[256,256]{1,0:T(8,128)(2,1)S(1)} %shard_map.100), channel_id=1, source_target_pairs={{0,4},{4,0},{8,12},{12,8},{16,20},{20,16},{24,28},{28,24},{1,5},{5... | collective-permute-start | bytes 393224 | tf_op jit(solution)/shard_map/ppermute | solution.py:415
  44.3 6.3 %copy-start.2 = (f32[1,8,256,256]{3,2,1,0:T(8,128)S(1)}, f32[1,8,256,256]{3,2,1,0:T(8,128)}, u32[]{:S(2)}) copy-start(f32[1,8,256,256]{3,2,1,0:T(8,128)} %refs_8_.1) | copy-start | bytes 6291460
  44.3 6.3 %copy-start.3 = (f32[1,8,256,256]{3,2,1,0:T(8,128)S(1)}, f32[1,8,256,256]{3,2,1,0:T(8,128)}, u32[]{:S(2)}) copy-start(f32[1,8,256,256]{3,2,1,0:T(8,128)} %refs_9_.1) | copy-start | bytes 6291460
  44.7 10.7 %collective-permute-start.8 = (bf16[256,256]{1,0:T(8,128)(2,1)S(1)}, bf16[256,256]{1,0:T(8,128)(2,1)S(1)}, u32[]{:S(2)}, u32[]{:S(2)}) collective-permute-start(bf16[256,256]{1,0:T(8,128)(2,1)S(1)} %shard_map.101), channel_id=1, source_target_pairs={{0,8},{4,12},{8,0},{12,4},{16,24},{20,28},{24,16},{28,20},{1,9},{5... | collective-permute-start | bytes 393224 | tf_op jit(solution)/shard_map/ppermute | solution.py:415
  46.8 9.8 %collective-permute-start.9 = (bf16[256,256]{1,0:T(8,128)(2,1)S(1)}, bf16[256,256]{1,0:T(8,128)(2,1)S(1)}, u32[]{:S(2)}, u32[]{:S(2)}) collective-permute-start(bf16[256,256]{1,0:T(8,128)(2,1)S(1)} %shard_map.102), channel_id=1, source_target_pairs={{0,12},{4,8},{8,4},{12,0},{16,28},{20,24},{24,20},{28,16},{1,13},{... | collective-permute-start | bytes 393224 | tf_op jit(solution)/shard_map/ppermute | solution.py:415
  50.6 6.0 %copy-start.4 = (s32[1,64,1]{1,2,0:T(1,128)S(1)}, s32[1,64,1]{1,2,0:T(1,128)}, u32[]{:S(2)}) copy-start(s32[1,64,1]{1,2,0:T(1,128)} %param.9) | copy-start | bytes 772

commit v4 on v2

--- a/solution.py
+++ b/solution.py
@@ -368,7 +368,7 @@
     me = lax.axis_index("fsdp").astype(jnp.int32).reshape(1)
     owner_list = owners[0, :, 0]
     half = count // 2
-    order = [0, half, *range(1, half), *range(half + 1, count)]
+    order = [*range(half - 1), half, half - 1, *range(half + 1, count)]
 
     def swap(value, m, axis="fsdp"):
         if m == 0:

time: 56.4 us -> 56.3 us (level)
  waiting for transfers between devices: 11.3 us -> 7.38 us
  starting transfers between devices: 30.8 us -> 34.6 us
    ppermute x16, waiting for transfers between devices: 11.3 us -> 7.38 us  [swap(): lax.ppermute(value, axis, [(i, i ^ m) for i in range(lax.axis_size(axis))])]
    ppermute x16, starting transfers between devices: 30.8 us -> 34.6 us  [swap(): lax.ppermute(value, axis, [(i, i ^ m) for i in range(lax.axis_size(axis))])]
  transfers between devices with their start and end apart: 16 -> 16, of which waited for: 5 -> 4; matrix products, arithmetic and copies ran while one was open for 0% -> 0% of each run, Pallas kernels for 18% -> 18%
where the time goes in v4:
time: 56.3 us; the launch traced here: 56.2 us
  starting transfers between devices  34.6 us (61%)
  Pallas kernels  13.2 us (23%)
  waiting for transfers between devices  7.38 us (13%)
  between operations  0.86 us (2%)
    ppermute x16, starting transfers between devices, swap(): lax.ppermute(value, axis, [(i, i ^ m) for i in range(lax.axis_size(axis))])  34.6 us
    ppermute x16, waiting for transfers between devices, swap(): lax.ppermute(value, axis, [(i, i ^ m) for i in range(lax.axis_size(axis))])  7.38 us
    pallas_call x1, Pallas kernels, gram_update(): pl.pallas_call(functools.partial(gram_kernel, order), grid_spec=pltpu.Pre...  4.68 us
    pallas_call x8, Pallas kernels, precondition(): pl.pallas_call(functools.partial(precondition_kernel, m, rows), grid_spec...  2.64 us
    pallas_call x1, Pallas kernels, adam_squares(): pl.pallas_call(adam_kernel, in_specs=[hbm, hbm], out_specs=[pl.BlockSpec(...  2.53 us
    pallas_call x1, Pallas kernels, finish(): pl.pallas_call(functools.partial(finish_kernel, order, entries), grid_spe...  1.81 us
    pallas_call x1, Pallas kernels, route(): pl.pallas_call(functools.partial(route_kernel, order), in_specs=[hbm, pl....  1.46 us
  transfers between devices with their start and end apart: 16, of which 4 were waited for; matrix products, arithmetic and copies ran while one was open for 0% of the time, Pallas kernels for 18%

profile of v4, /device:TPU:0, one launch (start us, length us, event | category | flops | bytes accessed | tf_op | source)
XLA Modules:
  0.0 56.2 jit_solution(6947878422930159913)
XLA Ops:
  0.7 1.5 %shard_map.94 = (bf16[256,256]{1,0:T(8,128)(2,1)S(1)}, bf16[256,256]{1,0:T(8,128)(2,1)S(1)}, bf16[256,256]{1,0:T(8,128)(2,1)S(1)}, bf16[256,256]{1,0:T(8,128)(2,...) custom-call(s32[64]{0:T(128)} %bitcast.2, ...), custom_call_target="tpu_custom_call" | custom-call | bytes 2097152 | tf_op jit(solution)/shard_map/pallas_call | solution.py:128
  2.1 6.0 %collective-permute-start.14 = (bf16[256,256]{1,0:T(8,128)(2,1)S(1)}, bf16[256,256]{1,0:T(8,128)(2,1)S(1)}, u32[]{:S(2)}, u32[]{:S(2)}) collective-permute-start(bf16[256,256]{1,0:T(8,128)(2,1)S(1)} %get-tuple-element.23), channel_id=1, source_target_pairs={{0,28},{4,24},{8,20},{12,16},{16,12},{20,8},{24,4},{28,0},{1,29},{... | collective-permute-start | bytes 393224 | tf_op jit(solution)/shard_map/ppermute | solution.py:376
  8.2 0.2 collective-permute-start.12
  8.4 0.4 collective-permute-start.2
  8.8 1.8 %collective-permute-start.10 = (bf16[256,256]{1,0:T(8,128)(2,1)S(1)}, bf16[256,256]{1,0:T(8,128)(2,1)S(1)}, u32[]{:S(2)}, u32[]{:S(2)}) collective-permute-start(bf16[256,256]{1,0:T(8,128)(2,1)S(1)} %get-tuple-element.21), channel_id=1, source_target_pairs={{0,20},{4,16},{8,28},{12,24},{16,4},{20,0},{24,12},{28,8},{1,21},{... | collective-permute-start | bytes 393224 | tf_op jit(solution)/shard_map/ppermute | solution.py:376
  10.6 2.5 %shard_map.95 = (f32[8,128]{1,0:T(8,128)S(1)}, f32[8,128]{1,0:T(8,128)S(1)}) custom-call(bf16[1,8,256,256]{3,2,1,0:T(8,128)(2,1)} %grad_hbm.3, f32[1,8,256,256]{3,2,1,0:T(8,128)} %moment_hbm.1), custom_call_target="tpu_custom_call" | custom-call | flops 4194304 | bytes 3145728 | tf_op jit(solution)/shard_map/pallas_call | solution.py:179
  13.2 0.1 collective-permute-start
  13.3 1.2 %collective-permute-done = f32[8,128]{1,0:T(8,128)S(1)} collective-permute-done((f32[8,128]{1,0:T(8,128)S(1)}, f32[8,128]{1,0:T(8,128)S(1)}, u32[]{:S(2)}, u32[]{:S(2)}) %collective-permute-start) | collective-permute-done | bytes 4128 | tf_op jit(solution)/shard_map/ppermute | solution.py:376
  14.4 1.5 %collective-permute-start.1 = (f32[8,128]{1,0:T(8,128)S(1)}, f32[8,128]{1,0:T(8,128)S(1)}, u32[]{:S(2)}, u32[]{:S(2)}) collective-permute-start(f32[8,128]{1,0:T(8,128)S(1)} %add.6), channel_id=1, source_target_pairs={{0,2},{1,3},{2,0},{3,1},{4,6},{5,7},{6,4},{7,5},{8,10},{9,11},{10,... | collective-permute-start | bytes 12296 | tf_op jit(solution)/shard_map/ppermute | solution.py:376
  15.9 2.1 %collective-permute-done.1 = f32[8,128]{1,0:T(8,128)S(1)} collective-permute-done((f32[8,128]{1,0:T(8,128)S(1)}, f32[8,128]{1,0:T(8,128)S(1)}, u32[]{:S(2)}, u32[]{:S(2)}) %collective-permute-start.1) | collective-permute-done | bytes 4128 | tf_op jit(solution)/shard_map/ppermute | solution.py:376
  18.0 2.1 %collective-permute-start.6 = (bf16[256,256]{1,0:T(8,128)(2,1)S(1)}, bf16[256,256]{1,0:T(8,128)(2,1)S(1)}, u32[]{:S(2)}, u32[]{:S(2)}) collective-permute-start(bf16[256,256]{1,0:T(8,128)(2,1)S(1)} %get-tuple-element.19), channel_id=1, source_target_pairs={{0,16},{4,20},{8,24},{12,28},{16,0},{20,4},{24,8},{28,12},{1,17},{... | collective-permute-start | bytes 393224 | tf_op jit(solution)/shard_map/ppermute | solution.py:376
  20.2 0.1 shard_map.96.tail_ref.refs_9_
  20.3 0.0 collective-permute-done.14.grad_ref.refs_7_
  20.3 1.3 %collective-permute-start.8 = (bf16[256,256]{1,0:T(8,128)(2,1)S(1)}, bf16[256,256]{1,0:T(8,128)(2,1)S(1)}, u32[]{:S(2)}, u32[]{:S(2)}) collective-permute-start(bf16[256,256]{1,0:T(8,128)(2,1)S(1)} %get-tuple-element.20), channel_id=1, source_target_pairs={{0,12},{4,8},{8,4},{12,0},{16,28},{20,24},{24,20},{28,16},{1,13},{... | collective-permute-start | bytes 393224 | tf_op jit(solution)/shard_map/ppermute | solution.py:376
  21.6 0.3 shard_map.104
  22.0 0.0 collective-permute-done.12.grad_ref.refs_6_
  22.0 2.7 %collective-permute-start.15 = (bf16[272,256]{1,0:T(8,128)(2,1)S(1)}, bf16[272,256]{1,0:T(8,128)(2,1)S(1)}, u32[]{:S(2)}, u32[]{:S(2)}) collective-permute-start(bf16[272,256]{1,0:T(8,128)(2,1)S(1)} %shard_map.104), channel_id=1, source_target_pairs={{0,28},{4,24},{8,20},{12,16},{16,12},{20,8},{24,4},{28,0},{1,29},{... | collective-permute-start | bytes 417800 | tf_op jit(solution)/shard_map/ppermute | solution.py:376
  24.7 0.3 shard_map.103
  25.1 0.0 collective-permute-done.2.grad_ref.refs_1_
  25.1 2.1 %collective-permute-start.13 = (bf16[272,256]{1,0:T(8,128)(2,1)S(1)}, bf16[272,256]{1,0:T(8,128)(2,1)S(1)}, u32[]{:S(2)}, u32[]{:S(2)}) collective-permute-start(bf16[272,256]{1,0:T(8,128)(2,1)S(1)} %shard_map.103), channel_id=1, source_target_pairs={{0,24},{4,28},{8,16},{12,20},{16,8},{20,12},{24,0},{28,4},{1,25},{... | collective-permute-start | bytes 417800 | tf_op jit(solution)/shard_map/ppermute | solution.py:376
  27.2 2.5 %collective-permute-done.10.grad_ref.refs_5_ = bf16[256,256]{1,0:T(8,128)(2,1)S(1)} collective-permute-done((bf16[256,256]{1,0:T(8,128)(2,1)S(1)}, bf16[256,256]{1,0:T(8,128)(2,1)S(1)}, u32[]{:S(2)}, u32[]{:S(2)}) %collective-permute-start.10) | collective-permute-done | bytes 131104 | tf_op jit(solution)/shard_map/ppermute | solution.py:376
  29.7 4.3 %collective-permute-start.4 = (bf16[256,256]{1,0:T(8,128)(2,1)S(1)}, bf16[256,256]{1,0:T(8,128)(2,1)S(1)}, u32[]{:S(2)}, u32[]{:S(2)}) collective-permute-start(bf16[256,256]{1,0:T(8,128)(2,1)S(1)} %get-tuple-element.18), channel_id=1, source_target_pairs={{0,8},{4,12},{8,0},{12,4},{16,24},{20,28},{24,16},{28,20},{1,9},{5... | collective-permute-start | bytes 393224 | tf_op jit(solution)/shard_map/ppermute | solution.py:376
  34.0 0.3 shard_map.98
  34.4 0.3 shard_map.102
  34.7 0.0 collective-permute-done.8.grad_ref.refs_4_
  34.7 6.4 %collective-permute-start.11 = (bf16[272,256]{1,0:T(8,128)(2,1)S(1)}, bf16[272,256]{1,0:T(8,128)(2,1)S(1)}, u32[]{:S(2)}, u32[]{:S(2)}) collective-permute-start(bf16[272,256]{1,0:T(8,128)(2,1)S(1)} %shard_map.102), channel_id=1, source_target_pairs={{0,20},{4,16},{8,28},{12,24},{16,4},{20,0},{24,12},{28,8},{1,21},{... | collective-permute-start | bytes 417800 | tf_op jit(solution)/shard_map/ppermute | solution.py:376
  41.1 0.3 shard_map.101
  41.4 0.0 collective-permute-done.6.grad_ref.refs_3_
  41.4 2.2 %collective-permute-start.9 = (bf16[272,256]{1,0:T(8,128)(2,1)S(1)}, bf16[272,256]{1,0:T(8,128)(2,1)S(1)}, u32[]{:S(2)}, u32[]{:S(2)}) collective-permute-start(bf16[272,256]{1,0:T(8,128)(2,1)S(1)} %shard_map.101), channel_id=1, source_target_pairs={{0,12},{4,8},{8,4},{12,0},{16,28},{20,24},{24,20},{28,16},{1,13},{... | collective-permute-start | bytes 417800 | tf_op jit(solution)/shard_map/ppermute | solution.py:376
  43.6 0.3 shard_map.100
  44.0 0.0 copy-start.2
  44.0 0.0 copy-start.3
  44.0 0.0 collective-permute-done.4.grad_ref.refs_2_
  44.0 0.1 collective-permute-start.7
  44.1 0.3 shard_map.99
  44.4 0.0 collective-permute-done.15.refs_7_
  44.4 1.7 %collective-permute-start.5 = (bf16[272,256]{1,0:T(8,128)(2,1)S(1)}, bf16[272,256]{1,0:T(8,128)(2,1)S(1)}, u32[]{:S(2)}, u32[]{:S(2)}) collective-permute-start(bf16[272,256]{1,0:T(8,128)(2,1)S(1)} %shard_map.99), channel_id=1, source_target_pairs={{0,8},{4,12},{8,0},{12,4},{16,24},{20,28},{24,16},{28,20},{1,9},{5... | collective-permute-start | bytes 417800 | tf_op jit(solution)/shard_map/ppermute | solution.py:376
  46.1 0.0 collective-permute-done.13.refs_6_
  46.1 1.6 %collective-permute-start.3 = (bf16[272,256]{1,0:T(8,128)(2,1)S(1)}, bf16[272,256]{1,0:T(8,128)(2,1)S(1)}, u32[]{:S(2)}, u32[]{:S(2)}) collective-permute-start(bf16[272,256]{1,0:T(8,128)(2,1)S(1)} %shard_map.98), channel_id=1, source_target_pairs={{0,4},{4,0},{8,12},{12,8},{16,20},{20,16},{24,28},{28,24},{1,5},{5... | collective-permute-start | bytes 417800 | tf_op jit(solution)/shard_map/ppermute | solution.py:376
  47.7 0.3 shard_map.97.refs_0_
  48.1 0.0 copy-start.4
  48.1 4.7 %shard_map.106 = (f32[1,8,256,256]{3,2,1,0:T(8,128)}, f32[1,8,256,256]{3,2,1,0:T(8,128)}) custom-call(s32[1]{0:T(128)} %bitcast.1.me_ref, bf16[256,256]{1,0:T(8,128)(2,1)S(1)} %get-tuple-element.15.grad_ref.refs_0_, bf16[256,256]{1,0:T(8,128)(2,1)S(1)} %collective-permute-done.2.grad_ref.refs_1_, ...), custom_call_target="tpu_custom_call" | custom-call | flops 536870912 | bytes 9437184 | tf_op jit(solution)/shard_map/pallas_call | solution.py:281
  52.8 0.0 collective-permute-done.11.refs_5_
  52.8 0.0 collective-permute-done.9.refs_4_
  52.8 1.6 %collective-permute-done.7.refs_3_ = bf16[272,256]{1,0:T(8,128)(2,1)S(1)} collective-permute-done((bf16[272,256]{1,0:T(8,128)(2,1)S(1)}, bf16[272,256]{1,0:T(8,128)(2,1)S(1)}, u32[]{:S(2)}, u32[]{:S(2)}) %collective-permute-start.7) | collective-permute-done | bytes 139296 | tf_op jit(solution)/shard_map/ppermute | solution.py:376
  54.4 0.0 collective-permute-done.5.refs_2_
  54.4 0.0 collective-permute-done.3.refs_1_
  54.4 1.8 %shard_map.105 = bf16[1,8,256,256]{3,2,1,0:T(8,128)(2,1)} custom-call(s32[64]{0:T(128)S(1)} %bitcast.3, s32[1]{0:T(128)} %bitcast.1.me_ref, bf16[256,256]{1,0:T(8,128)(2,1)S(1)} %shard_map.97.refs_0_, bf16[272,256]{1,0:T(8,128)(2,1)S(1)} %collective-permute-done.3.refs_1_, bf16[272,256]{1,0:T(8,128)(2,1)S(1)} %collective-permute-done.5.refs_2_, ...), custom_call_target="tpu_custom_call" | custom-call | flops 3145728 | bytes 2097152 | tf_op jit(solution)/shard_map/pallas_call | solution.py:337
  (9 shorter events, 0.0 us)
Async XLA Ops:
  0.6 21.0 %copy-start = (bf16[1,8,256,256]{3,2,1,0:T(8,128)(2,1)S(1)}, bf16[1,8,256,256]{3,2,1,0:T(8,128)(2,1)}, u32[]{:S(2)}) copy-start(bf16[1,8,256,256]{3,2,1,0:T(8,128)(2,1)} %left_ref.15) | copy-start | bytes 3145732
  0.6 21.0 %copy-start.1 = (bf16[1,8,256,256]{3,2,1,0:T(8,128)(2,1)S(1)}, bf16[1,8,256,256]{3,2,1,0:T(8,128)(2,1)}, u32[]{:S(2)}) copy-start(bf16[1,8,256,256]{3,2,1,0:T(8,128)(2,1)} %right_ref.15) | copy-start | bytes 3145732
  2.1 18.2 %collective-permute-start.14 = (bf16[256,256]{1,0:T(8,128)(2,1)S(1)}, bf16[256,256]{1,0:T(8,128)(2,1)S(1)}, u32[]{:S(2)}, u32[]{:S(2)}) collective-permute-start(bf16[256,256]{1,0:T(8,128)(2,1)S(1)} %get-tuple-element.23), channel_id=1, source_target_pairs={{0,28},{4,24},{8,20},{12,16},{16,12},{20,8},{24,4},{28,0},{1,29},{... | collective-permute-start | bytes 393224 | tf_op jit(solution)/shard_map/ppermute | solution.py:376
  8.2 13.8 %collective-permute-start.12 = (bf16[256,256]{1,0:T(8,128)(2,1)S(1)}, bf16[256,256]{1,0:T(8,128)(2,1)S(1)}, u32[]{:S(2)}, u32[]{:S(2)}) collective-permute-start(bf16[256,256]{1,0:T(8,128)(2,1)S(1)} %get-tuple-element.22), channel_id=1, source_target_pairs={{0,24},{4,28},{8,16},{12,20},{16,8},{20,12},{24,0},{28,4},{1,25},{... | collective-permute-start | bytes 393224 | tf_op jit(solution)/shard_map/ppermute | solution.py:376
  8.4 16.7 %collective-permute-start.2 = (bf16[256,256]{1,0:T(8,128)(2,1)S(1)}, bf16[256,256]{1,0:T(8,128)(2,1)S(1)}, u32[]{:S(2)}, u32[]{:S(2)}) collective-permute-start(bf16[256,256]{1,0:T(8,128)(2,1)S(1)} %get-tuple-element.17), channel_id=1, source_target_pairs={{0,4},{4,0},{8,12},{12,8},{16,20},{20,16},{24,28},{28,24},{1,5},{5... | collective-permute-start | bytes 393224 | tf_op jit(solution)/shard_map/ppermute | solution.py:376
  8.8 20.9 %collective-permute-start.10 = (bf16[256,256]{1,0:T(8,128)(2,1)S(1)}, bf16[256,256]{1,0:T(8,128)(2,1)S(1)}, u32[]{:S(2)}, u32[]{:S(2)}) collective-permute-start(bf16[256,256]{1,0:T(8,128)(2,1)S(1)} %get-tuple-element.21), channel_id=1, source_target_pairs={{0,20},{4,16},{8,28},{12,24},{16,4},{20,0},{24,12},{28,8},{1,21},{... | collective-permute-start | bytes 393224 | tf_op jit(solution)/shard_map/ppermute | solution.py:376
  13.2 1.2 %collective-permute-start = (f32[8,128]{1,0:T(8,128)S(1)}, f32[8,128]{1,0:T(8,128)S(1)}, u32[]{:S(2)}, u32[]{:S(2)}) collective-permute-start(f32[8,128]{1,0:T(8,128)S(1)} %get-tuple-element.16), channel_id=1, source_target_pairs={{0,1},{1,0},{2,3},{3,2},{4,5},{5,4},{6,7},{7,6},{8,9},{9,8},{10,11... | collective-permute-start | bytes 12296 | tf_op jit(solution)/shard_map/ppermute | solution.py:376
  14.4 3.6 %collective-permute-start.1 = (f32[8,128]{1,0:T(8,128)S(1)}, f32[8,128]{1,0:T(8,128)S(1)}, u32[]{:S(2)}, u32[]{:S(2)}) collective-permute-start(f32[8,128]{1,0:T(8,128)S(1)} %add.6), channel_id=1, source_target_pairs={{0,2},{1,3},{2,0},{3,1},{4,6},{5,7},{6,4},{7,5},{8,10},{9,11},{10,... | collective-permute-start | bytes 12296 | tf_op jit(solution)/shard_map/ppermute | solution.py:376
  18.0 23.4 %collective-permute-start.6 = (bf16[256,256]{1,0:T(8,128)(2,1)S(1)}, bf16[256,256]{1,0:T(8,128)(2,1)S(1)}, u32[]{:S(2)}, u32[]{:S(2)}) collective-permute-start(bf16[256,256]{1,0:T(8,128)(2,1)S(1)} %get-tuple-element.19), channel_id=1, source_target_pairs={{0,16},{4,20},{8,24},{12,28},{16,0},{20,4},{24,8},{28,12},{1,17},{... | collective-permute-start | bytes 393224 | tf_op jit(solution)/shard_map/ppermute | solution.py:376
  20.3 14.4 %collective-permute-start.8 = (bf16[256,256]{1,0:T(8,128)(2,1)S(1)}, bf16[256,256]{1,0:T(8,128)(2,1)S(1)}, u32[]{:S(2)}, u32[]{:S(2)}) collective-permute-start(bf16[256,256]{1,0:T(8,128)(2,1)S(1)} %get-tuple-element.20), channel_id=1, source_target_pairs={{0,12},{4,8},{8,4},{12,0},{16,28},{20,24},{24,20},{28,16},{1,13},{... | collective-permute-start | bytes 393224 | tf_op jit(solution)/shard_map/ppermute | solution.py:376
  22.0 22.5 %collective-permute-start.15 = (bf16[272,256]{1,0:T(8,128)(2,1)S(1)}, bf16[272,256]{1,0:T(8,128)(2,1)S(1)}, u32[]{:S(2)}, u32[]{:S(2)}) collective-permute-start(bf16[272,256]{1,0:T(8,128)(2,1)S(1)} %shard_map.104), channel_id=1, source_target_pairs={{0,28},{4,24},{8,20},{12,16},{16,12},{20,8},{24,4},{28,0},{1,29},{... | collective-permute-start | bytes 417800 | tf_op jit(solution)/shard_map/ppermute | solution.py:376
  25.1 21.1 %collective-permute-start.13 = (bf16[272,256]{1,0:T(8,128)(2,1)S(1)}, bf16[272,256]{1,0:T(8,128)(2,1)S(1)}, u32[]{:S(2)}, u32[]{:S(2)}) collective-permute-start(bf16[272,256]{1,0:T(8,128)(2,1)S(1)} %shard_map.103), channel_id=1, source_target_pairs={{0,24},{4,28},{8,16},{12,20},{16,8},{20,12},{24,0},{28,4},{1,25},{... | collective-permute-start | bytes 417800 | tf_op jit(solution)/shard_map/ppermute | solution.py:376
  29.7 14.3 %collective-permute-start.4 = (bf16[256,256]{1,0:T(8,128)(2,1)S(1)}, bf16[256,256]{1,0:T(8,128)(2,1)S(1)}, u32[]{:S(2)}, u32[]{:S(2)}) collective-permute-start(bf16[256,256]{1,0:T(8,128)(2,1)S(1)} %get-tuple-element.18), channel_id=1, source_target_pairs={{0,8},{4,12},{8,0},{12,4},{16,24},{20,28},{24,16},{28,20},{1,9},{5... | collective-permute-start | bytes 393224 | tf_op jit(solution)/shard_map/ppermute | solution.py:376
  34.7 18.0 %collective-permute-start.11 = (bf16[272,256]{1,0:T(8,128)(2,1)S(1)}, bf16[272,256]{1,0:T(8,128)(2,1)S(1)}, u32[]{:S(2)}, u32[]{:S(2)}) collective-permute-start(bf16[272,256]{1,0:T(8,128)(2,1)S(1)} %shard_map.102), channel_id=1, source_target_pairs={{0,20},{4,16},{8,28},{12,24},{16,4},{20,0},{24,12},{28,8},{1,21},{... | collective-permute-start | bytes 417800 | tf_op jit(solution)/shard_map/ppermute | solution.py:376
  41.4 11.3 %collective-permute-start.9 = (bf16[272,256]{1,0:T(8,128)(2,1)S(1)}, bf16[272,256]{1,0:T(8,128)(2,1)S(1)}, u32[]{:S(2)}, u32[]{:S(2)}) collective-permute-start(bf16[272,256]{1,0:T(8,128)(2,1)S(1)} %shard_map.101), channel_id=1, source_target_pairs={{0,12},{4,8},{8,4},{12,0},{16,28},{20,24},{24,20},{28,16},{1,13},{... | collective-permute-start | bytes 417800 | tf_op jit(solution)/shard_map/ppermute | solution.py:376
  44.0 4.1 %copy-start.2 = (f32[1,8,256,256]{3,2,1,0:T(8,128)S(1)}, f32[1,8,256,256]{3,2,1,0:T(8,128)}, u32[]{:S(2)}) copy-start(f32[1,8,256,256]{3,2,1,0:T(8,128)} %refs_8_.1) | copy-start | bytes 6291460
  44.0 4.1 %copy-start.3 = (f32[1,8,256,256]{3,2,1,0:T(8,128)S(1)}, f32[1,8,256,256]{3,2,1,0:T(8,128)}, u32[]{:S(2)}) copy-start(f32[1,8,256,256]{3,2,1,0:T(8,128)} %refs_9_.1) | copy-start | bytes 6291460
  44.0 10.4 %collective-permute-start.7 = (bf16[272,256]{1,0:T(8,128)(2,1)S(1)}, bf16[272,256]{1,0:T(8,128)(2,1)S(1)}, u32[]{:S(2)}, u32[]{:S(2)}) collective-permute-start(bf16[272,256]{1,0:T(8,128)(2,1)S(1)} %shard_map.100), channel_id=1, source_target_pairs={{0,16},{4,20},{8,24},{12,28},{16,0},{20,4},{24,8},{28,12},{1,17},{... | collective-permute-start | bytes 417800 | tf_op jit(solution)/shard_map/ppermute | solution.py:376
  44.4 9.9 %collective-permute-start.5 = (bf16[272,256]{1,0:T(8,128)(2,1)S(1)}, bf16[272,256]{1,0:T(8,128)(2,1)S(1)}, u32[]{:S(2)}, u32[]{:S(2)}) collective-permute-start(bf16[272,256]{1,0:T(8,128)(2,1)S(1)} %shard_map.99), channel_id=1, source_target_pairs={{0,8},{4,12},{8,0},{12,4},{16,24},{20,28},{24,16},{28,20},{1,9},{5... | collective-permute-start | bytes 417800 | tf_op jit(solution)/shard_map/ppermute | solution.py:376
  46.1 8.2 %collective-permute-start.3 = (bf16[272,256]{1,0:T(8,128)(2,1)S(1)}, bf16[272,256]{1,0:T(8,128)(2,1)S(1)}, u32[]{:S(2)}, u32[]{:S(2)}) collective-permute-start(bf16[272,256]{1,0:T(8,128)(2,1)S(1)} %shard_map.98), channel_id=1, source_target_pairs={{0,4},{4,0},{8,12},{12,8},{16,20},{20,16},{24,28},{28,24},{1,5},{5... | collective-permute-start | bytes 417800 | tf_op jit(solution)/shard_map/ppermute | solution.py:376
  48.1 6.3 %copy-start.4 = (s32[1,64,1]{1,2,0:T(1,128)S(1)}, s32[1,64,1]{1,2,0:T(1,128)}, u32[]{:S(2)}) copy-start(s32[1,64,1]{1,2,0:T(1,128)} %param.9) | copy-start | bytes 772

commit v5 on v4

--- a/solution.py
+++ b/solution.py
@@ -368,7 +368,7 @@
     me = lax.axis_index("fsdp").astype(jnp.int32).reshape(1)
     owner_list = owners[0, :, 0]
     half = count // 2
-    order = [*range(half - 1), half, half - 1, *range(half + 1, count)]
+    order = [*range(half - 1), count - 1, half - 1, *range(count - 2, half - 1, -1)]
 
     def swap(value, m, axis="fsdp"):
         if m == 0:

time: 56.3 us -> 59 us (1.048)
  waiting for transfers between devices: 7.38 us -> 13.4 us
  starting transfers between devices: 34.6 us -> 31.3 us
    ppermute x16, waiting for transfers between devices: 7.38 us -> 13.4 us  [swap(): lax.ppermute(value, axis, [(i, i ^ m) for i in range(lax.axis_size(axis))])]
    ppermute x16, starting transfers between devices: 34.6 us -> 31.3 us  [swap(): lax.ppermute(value, axis, [(i, i ^ m) for i in range(lax.axis_size(axis))])]
  transfers between devices with their start and end apart: 16 -> 16, of which waited for: 4 -> 4; matrix products, arithmetic and copies ran while one was open for 0% -> 0% of each run, Pallas kernels for 18% -> 17%
where the time goes in v5:
time: 59 us; the launch traced here: 58.9 us
  starting transfers between devices  31.3 us (53%)
  waiting for transfers between devices  13.4 us (23%)
  Pallas kernels  13.2 us (22%)
  between operations  0.9 us (2%)
    ppermute x16, starting transfers between devices, swap(): lax.ppermute(value, axis, [(i, i ^ m) for i in range(lax.axis_size(axis))])  31.3 us
    ppermute x16, waiting for transfers between devices, swap(): lax.ppermute(value, axis, [(i, i ^ m) for i in range(lax.axis_size(axis))])  13.4 us
    pallas_call x1, Pallas kernels, gram_update(): pl.pallas_call(functools.partial(gram_kernel, order), grid_spec=pltpu.Pre...  4.68 us
    pallas_call x8, Pallas kernels, precondition(): pl.pallas_call(functools.partial(precondition_kernel, m, rows), grid_spec...  2.64 us
    pallas_call x1, Pallas kernels, adam_squares(): pl.pallas_call(adam_kernel, in_specs=[hbm, hbm], out_specs=[pl.BlockSpec(...  2.53 us
    pallas_call x1, Pallas kernels, finish(): pl.pallas_call(functools.partial(finish_kernel, order, entries), grid_spe...  1.81 us
    pallas_call x1, Pallas kernels, route(): pl.pallas_call(functools.partial(route_kernel, order), in_specs=[hbm, pl....  1.46 us
  transfers between devices with their start and end apart: 16, of which 4 were waited for; matrix products, arithmetic and copies ran while one was open for 0% of the time, Pallas kernels for 17%

profile of v5, /device:TPU:0, one launch (start us, length us, event | category | flops | bytes accessed | tf_op | source)
XLA Modules:
  0.0 58.9 jit_solution(116943708907359638)
XLA Ops:
  0.7 1.5 %shard_map.94 = (bf16[256,256]{1,0:T(8,128)(2,1)S(1)}, bf16[256,256]{1,0:T(8,128)(2,1)S(1)}, bf16[256,256]{1,0:T(8,128)(2,1)S(1)}, bf16[256,256]{1,0:T(8,128)(2,...) custom-call(s32[64]{0:T(128)} %bitcast.2, ...), custom_call_target="tpu_custom_call" | custom-call | bytes 2097152 | tf_op jit(solution)/shard_map/pallas_call | solution.py:128
  2.1 4.1 %collective-permute-start.14 = (bf16[256,256]{1,0:T(8,128)(2,1)S(1)}, bf16[256,256]{1,0:T(8,128)(2,1)S(1)}, u32[]{:S(2)}, u32[]{:S(2)}) collective-permute-start(bf16[256,256]{1,0:T(8,128)(2,1)S(1)} %get-tuple-element.23), channel_id=1, source_target_pairs={{0,16},{4,20},{8,24},{12,28},{16,0},{20,4},{24,8},{28,12},{1,17},{... | collective-permute-start | bytes 393224 | tf_op jit(solution)/shard_map/ppermute | solution.py:376
  6.2 1.3 %collective-permute-start.12 = (bf16[256,256]{1,0:T(8,128)(2,1)S(1)}, bf16[256,256]{1,0:T(8,128)(2,1)S(1)}, u32[]{:S(2)}, u32[]{:S(2)}) collective-permute-start(bf16[256,256]{1,0:T(8,128)(2,1)S(1)} %get-tuple-element.22), channel_id=1, source_target_pairs={{0,20},{4,16},{8,28},{12,24},{16,4},{20,0},{24,12},{28,8},{1,21},{... | collective-permute-start | bytes 393224 | tf_op jit(solution)/shard_map/ppermute | solution.py:376
  7.5 0.3 collective-permute-start.2
  7.8 3.9 %collective-permute-start.10 = (bf16[256,256]{1,0:T(8,128)(2,1)S(1)}, bf16[256,256]{1,0:T(8,128)(2,1)S(1)}, u32[]{:S(2)}, u32[]{:S(2)}) collective-permute-start(bf16[256,256]{1,0:T(8,128)(2,1)S(1)} %get-tuple-element.21), channel_id=1, source_target_pairs={{0,24},{4,28},{8,16},{12,20},{16,8},{20,12},{24,0},{28,4},{1,25},{... | collective-permute-start | bytes 393224 | tf_op jit(solution)/shard_map/ppermute | solution.py:376
  11.6 2.5 %shard_map.95 = (f32[8,128]{1,0:T(8,128)S(1)}, f32[8,128]{1,0:T(8,128)S(1)}) custom-call(bf16[1,8,256,256]{3,2,1,0:T(8,128)(2,1)} %grad_hbm.3, f32[1,8,256,256]{3,2,1,0:T(8,128)} %moment_hbm.1), custom_call_target="tpu_custom_call" | custom-call | flops 4194304 | bytes 3145728 | tf_op jit(solution)/shard_map/pallas_call | solution.py:179
  14.2 0.1 collective-permute-start
  14.2 1.2 %collective-permute-done = f32[8,128]{1,0:T(8,128)S(1)} collective-permute-done((f32[8,128]{1,0:T(8,128)S(1)}, f32[8,128]{1,0:T(8,128)S(1)}, u32[]{:S(2)}, u32[]{:S(2)}) %collective-permute-start) | collective-permute-done | bytes 4128 | tf_op jit(solution)/shard_map/ppermute | solution.py:376
  15.4 1.5 %collective-permute-start.1 = (f32[8,128]{1,0:T(8,128)S(1)}, f32[8,128]{1,0:T(8,128)S(1)}, u32[]{:S(2)}, u32[]{:S(2)}) collective-permute-start(f32[8,128]{1,0:T(8,128)S(1)} %add.6), channel_id=1, source_target_pairs={{0,2},{1,3},{2,0},{3,1},{4,6},{5,7},{6,4},{7,5},{8,10},{9,11},{10,... | collective-permute-start | bytes 12296 | tf_op jit(solution)/shard_map/ppermute | solution.py:376
  16.9 2.1 %collective-permute-done.1 = f32[8,128]{1,0:T(8,128)S(1)} collective-permute-done((f32[8,128]{1,0:T(8,128)S(1)}, f32[8,128]{1,0:T(8,128)S(1)}, u32[]{:S(2)}, u32[]{:S(2)}) %collective-permute-start.1) | collective-permute-done | bytes 4128 | tf_op jit(solution)/shard_map/ppermute | solution.py:376
  19.0 1.1 %collective-permute-start.6 = (bf16[256,256]{1,0:T(8,128)(2,1)S(1)}, bf16[256,256]{1,0:T(8,128)(2,1)S(1)}, u32[]{:S(2)}, u32[]{:S(2)}) collective-permute-start(bf16[256,256]{1,0:T(8,128)(2,1)S(1)} %get-tuple-element.19), channel_id=1, source_target_pairs={{0,28},{4,24},{8,20},{12,16},{16,12},{20,8},{24,4},{28,0},{1,29},{... | collective-permute-start | bytes 393224 | tf_op jit(solution)/shard_map/ppermute | solution.py:376
  20.2 0.1 shard_map.96.tail_ref.refs_9_
  20.3 0.0 collective-permute-done.14.grad_ref.refs_7_
  20.3 0.1 collective-permute-start.8
  20.4 0.3 shard_map.104
  20.7 2.3 %collective-permute-done.12.grad_ref.refs_6_ = bf16[256,256]{1,0:T(8,128)(2,1)S(1)} collective-permute-done((bf16[256,256]{1,0:T(8,128)(2,1)S(1)}, bf16[256,256]{1,0:T(8,128)(2,1)S(1)}, u32[]{:S(2)}, u32[]{:S(2)}) %collective-permute-start.12) | collective-permute-done | bytes 131104 | tf_op jit(solution)/shard_map/ppermute | solution.py:376
  23.1 1.9 %collective-permute-start.15 = (bf16[272,256]{1,0:T(8,128)(2,1)S(1)}, bf16[272,256]{1,0:T(8,128)(2,1)S(1)}, u32[]{:S(2)}, u32[]{:S(2)}) collective-permute-start(bf16[272,256]{1,0:T(8,128)(2,1)S(1)} %shard_map.104), channel_id=1, source_target_pairs={{0,16},{4,20},{8,24},{12,28},{16,0},{20,4},{24,8},{28,12},{1,17},{... | collective-permute-start | bytes 417800 | tf_op jit(solution)/shard_map/ppermute | solution.py:376
  24.9 0.3 shard_map.103
  25.3 0.0 collective-permute-done.2.grad_ref.refs_1_
  25.3 1.0 %collective-permute-start.13 = (bf16[272,256]{1,0:T(8,128)(2,1)S(1)}, bf16[272,256]{1,0:T(8,128)(2,1)S(1)}, u32[]{:S(2)}, u32[]{:S(2)}) collective-permute-start(bf16[272,256]{1,0:T(8,128)(2,1)S(1)} %shard_map.103), channel_id=1, source_target_pairs={{0,20},{4,16},{8,28},{12,24},{16,4},{20,0},{24,12},{28,8},{1,21},{... | collective-permute-start | bytes 417800 | tf_op jit(solution)/shard_map/ppermute | solution.py:376
  26.3 0.0 collective-permute-done.10.grad_ref.refs_5_
  26.3 7.0 %collective-permute-start.4 = (bf16[256,256]{1,0:T(8,128)(2,1)S(1)}, bf16[256,256]{1,0:T(8,128)(2,1)S(1)}, u32[]{:S(2)}, u32[]{:S(2)}) collective-permute-start(bf16[256,256]{1,0:T(8,128)(2,1)S(1)} %get-tuple-element.18), channel_id=1, source_target_pairs={{0,8},{4,12},{8,0},{12,4},{16,24},{20,28},{24,16},{28,20},{1,9},{5... | collective-permute-start | bytes 393224 | tf_op jit(solution)/shard_map/ppermute | solution.py:376
  33.3 0.3 shard_map.98
  33.6 0.3 shard_map.102
  34.0 0.0 collective-permute-done.8.grad_ref.refs_4_
  34.0 3.5 %collective-permute-start.11 = (bf16[272,256]{1,0:T(8,128)(2,1)S(1)}, bf16[272,256]{1,0:T(8,128)(2,1)S(1)}, u32[]{:S(2)}, u32[]{:S(2)}) collective-permute-start(bf16[272,256]{1,0:T(8,128)(2,1)S(1)} %shard_map.102), channel_id=1, source_target_pairs={{0,24},{4,28},{8,16},{12,20},{16,8},{20,12},{24,0},{28,4},{1,25},{... | collective-permute-start | bytes 417800 | tf_op jit(solution)/shard_map/ppermute | solution.py:376
  37.5 0.3 shard_map.101
  37.8 0.0 collective-permute-done.6.grad_ref.refs_3_
  37.8 0.1 collective-permute-start.9
  38.0 0.3 shard_map.100
  38.3 0.0 copy-start.2
  38.3 0.0 copy-start.3
  38.3 7.8 %collective-permute-done.4.grad_ref.refs_2_ = bf16[256,256]{1,0:T(8,128)(2,1)S(1)} collective-permute-done((bf16[256,256]{1,0:T(8,128)(2,1)S(1)}, bf16[256,256]{1,0:T(8,128)(2,1)S(1)}, u32[]{:S(2)}, u32[]{:S(2)}) %collective-permute-start.4) | collective-permute-done | bytes 131104 | tf_op jit(solution)/shard_map/ppermute | solution.py:376
  46.1 4.8 %collective-permute-start.7 = (bf16[272,256]{1,0:T(8,128)(2,1)S(1)}, bf16[272,256]{1,0:T(8,128)(2,1)S(1)}, u32[]{:S(2)}, u32[]{:S(2)}) collective-permute-start(bf16[272,256]{1,0:T(8,128)(2,1)S(1)} %shard_map.100), channel_id=1, source_target_pairs={{0,28},{4,24},{8,20},{12,16},{16,12},{20,8},{24,4},{28,0},{1,29},{... | collective-permute-start | bytes 417800 | tf_op jit(solution)/shard_map/ppermute | solution.py:376
  50.9 0.3 shard_map.99
  51.3 0.0 collective-permute-done.15.refs_7_
  51.3 0.1 collective-permute-start.5
  51.4 0.0 collective-permute-done.13.refs_6_
  51.4 0.6 collective-permute-start.3
  52.0 0.3 shard_map.97.refs_0_
  52.3 0.0 copy-start.4
  52.3 4.7 %shard_map.106 = (f32[1,8,256,256]{3,2,1,0:T(8,128)}, f32[1,8,256,256]{3,2,1,0:T(8,128)}) custom-call(s32[1]{0:T(128)} %bitcast.1.me_ref, bf16[256,256]{1,0:T(8,128)(2,1)S(1)} %get-tuple-element.15.grad_ref.refs_0_, bf16[256,256]{1,0:T(8,128)(2,1)S(1)} %collective-permute-done.2.grad_ref.refs_1_, ...), custom_call_target="tpu_custom_call" | custom-call | flops 536870912 | bytes 9437184 | tf_op jit(solution)/shard_map/pallas_call | solution.py:281
  57.0 0.0 collective-permute-done.11.refs_5_
  57.0 0.0 collective-permute-done.9.refs_4_
  57.0 0.0 collective-permute-done.7.refs_3_
  57.0 0.0 collective-permute-done.5.refs_2_
  57.0 0.0 collective-permute-done.3.refs_1_
  57.1 1.8 %shard_map.105 = bf16[1,8,256,256]{3,2,1,0:T(8,128)(2,1)} custom-call(s32[64]{0:T(128)S(1)} %bitcast.3, s32[1]{0:T(128)} %bitcast.1.me_ref, bf16[256,256]{1,0:T(8,128)(2,1)S(1)} %shard_map.97.refs_0_, bf16[272,256]{1,0:T(8,128)(2,1)S(1)} %collective-permute-done.3.refs_1_, bf16[272,256]{1,0:T(8,128)(2,1)S(1)} %collective-permute-done.5.refs_2_, ...), custom_call_target="tpu_custom_call" | custom-call | flops 3145728 | bytes 2097152 | tf_op jit(solution)/shard_map/pallas_call | solution.py:337
  (9 shorter events, 0.0 us)
Async XLA Ops:
  0.6 19.8 %copy-start = (bf16[1,8,256,256]{3,2,1,0:T(8,128)(2,1)S(1)}, bf16[1,8,256,256]{3,2,1,0:T(8,128)(2,1)}, u32[]{:S(2)}) copy-start(bf16[1,8,256,256]{3,2,1,0:T(8,128)(2,1)} %left_ref.15) | copy-start | bytes 3145732
  0.6 19.8 %copy-start.1 = (bf16[1,8,256,256]{3,2,1,0:T(8,128)(2,1)S(1)}, bf16[1,8,256,256]{3,2,1,0:T(8,128)(2,1)}, u32[]{:S(2)}) copy-start(bf16[1,8,256,256]{3,2,1,0:T(8,128)(2,1)} %right_ref.15) | copy-start | bytes 3145732
  2.1 18.2 %collective-permute-start.14 = (bf16[256,256]{1,0:T(8,128)(2,1)S(1)}, bf16[256,256]{1,0:T(8,128)(2,1)S(1)}, u32[]{:S(2)}, u32[]{:S(2)}) collective-permute-start(bf16[256,256]{1,0:T(8,128)(2,1)S(1)} %get-tuple-element.23), channel_id=1, source_target_pairs={{0,16},{4,20},{8,24},{12,28},{16,0},{20,4},{24,8},{28,12},{1,17},{... | collective-permute-start | bytes 393224 | tf_op jit(solution)/shard_map/ppermute | solution.py:376
  6.2 16.8 %collective-permute-start.12 = (bf16[256,256]{1,0:T(8,128)(2,1)S(1)}, bf16[256,256]{1,0:T(8,128)(2,1)S(1)}, u32[]{:S(2)}, u32[]{:S(2)}) collective-permute-start(bf16[256,256]{1,0:T(8,128)(2,1)S(1)} %get-tuple-element.22), channel_id=1, source_target_pairs={{0,20},{4,16},{8,28},{12,24},{16,4},{20,0},{24,12},{28,8},{1,21},{... | collective-permute-start | bytes 393224 | tf_op jit(solution)/shard_map/ppermute | solution.py:376
  7.5 17.8 %collective-permute-start.2 = (bf16[256,256]{1,0:T(8,128)(2,1)S(1)}, bf16[256,256]{1,0:T(8,128)(2,1)S(1)}, u32[]{:S(2)}, u32[]{:S(2)}) collective-permute-start(bf16[256,256]{1,0:T(8,128)(2,1)S(1)} %get-tuple-element.17), channel_id=1, source_target_pairs={{0,4},{4,0},{8,12},{12,8},{16,20},{20,16},{24,28},{28,24},{1,5},{5... | collective-permute-start | bytes 393224 | tf_op jit(solution)/shard_map/ppermute | solution.py:376
  7.8 18.5 %collective-permute-start.10 = (bf16[256,256]{1,0:T(8,128)(2,1)S(1)}, bf16[256,256]{1,0:T(8,128)(2,1)S(1)}, u32[]{:S(2)}, u32[]{:S(2)}) collective-permute-start(bf16[256,256]{1,0:T(8,128)(2,1)S(1)} %get-tuple-element.21), channel_id=1, source_target_pairs={{0,24},{4,28},{8,16},{12,20},{16,8},{20,12},{24,0},{28,4},{1,25},{... | collective-permute-start | bytes 393224 | tf_op jit(solution)/shard_map/ppermute | solution.py:376
  14.2 1.2 %collective-permute-start = (f32[8,128]{1,0:T(8,128)S(1)}, f32[8,128]{1,0:T(8,128)S(1)}, u32[]{:S(2)}, u32[]{:S(2)}) collective-permute-start(f32[8,128]{1,0:T(8,128)S(1)} %get-tuple-element.16), channel_id=1, source_target_pairs={{0,1},{1,0},{2,3},{3,2},{4,5},{5,4},{6,7},{7,6},{8,9},{9,8},{10,11... | collective-permute-start | bytes 12296 | tf_op jit(solution)/shard_map/ppermute | solution.py:376
  15.4 3.6 %collective-permute-start.1 = (f32[8,128]{1,0:T(8,128)S(1)}, f32[8,128]{1,0:T(8,128)S(1)}, u32[]{:S(2)}, u32[]{:S(2)}) collective-permute-start(f32[8,128]{1,0:T(8,128)S(1)} %add.6), channel_id=1, source_target_pairs={{0,2},{1,3},{2,0},{3,1},{4,6},{5,7},{6,4},{7,5},{8,10},{9,11},{10,... | collective-permute-start | bytes 12296 | tf_op jit(solution)/shard_map/ppermute | solution.py:376
  19.0 18.8 %collective-permute-start.6 = (bf16[256,256]{1,0:T(8,128)(2,1)S(1)}, bf16[256,256]{1,0:T(8,128)(2,1)S(1)}, u32[]{:S(2)}, u32[]{:S(2)}) collective-permute-start(bf16[256,256]{1,0:T(8,128)(2,1)S(1)} %get-tuple-element.19), channel_id=1, source_target_pairs={{0,28},{4,24},{8,20},{12,16},{16,12},{20,8},{24,4},{28,0},{1,29},{... | collective-permute-start | bytes 393224 | tf_op jit(solution)/shard_map/ppermute | solution.py:376
  20.3 13.7 %collective-permute-start.8 = (bf16[256,256]{1,0:T(8,128)(2,1)S(1)}, bf16[256,256]{1,0:T(8,128)(2,1)S(1)}, u32[]{:S(2)}, u32[]{:S(2)}) collective-permute-start(bf16[256,256]{1,0:T(8,128)(2,1)S(1)} %get-tuple-element.20), channel_id=1, source_target_pairs={{0,12},{4,8},{8,4},{12,0},{16,28},{20,24},{24,20},{28,16},{1,13},{... | collective-permute-start | bytes 393224 | tf_op jit(solution)/shard_map/ppermute | solution.py:376
  23.1 28.2 %collective-permute-start.15 = (bf16[272,256]{1,0:T(8,128)(2,1)S(1)}, bf16[272,256]{1,0:T(8,128)(2,1)S(1)}, u32[]{:S(2)}, u32[]{:S(2)}) collective-permute-start(bf16[272,256]{1,0:T(8,128)(2,1)S(1)} %shard_map.104), channel_id=1, source_target_pairs={{0,16},{4,20},{8,24},{12,28},{16,0},{20,4},{24,8},{28,12},{1,17},{... | collective-permute-start | bytes 417800 | tf_op jit(solution)/shard_map/ppermute | solution.py:376
  25.3 26.1 %collective-permute-start.13 = (bf16[272,256]{1,0:T(8,128)(2,1)S(1)}, bf16[272,256]{1,0:T(8,128)(2,1)S(1)}, u32[]{:S(2)}, u32[]{:S(2)}) collective-permute-start(bf16[272,256]{1,0:T(8,128)(2,1)S(1)} %shard_map.103), channel_id=1, source_target_pairs={{0,20},{4,16},{8,28},{12,24},{16,4},{20,0},{24,12},{28,8},{1,21},{... | collective-permute-start | bytes 417800 | tf_op jit(solution)/shard_map/ppermute | solution.py:376
  26.3 19.9 %collective-permute-start.4 = (bf16[256,256]{1,0:T(8,128)(2,1)S(1)}, bf16[256,256]{1,0:T(8,128)(2,1)S(1)}, u32[]{:S(2)}, u32[]{:S(2)}) collective-permute-start(bf16[256,256]{1,0:T(8,128)(2,1)S(1)} %get-tuple-element.18), channel_id=1, source_target_pairs={{0,8},{4,12},{8,0},{12,4},{16,24},{20,28},{24,16},{28,20},{1,9},{5... | collective-permute-start | bytes 393224 | tf_op jit(solution)/shard_map/ppermute | solution.py:376
  34.0 23.0 %collective-permute-start.11 = (bf16[272,256]{1,0:T(8,128)(2,1)S(1)}, bf16[272,256]{1,0:T(8,128)(2,1)S(1)}, u32[]{:S(2)}, u32[]{:S(2)}) collective-permute-start(bf16[272,256]{1,0:T(8,128)(2,1)S(1)} %shard_map.102), channel_id=1, source_target_pairs={{0,24},{4,28},{8,16},{12,20},{16,8},{20,12},{24,0},{28,4},{1,25},{... | collective-permute-start | bytes 417800 | tf_op jit(solution)/shard_map/ppermute | solution.py:376
  37.8 19.2 %collective-permute-start.9 = (bf16[272,256]{1,0:T(8,128)(2,1)S(1)}, bf16[272,256]{1,0:T(8,128)(2,1)S(1)}, u32[]{:S(2)}, u32[]{:S(2)}) collective-permute-start(bf16[272,256]{1,0:T(8,128)(2,1)S(1)} %shard_map.101), channel_id=1, source_target_pairs={{0,12},{4,8},{8,4},{12,0},{16,28},{20,24},{24,20},{28,16},{1,13},{... | collective-permute-start | bytes 417800 | tf_op jit(solution)/shard_map/ppermute | solution.py:376
  38.3 14.0 %copy-start.2 = (f32[1,8,256,256]{3,2,1,0:T(8,128)S(1)}, f32[1,8,256,256]{3,2,1,0:T(8,128)}, u32[]{:S(2)}) copy-start(f32[1,8,256,256]{3,2,1,0:T(8,128)} %refs_8_.1) | copy-start | bytes 6291460
  38.3 14.0 %copy-start.3 = (f32[1,8,256,256]{3,2,1,0:T(8,128)S(1)}, f32[1,8,256,256]{3,2,1,0:T(8,128)}, u32[]{:S(2)}) copy-start(f32[1,8,256,256]{3,2,1,0:T(8,128)} %refs_9_.1) | copy-start | bytes 6291460
  46.1 10.9 %collective-permute-start.7 = (bf16[272,256]{1,0:T(8,128)(2,1)S(1)}, bf16[272,256]{1,0:T(8,128)(2,1)S(1)}, u32[]{:S(2)}, u32[]{:S(2)}) collective-permute-start(bf16[272,256]{1,0:T(8,128)(2,1)S(1)} %shard_map.100), channel_id=1, source_target_pairs={{0,28},{4,24},{8,20},{12,16},{16,12},{20,8},{24,4},{28,0},{1,29},{... | collective-permute-start | bytes 417800 | tf_op jit(solution)/shard_map/ppermute | solution.py:376
  51.3 5.7 %collective-permute-start.5 = (bf16[272,256]{1,0:T(8,128)(2,1)S(1)}, bf16[272,256]{1,0:T(8,128)(2,1)S(1)}, u32[]{:S(2)}, u32[]{:S(2)}) collective-permute-start(bf16[272,256]{1,0:T(8,128)(2,1)S(1)} %shard_map.99), channel_id=1, source_target_pairs={{0,8},{4,12},{8,0},{12,4},{16,24},{20,28},{24,16},{28,20},{1,9},{5... | collective-permute-start | bytes 417800 | tf_op jit(solution)/shard_map/ppermute | solution.py:376
  51.4 5.7 %collective-permute-start.3 = (bf16[272,256]{1,0:T(8,128)(2,1)S(1)}, bf16[272,256]{1,0:T(8,128)(2,1)S(1)}, u32[]{:S(2)}, u32[]{:S(2)}) collective-permute-start(bf16[272,256]{1,0:T(8,128)(2,1)S(1)} %shard_map.98), channel_id=1, source_target_pairs={{0,4},{4,0},{8,12},{12,8},{16,20},{20,16},{24,28},{28,24},{1,5},{5... | collective-permute-start | bytes 417800 | tf_op jit(solution)/shard_map/ppermute | solution.py:376
  52.3 4.7 %copy-start.4 = (s32[1,64,1]{1,2,0:T(1,128)S(1)}, s32[1,64,1]{1,2,0:T(1,128)}, u32[]{:S(2)}) copy-start(s32[1,64,1]{1,2,0:T(1,128)} %param.9) | copy-start | bytes 772

commit v6 on v5

--- a/solution.py
+++ b/solution.py
@@ -368,7 +368,7 @@
     me = lax.axis_index("fsdp").astype(jnp.int32).reshape(1)
     owner_list = owners[0, :, 0]
     half = count // 2
-    order = [*range(half - 1), count - 1, half - 1, *range(count - 2, half - 1, -1)]
+    order = [0, 1, 2, half + 1, 3, half, count - 1, count - 2] if count == 8 else list(range(count))
 
     def swap(value, m, axis="fsdp"):
         if m == 0:

time: 59 us -> 56.3 us (0.954)
  waiting for transfers between devices: 13.4 us -> 8.3 us
  starting transfers between devices: 31.3 us -> 33.8 us
    ppermute x16, waiting for transfers between devices: 13.4 us -> 8.3 us  [swap(): lax.ppermute(value, axis, [(i, i ^ m) for i in range(lax.axis_size(axis))])]
    ppermute x16, starting transfers between devices: 31.3 us -> 33.8 us  [swap(): lax.ppermute(value, axis, [(i, i ^ m) for i in range(lax.axis_size(axis))])]
  transfers between devices with their start and end apart: 16 -> 16, of which waited for: 4 -> 6; matrix products, arithmetic and copies ran while one was open for 0% -> 0% of each run, Pallas kernels for 17% -> 18%
where the time goes in v6:
time: 56.3 us; the launch traced here: 56.2 us
  starting transfers between devices  33.8 us (60%)
  Pallas kernels  13.2 us (23%)
  waiting for transfers between devices  8.3 us (15%)
  between operations  0.85 us (2%)
    ppermute x16, starting transfers between devices, swap(): lax.ppermute(value, axis, [(i, i ^ m) for i in range(lax.axis_size(axis))])  33.8 us
    ppermute x16, waiting for transfers between devices, swap(): lax.ppermute(value, axis, [(i, i ^ m) for i in range(lax.axis_size(axis))])  8.3 us
    pallas_call x1, Pallas kernels, gram_update(): pl.pallas_call(functools.partial(gram_kernel, order), grid_spec=pltpu.Pre...  4.68 us
    pallas_call x8, Pallas kernels, precondition(): pl.pallas_call(functools.partial(precondition_kernel, m, rows), grid_spec...  2.63 us
    pallas_call x1, Pallas kernels, adam_squares(): pl.pallas_call(adam_kernel, in_specs=[hbm, hbm], out_specs=[pl.BlockSpec(...  2.53 us
    pallas_call x1, Pallas kernels, finish(): pl.pallas_call(functools.partial(finish_kernel, order, entries), grid_spe...  1.81 us
    pallas_call x1, Pallas kernels, route(): pl.pallas_call(functools.partial(route_kernel, order), in_specs=[hbm, pl....  1.46 us
  transfers between devices with their start and end apart: 16, of which 6 were waited for; matrix products, arithmetic and copies ran while one was open for 0% of the time, Pallas kernels for 18%

profile of v6, /device:TPU:0, one launch (start us, length us, event | category | flops | bytes accessed | tf_op | source)
XLA Modules:
  0.0 56.2 jit_solution(10839314763335238646)
XLA Ops:
  0.7 1.5 %shard_map.94 = (bf16[256,256]{1,0:T(8,128)(2,1)S(1)}, bf16[256,256]{1,0:T(8,128)(2,1)S(1)}, bf16[256,256]{1,0:T(8,128)(2,1)S(1)}, bf16[256,256]{1,0:T(8,128)(2,...) custom-call(s32[64]{0:T(128)} %bitcast.2, ...), custom_call_target="tpu_custom_call" | custom-call | bytes 2097152 | tf_op jit(solution)/shard_map/pallas_call | solution.py:128
  2.1 5.1 %collective-permute-start.14 = (bf16[256,256]{1,0:T(8,128)(2,1)S(1)}, bf16[256,256]{1,0:T(8,128)(2,1)S(1)}, u32[]{:S(2)}, u32[]{:S(2)}) collective-permute-start(bf16[256,256]{1,0:T(8,128)(2,1)S(1)} %get-tuple-element.23), channel_id=1, source_target_pairs={{0,24},{4,28},{8,16},{12,20},{16,8},{20,12},{24,0},{28,4},{1,25},{... | collective-permute-start | bytes 393224 | tf_op jit(solution)/shard_map/ppermute | solution.py:376
  7.2 1.1 %collective-permute-start.12 = (bf16[256,256]{1,0:T(8,128)(2,1)S(1)}, bf16[256,256]{1,0:T(8,128)(2,1)S(1)}, u32[]{:S(2)}, u32[]{:S(2)}) collective-permute-start(bf16[256,256]{1,0:T(8,128)(2,1)S(1)} %get-tuple-element.22), channel_id=1, source_target_pairs={{0,28},{4,24},{8,20},{12,16},{16,12},{20,8},{24,4},{28,0},{1,29},{... | collective-permute-start | bytes 393224 | tf_op jit(solution)/shard_map/ppermute | solution.py:376
  8.4 0.4 collective-permute-start.2
  8.8 0.9 %collective-permute-start.10 = (bf16[256,256]{1,0:T(8,128)(2,1)S(1)}, bf16[256,256]{1,0:T(8,128)(2,1)S(1)}, u32[]{:S(2)}, u32[]{:S(2)}) collective-permute-start(bf16[256,256]{1,0:T(8,128)(2,1)S(1)} %get-tuple-element.21), channel_id=1, source_target_pairs={{0,16},{4,20},{8,24},{12,28},{16,0},{20,4},{24,8},{28,12},{1,17},{... | collective-permute-start | bytes 393224 | tf_op jit(solution)/shard_map/ppermute | solution.py:376
  9.7 2.5 %shard_map.95 = (f32[8,128]{1,0:T(8,128)S(1)}, f32[8,128]{1,0:T(8,128)S(1)}) custom-call(bf16[1,8,256,256]{3,2,1,0:T(8,128)(2,1)} %grad_hbm.3, f32[1,8,256,256]{3,2,1,0:T(8,128)} %moment_hbm.1), custom_call_target="tpu_custom_call" | custom-call | flops 4194304 | bytes 3145728 | tf_op jit(solution)/shard_map/pallas_call | solution.py:179
  12.3 0.1 collective-permute-start
  12.3 1.2 %collective-permute-done = f32[8,128]{1,0:T(8,128)S(1)} collective-permute-done((f32[8,128]{1,0:T(8,128)S(1)}, f32[8,128]{1,0:T(8,128)S(1)}, u32[]{:S(2)}, u32[]{:S(2)}) %collective-permute-start) | collective-permute-done | bytes 4128 | tf_op jit(solution)/shard_map/ppermute | solution.py:376
  13.5 1.5 %collective-permute-start.1 = (f32[8,128]{1,0:T(8,128)S(1)}, f32[8,128]{1,0:T(8,128)S(1)}, u32[]{:S(2)}, u32[]{:S(2)}) collective-permute-start(f32[8,128]{1,0:T(8,128)S(1)} %add.6), channel_id=1, source_target_pairs={{0,2},{1,3},{2,0},{3,1},{4,6},{5,7},{6,4},{7,5},{8,10},{9,11},{10,... | collective-permute-start | bytes 12296 | tf_op jit(solution)/shard_map/ppermute | solution.py:376
  15.0 2.1 %collective-permute-done.1 = f32[8,128]{1,0:T(8,128)S(1)} collective-permute-done((f32[8,128]{1,0:T(8,128)S(1)}, f32[8,128]{1,0:T(8,128)S(1)}, u32[]{:S(2)}, u32[]{:S(2)}) %collective-permute-start.1) | collective-permute-done | bytes 4128 | tf_op jit(solution)/shard_map/ppermute | solution.py:376
  17.1 3.1 %collective-permute-start.6 = (bf16[256,256]{1,0:T(8,128)(2,1)S(1)}, bf16[256,256]{1,0:T(8,128)(2,1)S(1)}, u32[]{:S(2)}, u32[]{:S(2)}) collective-permute-start(bf16[256,256]{1,0:T(8,128)(2,1)S(1)} %get-tuple-element.19), channel_id=1, source_target_pairs={{0,20},{4,16},{8,28},{12,24},{16,4},{20,0},{24,12},{28,8},{1,21},{... | collective-permute-start | bytes 393224 | tf_op jit(solution)/shard_map/ppermute | solution.py:376
  20.2 0.1 shard_map.96.tail_ref.refs_9_
  20.3 0.0 collective-permute-done.14.grad_ref.refs_7_
  20.3 1.3 %collective-permute-start.8 = (bf16[256,256]{1,0:T(8,128)(2,1)S(1)}, bf16[256,256]{1,0:T(8,128)(2,1)S(1)}, u32[]{:S(2)}, u32[]{:S(2)}) collective-permute-start(bf16[256,256]{1,0:T(8,128)(2,1)S(1)} %get-tuple-element.20), channel_id=1, source_target_pairs={{0,12},{4,8},{8,4},{12,0},{16,28},{20,24},{24,20},{28,16},{1,13},{... | collective-permute-start | bytes 393224 | tf_op jit(solution)/shard_map/ppermute | solution.py:376
  21.6 0.3 shard_map.104
  22.0 0.0 collective-permute-done.12.grad_ref.refs_6_
  22.0 2.5 %collective-permute-start.15 = (bf16[272,256]{1,0:T(8,128)(2,1)S(1)}, bf16[272,256]{1,0:T(8,128)(2,1)S(1)}, u32[]{:S(2)}, u32[]{:S(2)}) collective-permute-start(bf16[272,256]{1,0:T(8,128)(2,1)S(1)} %shard_map.104), channel_id=1, source_target_pairs={{0,24},{4,28},{8,16},{12,20},{16,8},{20,12},{24,0},{28,4},{1,25},{... | collective-permute-start | bytes 417800 | tf_op jit(solution)/shard_map/ppermute | solution.py:376
  24.4 0.3 shard_map.103
  24.8 0.0 collective-permute-done.2.grad_ref.refs_1_
  24.8 2.4 %collective-permute-start.13 = (bf16[272,256]{1,0:T(8,128)(2,1)S(1)}, bf16[272,256]{1,0:T(8,128)(2,1)S(1)}, u32[]{:S(2)}, u32[]{:S(2)}) collective-permute-start(bf16[272,256]{1,0:T(8,128)(2,1)S(1)} %shard_map.103), channel_id=1, source_target_pairs={{0,28},{4,24},{8,20},{12,16},{16,12},{20,8},{24,4},{28,0},{1,29},{... | collective-permute-start | bytes 417800 | tf_op jit(solution)/shard_map/ppermute | solution.py:376
  27.2 0.1 collective-permute-done.10.grad_ref.refs_5_
  27.3 5.0 %collective-permute-start.4 = (bf16[256,256]{1,0:T(8,128)(2,1)S(1)}, bf16[256,256]{1,0:T(8,128)(2,1)S(1)}, u32[]{:S(2)}, u32[]{:S(2)}) collective-permute-start(bf16[256,256]{1,0:T(8,128)(2,1)S(1)} %get-tuple-element.18), channel_id=1, source_target_pairs={{0,8},{4,12},{8,0},{12,4},{16,24},{20,28},{24,16},{28,20},{1,9},{5... | collective-permute-start | bytes 393224 | tf_op jit(solution)/shard_map/ppermute | solution.py:376
  32.3 0.3 shard_map.98
  32.6 0.3 shard_map.102
  32.9 0.0 collective-permute-done.8.grad_ref.refs_4_
  32.9 4.2 %collective-permute-start.11 = (bf16[272,256]{1,0:T(8,128)(2,1)S(1)}, bf16[272,256]{1,0:T(8,128)(2,1)S(1)}, u32[]{:S(2)}, u32[]{:S(2)}) collective-permute-start(bf16[272,256]{1,0:T(8,128)(2,1)S(1)} %shard_map.102), channel_id=1, source_target_pairs={{0,16},{4,20},{8,24},{12,28},{16,0},{20,4},{24,8},{28,12},{1,17},{... | collective-permute-start | bytes 417800 | tf_op jit(solution)/shard_map/ppermute | solution.py:376
  37.1 0.3 shard_map.101
  37.5 1.4 %collective-permute-done.6.grad_ref.refs_3_ = bf16[256,256]{1,0:T(8,128)(2,1)S(1)} collective-permute-done((bf16[256,256]{1,0:T(8,128)(2,1)S(1)}, bf16[256,256]{1,0:T(8,128)(2,1)S(1)}, u32[]{:S(2)}, u32[]{:S(2)}) %collective-permute-start.6) | collective-permute-done | bytes 131104 | tf_op jit(solution)/shard_map/ppermute | solution.py:376
  38.9 2.4 %collective-permute-start.9 = (bf16[272,256]{1,0:T(8,128)(2,1)S(1)}, bf16[272,256]{1,0:T(8,128)(2,1)S(1)}, u32[]{:S(2)}, u32[]{:S(2)}) collective-permute-start(bf16[272,256]{1,0:T(8,128)(2,1)S(1)} %shard_map.101), channel_id=1, source_target_pairs={{0,12},{4,8},{8,4},{12,0},{16,28},{20,24},{24,20},{28,16},{1,13},{... | collective-permute-start | bytes 417800 | tf_op jit(solution)/shard_map/ppermute | solution.py:376
  41.3 0.3 shard_map.100
  41.6 0.0 copy-start.2
  41.7 0.0 copy-start.3
  41.7 0.0 collective-permute-done.4.grad_ref.refs_2_
  41.7 2.4 %collective-permute-start.7 = (bf16[272,256]{1,0:T(8,128)(2,1)S(1)}, bf16[272,256]{1,0:T(8,128)(2,1)S(1)}, u32[]{:S(2)}, u32[]{:S(2)}) collective-permute-start(bf16[272,256]{1,0:T(8,128)(2,1)S(1)} %shard_map.100), channel_id=1, source_target_pairs={{0,20},{4,16},{8,28},{12,24},{16,4},{20,0},{24,12},{28,8},{1,21},{... | collective-permute-start | bytes 417800 | tf_op jit(solution)/shard_map/ppermute | solution.py:376
  44.1 0.3 shard_map.99
  44.4 0.0 collective-permute-done.15.refs_7_
  44.4 1.4 %collective-permute-start.5 = (bf16[272,256]{1,0:T(8,128)(2,1)S(1)}, bf16[272,256]{1,0:T(8,128)(2,1)S(1)}, u32[]{:S(2)}, u32[]{:S(2)}) collective-permute-start(bf16[272,256]{1,0:T(8,128)(2,1)S(1)} %shard_map.99), channel_id=1, source_target_pairs={{0,8},{4,12},{8,0},{12,4},{16,24},{20,28},{24,16},{28,20},{1,9},{5... | collective-permute-start | bytes 417800 | tf_op jit(solution)/shard_map/ppermute | solution.py:376
  45.8 0.0 collective-permute-done.13.refs_6_
  45.8 0.0 collective-permute-start.3
  45.8 0.3 shard_map.97.refs_0_
  46.2 0.0 copy-start.4
  46.2 4.7 %shard_map.106 = (f32[1,8,256,256]{3,2,1,0:T(8,128)}, f32[1,8,256,256]{3,2,1,0:T(8,128)}) custom-call(s32[1]{0:T(128)} %bitcast.1.me_ref, bf16[256,256]{1,0:T(8,128)(2,1)S(1)} %get-tuple-element.15.grad_ref.refs_0_, bf16[256,256]{1,0:T(8,128)(2,1)S(1)} %collective-permute-done.2.grad_ref.refs_1_, ...), custom_call_target="tpu_custom_call" | custom-call | flops 536870912 | bytes 9437184 | tf_op jit(solution)/shard_map/pallas_call | solution.py:281
  50.9 0.7 %collective-permute-done.11.refs_5_ = bf16[272,256]{1,0:T(8,128)(2,1)S(1)} collective-permute-done((bf16[272,256]{1,0:T(8,128)(2,1)S(1)}, bf16[272,256]{1,0:T(8,128)(2,1)S(1)}, u32[]{:S(2)}, u32[]{:S(2)}) %collective-permute-start.11) | collective-permute-done | bytes 139296 | tf_op jit(solution)/shard_map/ppermute | solution.py:376
  51.6 0.0 collective-permute-done.9.refs_4_
  51.6 2.8 %collective-permute-done.7.refs_3_ = bf16[272,256]{1,0:T(8,128)(2,1)S(1)} collective-permute-done((bf16[272,256]{1,0:T(8,128)(2,1)S(1)}, bf16[272,256]{1,0:T(8,128)(2,1)S(1)}, u32[]{:S(2)}, u32[]{:S(2)}) %collective-permute-start.7) | collective-permute-done | bytes 139296 | tf_op jit(solution)/shard_map/ppermute | solution.py:376
  54.4 0.0 collective-permute-done.5.refs_2_
  54.4 0.0 collective-permute-done.3.refs_1_
  54.4 1.8 %shard_map.105 = bf16[1,8,256,256]{3,2,1,0:T(8,128)(2,1)} custom-call(s32[64]{0:T(128)S(1)} %bitcast.3, s32[1]{0:T(128)} %bitcast.1.me_ref, bf16[256,256]{1,0:T(8,128)(2,1)S(1)} %shard_map.97.refs_0_, bf16[272,256]{1,0:T(8,128)(2,1)S(1)} %collective-permute-done.3.refs_1_, bf16[272,256]{1,0:T(8,128)(2,1)S(1)} %collective-permute-done.5.refs_2_, ...), custom_call_target="tpu_custom_call" | custom-call | flops 3145728 | bytes 2097152 | tf_op jit(solution)/shard_map/pallas_call | solution.py:337
  (9 shorter events, 0.0 us)
Async XLA Ops:
  0.6 21.0 %copy-start = (bf16[1,8,256,256]{3,2,1,0:T(8,128)(2,1)S(1)}, bf16[1,8,256,256]{3,2,1,0:T(8,128)(2,1)}, u32[]{:S(2)}) copy-start(bf16[1,8,256,256]{3,2,1,0:T(8,128)(2,1)} %left_ref.15) | copy-start | bytes 3145732
  0.6 21.0 %copy-start.1 = (bf16[1,8,256,256]{3,2,1,0:T(8,128)(2,1)S(1)}, bf16[1,8,256,256]{3,2,1,0:T(8,128)(2,1)}, u32[]{:S(2)}) copy-start(bf16[1,8,256,256]{3,2,1,0:T(8,128)(2,1)} %right_ref.15) | copy-start | bytes 3145732
  2.1 18.2 %collective-permute-start.14 = (bf16[256,256]{1,0:T(8,128)(2,1)S(1)}, bf16[256,256]{1,0:T(8,128)(2,1)S(1)}, u32[]{:S(2)}, u32[]{:S(2)}) collective-permute-start(bf16[256,256]{1,0:T(8,128)(2,1)S(1)} %get-tuple-element.23), channel_id=1, source_target_pairs={{0,24},{4,28},{8,16},{12,20},{16,8},{20,12},{24,0},{28,4},{1,25},{... | collective-permute-start | bytes 393224 | tf_op jit(solution)/shard_map/ppermute | solution.py:376
  7.2 14.7 %collective-permute-start.12 = (bf16[256,256]{1,0:T(8,128)(2,1)S(1)}, bf16[256,256]{1,0:T(8,128)(2,1)S(1)}, u32[]{:S(2)}, u32[]{:S(2)}) collective-permute-start(bf16[256,256]{1,0:T(8,128)(2,1)S(1)} %get-tuple-element.22), channel_id=1, source_target_pairs={{0,28},{4,24},{8,20},{12,16},{16,12},{20,8},{24,4},{28,0},{1,29},{... | collective-permute-start | bytes 393224 | tf_op jit(solution)/shard_map/ppermute | solution.py:376
  8.4 16.4 %collective-permute-start.2 = (bf16[256,256]{1,0:T(8,128)(2,1)S(1)}, bf16[256,256]{1,0:T(8,128)(2,1)S(1)}, u32[]{:S(2)}, u32[]{:S(2)}) collective-permute-start(bf16[256,256]{1,0:T(8,128)(2,1)S(1)} %get-tuple-element.17), channel_id=1, source_target_pairs={{0,4},{4,0},{8,12},{12,8},{16,20},{20,16},{24,28},{28,24},{1,5},{5... | collective-permute-start | bytes 393224 | tf_op jit(solution)/shard_map/ppermute | solution.py:376
  8.8 18.5 %collective-permute-start.10 = (bf16[256,256]{1,0:T(8,128)(2,1)S(1)}, bf16[256,256]{1,0:T(8,128)(2,1)S(1)}, u32[]{:S(2)}, u32[]{:S(2)}) collective-permute-start(bf16[256,256]{1,0:T(8,128)(2,1)S(1)} %get-tuple-element.21), channel_id=1, source_target_pairs={{0,16},{4,20},{8,24},{12,28},{16,0},{20,4},{24,8},{28,12},{1,17},{... | collective-permute-start | bytes 393224 | tf_op jit(solution)/shard_map/ppermute | solution.py:376
  12.3 1.2 %collective-permute-start = (f32[8,128]{1,0:T(8,128)S(1)}, f32[8,128]{1,0:T(8,128)S(1)}, u32[]{:S(2)}, u32[]{:S(2)}) collective-permute-start(f32[8,128]{1,0:T(8,128)S(1)} %get-tuple-element.16), channel_id=1, source_target_pairs={{0,1},{1,0},{2,3},{3,2},{4,5},{5,4},{6,7},{7,6},{8,9},{9,8},{10,11... | collective-permute-start | bytes 12296 | tf_op jit(solution)/shard_map/ppermute | solution.py:376
  13.5 3.6 %collective-permute-start.1 = (f32[8,128]{1,0:T(8,128)S(1)}, f32[8,128]{1,0:T(8,128)S(1)}, u32[]{:S(2)}, u32[]{:S(2)}) collective-permute-start(f32[8,128]{1,0:T(8,128)S(1)} %add.6), channel_id=1, source_target_pairs={{0,2},{1,3},{2,0},{3,1},{4,6},{5,7},{6,4},{7,5},{8,10},{9,11},{10,... | collective-permute-start | bytes 12296 | tf_op jit(solution)/shard_map/ppermute | solution.py:376
  17.1 21.8 %collective-permute-start.6 = (bf16[256,256]{1,0:T(8,128)(2,1)S(1)}, bf16[256,256]{1,0:T(8,128)(2,1)S(1)}, u32[]{:S(2)}, u32[]{:S(2)}) collective-permute-start(bf16[256,256]{1,0:T(8,128)(2,1)S(1)} %get-tuple-element.19), channel_id=1, source_target_pairs={{0,20},{4,16},{8,28},{12,24},{16,4},{20,0},{24,12},{28,8},{1,21},{... | collective-permute-start | bytes 393224 | tf_op jit(solution)/shard_map/ppermute | solution.py:376
  20.3 12.6 %collective-permute-start.8 = (bf16[256,256]{1,0:T(8,128)(2,1)S(1)}, bf16[256,256]{1,0:T(8,128)(2,1)S(1)}, u32[]{:S(2)}, u32[]{:S(2)}) collective-permute-start(bf16[256,256]{1,0:T(8,128)(2,1)S(1)} %get-tuple-element.20), channel_id=1, source_target_pairs={{0,12},{4,8},{8,4},{12,0},{16,28},{20,24},{24,20},{28,16},{1,13},{... | collective-permute-start | bytes 393224 | tf_op jit(solution)/shard_map/ppermute | solution.py:376
  22.0 22.5 %collective-permute-start.15 = (bf16[272,256]{1,0:T(8,128)(2,1)S(1)}, bf16[272,256]{1,0:T(8,128)(2,1)S(1)}, u32[]{:S(2)}, u32[]{:S(2)}) collective-permute-start(bf16[272,256]{1,0:T(8,128)(2,1)S(1)} %shard_map.104), channel_id=1, source_target_pairs={{0,24},{4,28},{8,16},{12,20},{16,8},{20,12},{24,0},{28,4},{1,25},{... | collective-permute-start | bytes 417800 | tf_op jit(solution)/shard_map/ppermute | solution.py:376
  24.8 21.0 %collective-permute-start.13 = (bf16[272,256]{1,0:T(8,128)(2,1)S(1)}, bf16[272,256]{1,0:T(8,128)(2,1)S(1)}, u32[]{:S(2)}, u32[]{:S(2)}) collective-permute-start(bf16[272,256]{1,0:T(8,128)(2,1)S(1)} %shard_map.103), channel_id=1, source_target_pairs={{0,28},{4,24},{8,20},{12,16},{16,12},{20,8},{24,4},{28,0},{1,29},{... | collective-permute-start | bytes 417800 | tf_op jit(solution)/shard_map/ppermute | solution.py:376
  27.3 14.4 %collective-permute-start.4 = (bf16[256,256]{1,0:T(8,128)(2,1)S(1)}, bf16[256,256]{1,0:T(8,128)(2,1)S(1)}, u32[]{:S(2)}, u32[]{:S(2)}) collective-permute-start(bf16[256,256]{1,0:T(8,128)(2,1)S(1)} %get-tuple-element.18), channel_id=1, source_target_pairs={{0,8},{4,12},{8,0},{12,4},{16,24},{20,28},{24,16},{28,20},{1,9},{5... | collective-permute-start | bytes 393224 | tf_op jit(solution)/shard_map/ppermute | solution.py:376
  32.9 18.6 %collective-permute-start.11 = (bf16[272,256]{1,0:T(8,128)(2,1)S(1)}, bf16[272,256]{1,0:T(8,128)(2,1)S(1)}, u32[]{:S(2)}, u32[]{:S(2)}) collective-permute-start(bf16[272,256]{1,0:T(8,128)(2,1)S(1)} %shard_map.102), channel_id=1, source_target_pairs={{0,16},{4,20},{8,24},{12,28},{16,0},{20,4},{24,8},{28,12},{1,17},{... | collective-permute-start | bytes 417800 | tf_op jit(solution)/shard_map/ppermute | solution.py:376
  38.9 12.7 %collective-permute-start.9 = (bf16[272,256]{1,0:T(8,128)(2,1)S(1)}, bf16[272,256]{1,0:T(8,128)(2,1)S(1)}, u32[]{:S(2)}, u32[]{:S(2)}) collective-permute-start(bf16[272,256]{1,0:T(8,128)(2,1)S(1)} %shard_map.101), channel_id=1, source_target_pairs={{0,12},{4,8},{8,4},{12,0},{16,28},{20,24},{24,20},{28,16},{1,13},{... | collective-permute-start | bytes 417800 | tf_op jit(solution)/shard_map/ppermute | solution.py:376
  41.6 4.5 %copy-start.2 = (f32[1,8,256,256]{3,2,1,0:T(8,128)S(1)}, f32[1,8,256,256]{3,2,1,0:T(8,128)}, u32[]{:S(2)}) copy-start(f32[1,8,256,256]{3,2,1,0:T(8,128)} %refs_8_.1) | copy-start | bytes 6291460
  41.7 4.5 %copy-start.3 = (f32[1,8,256,256]{3,2,1,0:T(8,128)S(1)}, f32[1,8,256,256]{3,2,1,0:T(8,128)}, u32[]{:S(2)}) copy-start(f32[1,8,256,256]{3,2,1,0:T(8,128)} %refs_9_.1) | copy-start | bytes 6291460
  41.7 12.7 %collective-permute-start.7 = (bf16[272,256]{1,0:T(8,128)(2,1)S(1)}, bf16[272,256]{1,0:T(8,128)(2,1)S(1)}, u32[]{:S(2)}, u32[]{:S(2)}) collective-permute-start(bf16[272,256]{1,0:T(8,128)(2,1)S(1)} %shard_map.100), channel_id=1, source_target_pairs={{0,20},{4,16},{8,28},{12,24},{16,4},{20,0},{24,12},{28,8},{1,21},{... | collective-permute-start | bytes 417800 | tf_op jit(solution)/shard_map/ppermute | solution.py:376
  44.4 9.9 %collective-permute-start.5 = (bf16[272,256]{1,0:T(8,128)(2,1)S(1)}, bf16[272,256]{1,0:T(8,128)(2,1)S(1)}, u32[]{:S(2)}, u32[]{:S(2)}) collective-permute-start(bf16[272,256]{1,0:T(8,128)(2,1)S(1)} %shard_map.99), channel_id=1, source_target_pairs={{0,8},{4,12},{8,0},{12,4},{16,24},{20,28},{24,16},{28,20},{1,9},{5... | collective-permute-start | bytes 417800 | tf_op jit(solution)/shard_map/ppermute | solution.py:376
  45.8 8.5 %collective-permute-start.3 = (bf16[272,256]{1,0:T(8,128)(2,1)S(1)}, bf16[272,256]{1,0:T(8,128)(2,1)S(1)}, u32[]{:S(2)}, u32[]{:S(2)}) collective-permute-start(bf16[272,256]{1,0:T(8,128)(2,1)S(1)} %shard_map.98), channel_id=1, source_target_pairs={{0,4},{4,0},{8,12},{12,8},{16,20},{20,16},{24,28},{28,24},{1,5},{5... | collective-permute-start | bytes 417800 | tf_op jit(solution)/shard_map/ppermute | solution.py:376
  46.2 8.2 %copy-start.4 = (s32[1,64,1]{1,2,0:T(1,128)S(1)}, s32[1,64,1]{1,2,0:T(1,128)}, u32[]{:S(2)}) copy-start(s32[1,64,1]{1,2,0:T(1,128)} %param.9) | copy-start | bytes 772

commit v7 on v4

--- a/solution.py
+++ b/solution.py
@@ -223,7 +223,8 @@
     )(total)
 
 
-def precondition_kernel(m, rows, me_ref, grad_ref, left_ref, right_ref, tail_ref, out_ref):
+def precondition_kernel(m, rows, me_ref, grad_ref, left_ref, right_ref, tail_ref, *refs):
+    out_ref = refs[-1]
     side = grad_ref.shape[0]
     slot = me_ref[0] ^ m
     half_done = jnp.dot(
@@ -236,14 +237,15 @@
         out_ref[side:, :] = tail_ref[...]
 
 
-def precondition(m, rows, me, block, left_root, right_root, tail):
+def precondition(m, rows, me, block, left_root, right_root, tail, after):
     side = block.shape[0]
     return pl.pallas_call(
         functools.partial(precondition_kernel, m, rows),
         grid_spec=pltpu.PrefetchScalarGridSpec(
             num_scalar_prefetch=1,
             grid=(),
-            in_specs=[pl.BlockSpec(memory_space=pltpu.VMEM)] * 4,
+            in_specs=[pl.BlockSpec(memory_space=pltpu.VMEM)] * 4
+            + [pl.BlockSpec(memory_space=pl.ANY)] * len(after),
             out_specs=pl.BlockSpec(memory_space=pltpu.VMEM),
         ),
         out_shape=jax.ShapeDtypeStruct((side + rows, side), jnp.bfloat16),
@@ -251,7 +253,7 @@
         cost_estimate=pl.CostEstimate(
             flops=4 * side**3, bytes_accessed=8 * side * side, transcendentals=0
         ),
-    )(me, block, left_root, right_root, tail)
+    )(me, block, left_root, right_root, tail, *after)
 
 
 def gram_kernel(order, me_ref, *refs):
@@ -381,10 +383,12 @@
     for k in doublings(layers):
         total = total + swap(total, k, "layer")
     tail = sum_tail(total, side)
+    landed = dict(zip(order, received))
     returned = []
     for m, block in zip(order, received):
         rows = TAIL if m else 0
-        done = precondition(m, rows, me, block, left_root, right_root, tail)
+        after = [landed[half + 1]] if m == count - 2 else []
+        done = precondition(m, rows, me, block, left_root, right_root, tail, after)
         returned.append(swap(done, m))
     new_left, new_right = gram_update(order, me, received, left_stats, right_stats)
     entries = float(owner_list.shape[0] * layers * side * side)

time: 56.3 us -> 56.8 us (level)
  waiting for transfers between devices: 7.38 us -> 12.5 us
  starting transfers between devices: 34.6 us -> 30 us
    ppermute x16, waiting for transfers between devices: 7.38 us -> 12.5 us  [swap(): lax.ppermute(value, axis, [(i, i ^ m) for i in range(lax.axis_size(axis))])]
    ppermute x16, starting transfers between devices: 34.6 us -> 30 us  [swap(): lax.ppermute(value, axis, [(i, i ^ m) for i in range(lax.axis_size(axis))])]
  transfers between devices with their start and end apart: 16 -> 16, of which waited for: 4 -> 8; matrix products, arithmetic and copies ran while one was open for 0% -> 0% of each run, Pallas kernels for 18% -> 18%
where the time goes in v7:
time: 56.8 us; the launch traced here: 56.6 us
  starting transfers between devices  30 us (53%)
  Pallas kernels  13.2 us (23%)
  waiting for transfers between devices  12.5 us (22%)
  between operations  0.84 us (1%)
    ppermute x16, starting transfers between devices, swap(): lax.ppermute(value, axis, [(i, i ^ m) for i in range(lax.axis_size(axis))])  30 us
    ppermute x16, waiting for transfers between devices, swap(): lax.ppermute(value, axis, [(i, i ^ m) for i in range(lax.axis_size(axis))])  12.5 us
    pallas_call x1, Pallas kernels, gram_update(): pl.pallas_call(functools.partial(gram_kernel, order), grid_spec=pltpu.Pre...  4.68 us
    pallas_call x8, Pallas kernels, precondition(): pl.pallas_call(functools.partial(precondition_kernel, m, rows), grid_spec...  2.63 us
    pallas_call x1, Pallas kernels, adam_squares(): pl.pallas_call(adam_kernel, in_specs=[hbm, hbm], out_specs=[pl.BlockSpec(...  2.53 us
    pallas_call x1, Pallas kernels, finish(): pl.pallas_call(functools.partial(finish_kernel, order, entries), grid_spe...  1.8 us
    pallas_call x1, Pallas kernels, route(): pl.pallas_call(functools.partial(route_kernel, order), in_specs=[hbm, pl....  1.46 us
  transfers between devices with their start and end apart: 16, of which 8 were waited for; matrix products, arithmetic and copies ran while one was open for 0% of the time, Pallas kernels for 18%

profile of v7, /device:TPU:0, one launch (start us, length us, event | category | flops | bytes accessed | tf_op | source)
XLA Modules:
  0.0 56.6 jit_solution(13559229208838214992)
XLA Ops:
  0.7 1.5 %shard_map.94 = (bf16[256,256]{1,0:T(8,128)(2,1)S(1)}, bf16[256,256]{1,0:T(8,128)(2,1)S(1)}, bf16[256,256]{1,0:T(8,128)(2,1)S(1)}, bf16[256,256]{1,0:T(8,128)(2,...) custom-call(s32[64]{0:T(128)} %bitcast.2, ...), custom_call_target="tpu_custom_call" | custom-call | bytes 2097152 | tf_op jit(solution)/shard_map/pallas_call | solution.py:128
  2.1 6.0 %collective-permute-start.14 = (bf16[256,256]{1,0:T(8,128)(2,1)S(1)}, bf16[256,256]{1,0:T(8,128)(2,1)S(1)}, u32[]{:S(2)}, u32[]{:S(2)}) collective-permute-start(bf16[256,256]{1,0:T(8,128)(2,1)S(1)} %get-tuple-element.23), channel_id=1, source_target_pairs={{0,28},{4,24},{8,20},{12,16},{16,12},{20,8},{24,4},{28,0},{1,29},{... | collective-permute-start | bytes 393224 | tf_op jit(solution)/shard_map/ppermute | solution.py:378
  8.2 0.0 collective-permute-start.10
  8.2 1.9 %collective-permute-start.12 = (bf16[256,256]{1,0:T(8,128)(2,1)S(1)}, bf16[256,256]{1,0:T(8,128)(2,1)S(1)}, u32[]{:S(2)}, u32[]{:S(2)}) collective-permute-start(bf16[256,256]{1,0:T(8,128)(2,1)S(1)} %get-tuple-element.22), channel_id=1, source_target_pairs={{0,24},{4,28},{8,16},{12,20},{16,8},{20,12},{24,0},{28,4},{1,25},{... | collective-permute-start | bytes 393224 | tf_op jit(solution)/shard_map/ppermute | solution.py:378
  10.1 1.5 %collective-permute-start.2 = (bf16[256,256]{1,0:T(8,128)(2,1)S(1)}, bf16[256,256]{1,0:T(8,128)(2,1)S(1)}, u32[]{:S(2)}, u32[]{:S(2)}) collective-permute-start(bf16[256,256]{1,0:T(8,128)(2,1)S(1)} %get-tuple-element.17), channel_id=1, source_target_pairs={{0,4},{4,0},{8,12},{12,8},{16,20},{20,16},{24,28},{28,24},{1,5},{5... | collective-permute-start | bytes 393224 | tf_op jit(solution)/shard_map/ppermute | solution.py:378
  11.5 2.5 %shard_map.95 = (f32[8,128]{1,0:T(8,128)S(1)}, f32[8,128]{1,0:T(8,128)S(1)}) custom-call(bf16[1,8,256,256]{3,2,1,0:T(8,128)(2,1)} %grad_hbm.3, f32[1,8,256,256]{3,2,1,0:T(8,128)} %moment_hbm.1), custom_call_target="tpu_custom_call" | custom-call | flops 4194304 | bytes 3145728 | tf_op jit(solution)/shard_map/pallas_call | solution.py:179
  14.1 0.1 collective-permute-start
  14.2 1.2 %collective-permute-done = f32[8,128]{1,0:T(8,128)S(1)} collective-permute-done((f32[8,128]{1,0:T(8,128)S(1)}, f32[8,128]{1,0:T(8,128)S(1)}, u32[]{:S(2)}, u32[]{:S(2)}) %collective-permute-start) | collective-permute-done | bytes 4128 | tf_op jit(solution)/shard_map/ppermute | solution.py:378
  15.3 1.5 %collective-permute-start.1 = (f32[8,128]{1,0:T(8,128)S(1)}, f32[8,128]{1,0:T(8,128)S(1)}, u32[]{:S(2)}, u32[]{:S(2)}) collective-permute-start(f32[8,128]{1,0:T(8,128)S(1)} %add.6), channel_id=1, source_target_pairs={{0,2},{1,3},{2,0},{3,1},{4,6},{5,7},{6,4},{7,5},{8,10},{9,11},{10,... | collective-permute-start | bytes 12296 | tf_op jit(solution)/shard_map/ppermute | solution.py:378
  16.8 2.1 %collective-permute-done.1 = f32[8,128]{1,0:T(8,128)S(1)} collective-permute-done((f32[8,128]{1,0:T(8,128)S(1)}, f32[8,128]{1,0:T(8,128)S(1)}, u32[]{:S(2)}, u32[]{:S(2)}) %collective-permute-start.1) | collective-permute-done | bytes 4128 | tf_op jit(solution)/shard_map/ppermute | solution.py:378
  18.9 1.0 %collective-permute-start.6 = (bf16[256,256]{1,0:T(8,128)(2,1)S(1)}, bf16[256,256]{1,0:T(8,128)(2,1)S(1)}, u32[]{:S(2)}, u32[]{:S(2)}) collective-permute-start(bf16[256,256]{1,0:T(8,128)(2,1)S(1)} %get-tuple-element.19), channel_id=1, source_target_pairs={{0,16},{4,20},{8,24},{12,28},{16,0},{20,4},{24,8},{28,12},{1,17},{... | collective-permute-start | bytes 393224 | tf_op jit(solution)/shard_map/ppermute | solution.py:378
  19.9 0.1 shard_map.96.tail_ref.refs_9_
  20.1 0.0 collective-permute-done.14.grad_ref.refs_7_
  20.1 1.5 %collective-permute-start.8 = (bf16[256,256]{1,0:T(8,128)(2,1)S(1)}, bf16[256,256]{1,0:T(8,128)(2,1)S(1)}, u32[]{:S(2)}, u32[]{:S(2)}) collective-permute-start(bf16[256,256]{1,0:T(8,128)(2,1)S(1)} %get-tuple-element.20), channel_id=1, source_target_pairs={{0,12},{4,8},{8,4},{12,0},{16,28},{20,24},{24,20},{28,16},{1,13},{... | collective-permute-start | bytes 393224 | tf_op jit(solution)/shard_map/ppermute | solution.py:378
  21.6 0.3 shard_map.104
  22.0 2.5 %collective-permute-done.10.grad_ref.refs_0_.refs_5_ = bf16[256,256]{1,0:T(8,128)(2,1)S(1)} collective-permute-done((bf16[256,256]{1,0:T(8,128)(2,1)S(1)}, bf16[256,256]{1,0:T(8,128)(2,1)S(1)}, u32[]{:S(2)}, u32[]{:S(2)}) %collective-permute-start.10) | collective-permute-done | bytes 131104 | tf_op jit(solution)/shard_map/ppermute | solution.py:378
  24.4 5.0 %collective-permute-start.15 = (bf16[272,256]{1,0:T(8,128)(2,1)S(1)}, bf16[272,256]{1,0:T(8,128)(2,1)S(1)}, u32[]{:S(2)}, u32[]{:S(2)}) collective-permute-start(bf16[272,256]{1,0:T(8,128)(2,1)S(1)} %shard_map.104), channel_id=1, source_target_pairs={{0,28},{4,24},{8,20},{12,16},{16,12},{20,8},{24,4},{28,0},{1,29},{... | collective-permute-start | bytes 417800 | tf_op jit(solution)/shard_map/ppermute | solution.py:378
  29.4 0.0 collective-permute-done.12.grad_ref.refs_6_
  29.4 0.3 shard_map.103
  29.7 0.1 collective-permute-start.13
  29.8 0.0 collective-permute-done.2.grad_ref.refs_1_
  29.8 4.5 %collective-permute-start.4 = (bf16[256,256]{1,0:T(8,128)(2,1)S(1)}, bf16[256,256]{1,0:T(8,128)(2,1)S(1)}, u32[]{:S(2)}, u32[]{:S(2)}) collective-permute-start(bf16[256,256]{1,0:T(8,128)(2,1)S(1)} %get-tuple-element.18), channel_id=1, source_target_pairs={{0,8},{4,12},{8,0},{12,4},{16,24},{20,28},{24,16},{28,20},{1,9},{5... | collective-permute-start | bytes 393224 | tf_op jit(solution)/shard_map/ppermute | solution.py:378
  34.3 0.3 shard_map.102
  34.7 0.3 shard_map.98
  35.0 0.0 collective-permute-done.8.grad_ref.refs_4_
  35.0 0.5 collective-permute-start.11
  35.5 0.3 shard_map.101
  35.8 3.0 %collective-permute-done.6.grad_ref.refs_3_ = bf16[256,256]{1,0:T(8,128)(2,1)S(1)} collective-permute-done((bf16[256,256]{1,0:T(8,128)(2,1)S(1)}, bf16[256,256]{1,0:T(8,128)(2,1)S(1)}, u32[]{:S(2)}, u32[]{:S(2)}) %collective-permute-start.6) | collective-permute-done | bytes 131104 | tf_op jit(solution)/shard_map/ppermute | solution.py:378
  38.8 0.1 collective-permute-start.9
  38.9 0.3 shard_map.100
  39.3 0.0 copy-start.2
  39.3 0.0 copy-start.3
  39.3 1.0 %collective-permute-done.4.grad_ref.refs_2_ = bf16[256,256]{1,0:T(8,128)(2,1)S(1)} collective-permute-done((bf16[256,256]{1,0:T(8,128)(2,1)S(1)}, bf16[256,256]{1,0:T(8,128)(2,1)S(1)}, u32[]{:S(2)}, u32[]{:S(2)}) %collective-permute-start.4) | collective-permute-done | bytes 131104 | tf_op jit(solution)/shard_map/ppermute | solution.py:378
  40.3 2.1 %collective-permute-start.7 = (bf16[272,256]{1,0:T(8,128)(2,1)S(1)}, bf16[272,256]{1,0:T(8,128)(2,1)S(1)}, u32[]{:S(2)}, u32[]{:S(2)}) collective-permute-start(bf16[272,256]{1,0:T(8,128)(2,1)S(1)} %shard_map.100), channel_id=1, source_target_pairs={{0,16},{4,20},{8,24},{12,28},{16,0},{20,4},{24,8},{28,12},{1,17},{... | collective-permute-start | bytes 417800 | tf_op jit(solution)/shard_map/ppermute | solution.py:378
  42.3 0.3 shard_map.99
  42.7 0.0 collective-permute-done.15.refs_7_
  42.7 3.3 %collective-permute-start.5 = (bf16[272,256]{1,0:T(8,128)(2,1)S(1)}, bf16[272,256]{1,0:T(8,128)(2,1)S(1)}, u32[]{:S(2)}, u32[]{:S(2)}) collective-permute-start(bf16[272,256]{1,0:T(8,128)(2,1)S(1)} %shard_map.99), channel_id=1, source_target_pairs={{0,8},{4,12},{8,0},{12,4},{16,24},{20,28},{24,16},{28,20},{1,9},{5... | collective-permute-start | bytes 417800 | tf_op jit(solution)/shard_map/ppermute | solution.py:378
  46.0 0.0 collective-permute-done.13.refs_6_
  46.0 0.9 %collective-permute-start.3 = (bf16[272,256]{1,0:T(8,128)(2,1)S(1)}, bf16[272,256]{1,0:T(8,128)(2,1)S(1)}, u32[]{:S(2)}, u32[]{:S(2)}) collective-permute-start(bf16[272,256]{1,0:T(8,128)(2,1)S(1)} %shard_map.98), channel_id=1, source_target_pairs={{0,4},{4,0},{8,12},{12,8},{16,20},{20,16},{24,28},{28,24},{1,5},{5... | collective-permute-start | bytes 417800 | tf_op jit(solution)/shard_map/ppermute | solution.py:378
  46.9 0.3 shard_map.97.refs_0_
  47.3 0.0 copy-start.4
  47.3 4.7 %shard_map.106 = (f32[1,8,256,256]{3,2,1,0:T(8,128)}, f32[1,8,256,256]{3,2,1,0:T(8,128)}) custom-call(s32[1]{0:T(128)} %bitcast.1.me_ref, bf16[256,256]{1,0:T(8,128)(2,1)S(1)} %get-tuple-element.15.grad_ref.refs_0_, bf16[256,256]{1,0:T(8,128)(2,1)S(1)} %collective-permute-done.2.grad_ref.refs_1_, ...), custom_call_target="tpu_custom_call" | custom-call | flops 536870912 | bytes 9437184 | tf_op jit(solution)/shard_map/pallas_call | solution.py:283
  52.0 0.5 collective-permute-done.11.refs_5_
  52.5 0.0 collective-permute-done.9.refs_4_
  52.5 2.0 %collective-permute-done.7.refs_3_ = bf16[272,256]{1,0:T(8,128)(2,1)S(1)} collective-permute-done((bf16[272,256]{1,0:T(8,128)(2,1)S(1)}, bf16[272,256]{1,0:T(8,128)(2,1)S(1)}, u32[]{:S(2)}, u32[]{:S(2)}) %collective-permute-start.7) | collective-permute-done | bytes 139296 | tf_op jit(solution)/shard_map/ppermute | solution.py:378
  54.5 0.4 collective-permute-done.5.refs_2_
  54.8 0.0 collective-permute-done.3.refs_1_
  54.8 1.8 %shard_map.105 = bf16[1,8,256,256]{3,2,1,0:T(8,128)(2,1)} custom-call(s32[64]{0:T(128)S(1)} %bitcast.3, s32[1]{0:T(128)} %bitcast.1.me_ref, bf16[256,256]{1,0:T(8,128)(2,1)S(1)} %shard_map.97.refs_0_, bf16[272,256]{1,0:T(8,128)(2,1)S(1)} %collective-permute-done.3.refs_1_, bf16[272,256]{1,0:T(8,128)(2,1)S(1)} %collective-permute-done.5.refs_2_, ...), custom_call_target="tpu_custom_call" | custom-call | flops 3145728 | bytes 2097152 | tf_op jit(solution)/shard_map/pallas_call | solution.py:339
  (9 shorter events, 0.0 us)
Async XLA Ops:
  0.6 21.0 %copy-start = (bf16[1,8,256,256]{3,2,1,0:T(8,128)(2,1)S(1)}, bf16[1,8,256,256]{3,2,1,0:T(8,128)(2,1)}, u32[]{:S(2)}) copy-start(bf16[1,8,256,256]{3,2,1,0:T(8,128)(2,1)} %left_ref.15) | copy-start | bytes 3145732
  0.6 21.0 %copy-start.1 = (bf16[1,8,256,256]{3,2,1,0:T(8,128)(2,1)S(1)}, bf16[1,8,256,256]{3,2,1,0:T(8,128)(2,1)}, u32[]{:S(2)}) copy-start(bf16[1,8,256,256]{3,2,1,0:T(8,128)(2,1)} %right_ref.15) | copy-start | bytes 3145732
  2.1 18.0 %collective-permute-start.14 = (bf16[256,256]{1,0:T(8,128)(2,1)S(1)}, bf16[256,256]{1,0:T(8,128)(2,1)S(1)}, u32[]{:S(2)}, u32[]{:S(2)}) collective-permute-start(bf16[256,256]{1,0:T(8,128)(2,1)S(1)} %get-tuple-element.23), channel_id=1, source_target_pairs={{0,28},{4,24},{8,20},{12,16},{16,12},{20,8},{24,4},{28,0},{1,29},{... | collective-permute-start | bytes 393224 | tf_op jit(solution)/shard_map/ppermute | solution.py:378
  8.2 16.2 %collective-permute-start.10 = (bf16[256,256]{1,0:T(8,128)(2,1)S(1)}, bf16[256,256]{1,0:T(8,128)(2,1)S(1)}, u32[]{:S(2)}, u32[]{:S(2)}) collective-permute-start(bf16[256,256]{1,0:T(8,128)(2,1)S(1)} %get-tuple-element.21), channel_id=1, source_target_pairs={{0,20},{4,16},{8,28},{12,24},{16,4},{20,0},{24,12},{28,8},{1,21},{... | collective-permute-start | bytes 393224 | tf_op jit(solution)/shard_map/ppermute | solution.py:378
  8.2 21.2 %collective-permute-start.12 = (bf16[256,256]{1,0:T(8,128)(2,1)S(1)}, bf16[256,256]{1,0:T(8,128)(2,1)S(1)}, u32[]{:S(2)}, u32[]{:S(2)}) collective-permute-start(bf16[256,256]{1,0:T(8,128)(2,1)S(1)} %get-tuple-element.22), channel_id=1, source_target_pairs={{0,24},{4,28},{8,16},{12,20},{16,8},{20,12},{24,0},{28,4},{1,25},{... | collective-permute-start | bytes 393224 | tf_op jit(solution)/shard_map/ppermute | solution.py:378
  10.1 19.8 %collective-permute-start.2 = (bf16[256,256]{1,0:T(8,128)(2,1)S(1)}, bf16[256,256]{1,0:T(8,128)(2,1)S(1)}, u32[]{:S(2)}, u32[]{:S(2)}) collective-permute-start(bf16[256,256]{1,0:T(8,128)(2,1)S(1)} %get-tuple-element.17), channel_id=1, source_target_pairs={{0,4},{4,0},{8,12},{12,8},{16,20},{20,16},{24,28},{28,24},{1,5},{5... | collective-permute-start | bytes 393224 | tf_op jit(solution)/shard_map/ppermute | solution.py:378
  14.1 1.2 %collective-permute-start = (f32[8,128]{1,0:T(8,128)S(1)}, f32[8,128]{1,0:T(8,128)S(1)}, u32[]{:S(2)}, u32[]{:S(2)}) collective-permute-start(f32[8,128]{1,0:T(8,128)S(1)} %get-tuple-element.16), channel_id=1, source_target_pairs={{0,1},{1,0},{2,3},{3,2},{4,5},{5,4},{6,7},{7,6},{8,9},{9,8},{10,11... | collective-permute-start | bytes 12296 | tf_op jit(solution)/shard_map/ppermute | solution.py:378
  15.3 3.6 %collective-permute-start.1 = (f32[8,128]{1,0:T(8,128)S(1)}, f32[8,128]{1,0:T(8,128)S(1)}, u32[]{:S(2)}, u32[]{:S(2)}) collective-permute-start(f32[8,128]{1,0:T(8,128)S(1)} %add.6), channel_id=1, source_target_pairs={{0,2},{1,3},{2,0},{3,1},{4,6},{5,7},{6,4},{7,5},{8,10},{9,11},{10,... | collective-permute-start | bytes 12296 | tf_op jit(solution)/shard_map/ppermute | solution.py:378
  18.9 19.9 %collective-permute-start.6 = (bf16[256,256]{1,0:T(8,128)(2,1)S(1)}, bf16[256,256]{1,0:T(8,128)(2,1)S(1)}, u32[]{:S(2)}, u32[]{:S(2)}) collective-permute-start(bf16[256,256]{1,0:T(8,128)(2,1)S(1)} %get-tuple-element.19), channel_id=1, source_target_pairs={{0,16},{4,20},{8,24},{12,28},{16,0},{20,4},{24,8},{28,12},{1,17},{... | collective-permute-start | bytes 393224 | tf_op jit(solution)/shard_map/ppermute | solution.py:378
  20.1 14.9 %collective-permute-start.8 = (bf16[256,256]{1,0:T(8,128)(2,1)S(1)}, bf16[256,256]{1,0:T(8,128)(2,1)S(1)}, u32[]{:S(2)}, u32[]{:S(2)}) collective-permute-start(bf16[256,256]{1,0:T(8,128)(2,1)S(1)} %get-tuple-element.20), channel_id=1, source_target_pairs={{0,12},{4,8},{8,4},{12,0},{16,28},{20,24},{24,20},{28,16},{1,13},{... | collective-permute-start | bytes 393224 | tf_op jit(solution)/shard_map/ppermute | solution.py:378
  24.4 18.3 %collective-permute-start.15 = (bf16[272,256]{1,0:T(8,128)(2,1)S(1)}, bf16[272,256]{1,0:T(8,128)(2,1)S(1)}, u32[]{:S(2)}, u32[]{:S(2)}) collective-permute-start(bf16[272,256]{1,0:T(8,128)(2,1)S(1)} %shard_map.104), channel_id=1, source_target_pairs={{0,28},{4,24},{8,20},{12,16},{16,12},{20,8},{24,4},{28,0},{1,29},{... | collective-permute-start | bytes 417800 | tf_op jit(solution)/shard_map/ppermute | solution.py:378
  29.7 16.3 %collective-permute-start.13 = (bf16[272,256]{1,0:T(8,128)(2,1)S(1)}, bf16[272,256]{1,0:T(8,128)(2,1)S(1)}, u32[]{:S(2)}, u32[]{:S(2)}) collective-permute-start(bf16[272,256]{1,0:T(8,128)(2,1)S(1)} %shard_map.103), channel_id=1, source_target_pairs={{0,24},{4,28},{8,16},{12,20},{16,8},{20,12},{24,0},{28,4},{1,25},{... | collective-permute-start | bytes 417800 | tf_op jit(solution)/shard_map/ppermute | solution.py:378
  29.8 10.5 %collective-permute-start.4 = (bf16[256,256]{1,0:T(8,128)(2,1)S(1)}, bf16[256,256]{1,0:T(8,128)(2,1)S(1)}, u32[]{:S(2)}, u32[]{:S(2)}) collective-permute-start(bf16[256,256]{1,0:T(8,128)(2,1)S(1)} %get-tuple-element.18), channel_id=1, source_target_pairs={{0,8},{4,12},{8,0},{12,4},{16,24},{20,28},{24,16},{28,20},{1,9},{5... | collective-permute-start | bytes 393224 | tf_op jit(solution)/shard_map/ppermute | solution.py:378
  35.0 17.4 %collective-permute-start.11 = (bf16[272,256]{1,0:T(8,128)(2,1)S(1)}, bf16[272,256]{1,0:T(8,128)(2,1)S(1)}, u32[]{:S(2)}, u32[]{:S(2)}) collective-permute-start(bf16[272,256]{1,0:T(8,128)(2,1)S(1)} %shard_map.102), channel_id=1, source_target_pairs={{0,20},{4,16},{8,28},{12,24},{16,4},{20,0},{24,12},{28,8},{1,21},{... | collective-permute-start | bytes 417800 | tf_op jit(solution)/shard_map/ppermute | solution.py:378
  38.8 13.6 %collective-permute-start.9 = (bf16[272,256]{1,0:T(8,128)(2,1)S(1)}, bf16[272,256]{1,0:T(8,128)(2,1)S(1)}, u32[]{:S(2)}, u32[]{:S(2)}) collective-permute-start(bf16[272,256]{1,0:T(8,128)(2,1)S(1)} %shard_map.101), channel_id=1, source_target_pairs={{0,12},{4,8},{8,4},{12,0},{16,28},{20,24},{24,20},{28,16},{1,13},{... | collective-permute-start | bytes 417800 | tf_op jit(solution)/shard_map/ppermute | solution.py:378
  39.3 8.0 %copy-start.2 = (f32[1,8,256,256]{3,2,1,0:T(8,128)S(1)}, f32[1,8,256,256]{3,2,1,0:T(8,128)}, u32[]{:S(2)}) copy-start(f32[1,8,256,256]{3,2,1,0:T(8,128)} %refs_8_.1) | copy-start | bytes 6291460
  39.3 8.0 %copy-start.3 = (f32[1,8,256,256]{3,2,1,0:T(8,128)S(1)}, f32[1,8,256,256]{3,2,1,0:T(8,128)}, u32[]{:S(2)}) copy-start(f32[1,8,256,256]{3,2,1,0:T(8,128)} %refs_9_.1) | copy-start | bytes 6291460
  40.3 14.2 %collective-permute-start.7 = (bf16[272,256]{1,0:T(8,128)(2,1)S(1)}, bf16[272,256]{1,0:T(8,128)(2,1)S(1)}, u32[]{:S(2)}, u32[]{:S(2)}) collective-permute-start(bf16[272,256]{1,0:T(8,128)(2,1)S(1)} %shard_map.100), channel_id=1, source_target_pairs={{0,16},{4,20},{8,24},{12,28},{16,0},{20,4},{24,8},{28,12},{1,17},{... | collective-permute-start | bytes 417800 | tf_op jit(solution)/shard_map/ppermute | solution.py:378
  42.7 12.1 %collective-permute-start.5 = (bf16[272,256]{1,0:T(8,128)(2,1)S(1)}, bf16[272,256]{1,0:T(8,128)(2,1)S(1)}, u32[]{:S(2)}, u32[]{:S(2)}) collective-permute-start(bf16[272,256]{1,0:T(8,128)(2,1)S(1)} %shard_map.99), channel_id=1, source_target_pairs={{0,8},{4,12},{8,0},{12,4},{16,24},{20,28},{24,16},{28,20},{1,9},{5... | collective-permute-start | bytes 417800 | tf_op jit(solution)/shard_map/ppermute | solution.py:378
  46.0 8.8 %collective-permute-start.3 = (bf16[272,256]{1,0:T(8,128)(2,1)S(1)}, bf16[272,256]{1,0:T(8,128)(2,1)S(1)}, u32[]{:S(2)}, u32[]{:S(2)}) collective-permute-start(bf16[272,256]{1,0:T(8,128)(2,1)S(1)} %shard_map.98), channel_id=1, source_target_pairs={{0,4},{4,0},{8,12},{12,8},{16,20},{20,16},{24,28},{28,24},{1,5},{5... | collective-permute-start | bytes 417800 | tf_op jit(solution)/shard_map/ppermute | solution.py:378
  47.3 7.5 %copy-start.4 = (s32[1,64,1]{1,2,0:T(1,128)S(1)}, s32[1,64,1]{1,2,0:T(1,128)}, u32[]{:S(2)}) copy-start(s32[1,64,1]{1,2,0:T(1,128)} %param.9) | copy-start | bytes 772

commit v8 on v6

--- a/solution.py
+++ b/solution.py
@@ -98,6 +98,18 @@
     return pltpu.CompilerParams(vmem_limit_bytes=mebibytes * 2**20)
 
 
+def partner_tables(count):
+    half = count // 2
+    even = [0, 1, 2, half, 3, *range(half + 1, count)]
+    odd = [{1: half, half: 1}.get(m, m) for m in even]
+    return even, odd
+
+
+def partner(me, step, count):
+    even, odd = partner_tables(count)
+    return jnp.where(me & 2 == 2, jnp.int32(odd[step]), jnp.int32(even[step]))
+
+
 def home_slot(named, target):
     block = jnp.int32(0)
     for j in range(1, len(named)):
@@ -105,7 +117,7 @@
     return block
 
 
-def route_kernel(order, owners_hbm, me_ref, grad_hbm, *refs):
+def route_kernel(owners_hbm, me_ref, grad_hbm, *refs):
     outs, (owners_ref, held, owner_sem, grad_sem) = refs[:-4], refs[-4:]
     count = held.shape[0]
     me = me_ref[0]
@@ -115,18 +127,18 @@
     fetch_grads.start()
     fetch_owners.wait()
     named = [owners_ref[me * count + j] for j in range(count)]
-    blocks = [home_slot(named, me ^ m) for m in order]
+    blocks = [home_slot(named, me ^ partner(me, step, count)) for step in range(count)]
     fetch_grads.wait()
     for block, out in zip(blocks, outs):
         out[...] = held[block]
 
 
-def route(order, owner_list, me, gradients):
+def route(owner_list, me, gradients):
     count, side = gradients.shape[1], gradients.shape[3]
     hbm = pl.BlockSpec(memory_space=pltpu.HBM)
     piece = jax.ShapeDtypeStruct((side, side), gradients.dtype)
     return pl.pallas_call(
-        functools.partial(route_kernel, order),
+        route_kernel,
         in_specs=[hbm, pl.BlockSpec(memory_space=pltpu.SMEM), hbm],
         out_specs=[pl.BlockSpec(memory_space=pltpu.VMEM)] * count,
         scratch_shapes=[
@@ -223,30 +235,31 @@
     )(total)
 
 
-def precondition_kernel(m, rows, me_ref, grad_ref, left_ref, right_ref, tail_ref, out_ref):
+def precondition_kernel(step, me_ref, grad_ref, left_ref, right_ref, tail_ref, out_ref):
     side = grad_ref.shape[0]
-    slot = me_ref[0] ^ m
+    me = me_ref[0]
+    slot = me ^ partner(me, step, left_ref.shape[1])
     half_done = jnp.dot(
         left_ref[0, slot], grad_ref[...], preferred_element_type=jnp.float32
     ).astype(jnp.bfloat16)
     out_ref[0:side, :] = jnp.dot(
         half_done, right_ref[0, slot], preferred_element_type=jnp.float32
     ).astype(jnp.bfloat16)
-    if rows:
+    if step:
         out_ref[side:, :] = tail_ref[...]
 
 
-def precondition(m, rows, me, block, left_root, right_root, tail):
+def precondition(step, me, block, left_root, right_root, tail):
     side = block.shape[0]
     return pl.pallas_call(
-        functools.partial(precondition_kernel, m, rows),
+        functools.partial(precondition_kernel, step),
         grid_spec=pltpu.PrefetchScalarGridSpec(
             num_scalar_prefetch=1,
             grid=(),
             in_specs=[pl.BlockSpec(memory_space=pltpu.VMEM)] * 4,
             out_specs=pl.BlockSpec(memory_space=pltpu.VMEM),
         ),
-        out_shape=jax.ShapeDtypeStruct((side + rows, side), jnp.bfloat16),
+        out_shape=jax.ShapeDtypeStruct((side + (TAIL if step else 0), side), jnp.bfloat16),
         compiler_params=kernel_params(6),
         cost_estimate=pl.CostEstimate(
             flops=4 * side**3, bytes_accessed=8 * side * side, transcendentals=0
@@ -254,14 +267,14 @@
     )(me, block, left_root, right_root, tail)
 
 
-def gram_kernel(order, me_ref, *refs):
+def gram_kernel(me_ref, *refs):
     count = len(refs) - 4
     grads = refs[:count]
     left_ref, right_ref, new_left_ref, new_right_ref = refs[count:]
     step = pl.program_id(0)
-    for k, m in enumerate(order):
-
-        @pl.when(step == m)
+    for k in range(count):
+
+        @pl.when(step == k)
         def _():
             block = grads[k][...]
             gram_left = lax.dot_general(
@@ -274,12 +287,20 @@
             new_right_ref[0, 0] = DECAY_RATE * right_ref[0, 0] + (1.0 - DECAY_RATE) * gram_right
 
 
-def gram_update(order, me, blocks, left_stats, right_stats):
+def gram_update(me, blocks, left_stats, right_stats):
     count, side = len(blocks), blocks[0].shape[0]
-    stat = pl.BlockSpec((1, 1, side, side), lambda i, me_ref: (0, me_ref[0] ^ i, 0, 0))
+
+    def slot(i, me_ref):
+        me = me_ref[0]
+        m = jnp.int32(0)
+        for step in range(1, count):
+            m = jnp.where(i == step, partner(me, step, count), m)
+        return (0, me ^ m, 0, 0)
+
+    stat = pl.BlockSpec((1, 1, side, side), slot)
     whole = pl.BlockSpec(memory_space=pltpu.VMEM)
     return pl.pallas_call(
-        functools.partial(gram_kernel, order),
+        gram_kernel,
         grid_spec=pltpu.PrefetchScalarGridSpec(
             num_scalar_prefetch=1,
             grid=(count,),
@@ -297,14 +318,14 @@
     )(me, *blocks, left_stats, right_stats)
 
 
-def finish_kernel(order, entries, owners_ref, me_ref, *refs):
-    count = len(order)
+def finish_kernel(entries, owners_ref, me_ref, *refs):
+    count = len(refs) - 6
     pieces = refs[:count]
     squares_ref, tail_ref, out_ref, held, sums, sems = refs[count:]
     side, lanes = out_ref.shape[3], squares_ref.shape[1]
     me = me_ref[0]
     named = [owners_ref[me * count + j] for j in range(count)]
-    blocks = [home_slot(named, me ^ m) for m in order]
+    blocks = [home_slot(named, me ^ partner(me, step, count)) for step in range(count)]
     global_sq = jnp.zeros((1, 1), jnp.float32)
     for rows in [tail_ref[...]] + [piece[side:, :] for piece in pieces if piece.shape[0] > side]:
         terms = rows[:, 0:1].astype(jnp.float32)
@@ -332,10 +353,10 @@
         copy.wait()
 
 
-def finish(order, owner_list, me, pieces, squares, tail, entries):
+def finish(owner_list, me, pieces, squares, tail, entries):
     count, side = len(pieces), pieces[0].shape[1]
     return pl.pallas_call(
-        functools.partial(finish_kernel, order, entries),
+        functools.partial(finish_kernel, entries),
         grid_spec=pltpu.PrefetchScalarGridSpec(
             num_scalar_prefetch=2,
             grid=(),
@@ -362,40 +383,37 @@
 def per_device_exchange(
     gradients, second_moment, owners, left_stats, right_stats, left_root, right_root
 ):
-    count = lax.axis_size("fsdp")
-    layers = lax.axis_size("layer")
+    count, layers = lax.axis_size("fsdp"), lax.axis_size("layer")
     side = gradients.shape[3]
     me = lax.axis_index("fsdp").astype(jnp.int32).reshape(1)
     owner_list = owners[0, :, 0]
-    half = count // 2
-    order = [0, 1, 2, half + 1, 3, half, count - 1, count - 2] if count == 8 else list(range(count))
-
-    def swap(value, m, axis="fsdp"):
-        if m == 0:
+    tables = partner_tables(count)
+
+    def swap(value, step):
+        if step == 0:
             return value
-        return lax.ppermute(value, axis, [(i, i ^ m) for i in range(lax.axis_size(axis))])
-
-    outgoing = route(order, owner_list, me, gradients)
-    received = [swap(block, m) for m, block in zip(order, outgoing)]
+        return lax.ppermute(value, "fsdp", [(i, i ^ tables[i // 2 % 2][step]) for i in range(count)])
+
+    outgoing = route(owner_list, me, gradients)
+    received = [swap(block, step) for step, block in enumerate(outgoing)]
     squares, total = adam_squares(gradients, second_moment)
     for k in doublings(layers):
-        total = total + swap(total, k, "layer")
+        total = total + lax.ppermute(total, "layer", [(i, i ^ k) for i in range(layers)])
     tail = sum_tail(total, side)
     returned = []
-    for m, block in zip(order, received):
-        rows = TAIL if m else 0
-        done = precondition(m, rows, me, block, left_root, right_root, tail)
-        returned.append(swap(done, m))
-    new_left, new_right = gram_update(order, me, received, left_stats, right_stats)
+    for step, block in enumerate(received):
+        done = precondition(step, me, block, left_root, right_root, tail)
+        returned.append(swap(done, step))
+    new_left, new_right = gram_update(me, received, left_stats, right_stats)
     entries = float(owner_list.shape[0] * layers * side * side)
-    update = finish(order, owner_list, me, returned, squares, tail, entries)
+    update = finish(owner_list, me, returned, squares, tail, entries)
     return (update, new_left, new_right)
 
 
 def per_device(gradients, second_moment, owners, left_stats, right_stats, left_root, right_root):
     owner_count, blocks, slots = lax.axis_size("fsdp"), gradients.shape[1], left_stats.shape[1]
     layers = lax.axis_size("layer")
-    paired = owner_count == blocks == slots
+    paired = owner_count == blocks == slots and owner_count >= 8
     paired = paired and owner_count & (owner_count - 1) == 0 and layers & (layers - 1) == 0
     body = per_device_exchange if paired else per_device_general
     return body(

time: 56.3 us -> 56.4 us (level)
  starting transfers between devices: 33.8 us -> 32.7 us
  waiting for transfers between devices: 8.3 us -> 9.32 us
    ppermute x16, starting transfers between devices: 33.8 us -> 32.7 us  [the longest x14 31.1 us: swap(): lax.ppermute(value, 'fsdp', [(i, i ^ tables[i // 2 % 2][step]) for i in r...]
    ppermute x16, waiting for transfers between devices: 8.3 us -> 9.32 us  [the longest x14 6.08 us: swap(): lax.ppermute(value, 'fsdp', [(i, i ^ tables[i // 2 % 2][step]) for i in r...]
  transfers between devices with their start and end apart: 16 -> 16, of which waited for: 6 -> 4; matrix products, arithmetic and copies ran while one was open for 0% -> 0% of each run, Pallas kernels for 18% -> 18%
where the time goes in v8:
time: 56.4 us; the launch traced here: 56.2 us
  starting transfers between devices  32.7 us (58%)
  Pallas kernels  13.3 us (24%)
  waiting for transfers between devices  9.32 us (17%)
  between operations  0.86 us (2%)
    ppermute x14, starting transfers between devices, swap(): lax.ppermute(value, 'fsdp', [(i, i ^ tables[i // 2 % 2][step]) for i in r...  31.1 us
    ppermute x14, waiting for transfers between devices, swap(): lax.ppermute(value, 'fsdp', [(i, i ^ tables[i // 2 % 2][step]) for i in r...  6.08 us
    pallas_call x1, Pallas kernels, gram_update(): pl.pallas_call(gram_kernel, grid_spec=pltpu.PrefetchScalarGridSpec(num_sc...  4.74 us
    ppermute x2, waiting for transfers between devices, per_device_exchange(): lax.ppermute(total, 'layer', [(i, i ^ k) for i in range(layers)])  3.24 us
    pallas_call x8, Pallas kernels, precondition(): pl.pallas_call(functools.partial(precondition_kernel, step), grid_spec=pl...  2.64 us
    pallas_call x1, Pallas kernels, adam_squares(): pl.pallas_call(adam_kernel, in_specs=[hbm, hbm], out_specs=[pl.BlockSpec(...  2.53 us
    pallas_call x1, Pallas kernels, finish(): pl.pallas_call(functools.partial(finish_kernel, entries), grid_spec=pltpu...  1.81 us
    ppermute x2, starting transfers between devices, per_device_exchange(): lax.ppermute(total, 'layer', [(i, i ^ k) for i in range(layers)])  1.59 us
  transfers between devices with their start and end apart: 16, of which 4 were waited for; matrix products, arithmetic and copies ran while one was open for 0% of the time, Pallas kernels for 18%

profile of v8, /device:TPU:0, one launch (start us, length us, event | category | flops | bytes accessed | tf_op | source)
XLA Modules:
  0.0 56.2 jit_solution(10005837138785673830)
XLA Ops:
  0.7 1.5 %shard_map.94 = (bf16[256,256]{1,0:T(8,128)(2,1)S(1)}, bf16[256,256]{1,0:T(8,128)(2,1)S(1)}, bf16[256,256]{1,0:T(8,128)(2,1)S(1)}, bf16[256,256]{1,0:T(8,128)(2,...) custom-call(s32[64]{0:T(128)} %bitcast.2, ...), custom_call_target="tpu_custom_call" | custom-call | bytes 2097152 | tf_op jit(solution)/shard_map/pallas_call | solution.py:140
  2.1 6.0 %collective-permute-start.14 = (bf16[256,256]{1,0:T(8,128)(2,1)S(1)}, bf16[256,256]{1,0:T(8,128)(2,1)S(1)}, u32[]{:S(2)}, u32[]{:S(2)}) collective-permute-start(bf16[256,256]{1,0:T(8,128)(2,1)S(1)} %get-tuple-element.23), channel_id=1, source_target_pairs={{0,28},{4,24},{8,20},{12,16},{16,12},{20,8},{24,4},{28,0},{1,29},{... | collective-permute-start | bytes 393224 | tf_op jit(solution)/shard_map/ppermute | solution.py:395
  8.2 0.2 collective-permute-start.12
  8.4 0.4 collective-permute-start.2
  8.8 1.8 %collective-permute-start.10 = (bf16[256,256]{1,0:T(8,128)(2,1)S(1)}, bf16[256,256]{1,0:T(8,128)(2,1)S(1)}, u32[]{:S(2)}, u32[]{:S(2)}) collective-permute-start(bf16[256,256]{1,0:T(8,128)(2,1)S(1)} %get-tuple-element.21), channel_id=1, source_target_pairs={{0,20},{4,16},{8,28},{12,24},{16,4},{20,0},{24,12},{28,8},{1,21},{... | collective-permute-start | bytes 393224 | tf_op jit(solution)/shard_map/ppermute | solution.py:395
  10.6 2.5 %shard_map.95 = (f32[8,128]{1,0:T(8,128)S(1)}, f32[8,128]{1,0:T(8,128)S(1)}) custom-call(bf16[1,8,256,256]{3,2,1,0:T(8,128)(2,1)} %grad_hbm.3, f32[1,8,256,256]{3,2,1,0:T(8,128)} %moment_hbm.1), custom_call_target="tpu_custom_call" | custom-call | flops 4194304 | bytes 3145728 | tf_op jit(solution)/shard_map/pallas_call | solution.py:191
  13.2 0.1 collective-permute-start
  13.3 1.2 %collective-permute-done = f32[8,128]{1,0:T(8,128)S(1)} collective-permute-done((f32[8,128]{1,0:T(8,128)S(1)}, f32[8,128]{1,0:T(8,128)S(1)}, u32[]{:S(2)}, u32[]{:S(2)}) %collective-permute-start) | collective-permute-done | bytes 4128 | tf_op jit(solution)/shard_map/ppermute | solution.py:401
  14.4 1.5 %collective-permute-start.1 = (f32[8,128]{1,0:T(8,128)S(1)}, f32[8,128]{1,0:T(8,128)S(1)}, u32[]{:S(2)}, u32[]{:S(2)}) collective-permute-start(f32[8,128]{1,0:T(8,128)S(1)} %add.6), channel_id=1, source_target_pairs={{0,2},{1,3},{2,0},{3,1},{4,6},{5,7},{6,4},{7,5},{8,10},{9,11},{10,... | collective-permute-start | bytes 12296 | tf_op jit(solution)/shard_map/ppermute | solution.py:401
  15.9 2.1 %collective-permute-done.1 = f32[8,128]{1,0:T(8,128)S(1)} collective-permute-done((f32[8,128]{1,0:T(8,128)S(1)}, f32[8,128]{1,0:T(8,128)S(1)}, u32[]{:S(2)}, u32[]{:S(2)}) %collective-permute-start.1) | collective-permute-done | bytes 4128 | tf_op jit(solution)/shard_map/ppermute | solution.py:401
  18.0 2.1 %collective-permute-start.6 = (bf16[256,256]{1,0:T(8,128)(2,1)S(1)}, bf16[256,256]{1,0:T(8,128)(2,1)S(1)}, u32[]{:S(2)}, u32[]{:S(2)}) collective-permute-start(bf16[256,256]{1,0:T(8,128)(2,1)S(1)} %get-tuple-element.19), channel_id=1, source_target_pairs={{0,16},{4,20},{8,12},{12,8},{16,0},{20,4},{24,28},{28,24},{1,17},{... | collective-permute-start | bytes 393224 | tf_op jit(solution)/shard_map/ppermute | solution.py:395
  20.2 0.1 shard_map.96.tail_ref.refs_9_
  20.3 0.0 collective-permute-done.14.grad_ref.refs_7_
  20.3 4.1 %collective-permute-start.8 = (bf16[256,256]{1,0:T(8,128)(2,1)S(1)}, bf16[256,256]{1,0:T(8,128)(2,1)S(1)}, u32[]{:S(2)}, u32[]{:S(2)}) collective-permute-start(bf16[256,256]{1,0:T(8,128)(2,1)S(1)} %get-tuple-element.20), channel_id=1, source_target_pairs={{0,12},{4,8},{8,4},{12,0},{16,28},{20,24},{24,20},{28,16},{1,13},{... | collective-permute-start | bytes 393224 | tf_op jit(solution)/shard_map/ppermute | solution.py:395
  24.4 0.3 shard_map.104
  24.8 0.0 collective-permute-done.12.grad_ref.refs_6_
  24.8 0.5 collective-permute-start.15
  25.3 0.3 shard_map.103
  25.6 0.0 collective-permute-done.2.grad_ref.refs_1_
  25.6 8.8 %collective-permute-start.13 = (bf16[272,256]{1,0:T(8,128)(2,1)S(1)}, bf16[272,256]{1,0:T(8,128)(2,1)S(1)}, u32[]{:S(2)}, u32[]{:S(2)}) collective-permute-start(bf16[272,256]{1,0:T(8,128)(2,1)S(1)} %shard_map.103), channel_id=1, source_target_pairs={{0,24},{4,28},{8,16},{12,20},{16,8},{20,12},{24,0},{28,4},{1,25},{... | collective-permute-start | bytes 417800 | tf_op jit(solution)/shard_map/ppermute | solution.py:395
  34.4 0.0 collective-permute-done.10.grad_ref.refs_5_
  34.4 1.4 %collective-permute-start.4 = (bf16[256,256]{1,0:T(8,128)(2,1)S(1)}, bf16[256,256]{1,0:T(8,128)(2,1)S(1)}, u32[]{:S(2)}, u32[]{:S(2)}) collective-permute-start(bf16[256,256]{1,0:T(8,128)(2,1)S(1)} %get-tuple-element.18), channel_id=1, source_target_pairs={{0,8},{4,12},{8,0},{12,4},{16,24},{20,28},{24,16},{28,20},{1,9},{5... | collective-permute-start | bytes 393224 | tf_op jit(solution)/shard_map/ppermute | solution.py:395
  35.8 0.3 shard_map.98
  36.1 0.3 shard_map.102
  36.5 2.9 %collective-permute-done.8.grad_ref.refs_4_ = bf16[256,256]{1,0:T(8,128)(2,1)S(1)} collective-permute-done((bf16[256,256]{1,0:T(8,128)(2,1)S(1)}, bf16[256,256]{1,0:T(8,128)(2,1)S(1)}, u32[]{:S(2)}, u32[]{:S(2)}) %collective-permute-start.8) | collective-permute-done | bytes 131104 | tf_op jit(solution)/shard_map/ppermute | solution.py:395
  39.4 1.5 %collective-permute-start.11 = (bf16[272,256]{1,0:T(8,128)(2,1)S(1)}, bf16[272,256]{1,0:T(8,128)(2,1)S(1)}, u32[]{:S(2)}, u32[]{:S(2)}) collective-permute-start(bf16[272,256]{1,0:T(8,128)(2,1)S(1)} %shard_map.102), channel_id=1, source_target_pairs={{0,20},{4,16},{8,28},{12,24},{16,4},{20,0},{24,12},{28,8},{1,21},{... | collective-permute-start | bytes 417800 | tf_op jit(solution)/shard_map/ppermute | solution.py:395
  40.8 0.3 shard_map.101
  41.2 0.0 collective-permute-done.6.grad_ref.refs_3_
  41.2 0.1 collective-permute-start.9
  41.3 0.3 shard_map.100
  41.6 0.0 copy-start.2
  41.6 0.0 copy-start.3
  41.6 0.0 collective-permute-done.4.grad_ref.refs_2_
  41.6 1.9 %collective-permute-start.7 = (bf16[272,256]{1,0:T(8,128)(2,1)S(1)}, bf16[272,256]{1,0:T(8,128)(2,1)S(1)}, u32[]{:S(2)}, u32[]{:S(2)}) collective-permute-start(bf16[272,256]{1,0:T(8,128)(2,1)S(1)} %shard_map.100), channel_id=1, source_target_pairs={{0,16},{4,20},{8,12},{12,8},{16,0},{20,4},{24,28},{28,24},{1,17},{... | collective-permute-start | bytes 417800 | tf_op jit(solution)/shard_map/ppermute | solution.py:395
  43.5 0.3 shard_map.99
  43.8 0.0 collective-permute-done.15.refs_7_
  43.8 1.8 %collective-permute-start.5 = (bf16[272,256]{1,0:T(8,128)(2,1)S(1)}, bf16[272,256]{1,0:T(8,128)(2,1)S(1)}, u32[]{:S(2)}, u32[]{:S(2)}) collective-permute-start(bf16[272,256]{1,0:T(8,128)(2,1)S(1)} %shard_map.99), channel_id=1, source_target_pairs={{0,8},{4,12},{8,0},{12,4},{16,24},{20,28},{24,16},{28,20},{1,9},{5... | collective-permute-start | bytes 417800 | tf_op jit(solution)/shard_map/ppermute | solution.py:395
  45.6 0.0 collective-permute-done.13.refs_6_
  45.6 0.5 collective-permute-start.3
  46.1 0.3 shard_map.97.refs_0_
  46.5 0.0 copy-start.4
  46.5 4.7 %shard_map.106 = (f32[1,8,256,256]{3,2,1,0:T(8,128)}, f32[1,8,256,256]{3,2,1,0:T(8,128)}) custom-call(s32[1]{0:T(128)} %bitcast.1.me_ref, bf16[256,256]{1,0:T(8,128)(2,1)S(1)} %get-tuple-element.15.grad_ref.refs_0_, bf16[256,256]{1,0:T(8,128)(2,1)S(1)} %collective-permute-done.2.grad_ref.refs_1_, ...), custom_call_target="tpu_custom_call" | custom-call | flops 536870912 | bytes 9437184 | tf_op jit(solution)/shard_map/pallas_call | solution.py:302
  51.2 0.0 collective-permute-done.11.refs_5_
  51.2 0.0 collective-permute-done.9.refs_4_
  51.2 3.2 %collective-permute-done.7.refs_3_ = bf16[272,256]{1,0:T(8,128)(2,1)S(1)} collective-permute-done((bf16[272,256]{1,0:T(8,128)(2,1)S(1)}, bf16[272,256]{1,0:T(8,128)(2,1)S(1)}, u32[]{:S(2)}, u32[]{:S(2)}) %collective-permute-start.7) | collective-permute-done | bytes 139296 | tf_op jit(solution)/shard_map/ppermute | solution.py:395
  54.4 0.0 collective-permute-done.5.refs_2_
  54.4 0.0 collective-permute-done.3.refs_1_
  54.4 1.8 %shard_map.105 = bf16[1,8,256,256]{3,2,1,0:T(8,128)(2,1)} custom-call(s32[64]{0:T(128)S(1)} %bitcast.3, s32[1]{0:T(128)} %bitcast.1.me_ref, bf16[256,256]{1,0:T(8,128)(2,1)S(1)} %shard_map.97.refs_0_, bf16[272,256]{1,0:T(8,128)(2,1)S(1)} %collective-permute-done.3.refs_1_, bf16[272,256]{1,0:T(8,128)(2,1)S(1)} %collective-permute-done.5.refs_2_, ...), custom_call_target="tpu_custom_call" | custom-call | flops 3145728 | bytes 2097152 | tf_op jit(solution)/shard_map/pallas_call | solution.py:358
  (9 shorter events, 0.0 us)
Async XLA Ops:
  0.6 23.8 %copy-start = (bf16[1,8,256,256]{3,2,1,0:T(8,128)(2,1)S(1)}, bf16[1,8,256,256]{3,2,1,0:T(8,128)(2,1)}, u32[]{:S(2)}) copy-start(bf16[1,8,256,256]{3,2,1,0:T(8,128)(2,1)} %left_ref.15) | copy-start | bytes 3145732
  0.6 23.8 %copy-start.1 = (bf16[1,8,256,256]{3,2,1,0:T(8,128)(2,1)S(1)}, bf16[1,8,256,256]{3,2,1,0:T(8,128)(2,1)}, u32[]{:S(2)}) copy-start(bf16[1,8,256,256]{3,2,1,0:T(8,128)(2,1)} %right_ref.15) | copy-start | bytes 3145732
  2.1 18.2 %collective-permute-start.14 = (bf16[256,256]{1,0:T(8,128)(2,1)S(1)}, bf16[256,256]{1,0:T(8,128)(2,1)S(1)}, u32[]{:S(2)}, u32[]{:S(2)}) collective-permute-start(bf16[256,256]{1,0:T(8,128)(2,1)S(1)} %get-tuple-element.23), channel_id=1, source_target_pairs={{0,28},{4,24},{8,20},{12,16},{16,12},{20,8},{24,4},{28,0},{1,29},{... | collective-permute-start | bytes 393224 | tf_op jit(solution)/shard_map/ppermute | solution.py:395
  8.2 16.6 %collective-permute-start.12 = (bf16[256,256]{1,0:T(8,128)(2,1)S(1)}, bf16[256,256]{1,0:T(8,128)(2,1)S(1)}, u32[]{:S(2)}, u32[]{:S(2)}) collective-permute-start(bf16[256,256]{1,0:T(8,128)(2,1)S(1)} %get-tuple-element.22), channel_id=1, source_target_pairs={{0,24},{4,28},{8,16},{12,20},{16,8},{20,12},{24,0},{28,4},{1,25},{... | collective-permute-start | bytes 393224 | tf_op jit(solution)/shard_map/ppermute | solution.py:395
  8.4 17.2 %collective-permute-start.2 = (bf16[256,256]{1,0:T(8,128)(2,1)S(1)}, bf16[256,256]{1,0:T(8,128)(2,1)S(1)}, u32[]{:S(2)}, u32[]{:S(2)}) collective-permute-start(bf16[256,256]{1,0:T(8,128)(2,1)S(1)} %get-tuple-element.17), channel_id=1, source_target_pairs={{0,4},{4,0},{8,24},{12,28},{16,20},{20,16},{24,8},{28,12},{1,5},{5... | collective-permute-start | bytes 393224 | tf_op jit(solution)/shard_map/ppermute | solution.py:395
  8.8 25.6 %collective-permute-start.10 = (bf16[256,256]{1,0:T(8,128)(2,1)S(1)}, bf16[256,256]{1,0:T(8,128)(2,1)S(1)}, u32[]{:S(2)}, u32[]{:S(2)}) collective-permute-start(bf16[256,256]{1,0:T(8,128)(2,1)S(1)} %get-tuple-element.21), channel_id=1, source_target_pairs={{0,20},{4,16},{8,28},{12,24},{16,4},{20,0},{24,12},{28,8},{1,21},{... | collective-permute-start | bytes 393224 | tf_op jit(solution)/shard_map/ppermute | solution.py:395
  13.2 1.2 %collective-permute-start = (f32[8,128]{1,0:T(8,128)S(1)}, f32[8,128]{1,0:T(8,128)S(1)}, u32[]{:S(2)}, u32[]{:S(2)}) collective-permute-start(f32[8,128]{1,0:T(8,128)S(1)} %get-tuple-element.16), channel_id=1, source_target_pairs={{0,1},{1,0},{2,3},{3,2},{4,5},{5,4},{6,7},{7,6},{8,9},{9,8},{10,11... | collective-permute-start | bytes 12296 | tf_op jit(solution)/shard_map/ppermute | solution.py:401
  14.4 3.6 %collective-permute-start.1 = (f32[8,128]{1,0:T(8,128)S(1)}, f32[8,128]{1,0:T(8,128)S(1)}, u32[]{:S(2)}, u32[]{:S(2)}) collective-permute-start(f32[8,128]{1,0:T(8,128)S(1)} %add.6), channel_id=1, source_target_pairs={{0,2},{1,3},{2,0},{3,1},{4,6},{5,7},{6,4},{7,5},{8,10},{9,11},{10,... | collective-permute-start | bytes 12296 | tf_op jit(solution)/shard_map/ppermute | solution.py:401
  18.0 23.1 %collective-permute-start.6 = (bf16[256,256]{1,0:T(8,128)(2,1)S(1)}, bf16[256,256]{1,0:T(8,128)(2,1)S(1)}, u32[]{:S(2)}, u32[]{:S(2)}) collective-permute-start(bf16[256,256]{1,0:T(8,128)(2,1)S(1)} %get-tuple-element.19), channel_id=1, source_target_pairs={{0,16},{4,20},{8,12},{12,8},{16,0},{20,4},{24,28},{28,24},{1,17},{... | collective-permute-start | bytes 393224 | tf_op jit(solution)/shard_map/ppermute | solution.py:395
  20.3 19.1 %collective-permute-start.8 = (bf16[256,256]{1,0:T(8,128)(2,1)S(1)}, bf16[256,256]{1,0:T(8,128)(2,1)S(1)}, u32[]{:S(2)}, u32[]{:S(2)}) collective-permute-start(bf16[256,256]{1,0:T(8,128)(2,1)S(1)} %get-tuple-element.20), channel_id=1, source_target_pairs={{0,12},{4,8},{8,4},{12,0},{16,28},{20,24},{24,20},{28,16},{1,13},{... | collective-permute-start | bytes 393224 | tf_op jit(solution)/shard_map/ppermute | solution.py:395
  24.8 19.1 %collective-permute-start.15 = (bf16[272,256]{1,0:T(8,128)(2,1)S(1)}, bf16[272,256]{1,0:T(8,128)(2,1)S(1)}, u32[]{:S(2)}, u32[]{:S(2)}) collective-permute-start(bf16[272,256]{1,0:T(8,128)(2,1)S(1)} %shard_map.104), channel_id=1, source_target_pairs={{0,28},{4,24},{8,20},{12,16},{16,12},{20,8},{24,4},{28,0},{1,29},{... | collective-permute-start | bytes 417800 | tf_op jit(solution)/shard_map/ppermute | solution.py:395
  25.6 20.0 %collective-permute-start.13 = (bf16[272,256]{1,0:T(8,128)(2,1)S(1)}, bf16[272,256]{1,0:T(8,128)(2,1)S(1)}, u32[]{:S(2)}, u32[]{:S(2)}) collective-permute-start(bf16[272,256]{1,0:T(8,128)(2,1)S(1)} %shard_map.103), channel_id=1, source_target_pairs={{0,24},{4,28},{8,16},{12,20},{16,8},{20,12},{24,0},{28,4},{1,25},{... | collective-permute-start | bytes 417800 | tf_op jit(solution)/shard_map/ppermute | solution.py:395
  34.4 7.3 %collective-permute-start.4 = (bf16[256,256]{1,0:T(8,128)(2,1)S(1)}, bf16[256,256]{1,0:T(8,128)(2,1)S(1)}, u32[]{:S(2)}, u32[]{:S(2)}) collective-permute-start(bf16[256,256]{1,0:T(8,128)(2,1)S(1)} %get-tuple-element.18), channel_id=1, source_target_pairs={{0,8},{4,12},{8,0},{12,4},{16,24},{20,28},{24,16},{28,20},{1,9},{5... | collective-permute-start | bytes 393224 | tf_op jit(solution)/shard_map/ppermute | solution.py:395
  39.4 11.9 %collective-permute-start.11 = (bf16[272,256]{1,0:T(8,128)(2,1)S(1)}, bf16[272,256]{1,0:T(8,128)(2,1)S(1)}, u32[]{:S(2)}, u32[]{:S(2)}) collective-permute-start(bf16[272,256]{1,0:T(8,128)(2,1)S(1)} %shard_map.102), channel_id=1, source_target_pairs={{0,20},{4,16},{8,28},{12,24},{16,4},{20,0},{24,12},{28,8},{1,21},{... | collective-permute-start | bytes 417800 | tf_op jit(solution)/shard_map/ppermute | solution.py:395
  41.2 10.1 %collective-permute-start.9 = (bf16[272,256]{1,0:T(8,128)(2,1)S(1)}, bf16[272,256]{1,0:T(8,128)(2,1)S(1)}, u32[]{:S(2)}, u32[]{:S(2)}) collective-permute-start(bf16[272,256]{1,0:T(8,128)(2,1)S(1)} %shard_map.101), channel_id=1, source_target_pairs={{0,12},{4,8},{8,4},{12,0},{16,28},{20,24},{24,20},{28,16},{1,13},{... | collective-permute-start | bytes 417800 | tf_op jit(solution)/shard_map/ppermute | solution.py:395
  41.6 4.9 %copy-start.2 = (f32[1,8,256,256]{3,2,1,0:T(8,128)S(1)}, f32[1,8,256,256]{3,2,1,0:T(8,128)}, u32[]{:S(2)}) copy-start(f32[1,8,256,256]{3,2,1,0:T(8,128)} %refs_8_.1) | copy-start | bytes 6291460
  41.6 4.9 %copy-start.3 = (f32[1,8,256,256]{3,2,1,0:T(8,128)S(1)}, f32[1,8,256,256]{3,2,1,0:T(8,128)}, u32[]{:S(2)}) copy-start(f32[1,8,256,256]{3,2,1,0:T(8,128)} %refs_9_.1) | copy-start | bytes 6291460
  41.6 12.8 %collective-permute-start.7 = (bf16[272,256]{1,0:T(8,128)(2,1)S(1)}, bf16[272,256]{1,0:T(8,128)(2,1)S(1)}, u32[]{:S(2)}, u32[]{:S(2)}) collective-permute-start(bf16[272,256]{1,0:T(8,128)(2,1)S(1)} %shard_map.100), channel_id=1, source_target_pairs={{0,16},{4,20},{8,12},{12,8},{16,0},{20,4},{24,28},{28,24},{1,17},{... | collective-permute-start | bytes 417800 | tf_op jit(solution)/shard_map/ppermute | solution.py:395
  43.8 10.6 %collective-permute-start.5 = (bf16[272,256]{1,0:T(8,128)(2,1)S(1)}, bf16[272,256]{1,0:T(8,128)(2,1)S(1)}, u32[]{:S(2)}, u32[]{:S(2)}) collective-permute-start(bf16[272,256]{1,0:T(8,128)(2,1)S(1)} %shard_map.99), channel_id=1, source_target_pairs={{0,8},{4,12},{8,0},{12,4},{16,24},{20,28},{24,16},{28,20},{1,9},{5... | collective-permute-start | bytes 417800 | tf_op jit(solution)/shard_map/ppermute | solution.py:395
  45.6 8.8 %collective-permute-start.3 = (bf16[272,256]{1,0:T(8,128)(2,1)S(1)}, bf16[272,256]{1,0:T(8,128)(2,1)S(1)}, u32[]{:S(2)}, u32[]{:S(2)}) collective-permute-start(bf16[272,256]{1,0:T(8,128)(2,1)S(1)} %shard_map.98), channel_id=1, source_target_pairs={{0,4},{4,0},{8,24},{12,28},{16,20},{20,16},{24,8},{28,12},{1,5},{5... | collective-permute-start | bytes 417800 | tf_op jit(solution)/shard_map/ppermute | solution.py:395
  46.5 7.9 %copy-start.4 = (s32[1,64,1]{1,2,0:T(1,128)S(1)}, s32[1,64,1]{1,2,0:T(1,128)}, u32[]{:S(2)}) copy-start(s32[1,64,1]{1,2,0:T(1,128)} %param.9) | copy-start | bytes 772

commit v9 on v8

--- a/solution.py
+++ b/solution.py
@@ -100,14 +100,18 @@
 
 def partner_tables(count):
     half = count // 2
-    even = [0, 1, 2, half, 3, *range(half + 1, count)]
+    even = [*range(half - 1), half, half - 1, *range(half + 1, count)]
     odd = [{1: half, half: 1}.get(m, m) for m in even]
     return even, odd
 
 
-def partner(me, step, count):
+def fsdp_index(who, layers):
+    return lax.shift_right_logical(who, jnp.int32(layers.bit_length() - 1))
+
+
+def partner(who, step, count):
     even, odd = partner_tables(count)
-    return jnp.where(me & 2 == 2, jnp.int32(odd[step]), jnp.int32(even[step]))
+    return jnp.where(who & 1 == 1, jnp.int32(odd[step]), jnp.int32(even[step]))
 
 
 def home_slot(named, target):
@@ -117,28 +121,29 @@
     return block
 
 
-def route_kernel(owners_hbm, me_ref, grad_hbm, *refs):
+def route_kernel(layers, owners_hbm, who_ref, grad_hbm, *refs):
     outs, (owners_ref, held, owner_sem, grad_sem) = refs[:-4], refs[-4:]
     count = held.shape[0]
-    me = me_ref[0]
+    who = who_ref[0]
+    me = fsdp_index(who, layers)
     fetch_owners = pltpu.make_async_copy(owners_hbm, owners_ref, owner_sem)
     fetch_grads = pltpu.make_async_copy(grad_hbm.at[0], held, grad_sem)
     fetch_owners.start()
     fetch_grads.start()
     fetch_owners.wait()
     named = [owners_ref[me * count + j] for j in range(count)]
-    blocks = [home_slot(named, me ^ partner(me, step, count)) for step in range(count)]
+    blocks = [home_slot(named, me ^ partner(who, step, count)) for step in range(count)]
     fetch_grads.wait()
     for block, out in zip(blocks, outs):
         out[...] = held[block]
 
 
-def route(owner_list, me, gradients):
+def route(layers, owner_list, who, gradients):
     count, side = gradients.shape[1], gradients.shape[3]
     hbm = pl.BlockSpec(memory_space=pltpu.HBM)
     piece = jax.ShapeDtypeStruct((side, side), gradients.dtype)
     return pl.pallas_call(
-        route_kernel,
+        functools.partial(route_kernel, layers),
         in_specs=[hbm, pl.BlockSpec(memory_space=pltpu.SMEM), hbm],
         out_specs=[pl.BlockSpec(memory_space=pltpu.VMEM)] * count,
         scratch_shapes=[
@@ -154,7 +159,7 @@
         ),
     )(
         pltpu.with_memory_space_constraint(owner_list, pltpu.HBM),
-        me,
+        who,
         pltpu.with_memory_space_constraint(gradients, pltpu.HBM),
     )
 
@@ -235,10 +240,10 @@
     )(total)
 
 
-def precondition_kernel(step, me_ref, grad_ref, left_ref, right_ref, tail_ref, out_ref):
+def precondition_kernel(step, layers, who_ref, grad_ref, left_ref, right_ref, tail_ref, out_ref):
     side = grad_ref.shape[0]
-    me = me_ref[0]
-    slot = me ^ partner(me, step, left_ref.shape[1])
+    who = who_ref[0]
+    slot = fsdp_index(who, layers) ^ partner(who, step, left_ref.shape[1])
     half_done = jnp.dot(
         left_ref[0, slot], grad_ref[...], preferred_element_type=jnp.float32
     ).astype(jnp.bfloat16)
@@ -249,10 +254,10 @@
         out_ref[side:, :] = tail_ref[...]
 
 
-def precondition(step, me, block, left_root, right_root, tail):
+def precondition(step, layers, who, block, left_root, right_root, tail):
     side = block.shape[0]
     return pl.pallas_call(
-        functools.partial(precondition_kernel, step),
+        functools.partial(precondition_kernel, step, layers),
         grid_spec=pltpu.PrefetchScalarGridSpec(
             num_scalar_prefetch=1,
             grid=(),
@@ -264,10 +269,10 @@
         cost_estimate=pl.CostEstimate(
             flops=4 * side**3, bytes_accessed=8 * side * side, transcendentals=0
         ),
-    )(me, block, left_root, right_root, tail)
-
-
-def gram_kernel(me_ref, *refs):
+    )(who, block, left_root, right_root, tail)
+
+
+def gram_kernel(who_ref, *refs):
     count = len(refs) - 4
     grads = refs[:count]
     left_ref, right_ref, new_left_ref, new_right_ref = refs[count:]
@@ -287,15 +292,15 @@
             new_right_ref[0, 0] = DECAY_RATE * right_ref[0, 0] + (1.0 - DECAY_RATE) * gram_right
 
 
-def gram_update(me, blocks, left_stats, right_stats):
+def gram_update(layers, who, blocks, left_stats, right_stats):
     count, side = len(blocks), blocks[0].shape[0]
 
-    def slot(i, me_ref):
-        me = me_ref[0]
+    def slot(i, who_ref):
+        who = who_ref[0]
         m = jnp.int32(0)
         for step in range(1, count):
-            m = jnp.where(i == step, partner(me, step, count), m)
-        return (0, me ^ m, 0, 0)
+            m = jnp.where(i == step, partner(who, step, count), m)
+        return (0, fsdp_index(who, layers) ^ m, 0, 0)
 
     stat = pl.BlockSpec((1, 1, side, side), slot)
     whole = pl.BlockSpec(memory_space=pltpu.VMEM)
@@ -315,17 +320,18 @@
         cost_estimate=pl.CostEstimate(
             flops=4 * count * side**3, bytes_accessed=18 * count * side * side, transcendentals=0
         ),
-    )(me, *blocks, left_stats, right_stats)
-
-
-def finish_kernel(entries, owners_ref, me_ref, *refs):
+    )(who, *blocks, left_stats, right_stats)
+
+
+def finish_kernel(layers, entries, owners_ref, who_ref, *refs):
     count = len(refs) - 6
     pieces = refs[:count]
     squares_ref, tail_ref, out_ref, held, sums, sems = refs[count:]
     side, lanes = out_ref.shape[3], squares_ref.shape[1]
-    me = me_ref[0]
+    who = who_ref[0]
+    me = fsdp_index(who, layers)
     named = [owners_ref[me * count + j] for j in range(count)]
-    blocks = [home_slot(named, me ^ partner(me, step, count)) for step in range(count)]
+    blocks = [home_slot(named, me ^ partner(who, step, count)) for step in range(count)]
     global_sq = jnp.zeros((1, 1), jnp.float32)
     for rows in [tail_ref[...]] + [piece[side:, :] for piece in pieces if piece.shape[0] > side]:
         terms = rows[:, 0:1].astype(jnp.float32)
@@ -353,10 +359,10 @@
         copy.wait()
 
 
-def finish(owner_list, me, pieces, squares, tail, entries):
+def finish(layers, owner_list, who, pieces, squares, tail, entries):
     count, side = len(pieces), pieces[0].shape[1]
     return pl.pallas_call(
-        functools.partial(finish_kernel, entries),
+        functools.partial(finish_kernel, layers, entries),
         grid_spec=pltpu.PrefetchScalarGridSpec(
             num_scalar_prefetch=2,
             grid=(),
@@ -373,7 +379,7 @@
         cost_estimate=pl.CostEstimate(
             flops=6 * count * side * side, bytes_accessed=4 * count * side * side, transcendentals=0
         ),
-    )(owner_list, me, *pieces, squares, tail)
+    )(owner_list, who, *pieces, squares, tail)
 
 
 def doublings(size):
@@ -385,16 +391,21 @@
 ):
     count, layers = lax.axis_size("fsdp"), lax.axis_size("layer")
     side = gradients.shape[3]
-    me = lax.axis_index("fsdp").astype(jnp.int32).reshape(1)
+    who = lax.axis_index(("fsdp", "layer")).astype(jnp.int32).reshape(1)
     owner_list = owners[0, :, 0]
     tables = partner_tables(count)
 
     def swap(value, step):
         if step == 0:
             return value
-        return lax.ppermute(value, "fsdp", [(i, i ^ tables[i // 2 % 2][step]) for i in range(count)])
-
-    outgoing = route(owner_list, me, gradients)
+        pairs = [
+            (i * layers + k, (i ^ tables[k % 2][step]) * layers + k)
+            for i in range(count)
+            for k in range(layers)
+        ]
+        return lax.ppermute(value, ("fsdp", "layer"), pairs)
+
+    outgoing = route(layers, owner_list, who, gradients)
     received = [swap(block, step) for step, block in enumerate(outgoing)]
     squares, total = adam_squares(gradients, second_moment)
     for k in doublings(layers):
@@ -402,11 +413,11 @@
     tail = sum_tail(total, side)
     returned = []
     for step, block in enumerate(received):
-        done = precondition(step, me, block, left_root, right_root, tail)
+        done = precondition(step, layers, who, block, left_root, right_root, tail)
         returned.append(swap(done, step))
-    new_left, new_right = gram_update(me, received, left_stats, right_stats)
+    new_left, new_right = gram_update(layers, who, received, left_stats, right_stats)
     entries = float(owner_list.shape[0] * layers * side * side)
-    update = finish(owner_list, me, returned, squares, tail, entries)
+    update = finish(layers, owner_list, who, returned, squares, tail, entries)
     return (update, new_left, new_right)
 
 

time: 56.4 us -> 56.3 us (level)
  starting transfers between devices: 32.7 us -> 31.4 us
  waiting for transfers between devices: 9.32 us -> 10.6 us
    ppermute x14, starting transfers between devices: 31.1 us -> 29.8 us  [swap(): return lax.ppermute(value, ('fsdp', 'layer'), pairs)]
    ppermute x14, waiting for transfers between devices: 6.08 us -> 7.36 us  [swap(): return lax.ppermute(value, ('fsdp', 'layer'), pairs)]
  transfers between devices with their start and end apart: 16 -> 16, of which waited for: 4 -> 6; matrix products, arithmetic and copies ran while one was open for 0% -> 0% of each run, Pallas kernels for 18% -> 18%
where the time goes in v9:
time: 56.3 us; the launch traced here: 56.2 us
  starting transfers between devices  31.4 us (56%)
  Pallas kernels  13.3 us (24%)
  waiting for transfers between devices  10.6 us (19%)
  between operations  0.86 us (2%)
    ppermute x14, starting transfers between devices, swap(): return lax.ppermute(value, ('fsdp', 'layer'), pairs)  29.8 us
    ppermute x14, waiting for transfers between devices, swap(): return lax.ppermute(value, ('fsdp', 'layer'), pairs)  7.36 us
    pallas_call x1, Pallas kernels, gram_update(): pl.pallas_call(gram_kernel, grid_spec=pltpu.PrefetchScalarGridSpec(num_sc...  4.75 us
    ppermute x2, waiting for transfers between devices, per_device_exchange(): lax.ppermute(total, 'layer', [(i, i ^ k) for i in range(layers)])  3.24 us
    pallas_call x8, Pallas kernels, precondition(): pl.pallas_call(functools.partial(precondition_kernel, step, layers), grid...  2.63 us
    pallas_call x1, Pallas kernels, adam_squares(): pl.pallas_call(adam_kernel, in_specs=[hbm, hbm], out_specs=[pl.BlockSpec(...  2.53 us
    pallas_call x1, Pallas kernels, finish(): pl.pallas_call(functools.partial(finish_kernel, layers, entries), grid_sp...  1.81 us
    ppermute x2, starting transfers between devices, per_device_exchange(): lax.ppermute(total, 'layer', [(i, i ^ k) for i in range(layers)])  1.59 us
  transfers between devices with their start and end apart: 16, of which 6 were waited for; matrix products, arithmetic and copies ran while one was open for 0% of the time, Pallas kernels for 18%

profile of v9, /device:TPU:0, one launch (start us, length us, event | category | flops | bytes accessed | tf_op | source)
XLA Modules:
  0.0 56.2 jit_solution(12235107953443411047)
XLA Ops:
  0.7 1.5 %shard_map.94 = (bf16[256,256]{1,0:T(8,128)(2,1)S(1)}, bf16[256,256]{1,0:T(8,128)(2,1)S(1)}, bf16[256,256]{1,0:T(8,128)(2,1)S(1)}, bf16[256,256]{1,0:T(8,128)(2,...) custom-call(s32[64]{0:T(128)} %bitcast.2, ...), custom_call_target="tpu_custom_call" | custom-call | bytes 2097152 | tf_op jit(solution)/shard_map/pallas_call | solution.py:145
  2.1 6.0 %collective-permute-start.14 = (bf16[256,256]{1,0:T(8,128)(2,1)S(1)}, bf16[256,256]{1,0:T(8,128)(2,1)S(1)}, u32[]{:S(2)}, u32[]{:S(2)}) collective-permute-start(bf16[256,256]{1,0:T(8,128)(2,1)S(1)} %get-tuple-element.23), channel_id=1, source_target_pairs={{0,28},{1,29},{2,30},{3,31},{4,24},{5,25},{6,26},{7,27},{8,20},{9,... | collective-permute-start | bytes 393224 | tf_op jit(solution)/shard_map/ppermute | solution.py:406
  8.2 0.2 collective-permute-start.12
  8.4 0.4 collective-permute-start.2
  8.8 1.8 %collective-permute-start.10 = (bf16[256,256]{1,0:T(8,128)(2,1)S(1)}, bf16[256,256]{1,0:T(8,128)(2,1)S(1)}, u32[]{:S(2)}, u32[]{:S(2)}) collective-permute-start(bf16[256,256]{1,0:T(8,128)(2,1)S(1)} %get-tuple-element.21), channel_id=1, source_target_pairs={{0,20},{1,21},{2,22},{3,23},{4,16},{5,17},{6,18},{7,19},{8,28},{9,... | collective-permute-start | bytes 393224 | tf_op jit(solution)/shard_map/ppermute | solution.py:406
  10.6 2.5 %shard_map.95 = (f32[8,128]{1,0:T(8,128)S(1)}, f32[8,128]{1,0:T(8,128)S(1)}) custom-call(bf16[1,8,256,256]{3,2,1,0:T(8,128)(2,1)} %grad_hbm.3, f32[1,8,256,256]{3,2,1,0:T(8,128)} %moment_hbm.1), custom_call_target="tpu_custom_call" | custom-call | flops 4194304 | bytes 3145728 | tf_op jit(solution)/shard_map/pallas_call | solution.py:196
  13.2 0.1 collective-permute-start
  13.3 1.2 %collective-permute-done = f32[8,128]{1,0:T(8,128)S(1)} collective-permute-done((f32[8,128]{1,0:T(8,128)S(1)}, f32[8,128]{1,0:T(8,128)S(1)}, u32[]{:S(2)}, u32[]{:S(2)}) %collective-permute-start) | collective-permute-done | bytes 4128 | tf_op jit(solution)/shard_map/ppermute | solution.py:412
  14.4 1.5 %collective-permute-start.1 = (f32[8,128]{1,0:T(8,128)S(1)}, f32[8,128]{1,0:T(8,128)S(1)}, u32[]{:S(2)}, u32[]{:S(2)}) collective-permute-start(f32[8,128]{1,0:T(8,128)S(1)} %add.10), channel_id=1, source_target_pairs={{0,2},{1,3},{2,0},{3,1},{4,6},{5,7},{6,4},{7,5},{8,10},{9,11},{10,... | collective-permute-start | bytes 12296 | tf_op jit(solution)/shard_map/ppermute | solution.py:412
  15.9 2.1 %collective-permute-done.1 = f32[8,128]{1,0:T(8,128)S(1)} collective-permute-done((f32[8,128]{1,0:T(8,128)S(1)}, f32[8,128]{1,0:T(8,128)S(1)}, u32[]{:S(2)}, u32[]{:S(2)}) %collective-permute-start.1) | collective-permute-done | bytes 4128 | tf_op jit(solution)/shard_map/ppermute | solution.py:412
  18.0 2.1 %collective-permute-start.6 = (bf16[256,256]{1,0:T(8,128)(2,1)S(1)}, bf16[256,256]{1,0:T(8,128)(2,1)S(1)}, u32[]{:S(2)}, u32[]{:S(2)}) collective-permute-start(bf16[256,256]{1,0:T(8,128)(2,1)S(1)} %get-tuple-element.19), channel_id=1, source_target_pairs={{0,16},{1,5},{2,18},{3,7},{4,20},{5,1},{6,22},{7,3},{8,24},{9,13},... | collective-permute-start | bytes 393224 | tf_op jit(solution)/shard_map/ppermute | solution.py:406
  20.2 0.1 shard_map.96.tail_ref.refs_9_
  20.3 0.0 collective-permute-done.14.grad_ref.refs_7_
  20.3 2.7 %collective-permute-start.8 = (bf16[256,256]{1,0:T(8,128)(2,1)S(1)}, bf16[256,256]{1,0:T(8,128)(2,1)S(1)}, u32[]{:S(2)}, u32[]{:S(2)}) collective-permute-start(bf16[256,256]{1,0:T(8,128)(2,1)S(1)} %get-tuple-element.20), channel_id=1, source_target_pairs={{0,12},{1,13},{2,14},{3,15},{4,8},{5,9},{6,10},{7,11},{8,4},{9,5},... | collective-permute-start | bytes 393224 | tf_op jit(solution)/shard_map/ppermute | solution.py:406
  23.0 0.3 shard_map.104
  23.4 0.0 collective-permute-done.12.grad_ref.refs_6_
  23.4 2.9 %collective-permute-start.15 = (bf16[272,256]{1,0:T(8,128)(2,1)S(1)}, bf16[272,256]{1,0:T(8,128)(2,1)S(1)}, u32[]{:S(2)}, u32[]{:S(2)}) collective-permute-start(bf16[272,256]{1,0:T(8,128)(2,1)S(1)} %shard_map.104), channel_id=1, source_target_pairs={{0,28},{1,29},{2,30},{3,31},{4,24},{5,25},{6,26},{7,27},{8,20},{9,... | collective-permute-start | bytes 417800 | tf_op jit(solution)/shard_map/ppermute | solution.py:406
  26.2 0.3 shard_map.103
  26.6 0.0 collective-permute-done.2.grad_ref.refs_1_
  26.6 1.1 %collective-permute-start.13 = (bf16[272,256]{1,0:T(8,128)(2,1)S(1)}, bf16[272,256]{1,0:T(8,128)(2,1)S(1)}, u32[]{:S(2)}, u32[]{:S(2)}) collective-permute-start(bf16[272,256]{1,0:T(8,128)(2,1)S(1)} %shard_map.103), channel_id=1, source_target_pairs={{0,24},{1,25},{2,26},{3,27},{4,28},{5,29},{6,30},{7,31},{8,16},{9,... | collective-permute-start | bytes 417800 | tf_op jit(solution)/shard_map/ppermute | solution.py:406
  27.7 2.1 %collective-permute-done.10.grad_ref.refs_5_ = bf16[256,256]{1,0:T(8,128)(2,1)S(1)} collective-permute-done((bf16[256,256]{1,0:T(8,128)(2,1)S(1)}, bf16[256,256]{1,0:T(8,128)(2,1)S(1)}, u32[]{:S(2)}, u32[]{:S(2)}) %collective-permute-start.10) | collective-permute-done | bytes 131104 | tf_op jit(solution)/shard_map/ppermute | solution.py:406
  29.9 4.6 %collective-permute-start.4 = (bf16[256,256]{1,0:T(8,128)(2,1)S(1)}, bf16[256,256]{1,0:T(8,128)(2,1)S(1)}, u32[]{:S(2)}, u32[]{:S(2)}) collective-permute-start(bf16[256,256]{1,0:T(8,128)(2,1)S(1)} %get-tuple-element.18), channel_id=1, source_target_pairs={{0,8},{1,9},{2,10},{3,11},{4,12},{5,13},{6,14},{7,15},{8,0},{9,1},... | collective-permute-start | bytes 393224 | tf_op jit(solution)/shard_map/ppermute | solution.py:406
  34.4 0.3 shard_map.98
  34.8 0.3 shard_map.102
  35.1 1.6 %collective-permute-done.8.grad_ref.refs_4_ = bf16[256,256]{1,0:T(8,128)(2,1)S(1)} collective-permute-done((bf16[256,256]{1,0:T(8,128)(2,1)S(1)}, bf16[256,256]{1,0:T(8,128)(2,1)S(1)}, u32[]{:S(2)}, u32[]{:S(2)}) %collective-permute-start.8) | collective-permute-done | bytes 131104 | tf_op jit(solution)/shard_map/ppermute | solution.py:406
  36.7 2.8 %collective-permute-start.11 = (bf16[272,256]{1,0:T(8,128)(2,1)S(1)}, bf16[272,256]{1,0:T(8,128)(2,1)S(1)}, u32[]{:S(2)}, u32[]{:S(2)}) collective-permute-start(bf16[272,256]{1,0:T(8,128)(2,1)S(1)} %shard_map.102), channel_id=1, source_target_pairs={{0,20},{1,21},{2,22},{3,23},{4,16},{5,17},{6,18},{7,19},{8,28},{9,... | collective-permute-start | bytes 417800 | tf_op jit(solution)/shard_map/ppermute | solution.py:406
  39.5 0.3 shard_map.101
  39.9 0.0 collective-permute-done.6.grad_ref.refs_3_
  39.9 2.2 %collective-permute-start.9 = (bf16[272,256]{1,0:T(8,128)(2,1)S(1)}, bf16[272,256]{1,0:T(8,128)(2,1)S(1)}, u32[]{:S(2)}, u32[]{:S(2)}) collective-permute-start(bf16[272,256]{1,0:T(8,128)(2,1)S(1)} %shard_map.101), channel_id=1, source_target_pairs={{0,12},{1,13},{2,14},{3,15},{4,8},{5,9},{6,10},{7,11},{8,4},{9,5},... | collective-permute-start | bytes 417800 | tf_op jit(solution)/shard_map/ppermute | solution.py:406
  42.1 0.3 shard_map.100
  42.4 0.0 copy-start.2
  42.5 0.0 copy-start.3
  42.5 0.0 collective-permute-done.4.grad_ref.refs_2_
  42.5 0.1 collective-permute-start.7
  42.6 0.3 shard_map.99
  42.9 0.0 collective-permute-done.15.refs_7_
  42.9 1.1 %collective-permute-start.5 = (bf16[272,256]{1,0:T(8,128)(2,1)S(1)}, bf16[272,256]{1,0:T(8,128)(2,1)S(1)}, u32[]{:S(2)}, u32[]{:S(2)}) collective-permute-start(bf16[272,256]{1,0:T(8,128)(2,1)S(1)} %shard_map.99), channel_id=1, source_target_pairs={{0,8},{1,9},{2,10},{3,11},{4,12},{5,13},{6,14},{7,15},{8,0},{9,1},... | collective-permute-start | bytes 417800 | tf_op jit(solution)/shard_map/ppermute | solution.py:406
  44.0 0.0 collective-permute-done.13.refs_6_
  44.0 1.7 %collective-permute-start.3 = (bf16[272,256]{1,0:T(8,128)(2,1)S(1)}, bf16[272,256]{1,0:T(8,128)(2,1)S(1)}, u32[]{:S(2)}, u32[]{:S(2)}) collective-permute-start(bf16[272,256]{1,0:T(8,128)(2,1)S(1)} %shard_map.98), channel_id=1, source_target_pairs={{0,4},{1,17},{2,6},{3,19},{4,0},{5,21},{6,2},{7,23},{8,12},{9,25},... | collective-permute-start | bytes 417800 | tf_op jit(solution)/shard_map/ppermute | solution.py:406
  45.6 0.3 shard_map.97.refs_0_
  46.0 0.0 copy-start.4
  46.0 4.7 %shard_map.106 = (f32[1,8,256,256]{3,2,1,0:T(8,128)}, f32[1,8,256,256]{3,2,1,0:T(8,128)}) custom-call(s32[1]{0:T(128)} %bitcast.1.who_ref, bf16[256,256]{1,0:T(8,128)(2,1)S(1)} %get-tuple-element.15.grad_ref.refs_0_, bf16[256,256]{1,0:T(8,128)(2,1)S(1)} %collective-permute-done.2.grad_ref.refs_1_, ...), custom_call_target="tpu_custom_call" | custom-call | flops 536870912 | bytes 9437184 | tf_op jit(solution)/shard_map/pallas_call | solution.py:307
  50.8 0.0 collective-permute-done.11.refs_5_
  50.8 1.0 %collective-permute-done.9.refs_4_ = bf16[272,256]{1,0:T(8,128)(2,1)S(1)} collective-permute-done((bf16[272,256]{1,0:T(8,128)(2,1)S(1)}, bf16[272,256]{1,0:T(8,128)(2,1)S(1)}, u32[]{:S(2)}, u32[]{:S(2)}) %collective-permute-start.9) | collective-permute-done | bytes 139296 | tf_op jit(solution)/shard_map/ppermute | solution.py:406
  51.8 2.6 %collective-permute-done.7.refs_3_ = bf16[272,256]{1,0:T(8,128)(2,1)S(1)} collective-permute-done((bf16[272,256]{1,0:T(8,128)(2,1)S(1)}, bf16[272,256]{1,0:T(8,128)(2,1)S(1)}, u32[]{:S(2)}, u32[]{:S(2)}) %collective-permute-start.7) | collective-permute-done | bytes 139296 | tf_op jit(solution)/shard_map/ppermute | solution.py:406
  54.4 0.0 collective-permute-done.5.refs_2_
  54.4 0.0 collective-permute-done.3.refs_1_
  54.4 1.8 %shard_map.105 = bf16[1,8,256,256]{3,2,1,0:T(8,128)(2,1)} custom-call(s32[64]{0:T(128)S(1)} %bitcast.3, s32[1]{0:T(128)} %bitcast.1.who_ref, bf16[256,256]{1,0:T(8,128)(2,1)S(1)} %shard_map.97.refs_0_, bf16[272,256]{1,0:T(8,128)(2,1)S(1)} %collective-permute-done.3.refs_1_, bf16[272,256]{1,0:T(8,128)(2,1)S(1)} %collective-permute-done.5.refs_2_, ...), custom_call_target="tpu_custom_call" | custom-call | flops 3145728 | bytes 2097152 | tf_op jit(solution)/shard_map/pallas_call | solution.py:364
  (9 shorter events, 0.0 us)
Async XLA Ops:
  0.6 22.4 %copy-start = (bf16[1,8,256,256]{3,2,1,0:T(8,128)(2,1)S(1)}, bf16[1,8,256,256]{3,2,1,0:T(8,128)(2,1)}, u32[]{:S(2)}) copy-start(bf16[1,8,256,256]{3,2,1,0:T(8,128)(2,1)} %left_ref.15) | copy-start | bytes 3145732
  0.6 22.4 %copy-start.1 = (bf16[1,8,256,256]{3,2,1,0:T(8,128)(2,1)S(1)}, bf16[1,8,256,256]{3,2,1,0:T(8,128)(2,1)}, u32[]{:S(2)}) copy-start(bf16[1,8,256,256]{3,2,1,0:T(8,128)(2,1)} %right_ref.15) | copy-start | bytes 3145732
  2.1 18.2 %collective-permute-start.14 = (bf16[256,256]{1,0:T(8,128)(2,1)S(1)}, bf16[256,256]{1,0:T(8,128)(2,1)S(1)}, u32[]{:S(2)}, u32[]{:S(2)}) collective-permute-start(bf16[256,256]{1,0:T(8,128)(2,1)S(1)} %get-tuple-element.23), channel_id=1, source_target_pairs={{0,28},{1,29},{2,30},{3,31},{4,24},{5,25},{6,26},{7,27},{8,20},{9,... | collective-permute-start | bytes 393224 | tf_op jit(solution)/shard_map/ppermute | solution.py:406
  8.2 15.2 %collective-permute-start.12 = (bf16[256,256]{1,0:T(8,128)(2,1)S(1)}, bf16[256,256]{1,0:T(8,128)(2,1)S(1)}, u32[]{:S(2)}, u32[]{:S(2)}) collective-permute-start(bf16[256,256]{1,0:T(8,128)(2,1)S(1)} %get-tuple-element.22), channel_id=1, source_target_pairs={{0,24},{1,25},{2,26},{3,27},{4,28},{5,29},{6,30},{7,31},{8,16},{9,... | collective-permute-start | bytes 393224 | tf_op jit(solution)/shard_map/ppermute | solution.py:406
  8.4 18.2 %collective-permute-start.2 = (bf16[256,256]{1,0:T(8,128)(2,1)S(1)}, bf16[256,256]{1,0:T(8,128)(2,1)S(1)}, u32[]{:S(2)}, u32[]{:S(2)}) collective-permute-start(bf16[256,256]{1,0:T(8,128)(2,1)S(1)} %get-tuple-element.17), channel_id=1, source_target_pairs={{0,4},{1,17},{2,6},{3,19},{4,0},{5,21},{6,2},{7,23},{8,12},{9,25},... | collective-permute-start | bytes 393224 | tf_op jit(solution)/shard_map/ppermute | solution.py:406
  8.8 21.0 %collective-permute-start.10 = (bf16[256,256]{1,0:T(8,128)(2,1)S(1)}, bf16[256,256]{1,0:T(8,128)(2,1)S(1)}, u32[]{:S(2)}, u32[]{:S(2)}) collective-permute-start(bf16[256,256]{1,0:T(8,128)(2,1)S(1)} %get-tuple-element.21), channel_id=1, source_target_pairs={{0,20},{1,21},{2,22},{3,23},{4,16},{5,17},{6,18},{7,19},{8,28},{9,... | collective-permute-start | bytes 393224 | tf_op jit(solution)/shard_map/ppermute | solution.py:406
  13.2 1.2 %collective-permute-start = (f32[8,128]{1,0:T(8,128)S(1)}, f32[8,128]{1,0:T(8,128)S(1)}, u32[]{:S(2)}, u32[]{:S(2)}) collective-permute-start(f32[8,128]{1,0:T(8,128)S(1)} %get-tuple-element.16), channel_id=1, source_target_pairs={{0,1},{1,0},{2,3},{3,2},{4,5},{5,4},{6,7},{7,6},{8,9},{9,8},{10,11... | collective-permute-start | bytes 12296 | tf_op jit(solution)/shard_map/ppermute | solution.py:412
  14.4 3.6 %collective-permute-start.1 = (f32[8,128]{1,0:T(8,128)S(1)}, f32[8,128]{1,0:T(8,128)S(1)}, u32[]{:S(2)}, u32[]{:S(2)}) collective-permute-start(f32[8,128]{1,0:T(8,128)S(1)} %add.10), channel_id=1, source_target_pairs={{0,2},{1,3},{2,0},{3,1},{4,6},{5,7},{6,4},{7,5},{8,10},{9,11},{10,... | collective-permute-start | bytes 12296 | tf_op jit(solution)/shard_map/ppermute | solution.py:412
  18.0 21.8 %collective-permute-start.6 = (bf16[256,256]{1,0:T(8,128)(2,1)S(1)}, bf16[256,256]{1,0:T(8,128)(2,1)S(1)}, u32[]{:S(2)}, u32[]{:S(2)}) collective-permute-start(bf16[256,256]{1,0:T(8,128)(2,1)S(1)} %get-tuple-element.19), channel_id=1, source_target_pairs={{0,16},{1,5},{2,18},{3,7},{4,20},{5,1},{6,22},{7,3},{8,24},{9,13},... | collective-permute-start | bytes 393224 | tf_op jit(solution)/shard_map/ppermute | solution.py:406
  20.3 16.4 %collective-permute-start.8 = (bf16[256,256]{1,0:T(8,128)(2,1)S(1)}, bf16[256,256]{1,0:T(8,128)(2,1)S(1)}, u32[]{:S(2)}, u32[]{:S(2)}) collective-permute-start(bf16[256,256]{1,0:T(8,128)(2,1)S(1)} %get-tuple-element.20), channel_id=1, source_target_pairs={{0,12},{1,13},{2,14},{3,15},{4,8},{5,9},{6,10},{7,11},{8,4},{9,5},... | collective-permute-start | bytes 393224 | tf_op jit(solution)/shard_map/ppermute | solution.py:406
  23.4 19.5 %collective-permute-start.15 = (bf16[272,256]{1,0:T(8,128)(2,1)S(1)}, bf16[272,256]{1,0:T(8,128)(2,1)S(1)}, u32[]{:S(2)}, u32[]{:S(2)}) collective-permute-start(bf16[272,256]{1,0:T(8,128)(2,1)S(1)} %shard_map.104), channel_id=1, source_target_pairs={{0,28},{1,29},{2,30},{3,31},{4,24},{5,25},{6,26},{7,27},{8,20},{9,... | collective-permute-start | bytes 417800 | tf_op jit(solution)/shard_map/ppermute | solution.py:406
  26.6 17.4 %collective-permute-start.13 = (bf16[272,256]{1,0:T(8,128)(2,1)S(1)}, bf16[272,256]{1,0:T(8,128)(2,1)S(1)}, u32[]{:S(2)}, u32[]{:S(2)}) collective-permute-start(bf16[272,256]{1,0:T(8,128)(2,1)S(1)} %shard_map.103), channel_id=1, source_target_pairs={{0,24},{1,25},{2,26},{3,27},{4,28},{5,29},{6,30},{7,31},{8,16},{9,... | collective-permute-start | bytes 417800 | tf_op jit(solution)/shard_map/ppermute | solution.py:406
  29.9 12.6 %collective-permute-start.4 = (bf16[256,256]{1,0:T(8,128)(2,1)S(1)}, bf16[256,256]{1,0:T(8,128)(2,1)S(1)}, u32[]{:S(2)}, u32[]{:S(2)}) collective-permute-start(bf16[256,256]{1,0:T(8,128)(2,1)S(1)} %get-tuple-element.18), channel_id=1, source_target_pairs={{0,8},{1,9},{2,10},{3,11},{4,12},{5,13},{6,14},{7,15},{8,0},{9,1},... | collective-permute-start | bytes 393224 | tf_op jit(solution)/shard_map/ppermute | solution.py:406
  36.7 14.0 %collective-permute-start.11 = (bf16[272,256]{1,0:T(8,128)(2,1)S(1)}, bf16[272,256]{1,0:T(8,128)(2,1)S(1)}, u32[]{:S(2)}, u32[]{:S(2)}) collective-permute-start(bf16[272,256]{1,0:T(8,128)(2,1)S(1)} %shard_map.102), channel_id=1, source_target_pairs={{0,20},{1,21},{2,22},{3,23},{4,16},{5,17},{6,18},{7,19},{8,28},{9,... | collective-permute-start | bytes 417800 | tf_op jit(solution)/shard_map/ppermute | solution.py:406
  39.9 11.9 %collective-permute-start.9 = (bf16[272,256]{1,0:T(8,128)(2,1)S(1)}, bf16[272,256]{1,0:T(8,128)(2,1)S(1)}, u32[]{:S(2)}, u32[]{:S(2)}) collective-permute-start(bf16[272,256]{1,0:T(8,128)(2,1)S(1)} %shard_map.101), channel_id=1, source_target_pairs={{0,12},{1,13},{2,14},{3,15},{4,8},{5,9},{6,10},{7,11},{8,4},{9,5},... | collective-permute-start | bytes 417800 | tf_op jit(solution)/shard_map/ppermute | solution.py:406
  42.4 3.5 %copy-start.2 = (f32[1,8,256,256]{3,2,1,0:T(8,128)S(1)}, f32[1,8,256,256]{3,2,1,0:T(8,128)}, u32[]{:S(2)}) copy-start(f32[1,8,256,256]{3,2,1,0:T(8,128)} %refs_8_.1) | copy-start | bytes 6291460
  42.5 3.5 %copy-start.3 = (f32[1,8,256,256]{3,2,1,0:T(8,128)S(1)}, f32[1,8,256,256]{3,2,1,0:T(8,128)}, u32[]{:S(2)}) copy-start(f32[1,8,256,256]{3,2,1,0:T(8,128)} %refs_9_.1) | copy-start | bytes 6291460
  42.5 11.9 %collective-permute-start.7 = (bf16[272,256]{1,0:T(8,128)(2,1)S(1)}, bf16[272,256]{1,0:T(8,128)(2,1)S(1)}, u32[]{:S(2)}, u32[]{:S(2)}) collective-permute-start(bf16[272,256]{1,0:T(8,128)(2,1)S(1)} %shard_map.100), channel_id=1, source_target_pairs={{0,16},{1,5},{2,18},{3,7},{4,20},{5,1},{6,22},{7,3},{8,24},{9,13},... | collective-permute-start | bytes 417800 | tf_op jit(solution)/shard_map/ppermute | solution.py:406
  42.9 11.4 %collective-permute-start.5 = (bf16[272,256]{1,0:T(8,128)(2,1)S(1)}, bf16[272,256]{1,0:T(8,128)(2,1)S(1)}, u32[]{:S(2)}, u32[]{:S(2)}) collective-permute-start(bf16[272,256]{1,0:T(8,128)(2,1)S(1)} %shard_map.99), channel_id=1, source_target_pairs={{0,8},{1,9},{2,10},{3,11},{4,12},{5,13},{6,14},{7,15},{8,0},{9,1},... | collective-permute-start | bytes 417800 | tf_op jit(solution)/shard_map/ppermute | solution.py:406
  44.0 10.4 %collective-permute-start.3 = (bf16[272,256]{1,0:T(8,128)(2,1)S(1)}, bf16[272,256]{1,0:T(8,128)(2,1)S(1)}, u32[]{:S(2)}, u32[]{:S(2)}) collective-permute-start(bf16[272,256]{1,0:T(8,128)(2,1)S(1)} %shard_map.98), channel_id=1, source_target_pairs={{0,4},{1,17},{2,6},{3,19},{4,0},{5,21},{6,2},{7,23},{8,12},{9,25},... | collective-permute-start | bytes 417800 | tf_op jit(solution)/shard_map/ppermute | solution.py:406
  46.0 8.4 %copy-start.4 = (s32[1,64,1]{1,2,0:T(1,128)S(1)}, s32[1,64,1]{1,2,0:T(1,128)}, u32[]{:S(2)}) copy-start(s32[1,64,1]{1,2,0:T(1,128)} %param.9) | copy-start | bytes 772

commit v10 on v4

--- a/solution.py
+++ b/solution.py
@@ -201,15 +201,24 @@
     )
 
 
+def split_terms(value):
+    high = value.astype(jnp.bfloat16).astype(jnp.float32)
+    rest = value - high
+    middle = rest.astype(jnp.bfloat16).astype(jnp.float32)
+    return high, middle, rest - middle
+
+
+def with_rows(rest, first, terms):
+    row = lax.broadcasted_iota(jnp.int32, rest.shape, 0)
+    for k, term in enumerate(terms):
+        rest = jnp.where(row == first + k, term, rest)
+    return rest
+
+
 def tail_kernel(total_ref, out_ref):
     total = jnp.sum(total_ref[0:1, :], keepdims=True)
-    high = total.astype(jnp.bfloat16).astype(jnp.float32)
-    rest = total - high
-    middle = rest.astype(jnp.bfloat16).astype(jnp.float32)
-    low = rest - middle
-    row = lax.broadcasted_iota(jnp.int32, out_ref.shape, 0)
-    value = jnp.where(row == 0, high, jnp.where(row == 1, middle, jnp.where(row == 2, low, 0.0)))
-    out_ref[...] = value.astype(jnp.bfloat16)
+    rows = with_rows(jnp.zeros(out_ref.shape, jnp.float32), 0, split_terms(total))
+    out_ref[...] = rows.astype(jnp.bfloat16)
 
 
 def sum_tail(total, side):
@@ -223,30 +232,33 @@
     )(total)
 
 
-def precondition_kernel(m, rows, me_ref, grad_ref, left_ref, right_ref, tail_ref, out_ref):
+def precondition_kernel(m, me_ref, grad_ref, left_ref, right_ref, tail_ref, out_ref):
     side = grad_ref.shape[0]
     slot = me_ref[0] ^ m
     half_done = jnp.dot(
         left_ref[0, slot], grad_ref[...], preferred_element_type=jnp.float32
     ).astype(jnp.bfloat16)
-    out_ref[0:side, :] = jnp.dot(
+    preconditioned = jnp.dot(
         half_done, right_ref[0, slot], preferred_element_type=jnp.float32
     ).astype(jnp.bfloat16)
-    if rows:
-        out_ref[side:, :] = tail_ref[...]
-
-
-def precondition(m, rows, me, block, left_root, right_root, tail):
+    out_ref[0:side, :] = preconditioned
+    pre_float = preconditioned.astype(jnp.float32)
+    squares = jnp.sum(pre_float * pre_float, axis=0, keepdims=True)
+    rows = with_rows(tail_ref[...].astype(jnp.float32), 3, split_terms(squares))
+    out_ref[side:, :] = rows.astype(jnp.bfloat16)
+
+
+def precondition(m, me, block, left_root, right_root, tail):
     side = block.shape[0]
     return pl.pallas_call(
-        functools.partial(precondition_kernel, m, rows),
+        functools.partial(precondition_kernel, m),
         grid_spec=pltpu.PrefetchScalarGridSpec(
             num_scalar_prefetch=1,
             grid=(),
             in_specs=[pl.BlockSpec(memory_space=pltpu.VMEM)] * 4,
             out_specs=pl.BlockSpec(memory_space=pltpu.VMEM),
         ),
-        out_shape=jax.ShapeDtypeStruct((side + rows, side), jnp.bfloat16),
+        out_shape=jax.ShapeDtypeStruct((side + TAIL, side), jnp.bfloat16),
         compiler_params=kernel_params(6),
         cost_estimate=pl.CostEstimate(
             flops=4 * side**3, bytes_accessed=8 * side * side, transcendentals=0
@@ -300,18 +312,16 @@
 def finish_kernel(order, entries, owners_ref, me_ref, *refs):
     count = len(order)
     pieces = refs[:count]
-    squares_ref, tail_ref, out_ref, held, sums, sems = refs[count:]
+    squares_ref, out_ref, held, sums, sems = refs[count:]
     side, lanes = out_ref.shape[3], squares_ref.shape[1]
     me = me_ref[0]
     named = [owners_ref[me * count + j] for j in range(count)]
     blocks = [home_slot(named, me ^ m) for m in order]
     global_sq = jnp.zeros((1, 1), jnp.float32)
-    for rows in [tail_ref[...]] + [piece[side:, :] for piece in pieces if piece.shape[0] > side]:
-        terms = rows[:, 0:1].astype(jnp.float32)
-        global_sq = global_sq + jnp.sum(terms, axis=0, keepdims=True)
     for k, piece in enumerate(pieces):
-        pre_float = piece[0:side, :].astype(jnp.float32)
-        row = jnp.sum(pre_float * pre_float, axis=0, keepdims=True)
+        rows = piece[side:, :].astype(jnp.float32)
+        global_sq = global_sq + jnp.sum(rows[0:3, 0:1], axis=0, keepdims=True)
+        row = jnp.sum(rows[3:6, :], axis=0, keepdims=True)
         parts = [row[:, i : i + lanes] for i in range(0, side, lanes)]
         sums[0, k : k + 1, :] = functools.reduce(jnp.add, parts)
         sums[1, k : k + 1, :] = squares_ref[pl.ds(blocks[k], 1), :]
@@ -332,14 +342,14 @@
         copy.wait()
 
 
-def finish(order, owner_list, me, pieces, squares, tail, entries):
+def finish(order, owner_list, me, pieces, squares, entries):
     count, side = len(pieces), pieces[0].shape[1]
     return pl.pallas_call(
         functools.partial(finish_kernel, order, entries),
         grid_spec=pltpu.PrefetchScalarGridSpec(
             num_scalar_prefetch=2,
             grid=(),
-            in_specs=[pl.BlockSpec(memory_space=pltpu.VMEM)] * (count + 2),
+            in_specs=[pl.BlockSpec(memory_space=pltpu.VMEM)] * (count + 1),
             out_specs=pl.BlockSpec(memory_space=pl.ANY),
             scratch_shapes=[
                 pltpu.VMEM((count, side, side), jnp.bfloat16),
@@ -352,7 +362,7 @@
         cost_estimate=pl.CostEstimate(
             flops=6 * count * side * side, bytes_accessed=4 * count * side * side, transcendentals=0
         ),
-    )(owner_list, me, *pieces, squares, tail)
+    )(owner_list, me, *pieces, squares)
 
 
 def doublings(size):
@@ -383,12 +393,11 @@
     tail = sum_tail(total, side)
     returned = []
     for m, block in zip(order, received):
-        rows = TAIL if m else 0
-        done = precondition(m, rows, me, block, left_root, right_root, tail)
+        done = precondition(m, me, block, left_root, right_root, tail)
         returned.append(swap(done, m))
     new_left, new_right = gram_update(order, me, received, left_stats, right_stats)
     entries = float(owner_list.shape[0] * layers * side * side)
-    update = finish(order, owner_list, me, returned, squares, tail, entries)
+    update = finish(order, owner_list, me, returned, squares, entries)
     return (update, new_left, new_right)
 
 

time: 56.3 us -> 56.3 us (level)
  no operation moved by 1% of the time
where the time goes in v10:
time: 56.3 us; the launch traced here: 56.1 us
  starting transfers between devices  34.6 us (61%)
  Pallas kernels  13.4 us (24%)
  waiting for transfers between devices  7.29 us (13%)
  between operations  0.86 us (2%)
    ppermute x16, starting transfers between devices, swap(): lax.ppermute(value, axis, [(i, i ^ m) for i in range(lax.axis_size(axis))])  34.6 us
    ppermute x16, waiting for transfers between devices, swap(): lax.ppermute(value, axis, [(i, i ^ m) for i in range(lax.axis_size(axis))])  7.29 us
    pallas_call x1, Pallas kernels, gram_update(): pl.pallas_call(functools.partial(gram_kernel, order), grid_spec=pltpu.Pre...  4.68 us
    pallas_call x8, Pallas kernels, precondition(): pl.pallas_call(functools.partial(precondition_kernel, m), grid_spec=pltpu...  2.81 us
    pallas_call x1, Pallas kernels, adam_squares(): pl.pallas_call(adam_kernel, in_specs=[hbm, hbm], out_specs=[pl.BlockSpec(...  2.53 us
    pallas_call x1, Pallas kernels, finish(): pl.pallas_call(functools.partial(finish_kernel, order, entries), grid_spe...  1.76 us
    pallas_call x1, Pallas kernels, route(): pl.pallas_call(functools.partial(route_kernel, order), in_specs=[hbm, pl....  1.46 us
  transfers between devices with their start and end apart: 16, of which 4 were waited for; matrix products, arithmetic and copies ran while one was open for 0% of the time, Pallas kernels for 18%

profile of v10, /device:TPU:0, one launch (start us, length us, event | category | flops | bytes accessed | tf_op | source)
XLA Modules:
  0.0 56.1 jit_solution(6401941847082821377)
XLA Ops:
  0.7 1.5 %shard_map.94 = (bf16[256,256]{1,0:T(8,128)(2,1)S(1)}, bf16[256,256]{1,0:T(8,128)(2,1)S(1)}, bf16[256,256]{1,0:T(8,128)(2,1)S(1)}, bf16[256,256]{1,0:T(8,128)(2,...) custom-call(s32[64]{0:T(128)} %bitcast.2, ...), custom_call_target="tpu_custom_call" | custom-call | bytes 2097152 | tf_op jit(solution)/shard_map/pallas_call | solution.py:128
  2.1 6.0 %collective-permute-start.14 = (bf16[256,256]{1,0:T(8,128)(2,1)S(1)}, bf16[256,256]{1,0:T(8,128)(2,1)S(1)}, u32[]{:S(2)}, u32[]{:S(2)}) collective-permute-start(bf16[256,256]{1,0:T(8,128)(2,1)S(1)} %get-tuple-element.23), channel_id=1, source_target_pairs={{0,28},{4,24},{8,20},{12,16},{16,12},{20,8},{24,4},{28,0},{1,29},{... | collective-permute-start | bytes 393224 | tf_op jit(solution)/shard_map/ppermute | solution.py:386
  8.2 0.2 collective-permute-start.12
  8.4 0.4 collective-permute-start.2
  8.8 1.8 %collective-permute-start.10 = (bf16[256,256]{1,0:T(8,128)(2,1)S(1)}, bf16[256,256]{1,0:T(8,128)(2,1)S(1)}, u32[]{:S(2)}, u32[]{:S(2)}) collective-permute-start(bf16[256,256]{1,0:T(8,128)(2,1)S(1)} %get-tuple-element.21), channel_id=1, source_target_pairs={{0,20},{4,16},{8,28},{12,24},{16,4},{20,0},{24,12},{28,8},{1,21},{... | collective-permute-start | bytes 393224 | tf_op jit(solution)/shard_map/ppermute | solution.py:386
  10.6 2.5 %shard_map.95 = (f32[8,128]{1,0:T(8,128)S(1)}, f32[8,128]{1,0:T(8,128)S(1)}) custom-call(bf16[1,8,256,256]{3,2,1,0:T(8,128)(2,1)} %grad_hbm.3, f32[1,8,256,256]{3,2,1,0:T(8,128)} %moment_hbm.1), custom_call_target="tpu_custom_call" | custom-call | flops 4194304 | bytes 3145728 | tf_op jit(solution)/shard_map/pallas_call | solution.py:179
  13.2 0.1 collective-permute-start
  13.3 1.2 %collective-permute-done = f32[8,128]{1,0:T(8,128)S(1)} collective-permute-done((f32[8,128]{1,0:T(8,128)S(1)}, f32[8,128]{1,0:T(8,128)S(1)}, u32[]{:S(2)}, u32[]{:S(2)}) %collective-permute-start) | collective-permute-done | bytes 4128 | tf_op jit(solution)/shard_map/ppermute | solution.py:386
  14.4 1.5 %collective-permute-start.1 = (f32[8,128]{1,0:T(8,128)S(1)}, f32[8,128]{1,0:T(8,128)S(1)}, u32[]{:S(2)}, u32[]{:S(2)}) collective-permute-start(f32[8,128]{1,0:T(8,128)S(1)} %add.6), channel_id=1, source_target_pairs={{0,2},{1,3},{2,0},{3,1},{4,6},{5,7},{6,4},{7,5},{8,10},{9,11},{10,... | collective-permute-start | bytes 12296 | tf_op jit(solution)/shard_map/ppermute | solution.py:386
  15.9 2.1 %collective-permute-done.1 = f32[8,128]{1,0:T(8,128)S(1)} collective-permute-done((f32[8,128]{1,0:T(8,128)S(1)}, f32[8,128]{1,0:T(8,128)S(1)}, u32[]{:S(2)}, u32[]{:S(2)}) %collective-permute-start.1) | collective-permute-done | bytes 4128 | tf_op jit(solution)/shard_map/ppermute | solution.py:386
  18.0 2.1 %collective-permute-start.6 = (bf16[256,256]{1,0:T(8,128)(2,1)S(1)}, bf16[256,256]{1,0:T(8,128)(2,1)S(1)}, u32[]{:S(2)}, u32[]{:S(2)}) collective-permute-start(bf16[256,256]{1,0:T(8,128)(2,1)S(1)} %get-tuple-element.19), channel_id=1, source_target_pairs={{0,16},{4,20},{8,24},{12,28},{16,0},{20,4},{24,8},{28,12},{1,17},{... | collective-permute-start | bytes 393224 | tf_op jit(solution)/shard_map/ppermute | solution.py:386
  20.2 0.1 shard_map.96.tail_ref
  20.3 0.0 collective-permute-done.14.grad_ref.refs_7_
  20.3 1.3 %collective-permute-start.8 = (bf16[256,256]{1,0:T(8,128)(2,1)S(1)}, bf16[256,256]{1,0:T(8,128)(2,1)S(1)}, u32[]{:S(2)}, u32[]{:S(2)}) collective-permute-start(bf16[256,256]{1,0:T(8,128)(2,1)S(1)} %get-tuple-element.20), channel_id=1, source_target_pairs={{0,12},{4,8},{8,4},{12,0},{16,28},{20,24},{24,20},{28,16},{1,13},{... | collective-permute-start | bytes 393224 | tf_op jit(solution)/shard_map/ppermute | solution.py:386
  21.6 0.4 shard_map.104
  22.0 0.0 collective-permute-done.12.grad_ref.refs_6_
  22.0 2.7 %collective-permute-start.15 = (bf16[272,256]{1,0:T(8,128)(2,1)S(1)}, bf16[272,256]{1,0:T(8,128)(2,1)S(1)}, u32[]{:S(2)}, u32[]{:S(2)}) collective-permute-start(bf16[272,256]{1,0:T(8,128)(2,1)S(1)} %shard_map.104), channel_id=1, source_target_pairs={{0,28},{4,24},{8,20},{12,16},{16,12},{20,8},{24,4},{28,0},{1,29},{... | collective-permute-start | bytes 417800 | tf_op jit(solution)/shard_map/ppermute | solution.py:386
  24.7 0.3 shard_map.103
  25.1 0.0 collective-permute-done.2.grad_ref.refs_1_
  25.1 2.1 %collective-permute-start.13 = (bf16[272,256]{1,0:T(8,128)(2,1)S(1)}, bf16[272,256]{1,0:T(8,128)(2,1)S(1)}, u32[]{:S(2)}, u32[]{:S(2)}) collective-permute-start(bf16[272,256]{1,0:T(8,128)(2,1)S(1)} %shard_map.103), channel_id=1, source_target_pairs={{0,24},{4,28},{8,16},{12,20},{16,8},{20,12},{24,0},{28,4},{1,25},{... | collective-permute-start | bytes 417800 | tf_op jit(solution)/shard_map/ppermute | solution.py:386
  27.2 2.5 %collective-permute-done.10.grad_ref.refs_5_ = bf16[256,256]{1,0:T(8,128)(2,1)S(1)} collective-permute-done((bf16[256,256]{1,0:T(8,128)(2,1)S(1)}, bf16[256,256]{1,0:T(8,128)(2,1)S(1)}, u32[]{:S(2)}, u32[]{:S(2)}) %collective-permute-start.10) | collective-permute-done | bytes 131104 | tf_op jit(solution)/shard_map/ppermute | solution.py:386
  29.7 4.3 %collective-permute-start.4 = (bf16[256,256]{1,0:T(8,128)(2,1)S(1)}, bf16[256,256]{1,0:T(8,128)(2,1)S(1)}, u32[]{:S(2)}, u32[]{:S(2)}) collective-permute-start(bf16[256,256]{1,0:T(8,128)(2,1)S(1)} %get-tuple-element.18), channel_id=1, source_target_pairs={{0,8},{4,12},{8,0},{12,4},{16,24},{20,28},{24,16},{28,20},{1,9},{5... | collective-permute-start | bytes 393224 | tf_op jit(solution)/shard_map/ppermute | solution.py:386
  34.0 0.3 shard_map.98
  34.4 0.4 shard_map.102
  34.7 0.0 collective-permute-done.8.grad_ref.refs_4_
  34.8 6.4 %collective-permute-start.11 = (bf16[272,256]{1,0:T(8,128)(2,1)S(1)}, bf16[272,256]{1,0:T(8,128)(2,1)S(1)}, u32[]{:S(2)}, u32[]{:S(2)}) collective-permute-start(bf16[272,256]{1,0:T(8,128)(2,1)S(1)} %shard_map.102), channel_id=1, source_target_pairs={{0,20},{4,16},{8,28},{12,24},{16,4},{20,0},{24,12},{28,8},{1,21},{... | collective-permute-start | bytes 417800 | tf_op jit(solution)/shard_map/ppermute | solution.py:386
  41.1 0.4 shard_map.101
  41.5 0.0 collective-permute-done.6.grad_ref.refs_3_
  41.5 2.2 %collective-permute-start.9 = (bf16[272,256]{1,0:T(8,128)(2,1)S(1)}, bf16[272,256]{1,0:T(8,128)(2,1)S(1)}, u32[]{:S(2)}, u32[]{:S(2)}) collective-permute-start(bf16[272,256]{1,0:T(8,128)(2,1)S(1)} %shard_map.101), channel_id=1, source_target_pairs={{0,12},{4,8},{8,4},{12,0},{16,28},{20,24},{24,20},{28,16},{1,13},{... | collective-permute-start | bytes 417800 | tf_op jit(solution)/shard_map/ppermute | solution.py:386
  43.6 0.3 shard_map.100
  44.0 0.0 copy-start.2
  44.0 0.0 copy-start.3
  44.0 0.0 collective-permute-done.4.grad_ref.refs_2_
  44.0 0.1 collective-permute-start.7
  44.1 0.4 shard_map.99
  44.5 0.0 collective-permute-done.15.refs_7_
  44.5 1.7 %collective-permute-start.5 = (bf16[272,256]{1,0:T(8,128)(2,1)S(1)}, bf16[272,256]{1,0:T(8,128)(2,1)S(1)}, u32[]{:S(2)}, u32[]{:S(2)}) collective-permute-start(bf16[272,256]{1,0:T(8,128)(2,1)S(1)} %shard_map.99), channel_id=1, source_target_pairs={{0,8},{4,12},{8,0},{12,4},{16,24},{20,28},{24,16},{28,20},{1,9},{5... | collective-permute-start | bytes 417800 | tf_op jit(solution)/shard_map/ppermute | solution.py:386
  46.1 0.0 collective-permute-done.13.refs_6_
  46.2 1.6 %collective-permute-start.3 = (bf16[272,256]{1,0:T(8,128)(2,1)S(1)}, bf16[272,256]{1,0:T(8,128)(2,1)S(1)}, u32[]{:S(2)}, u32[]{:S(2)}) collective-permute-start(bf16[272,256]{1,0:T(8,128)(2,1)S(1)} %shard_map.98), channel_id=1, source_target_pairs={{0,4},{4,0},{8,12},{12,8},{16,20},{20,16},{24,28},{28,24},{1,5},{5... | collective-permute-start | bytes 417800 | tf_op jit(solution)/shard_map/ppermute | solution.py:386
  47.7 0.4 shard_map.97.refs_0_
  48.1 0.0 copy-start.4
  48.1 4.7 %shard_map.106 = (f32[1,8,256,256]{3,2,1,0:T(8,128)}, f32[1,8,256,256]{3,2,1,0:T(8,128)}) custom-call(s32[1]{0:T(128)} %bitcast.1.me_ref, bf16[256,256]{1,0:T(8,128)(2,1)S(1)} %get-tuple-element.15.grad_ref.refs_0_, bf16[256,256]{1,0:T(8,128)(2,1)S(1)} %collective-permute-done.2.grad_ref.refs_1_, ...), custom_call_target="tpu_custom_call" | custom-call | flops 536870912 | bytes 9437184 | tf_op jit(solution)/shard_map/pallas_call | solution.py:293
  52.8 0.0 collective-permute-done.11.refs_5_
  52.8 0.0 collective-permute-done.9.refs_4_
  52.8 1.5 %collective-permute-done.7.refs_3_ = bf16[272,256]{1,0:T(8,128)(2,1)S(1)} collective-permute-done((bf16[272,256]{1,0:T(8,128)(2,1)S(1)}, bf16[272,256]{1,0:T(8,128)(2,1)S(1)}, u32[]{:S(2)}, u32[]{:S(2)}) %collective-permute-start.7) | collective-permute-done | bytes 139296 | tf_op jit(solution)/shard_map/ppermute | solution.py:386
  54.4 0.0 collective-permute-done.5.refs_2_
  54.4 0.0 collective-permute-done.3.refs_1_
  54.4 1.8 %shard_map.105 = bf16[1,8,256,256]{3,2,1,0:T(8,128)(2,1)} custom-call(s32[64]{0:T(128)S(1)} %bitcast.3, s32[1]{0:T(128)} %bitcast.1.me_ref, bf16[272,256]{1,0:T(8,128)(2,1)S(1)} %shard_map.97.refs_0_, bf16[272,256]{1,0:T(8,128)(2,1)S(1)} %collective-permute-done.3.refs_1_, bf16[272,256]{1,0:T(8,128)(2,1)S(1)} %collective-permute-done.5.refs_2_, ...), custom_call_target="tpu_custom_call" | custom-call | flops 3145728 | bytes 2097152 | tf_op jit(solution)/shard_map/pallas_call | solution.py:347
  (9 shorter events, 0.0 us)
Async XLA Ops:
  0.6 21.0 %copy-start = (bf16[1,8,256,256]{3,2,1,0:T(8,128)(2,1)S(1)}, bf16[1,8,256,256]{3,2,1,0:T(8,128)(2,1)}, u32[]{:S(2)}) copy-start(bf16[1,8,256,256]{3,2,1,0:T(8,128)(2,1)} %left_ref.15) | copy-start | bytes 3145732
  0.6 21.0 %copy-start.1 = (bf16[1,8,256,256]{3,2,1,0:T(8,128)(2,1)S(1)}, bf16[1,8,256,256]{3,2,1,0:T(8,128)(2,1)}, u32[]{:S(2)}) copy-start(bf16[1,8,256,256]{3,2,1,0:T(8,128)(2,1)} %right_ref.15) | copy-start | bytes 3145732
  2.1 18.2 %collective-permute-start.14 = (bf16[256,256]{1,0:T(8,128)(2,1)S(1)}, bf16[256,256]{1,0:T(8,128)(2,1)S(1)}, u32[]{:S(2)}, u32[]{:S(2)}) collective-permute-start(bf16[256,256]{1,0:T(8,128)(2,1)S(1)} %get-tuple-element.23), channel_id=1, source_target_pairs={{0,28},{4,24},{8,20},{12,16},{16,12},{20,8},{24,4},{28,0},{1,29},{... | collective-permute-start | bytes 393224 | tf_op jit(solution)/shard_map/ppermute | solution.py:386
  8.2 13.8 %collective-permute-start.12 = (bf16[256,256]{1,0:T(8,128)(2,1)S(1)}, bf16[256,256]{1,0:T(8,128)(2,1)S(1)}, u32[]{:S(2)}, u32[]{:S(2)}) collective-permute-start(bf16[256,256]{1,0:T(8,128)(2,1)S(1)} %get-tuple-element.22), channel_id=1, source_target_pairs={{0,24},{4,28},{8,16},{12,20},{16,8},{20,12},{24,0},{28,4},{1,25},{... | collective-permute-start | bytes 393224 | tf_op jit(solution)/shard_map/ppermute | solution.py:386
  8.4 16.7 %collective-permute-start.2 = (bf16[256,256]{1,0:T(8,128)(2,1)S(1)}, bf16[256,256]{1,0:T(8,128)(2,1)S(1)}, u32[]{:S(2)}, u32[]{:S(2)}) collective-permute-start(bf16[256,256]{1,0:T(8,128)(2,1)S(1)} %get-tuple-element.17), channel_id=1, source_target_pairs={{0,4},{4,0},{8,12},{12,8},{16,20},{20,16},{24,28},{28,24},{1,5},{5... | collective-permute-start | bytes 393224 | tf_op jit(solution)/shard_map/ppermute | solution.py:386
  8.8 20.9 %collective-permute-start.10 = (bf16[256,256]{1,0:T(8,128)(2,1)S(1)}, bf16[256,256]{1,0:T(8,128)(2,1)S(1)}, u32[]{:S(2)}, u32[]{:S(2)}) collective-permute-start(bf16[256,256]{1,0:T(8,128)(2,1)S(1)} %get-tuple-element.21), channel_id=1, source_target_pairs={{0,20},{4,16},{8,28},{12,24},{16,4},{20,0},{24,12},{28,8},{1,21},{... | collective-permute-start | bytes 393224 | tf_op jit(solution)/shard_map/ppermute | solution.py:386
  13.2 1.2 %collective-permute-start = (f32[8,128]{1,0:T(8,128)S(1)}, f32[8,128]{1,0:T(8,128)S(1)}, u32[]{:S(2)}, u32[]{:S(2)}) collective-permute-start(f32[8,128]{1,0:T(8,128)S(1)} %get-tuple-element.16), channel_id=1, source_target_pairs={{0,1},{1,0},{2,3},{3,2},{4,5},{5,4},{6,7},{7,6},{8,9},{9,8},{10,11... | collective-permute-start | bytes 12296 | tf_op jit(solution)/shard_map/ppermute | solution.py:386
  14.4 3.6 %collective-permute-start.1 = (f32[8,128]{1,0:T(8,128)S(1)}, f32[8,128]{1,0:T(8,128)S(1)}, u32[]{:S(2)}, u32[]{:S(2)}) collective-permute-start(f32[8,128]{1,0:T(8,128)S(1)} %add.6), channel_id=1, source_target_pairs={{0,2},{1,3},{2,0},{3,1},{4,6},{5,7},{6,4},{7,5},{8,10},{9,11},{10,... | collective-permute-start | bytes 12296 | tf_op jit(solution)/shard_map/ppermute | solution.py:386
  18.0 23.4 %collective-permute-start.6 = (bf16[256,256]{1,0:T(8,128)(2,1)S(1)}, bf16[256,256]{1,0:T(8,128)(2,1)S(1)}, u32[]{:S(2)}, u32[]{:S(2)}) collective-permute-start(bf16[256,256]{1,0:T(8,128)(2,1)S(1)} %get-tuple-element.19), channel_id=1, source_target_pairs={{0,16},{4,20},{8,24},{12,28},{16,0},{20,4},{24,8},{28,12},{1,17},{... | collective-permute-start | bytes 393224 | tf_op jit(solution)/shard_map/ppermute | solution.py:386
  20.3 14.4 %collective-permute-start.8 = (bf16[256,256]{1,0:T(8,128)(2,1)S(1)}, bf16[256,256]{1,0:T(8,128)(2,1)S(1)}, u32[]{:S(2)}, u32[]{:S(2)}) collective-permute-start(bf16[256,256]{1,0:T(8,128)(2,1)S(1)} %get-tuple-element.20), channel_id=1, source_target_pairs={{0,12},{4,8},{8,4},{12,0},{16,28},{20,24},{24,20},{28,16},{1,13},{... | collective-permute-start | bytes 393224 | tf_op jit(solution)/shard_map/ppermute | solution.py:386
  22.0 22.5 %collective-permute-start.15 = (bf16[272,256]{1,0:T(8,128)(2,1)S(1)}, bf16[272,256]{1,0:T(8,128)(2,1)S(1)}, u32[]{:S(2)}, u32[]{:S(2)}) collective-permute-start(bf16[272,256]{1,0:T(8,128)(2,1)S(1)} %shard_map.104), channel_id=1, source_target_pairs={{0,28},{4,24},{8,20},{12,16},{16,12},{20,8},{24,4},{28,0},{1,29},{... | collective-permute-start | bytes 417800 | tf_op jit(solution)/shard_map/ppermute | solution.py:386
  25.1 21.0 %collective-permute-start.13 = (bf16[272,256]{1,0:T(8,128)(2,1)S(1)}, bf16[272,256]{1,0:T(8,128)(2,1)S(1)}, u32[]{:S(2)}, u32[]{:S(2)}) collective-permute-start(bf16[272,256]{1,0:T(8,128)(2,1)S(1)} %shard_map.103), channel_id=1, source_target_pairs={{0,24},{4,28},{8,16},{12,20},{16,8},{20,12},{24,0},{28,4},{1,25},{... | collective-permute-start | bytes 417800 | tf_op jit(solution)/shard_map/ppermute | solution.py:386
  29.7 14.3 %collective-permute-start.4 = (bf16[256,256]{1,0:T(8,128)(2,1)S(1)}, bf16[256,256]{1,0:T(8,128)(2,1)S(1)}, u32[]{:S(2)}, u32[]{:S(2)}) collective-permute-start(bf16[256,256]{1,0:T(8,128)(2,1)S(1)} %get-tuple-element.18), channel_id=1, source_target_pairs={{0,8},{4,12},{8,0},{12,4},{16,24},{20,28},{24,16},{28,20},{1,9},{5... | collective-permute-start | bytes 393224 | tf_op jit(solution)/shard_map/ppermute | solution.py:386
  34.8 18.1 %collective-permute-start.11 = (bf16[272,256]{1,0:T(8,128)(2,1)S(1)}, bf16[272,256]{1,0:T(8,128)(2,1)S(1)}, u32[]{:S(2)}, u32[]{:S(2)}) collective-permute-start(bf16[272,256]{1,0:T(8,128)(2,1)S(1)} %shard_map.102), channel_id=1, source_target_pairs={{0,20},{4,16},{8,28},{12,24},{16,4},{20,0},{24,12},{28,8},{1,21},{... | collective-permute-start | bytes 417800 | tf_op jit(solution)/shard_map/ppermute | solution.py:386
  41.5 11.3 %collective-permute-start.9 = (bf16[272,256]{1,0:T(8,128)(2,1)S(1)}, bf16[272,256]{1,0:T(8,128)(2,1)S(1)}, u32[]{:S(2)}, u32[]{:S(2)}) collective-permute-start(bf16[272,256]{1,0:T(8,128)(2,1)S(1)} %shard_map.101), channel_id=1, source_target_pairs={{0,12},{4,8},{8,4},{12,0},{16,28},{20,24},{24,20},{28,16},{1,13},{... | collective-permute-start | bytes 417800 | tf_op jit(solution)/shard_map/ppermute | solution.py:386
  44.0 4.1 %copy-start.2 = (f32[1,8,256,256]{3,2,1,0:T(8,128)S(1)}, f32[1,8,256,256]{3,2,1,0:T(8,128)}, u32[]{:S(2)}) copy-start(f32[1,8,256,256]{3,2,1,0:T(8,128)} %refs_8_.1) | copy-start | bytes 6291460
  44.0 4.1 %copy-start.3 = (f32[1,8,256,256]{3,2,1,0:T(8,128)S(1)}, f32[1,8,256,256]{3,2,1,0:T(8,128)}, u32[]{:S(2)}) copy-start(f32[1,8,256,256]{3,2,1,0:T(8,128)} %refs_9_.1) | copy-start | bytes 6291460
  44.0 10.3 %collective-permute-start.7 = (bf16[272,256]{1,0:T(8,128)(2,1)S(1)}, bf16[272,256]{1,0:T(8,128)(2,1)S(1)}, u32[]{:S(2)}, u32[]{:S(2)}) collective-permute-start(bf16[272,256]{1,0:T(8,128)(2,1)S(1)} %shard_map.100), channel_id=1, source_target_pairs={{0,16},{4,20},{8,24},{12,28},{16,0},{20,4},{24,8},{28,12},{1,17},{... | collective-permute-start | bytes 417800 | tf_op jit(solution)/shard_map/ppermute | solution.py:386
  44.5 9.9 %collective-permute-start.5 = (bf16[272,256]{1,0:T(8,128)(2,1)S(1)}, bf16[272,256]{1,0:T(8,128)(2,1)S(1)}, u32[]{:S(2)}, u32[]{:S(2)}) collective-permute-start(bf16[272,256]{1,0:T(8,128)(2,1)S(1)} %shard_map.99), channel_id=1, source_target_pairs={{0,8},{4,12},{8,0},{12,4},{16,24},{20,28},{24,16},{28,20},{1,9},{5... | collective-permute-start | bytes 417800 | tf_op jit(solution)/shard_map/ppermute | solution.py:386
  46.2 8.2 %collective-permute-start.3 = (bf16[272,256]{1,0:T(8,128)(2,1)S(1)}, bf16[272,256]{1,0:T(8,128)(2,1)S(1)}, u32[]{:S(2)}, u32[]{:S(2)}) collective-permute-start(bf16[272,256]{1,0:T(8,128)(2,1)S(1)} %shard_map.98), channel_id=1, source_target_pairs={{0,4},{4,0},{8,12},{12,8},{16,20},{20,16},{24,28},{28,24},{1,5},{5... | collective-permute-start | bytes 417800 | tf_op jit(solution)/shard_map/ppermute | solution.py:386
  48.1 6.2 %copy-start.4 = (s32[1,64,1]{1,2,0:T(1,128)S(1)}, s32[1,64,1]{1,2,0:T(1,128)}, u32[]{:S(2)}) copy-start(s32[1,64,1]{1,2,0:T(1,128)} %param.9) | copy-start | bytes 772

commit v11 on v10

--- a/solution.py
+++ b/solution.py
@@ -378,7 +378,7 @@
     me = lax.axis_index("fsdp").astype(jnp.int32).reshape(1)
     owner_list = owners[0, :, 0]
     half = count // 2
-    order = [*range(half - 1), half, half - 1, *range(half + 1, count)]
+    order = [0, *range(half - 2, 0, -1), half, half - 1, *range(half + 1, count)]
 
     def swap(value, m, axis="fsdp"):
         if m == 0:

time: 56.3 us -> 57.7 us (1.025)
  waiting for transfers between devices: 7.29 us -> 8.55 us
    ppermute x16, waiting for transfers between devices: 7.29 us -> 8.55 us  [swap(): lax.ppermute(value, axis, [(i, i ^ m) for i in range(lax.axis_size(axis))])]
  transfers between devices with their start and end apart: 16 -> 16, of which waited for: 4 -> 6; matrix products, arithmetic and copies ran while one was open for 0% -> 0% of each run, Pallas kernels for 18% -> 18%
where the time goes in v11:
time: 57.7 us; the launch traced here: 57.6 us
  starting transfers between devices  34.7 us (60%)
  Pallas kernels  13.4 us (23%)
  waiting for transfers between devices  8.55 us (15%)
  between operations  0.86 us (1%)
    ppermute x16, starting transfers between devices, swap(): lax.ppermute(value, axis, [(i, i ^ m) for i in range(lax.axis_size(axis))])  34.7 us
    ppermute x16, waiting for transfers between devices, swap(): lax.ppermute(value, axis, [(i, i ^ m) for i in range(lax.axis_size(axis))])  8.55 us
    pallas_call x1, Pallas kernels, gram_update(): pl.pallas_call(functools.partial(gram_kernel, order), grid_spec=pltpu.Pre...  4.69 us
    pallas_call x8, Pallas kernels, precondition(): pl.pallas_call(functools.partial(precondition_kernel, m), grid_spec=pltpu...  2.81 us
    pallas_call x1, Pallas kernels, adam_squares(): pl.pallas_call(adam_kernel, in_specs=[hbm, hbm], out_specs=[pl.BlockSpec(...  2.53 us
    pallas_call x1, Pallas kernels, finish(): pl.pallas_call(functools.partial(finish_kernel, order, entries), grid_spe...  1.76 us
    pallas_call x1, Pallas kernels, route(): pl.pallas_call(functools.partial(route_kernel, order), in_specs=[hbm, pl....  1.46 us
  transfers between devices with their start and end apart: 16, of which 6 were waited for; matrix products, arithmetic and copies ran while one was open for 0% of the time, Pallas kernels for 18%

profile of v11, /device:TPU:0, one launch (start us, length us, event | category | flops | bytes accessed | tf_op | source)
XLA Modules:
  0.0 57.6 jit_solution(14061132641960217058)
XLA Ops:
  0.7 1.5 %shard_map.94 = (bf16[256,256]{1,0:T(8,128)(2,1)S(1)}, bf16[256,256]{1,0:T(8,128)(2,1)S(1)}, bf16[256,256]{1,0:T(8,128)(2,1)S(1)}, bf16[256,256]{1,0:T(8,128)(2,...) custom-call(s32[64]{0:T(128)} %bitcast.2, ...), custom_call_target="tpu_custom_call" | custom-call | bytes 2097152 | tf_op jit(solution)/shard_map/pallas_call | solution.py:128
  2.1 6.0 %collective-permute-start.14 = (bf16[256,256]{1,0:T(8,128)(2,1)S(1)}, bf16[256,256]{1,0:T(8,128)(2,1)S(1)}, u32[]{:S(2)}, u32[]{:S(2)}) collective-permute-start(bf16[256,256]{1,0:T(8,128)(2,1)S(1)} %get-tuple-element.23), channel_id=1, source_target_pairs={{0,28},{4,24},{8,20},{12,16},{16,12},{20,8},{24,4},{28,0},{1,29},{... | collective-permute-start | bytes 393224 | tf_op jit(solution)/shard_map/ppermute | solution.py:386
  8.2 0.2 collective-permute-start.12
  8.4 0.0 collective-permute-start.2
  8.4 4.1 %collective-permute-start.10 = (bf16[256,256]{1,0:T(8,128)(2,1)S(1)}, bf16[256,256]{1,0:T(8,128)(2,1)S(1)}, u32[]{:S(2)}, u32[]{:S(2)}) collective-permute-start(bf16[256,256]{1,0:T(8,128)(2,1)S(1)} %get-tuple-element.21), channel_id=1, source_target_pairs={{0,20},{4,16},{8,28},{12,24},{16,4},{20,0},{24,12},{28,8},{1,21},{... | collective-permute-start | bytes 393224 | tf_op jit(solution)/shard_map/ppermute | solution.py:386
  12.5 2.5 %shard_map.95 = (f32[8,128]{1,0:T(8,128)S(1)}, f32[8,128]{1,0:T(8,128)S(1)}) custom-call(bf16[1,8,256,256]{3,2,1,0:T(8,128)(2,1)} %grad_hbm.3, f32[1,8,256,256]{3,2,1,0:T(8,128)} %moment_hbm.1), custom_call_target="tpu_custom_call" | custom-call | flops 4194304 | bytes 3145728 | tf_op jit(solution)/shard_map/pallas_call | solution.py:179
  15.1 0.1 collective-permute-start
  15.1 1.2 %collective-permute-done = f32[8,128]{1,0:T(8,128)S(1)} collective-permute-done((f32[8,128]{1,0:T(8,128)S(1)}, f32[8,128]{1,0:T(8,128)S(1)}, u32[]{:S(2)}, u32[]{:S(2)}) %collective-permute-start) | collective-permute-done | bytes 4128 | tf_op jit(solution)/shard_map/ppermute | solution.py:386
  16.3 1.5 %collective-permute-start.1 = (f32[8,128]{1,0:T(8,128)S(1)}, f32[8,128]{1,0:T(8,128)S(1)}, u32[]{:S(2)}, u32[]{:S(2)}) collective-permute-start(f32[8,128]{1,0:T(8,128)S(1)} %add.6), channel_id=1, source_target_pairs={{0,2},{1,3},{2,0},{3,1},{4,6},{5,7},{6,4},{7,5},{8,10},{9,11},{10,... | collective-permute-start | bytes 12296 | tf_op jit(solution)/shard_map/ppermute | solution.py:386
  17.8 2.1 %collective-permute-done.1 = f32[8,128]{1,0:T(8,128)S(1)} collective-permute-done((f32[8,128]{1,0:T(8,128)S(1)}, f32[8,128]{1,0:T(8,128)S(1)}, u32[]{:S(2)}, u32[]{:S(2)}) %collective-permute-start.1) | collective-permute-done | bytes 4128 | tf_op jit(solution)/shard_map/ppermute | solution.py:386
  19.9 0.0 collective-permute-start.6
  19.9 0.1 shard_map.96.tail_ref
  20.1 0.0 collective-permute-done.14.grad_ref.refs_7_
  20.1 1.7 %collective-permute-start.8 = (bf16[256,256]{1,0:T(8,128)(2,1)S(1)}, bf16[256,256]{1,0:T(8,128)(2,1)S(1)}, u32[]{:S(2)}, u32[]{:S(2)}) collective-permute-start(bf16[256,256]{1,0:T(8,128)(2,1)S(1)} %get-tuple-element.20), channel_id=1, source_target_pairs={{0,12},{4,8},{8,4},{12,0},{16,28},{20,24},{24,20},{28,16},{1,13},{... | collective-permute-start | bytes 393224 | tf_op jit(solution)/shard_map/ppermute | solution.py:386
  21.8 0.4 shard_map.104
  22.2 0.0 collective-permute-done.12.grad_ref.refs_6_
  22.2 3.6 %collective-permute-start.15 = (bf16[272,256]{1,0:T(8,128)(2,1)S(1)}, bf16[272,256]{1,0:T(8,128)(2,1)S(1)}, u32[]{:S(2)}, u32[]{:S(2)}) collective-permute-start(bf16[272,256]{1,0:T(8,128)(2,1)S(1)} %shard_map.104), channel_id=1, source_target_pairs={{0,28},{4,24},{8,20},{12,16},{16,12},{20,8},{24,4},{28,0},{1,29},{... | collective-permute-start | bytes 417800 | tf_op jit(solution)/shard_map/ppermute | solution.py:386
  25.8 0.3 shard_map.103
  26.2 0.0 collective-permute-done.2.grad_ref.refs_1_
  26.2 0.2 collective-permute-start.13
  26.4 3.4 %collective-permute-done.10.grad_ref.refs_5_ = bf16[256,256]{1,0:T(8,128)(2,1)S(1)} collective-permute-done((bf16[256,256]{1,0:T(8,128)(2,1)S(1)}, bf16[256,256]{1,0:T(8,128)(2,1)S(1)}, u32[]{:S(2)}, u32[]{:S(2)}) %collective-permute-start.10) | collective-permute-done | bytes 131104 | tf_op jit(solution)/shard_map/ppermute | solution.py:386
  29.8 7.8 %collective-permute-start.4 = (bf16[256,256]{1,0:T(8,128)(2,1)S(1)}, bf16[256,256]{1,0:T(8,128)(2,1)S(1)}, u32[]{:S(2)}, u32[]{:S(2)}) collective-permute-start(bf16[256,256]{1,0:T(8,128)(2,1)S(1)} %get-tuple-element.18), channel_id=1, source_target_pairs={{0,4},{4,0},{8,12},{12,8},{16,20},{20,16},{24,28},{28,24},{1,5},{5... | collective-permute-start | bytes 393224 | tf_op jit(solution)/shard_map/ppermute | solution.py:386
  37.5 0.3 shard_map.98
  37.9 0.4 shard_map.102
  38.3 0.0 collective-permute-done.8.grad_ref.refs_4_
  38.3 0.1 collective-permute-start.11
  38.3 0.4 shard_map.101
  38.7 0.2 collective-permute-done.6.grad_ref.refs_3_
  38.9 4.1 %collective-permute-start.9 = (bf16[272,256]{1,0:T(8,128)(2,1)S(1)}, bf16[272,256]{1,0:T(8,128)(2,1)S(1)}, u32[]{:S(2)}, u32[]{:S(2)}) collective-permute-start(bf16[272,256]{1,0:T(8,128)(2,1)S(1)} %shard_map.101), channel_id=1, source_target_pairs={{0,12},{4,8},{8,4},{12,0},{16,28},{20,24},{24,20},{28,16},{1,13},{... | collective-permute-start | bytes 417800 | tf_op jit(solution)/shard_map/ppermute | solution.py:386
  42.9 0.3 shard_map.100
  43.3 0.0 copy-start.2
  43.3 0.0 copy-start.3
  43.3 0.0 collective-permute-done.4.grad_ref.refs_2_
  43.3 3.1 %collective-permute-start.7 = (bf16[272,256]{1,0:T(8,128)(2,1)S(1)}, bf16[272,256]{1,0:T(8,128)(2,1)S(1)}, u32[]{:S(2)}, u32[]{:S(2)}) collective-permute-start(bf16[272,256]{1,0:T(8,128)(2,1)S(1)} %shard_map.100), channel_id=1, source_target_pairs={{0,16},{4,20},{8,24},{12,28},{16,0},{20,4},{24,8},{28,12},{1,17},{... | collective-permute-start | bytes 417800 | tf_op jit(solution)/shard_map/ppermute | solution.py:386
  46.4 0.4 shard_map.99
  46.8 0.0 collective-permute-done.15.refs_7_
  46.8 0.1 collective-permute-start.5
  46.9 0.0 collective-permute-done.13.refs_6_
  46.9 2.1 %collective-permute-start.3 = (bf16[272,256]{1,0:T(8,128)(2,1)S(1)}, bf16[272,256]{1,0:T(8,128)(2,1)S(1)}, u32[]{:S(2)}, u32[]{:S(2)}) collective-permute-start(bf16[272,256]{1,0:T(8,128)(2,1)S(1)} %shard_map.98), channel_id=1, source_target_pairs={{0,8},{4,12},{8,0},{12,4},{16,24},{20,28},{24,16},{28,20},{1,9},{5... | collective-permute-start | bytes 417800 | tf_op jit(solution)/shard_map/ppermute | solution.py:386
  49.0 0.4 shard_map.97.refs_0_
  49.3 0.0 copy-start.4
  49.4 4.7 %shard_map.106 = (f32[1,8,256,256]{3,2,1,0:T(8,128)}, f32[1,8,256,256]{3,2,1,0:T(8,128)}) custom-call(s32[1]{0:T(128)} %bitcast.1.me_ref, bf16[256,256]{1,0:T(8,128)(2,1)S(1)} %get-tuple-element.15.grad_ref.refs_0_, bf16[256,256]{1,0:T(8,128)(2,1)S(1)} %collective-permute-done.2.grad_ref.refs_1_, ...), custom_call_target="tpu_custom_call" | custom-call | flops 536870912 | bytes 9437184 | tf_op jit(solution)/shard_map/pallas_call | solution.py:293
  54.0 0.0 collective-permute-done.11.refs_5_
  54.0 0.0 collective-permute-done.9.refs_4_
  54.1 0.5 collective-permute-done.7.refs_3_
  54.6 0.0 collective-permute-done.5.refs_2_
  54.6 1.2 %collective-permute-done.3.refs_1_ = bf16[272,256]{1,0:T(8,128)(2,1)S(1)} collective-permute-done((bf16[272,256]{1,0:T(8,128)(2,1)S(1)}, bf16[272,256]{1,0:T(8,128)(2,1)S(1)}, u32[]{:S(2)}, u32[]{:S(2)}) %collective-permute-start.3) | collective-permute-done | bytes 139296 | tf_op jit(solution)/shard_map/ppermute | solution.py:386
  55.8 1.8 %shard_map.105 = bf16[1,8,256,256]{3,2,1,0:T(8,128)(2,1)} custom-call(s32[64]{0:T(128)S(1)} %bitcast.3, s32[1]{0:T(128)} %bitcast.1.me_ref, bf16[272,256]{1,0:T(8,128)(2,1)S(1)} %shard_map.97.refs_0_, bf16[272,256]{1,0:T(8,128)(2,1)S(1)} %collective-permute-done.3.refs_1_, bf16[272,256]{1,0:T(8,128)(2,1)S(1)} %collective-permute-done.5.refs_2_, ...), custom_call_target="tpu_custom_call" | custom-call | flops 3145728 | bytes 2097152 | tf_op jit(solution)/shard_map/pallas_call | solution.py:347
  (9 shorter events, 0.0 us)
Async XLA Ops:
  0.6 21.2 %copy-start = (bf16[1,8,256,256]{3,2,1,0:T(8,128)(2,1)S(1)}, bf16[1,8,256,256]{3,2,1,0:T(8,128)(2,1)}, u32[]{:S(2)}) copy-start(bf16[1,8,256,256]{3,2,1,0:T(8,128)(2,1)} %left_ref.15) | copy-start | bytes 3145732
  0.6 21.2 %copy-start.1 = (bf16[1,8,256,256]{3,2,1,0:T(8,128)(2,1)S(1)}, bf16[1,8,256,256]{3,2,1,0:T(8,128)(2,1)}, u32[]{:S(2)}) copy-start(bf16[1,8,256,256]{3,2,1,0:T(8,128)(2,1)} %right_ref.15) | copy-start | bytes 3145732
  2.1 18.0 %collective-permute-start.14 = (bf16[256,256]{1,0:T(8,128)(2,1)S(1)}, bf16[256,256]{1,0:T(8,128)(2,1)S(1)}, u32[]{:S(2)}, u32[]{:S(2)}) collective-permute-start(bf16[256,256]{1,0:T(8,128)(2,1)S(1)} %get-tuple-element.23), channel_id=1, source_target_pairs={{0,28},{4,24},{8,20},{12,16},{16,12},{20,8},{24,4},{28,0},{1,29},{... | collective-permute-start | bytes 393224 | tf_op jit(solution)/shard_map/ppermute | solution.py:386
  8.2 14.0 %collective-permute-start.12 = (bf16[256,256]{1,0:T(8,128)(2,1)S(1)}, bf16[256,256]{1,0:T(8,128)(2,1)S(1)}, u32[]{:S(2)}, u32[]{:S(2)}) collective-permute-start(bf16[256,256]{1,0:T(8,128)(2,1)S(1)} %get-tuple-element.22), channel_id=1, source_target_pairs={{0,24},{4,28},{8,16},{12,20},{16,8},{20,12},{24,0},{28,4},{1,25},{... | collective-permute-start | bytes 393224 | tf_op jit(solution)/shard_map/ppermute | solution.py:386
  8.4 17.8 %collective-permute-start.2 = (bf16[256,256]{1,0:T(8,128)(2,1)S(1)}, bf16[256,256]{1,0:T(8,128)(2,1)S(1)}, u32[]{:S(2)}, u32[]{:S(2)}) collective-permute-start(bf16[256,256]{1,0:T(8,128)(2,1)S(1)} %get-tuple-element.17), channel_id=1, source_target_pairs={{0,8},{4,12},{8,0},{12,4},{16,24},{20,28},{24,16},{28,20},{1,9},{5... | collective-permute-start | bytes 393224 | tf_op jit(solution)/shard_map/ppermute | solution.py:386
  8.4 21.4 %collective-permute-start.10 = (bf16[256,256]{1,0:T(8,128)(2,1)S(1)}, bf16[256,256]{1,0:T(8,128)(2,1)S(1)}, u32[]{:S(2)}, u32[]{:S(2)}) collective-permute-start(bf16[256,256]{1,0:T(8,128)(2,1)S(1)} %get-tuple-element.21), channel_id=1, source_target_pairs={{0,20},{4,16},{8,28},{12,24},{16,4},{20,0},{24,12},{28,8},{1,21},{... | collective-permute-start | bytes 393224 | tf_op jit(solution)/shard_map/ppermute | solution.py:386
  15.1 1.2 %collective-permute-start = (f32[8,128]{1,0:T(8,128)S(1)}, f32[8,128]{1,0:T(8,128)S(1)}, u32[]{:S(2)}, u32[]{:S(2)}) collective-permute-start(f32[8,128]{1,0:T(8,128)S(1)} %get-tuple-element.16), channel_id=1, source_target_pairs={{0,1},{1,0},{2,3},{3,2},{4,5},{5,4},{6,7},{7,6},{8,9},{9,8},{10,11... | collective-permute-start | bytes 12296 | tf_op jit(solution)/shard_map/ppermute | solution.py:386
  16.3 3.6 %collective-permute-start.1 = (f32[8,128]{1,0:T(8,128)S(1)}, f32[8,128]{1,0:T(8,128)S(1)}, u32[]{:S(2)}, u32[]{:S(2)}) collective-permute-start(f32[8,128]{1,0:T(8,128)S(1)} %add.6), channel_id=1, source_target_pairs={{0,2},{1,3},{2,0},{3,1},{4,6},{5,7},{6,4},{7,5},{8,10},{9,11},{10,... | collective-permute-start | bytes 12296 | tf_op jit(solution)/shard_map/ppermute | solution.py:386
  19.9 19.0 %collective-permute-start.6 = (bf16[256,256]{1,0:T(8,128)(2,1)S(1)}, bf16[256,256]{1,0:T(8,128)(2,1)S(1)}, u32[]{:S(2)}, u32[]{:S(2)}) collective-permute-start(bf16[256,256]{1,0:T(8,128)(2,1)S(1)} %get-tuple-element.19), channel_id=1, source_target_pairs={{0,16},{4,20},{8,24},{12,28},{16,0},{20,4},{24,8},{28,12},{1,17},{... | collective-permute-start | bytes 393224 | tf_op jit(solution)/shard_map/ppermute | solution.py:386
  20.1 18.2 %collective-permute-start.8 = (bf16[256,256]{1,0:T(8,128)(2,1)S(1)}, bf16[256,256]{1,0:T(8,128)(2,1)S(1)}, u32[]{:S(2)}, u32[]{:S(2)}) collective-permute-start(bf16[256,256]{1,0:T(8,128)(2,1)S(1)} %get-tuple-element.20), channel_id=1, source_target_pairs={{0,12},{4,8},{8,4},{12,0},{16,28},{20,24},{24,20},{28,16},{1,13},{... | collective-permute-start | bytes 393224 | tf_op jit(solution)/shard_map/ppermute | solution.py:386
  22.2 24.6 %collective-permute-start.15 = (bf16[272,256]{1,0:T(8,128)(2,1)S(1)}, bf16[272,256]{1,0:T(8,128)(2,1)S(1)}, u32[]{:S(2)}, u32[]{:S(2)}) collective-permute-start(bf16[272,256]{1,0:T(8,128)(2,1)S(1)} %shard_map.104), channel_id=1, source_target_pairs={{0,28},{4,24},{8,20},{12,16},{16,12},{20,8},{24,4},{28,0},{1,29},{... | collective-permute-start | bytes 417800 | tf_op jit(solution)/shard_map/ppermute | solution.py:386
  26.2 20.7 %collective-permute-start.13 = (bf16[272,256]{1,0:T(8,128)(2,1)S(1)}, bf16[272,256]{1,0:T(8,128)(2,1)S(1)}, u32[]{:S(2)}, u32[]{:S(2)}) collective-permute-start(bf16[272,256]{1,0:T(8,128)(2,1)S(1)} %shard_map.103), channel_id=1, source_target_pairs={{0,24},{4,28},{8,16},{12,20},{16,8},{20,12},{24,0},{28,4},{1,25},{... | collective-permute-start | bytes 417800 | tf_op jit(solution)/shard_map/ppermute | solution.py:386
  29.8 13.6 %collective-permute-start.4 = (bf16[256,256]{1,0:T(8,128)(2,1)S(1)}, bf16[256,256]{1,0:T(8,128)(2,1)S(1)}, u32[]{:S(2)}, u32[]{:S(2)}) collective-permute-start(bf16[256,256]{1,0:T(8,128)(2,1)S(1)} %get-tuple-element.18), channel_id=1, source_target_pairs={{0,4},{4,0},{8,12},{12,8},{16,20},{20,16},{24,28},{28,24},{1,5},{5... | collective-permute-start | bytes 393224 | tf_op jit(solution)/shard_map/ppermute | solution.py:386
  38.3 15.8 %collective-permute-start.11 = (bf16[272,256]{1,0:T(8,128)(2,1)S(1)}, bf16[272,256]{1,0:T(8,128)(2,1)S(1)}, u32[]{:S(2)}, u32[]{:S(2)}) collective-permute-start(bf16[272,256]{1,0:T(8,128)(2,1)S(1)} %shard_map.102), channel_id=1, source_target_pairs={{0,20},{4,16},{8,28},{12,24},{16,4},{20,0},{24,12},{28,8},{1,21},{... | collective-permute-start | bytes 417800 | tf_op jit(solution)/shard_map/ppermute | solution.py:386
  38.9 15.2 %collective-permute-start.9 = (bf16[272,256]{1,0:T(8,128)(2,1)S(1)}, bf16[272,256]{1,0:T(8,128)(2,1)S(1)}, u32[]{:S(2)}, u32[]{:S(2)}) collective-permute-start(bf16[272,256]{1,0:T(8,128)(2,1)S(1)} %shard_map.101), channel_id=1, source_target_pairs={{0,12},{4,8},{8,4},{12,0},{16,28},{20,24},{24,20},{28,16},{1,13},{... | collective-permute-start | bytes 417800 | tf_op jit(solution)/shard_map/ppermute | solution.py:386
  43.3 6.0 %copy-start.2 = (f32[1,8,256,256]{3,2,1,0:T(8,128)S(1)}, f32[1,8,256,256]{3,2,1,0:T(8,128)}, u32[]{:S(2)}) copy-start(f32[1,8,256,256]{3,2,1,0:T(8,128)} %refs_8_.1) | copy-start | bytes 6291460
  43.3 6.0 %copy-start.3 = (f32[1,8,256,256]{3,2,1,0:T(8,128)S(1)}, f32[1,8,256,256]{3,2,1,0:T(8,128)}, u32[]{:S(2)}) copy-start(f32[1,8,256,256]{3,2,1,0:T(8,128)} %refs_9_.1) | copy-start | bytes 6291460
  43.3 11.3 %collective-permute-start.7 = (bf16[272,256]{1,0:T(8,128)(2,1)S(1)}, bf16[272,256]{1,0:T(8,128)(2,1)S(1)}, u32[]{:S(2)}, u32[]{:S(2)}) collective-permute-start(bf16[272,256]{1,0:T(8,128)(2,1)S(1)} %shard_map.100), channel_id=1, source_target_pairs={{0,16},{4,20},{8,24},{12,28},{16,0},{20,4},{24,8},{28,12},{1,17},{... | collective-permute-start | bytes 417800 | tf_op jit(solution)/shard_map/ppermute | solution.py:386
  46.8 7.8 %collective-permute-start.5 = (bf16[272,256]{1,0:T(8,128)(2,1)S(1)}, bf16[272,256]{1,0:T(8,128)(2,1)S(1)}, u32[]{:S(2)}, u32[]{:S(2)}) collective-permute-start(bf16[272,256]{1,0:T(8,128)(2,1)S(1)} %shard_map.99), channel_id=1, source_target_pairs={{0,4},{4,0},{8,12},{12,8},{16,20},{20,16},{24,28},{28,24},{1,5},{5... | collective-permute-start | bytes 417800 | tf_op jit(solution)/shard_map/ppermute | solution.py:386
  46.9 8.9 %collective-permute-start.3 = (bf16[272,256]{1,0:T(8,128)(2,1)S(1)}, bf16[272,256]{1,0:T(8,128)(2,1)S(1)}, u32[]{:S(2)}, u32[]{:S(2)}) collective-permute-start(bf16[272,256]{1,0:T(8,128)(2,1)S(1)} %shard_map.98), channel_id=1, source_target_pairs={{0,8},{4,12},{8,0},{12,4},{16,24},{20,28},{24,16},{28,20},{1,9},{5... | collective-permute-start | bytes 417800 | tf_op jit(solution)/shard_map/ppermute | solution.py:386
  49.3 6.5 %copy-start.4 = (s32[1,64,1]{1,2,0:T(1,128)S(1)}, s32[1,64,1]{1,2,0:T(1,128)}, u32[]{:S(2)}) copy-start(s32[1,64,1]{1,2,0:T(1,128)} %param.9) | copy-start | bytes 772

commit v12 on v9

--- a/solution.py
+++ b/solution.py
@@ -109,9 +109,10 @@
     return lax.shift_right_logical(who, jnp.int32(layers.bit_length() - 1))
 
 
-def partner(who, step, count):
+def partner(who, layers, step, count):
     even, odd = partner_tables(count)
-    return jnp.where(who & 1 == 1, jnp.int32(odd[step]), jnp.int32(even[step]))
+    turn = who ^ lax.shift_right_logical(fsdp_index(who, layers), jnp.int32(1))
+    return jnp.where(turn & 1 == 1, jnp.int32(odd[step]), jnp.int32(even[step]))
 
 
 def home_slot(named, target):
@@ -132,7 +133,7 @@
     fetch_grads.start()
     fetch_owners.wait()
     named = [owners_ref[me * count + j] for j in range(count)]
-    blocks = [home_slot(named, me ^ partner(who, step, count)) for step in range(count)]
+    blocks = [home_slot(named, me ^ partner(who, layers, step, count)) for step in range(count)]
     fetch_grads.wait()
     for block, out in zip(blocks, outs):
         out[...] = held[block]
@@ -243,7 +244,7 @@
 def precondition_kernel(step, layers, who_ref, grad_ref, left_ref, right_ref, tail_ref, out_ref):
     side = grad_ref.shape[0]
     who = who_ref[0]
-    slot = fsdp_index(who, layers) ^ partner(who, step, left_ref.shape[1])
+    slot = fsdp_index(who, layers) ^ partner(who, layers, step, left_ref.shape[1])
     half_done = jnp.dot(
         left_ref[0, slot], grad_ref[...], preferred_element_type=jnp.float32
     ).astype(jnp.bfloat16)
@@ -299,7 +300,7 @@
         who = who_ref[0]
         m = jnp.int32(0)
         for step in range(1, count):
-            m = jnp.where(i == step, partner(who, step, count), m)
+            m = jnp.where(i == step, partner(who, layers, step, count), m)
         return (0, fsdp_index(who, layers) ^ m, 0, 0)
 
     stat = pl.BlockSpec((1, 1, side, side), slot)
@@ -331,7 +332,7 @@
     who = who_ref[0]
     me = fsdp_index(who, layers)
     named = [owners_ref[me * count + j] for j in range(count)]
-    blocks = [home_slot(named, me ^ partner(who, step, count)) for step in range(count)]
+    blocks = [home_slot(named, me ^ partner(who, layers, step, count)) for step in range(count)]
     global_sq = jnp.zeros((1, 1), jnp.float32)
     for rows in [tail_ref[...]] + [piece[side:, :] for piece in pieces if piece.shape[0] > side]:
         terms = rows[:, 0:1].astype(jnp.float32)
@@ -399,7 +400,7 @@
         if step == 0:
             return value
         pairs = [
-            (i * layers + k, (i ^ tables[k % 2][step]) * layers + k)
+            (i * layers + k, (i ^ tables[(k ^ (i >> 1)) & 1][step]) * layers + k)
             for i in range(count)
             for k in range(layers)
         ]

time: 56.3 us -> 56.7 us (level)
  starting transfers between devices: 31.4 us -> 36 us
  waiting for transfers between devices: 10.6 us -> 6.37 us
    ppermute x14, starting transfers between devices: 29.8 us -> 34.4 us  [swap(): return lax.ppermute(value, ('fsdp', 'layer'), pairs)]
    ppermute x14, waiting for transfers between devices: 7.36 us -> 3.13 us  [swap(): return lax.ppermute(value, ('fsdp', 'layer'), pairs)]
  transfers between devices with their start and end apart: 16 -> 16, of which waited for: 6 -> 4; matrix products, arithmetic and copies ran while one was open for 0% -> 0% of each run, Pallas kernels for 18% -> 18%
where the time goes in v12:
time: 56.7 us; the launch traced here: 56.5 us
  starting transfers between devices  36 us (63%)
  Pallas kernels  13.3 us (23%)
  waiting for transfers between devices  6.37 us (11%)
  between operations  0.85 us (1%)
    ppermute x14, starting transfers between devices, swap(): return lax.ppermute(value, ('fsdp', 'layer'), pairs)  34.4 us
    pallas_call x1, Pallas kernels, gram_update(): pl.pallas_call(gram_kernel, grid_spec=pltpu.PrefetchScalarGridSpec(num_sc...  4.76 us
    ppermute x2, waiting for transfers between devices, per_device_exchange(): lax.ppermute(total, 'layer', [(i, i ^ k) for i in range(layers)])  3.24 us
    ppermute x14, waiting for transfers between devices, swap(): return lax.ppermute(value, ('fsdp', 'layer'), pairs)  3.13 us
    pallas_call x8, Pallas kernels, precondition(): pl.pallas_call(functools.partial(precondition_kernel, step, layers), grid...  2.63 us
    pallas_call x1, Pallas kernels, adam_squares(): pl.pallas_call(adam_kernel, in_specs=[hbm, hbm], out_specs=[pl.BlockSpec(...  2.53 us
    pallas_call x1, Pallas kernels, finish(): pl.pallas_call(functools.partial(finish_kernel, layers, entries), grid_sp...  1.8 us
    ppermute x2, starting transfers between devices, per_device_exchange(): lax.ppermute(total, 'layer', [(i, i ^ k) for i in range(layers)])  1.59 us
  transfers between devices with their start and end apart: 16, of which 4 were waited for; matrix products, arithmetic and copies ran while one was open for 0% of the time, Pallas kernels for 18%

profile of v12, /device:TPU:0, one launch (start us, length us, event | category | flops | bytes accessed | tf_op | source)
XLA Modules:
  0.0 56.5 jit_solution(8422927874051258903)
XLA Ops:
  0.7 1.5 %shard_map.94 = (bf16[256,256]{1,0:T(8,128)(2,1)S(1)}, bf16[256,256]{1,0:T(8,128)(2,1)S(1)}, bf16[256,256]{1,0:T(8,128)(2,1)S(1)}, bf16[256,256]{1,0:T(8,128)(2,...) custom-call(s32[64]{0:T(128)} %bitcast.2, ...), custom_call_target="tpu_custom_call" | custom-call | bytes 2097152 | tf_op jit(solution)/shard_map/pallas_call | solution.py:146
  2.1 6.0 %collective-permute-start.14 = (bf16[256,256]{1,0:T(8,128)(2,1)S(1)}, bf16[256,256]{1,0:T(8,128)(2,1)S(1)}, u32[]{:S(2)}, u32[]{:S(2)}) collective-permute-start(bf16[256,256]{1,0:T(8,128)(2,1)S(1)} %get-tuple-element.23), channel_id=1, source_target_pairs={{0,28},{1,29},{2,30},{3,31},{4,24},{5,25},{6,26},{7,27},{8,20},{9,... | collective-permute-start | bytes 393224 | tf_op jit(solution)/shard_map/ppermute | solution.py:407
  8.2 0.2 collective-permute-start.12
  8.4 0.4 collective-permute-start.2
  8.8 1.8 %collective-permute-start.10 = (bf16[256,256]{1,0:T(8,128)(2,1)S(1)}, bf16[256,256]{1,0:T(8,128)(2,1)S(1)}, u32[]{:S(2)}, u32[]{:S(2)}) collective-permute-start(bf16[256,256]{1,0:T(8,128)(2,1)S(1)} %get-tuple-element.21), channel_id=1, source_target_pairs={{0,20},{1,21},{2,22},{3,23},{4,16},{5,17},{6,18},{7,19},{8,28},{9,... | collective-permute-start | bytes 393224 | tf_op jit(solution)/shard_map/ppermute | solution.py:407
  10.6 2.5 %shard_map.95 = (f32[8,128]{1,0:T(8,128)S(1)}, f32[8,128]{1,0:T(8,128)S(1)}) custom-call(bf16[1,8,256,256]{3,2,1,0:T(8,128)(2,1)} %grad_hbm.3, f32[1,8,256,256]{3,2,1,0:T(8,128)} %moment_hbm.1), custom_call_target="tpu_custom_call" | custom-call | flops 4194304 | bytes 3145728 | tf_op jit(solution)/shard_map/pallas_call | solution.py:197
  13.2 0.1 collective-permute-start
  13.3 1.2 %collective-permute-done = f32[8,128]{1,0:T(8,128)S(1)} collective-permute-done((f32[8,128]{1,0:T(8,128)S(1)}, f32[8,128]{1,0:T(8,128)S(1)}, u32[]{:S(2)}, u32[]{:S(2)}) %collective-permute-start) | collective-permute-done | bytes 4128 | tf_op jit(solution)/shard_map/ppermute | solution.py:413
  14.4 1.5 %collective-permute-start.1 = (f32[8,128]{1,0:T(8,128)S(1)}, f32[8,128]{1,0:T(8,128)S(1)}, u32[]{:S(2)}, u32[]{:S(2)}) collective-permute-start(f32[8,128]{1,0:T(8,128)S(1)} %add.10), channel_id=1, source_target_pairs={{0,2},{1,3},{2,0},{3,1},{4,6},{5,7},{6,4},{7,5},{8,10},{9,11},{10,... | collective-permute-start | bytes 12296 | tf_op jit(solution)/shard_map/ppermute | solution.py:413
  15.9 2.1 %collective-permute-done.1 = f32[8,128]{1,0:T(8,128)S(1)} collective-permute-done((f32[8,128]{1,0:T(8,128)S(1)}, f32[8,128]{1,0:T(8,128)S(1)}, u32[]{:S(2)}, u32[]{:S(2)}) %collective-permute-start.1) | collective-permute-done | bytes 4128 | tf_op jit(solution)/shard_map/ppermute | solution.py:413
  18.0 2.1 %collective-permute-start.6 = (bf16[256,256]{1,0:T(8,128)(2,1)S(1)}, bf16[256,256]{1,0:T(8,128)(2,1)S(1)}, u32[]{:S(2)}, u32[]{:S(2)}) collective-permute-start(bf16[256,256]{1,0:T(8,128)(2,1)S(1)} %get-tuple-element.19), channel_id=1, source_target_pairs={{0,16},{1,5},{2,18},{3,7},{4,20},{5,1},{6,22},{7,3},{8,12},{9,25},... | collective-permute-start | bytes 393224 | tf_op jit(solution)/shard_map/ppermute | solution.py:407
  20.2 0.1 shard_map.96.tail_ref.refs_9_
  20.3 0.0 collective-permute-done.14.grad_ref.refs_7_
  20.3 2.7 %collective-permute-start.8 = (bf16[256,256]{1,0:T(8,128)(2,1)S(1)}, bf16[256,256]{1,0:T(8,128)(2,1)S(1)}, u32[]{:S(2)}, u32[]{:S(2)}) collective-permute-start(bf16[256,256]{1,0:T(8,128)(2,1)S(1)} %get-tuple-element.20), channel_id=1, source_target_pairs={{0,12},{1,13},{2,14},{3,15},{4,8},{5,9},{6,10},{7,11},{8,4},{9,5},... | collective-permute-start | bytes 393224 | tf_op jit(solution)/shard_map/ppermute | solution.py:407
  23.0 0.3 shard_map.104
  23.4 0.0 collective-permute-done.12.grad_ref.refs_6_
  23.4 2.8 %collective-permute-start.15 = (bf16[272,256]{1,0:T(8,128)(2,1)S(1)}, bf16[272,256]{1,0:T(8,128)(2,1)S(1)}, u32[]{:S(2)}, u32[]{:S(2)}) collective-permute-start(bf16[272,256]{1,0:T(8,128)(2,1)S(1)} %shard_map.104), channel_id=1, source_target_pairs={{0,28},{1,29},{2,30},{3,31},{4,24},{5,25},{6,26},{7,27},{8,20},{9,... | collective-permute-start | bytes 417800 | tf_op jit(solution)/shard_map/ppermute | solution.py:407
  26.1 0.3 shard_map.103
  26.5 0.0 collective-permute-done.2.grad_ref.refs_1_
  26.5 9.4 %collective-permute-start.13 = (bf16[272,256]{1,0:T(8,128)(2,1)S(1)}, bf16[272,256]{1,0:T(8,128)(2,1)S(1)}, u32[]{:S(2)}, u32[]{:S(2)}) collective-permute-start(bf16[272,256]{1,0:T(8,128)(2,1)S(1)} %shard_map.103), channel_id=1, source_target_pairs={{0,24},{1,25},{2,26},{3,27},{4,28},{5,29},{6,30},{7,31},{8,16},{9,... | collective-permute-start | bytes 417800 | tf_op jit(solution)/shard_map/ppermute | solution.py:407
  35.9 0.0 collective-permute-done.10.grad_ref.refs_5_
  35.9 0.0 collective-permute-start.4
  35.9 0.3 shard_map.98
  36.2 0.3 shard_map.102
  36.5 0.0 collective-permute-done.8.grad_ref.refs_4_
  36.6 4.3 %collective-permute-start.11 = (bf16[272,256]{1,0:T(8,128)(2,1)S(1)}, bf16[272,256]{1,0:T(8,128)(2,1)S(1)}, u32[]{:S(2)}, u32[]{:S(2)}) collective-permute-start(bf16[272,256]{1,0:T(8,128)(2,1)S(1)} %shard_map.102), channel_id=1, source_target_pairs={{0,20},{1,21},{2,22},{3,23},{4,16},{5,17},{6,18},{7,19},{8,28},{9,... | collective-permute-start | bytes 417800 | tf_op jit(solution)/shard_map/ppermute | solution.py:407
  40.8 0.3 shard_map.101
  41.2 0.0 collective-permute-done.6.grad_ref.refs_3_
  41.2 0.8 %collective-permute-start.9 = (bf16[272,256]{1,0:T(8,128)(2,1)S(1)}, bf16[272,256]{1,0:T(8,128)(2,1)S(1)}, u32[]{:S(2)}, u32[]{:S(2)}) collective-permute-start(bf16[272,256]{1,0:T(8,128)(2,1)S(1)} %shard_map.101), channel_id=1, source_target_pairs={{0,12},{1,13},{2,14},{3,15},{4,8},{5,9},{6,10},{7,11},{8,4},{9,5},... | collective-permute-start | bytes 417800 | tf_op jit(solution)/shard_map/ppermute | solution.py:407
  42.0 0.3 shard_map.100
  42.3 0.0 copy-start.2
  42.3 0.0 copy-start.3
  42.3 0.0 collective-permute-done.4.grad_ref.refs_2_
  42.3 1.6 %collective-permute-start.7 = (bf16[272,256]{1,0:T(8,128)(2,1)S(1)}, bf16[272,256]{1,0:T(8,128)(2,1)S(1)}, u32[]{:S(2)}, u32[]{:S(2)}) collective-permute-start(bf16[272,256]{1,0:T(8,128)(2,1)S(1)} %shard_map.100), channel_id=1, source_target_pairs={{0,16},{1,5},{2,18},{3,7},{4,20},{5,1},{6,22},{7,3},{8,12},{9,25},... | collective-permute-start | bytes 417800 | tf_op jit(solution)/shard_map/ppermute | solution.py:407
  43.9 0.3 shard_map.99
  44.3 0.0 collective-permute-done.15.refs_7_
  44.3 2.0 %collective-permute-start.5 = (bf16[272,256]{1,0:T(8,128)(2,1)S(1)}, bf16[272,256]{1,0:T(8,128)(2,1)S(1)}, u32[]{:S(2)}, u32[]{:S(2)}) collective-permute-start(bf16[272,256]{1,0:T(8,128)(2,1)S(1)} %shard_map.99), channel_id=1, source_target_pairs={{0,8},{1,9},{2,10},{3,11},{4,12},{5,13},{6,14},{7,15},{8,0},{9,1},... | collective-permute-start | bytes 417800 | tf_op jit(solution)/shard_map/ppermute | solution.py:407
  46.3 0.0 collective-permute-done.13.refs_6_
  46.3 0.2 collective-permute-start.3
  46.5 0.3 shard_map.97.refs_0_
  46.9 0.0 copy-start.4
  46.9 4.8 %shard_map.106 = (f32[1,8,256,256]{3,2,1,0:T(8,128)}, f32[1,8,256,256]{3,2,1,0:T(8,128)}) custom-call(s32[1]{0:T(128)} %bitcast.1.who_ref, bf16[256,256]{1,0:T(8,128)(2,1)S(1)} %get-tuple-element.15.grad_ref.refs_0_, bf16[256,256]{1,0:T(8,128)(2,1)S(1)} %collective-permute-done.2.grad_ref.refs_1_, ...), custom_call_target="tpu_custom_call" | custom-call | flops 536870912 | bytes 9437184 | tf_op jit(solution)/shard_map/pallas_call | solution.py:308
  51.6 0.0 collective-permute-done.11.refs_5_
  51.6 0.0 collective-permute-done.9.refs_4_
  51.6 2.9 %collective-permute-done.7.refs_3_ = bf16[272,256]{1,0:T(8,128)(2,1)S(1)} collective-permute-done((bf16[272,256]{1,0:T(8,128)(2,1)S(1)}, bf16[272,256]{1,0:T(8,128)(2,1)S(1)}, u32[]{:S(2)}, u32[]{:S(2)}) %collective-permute-start.7) | collective-permute-done | bytes 139296 | tf_op jit(solution)/shard_map/ppermute | solution.py:407
  54.5 0.2 collective-permute-done.5.refs_2_
  54.7 0.0 collective-permute-done.3.refs_1_
  54.7 1.8 %shard_map.105 = bf16[1,8,256,256]{3,2,1,0:T(8,128)(2,1)} custom-call(s32[64]{0:T(128)S(1)} %bitcast.3, s32[1]{0:T(128)} %bitcast.1.who_ref, bf16[256,256]{1,0:T(8,128)(2,1)S(1)} %shard_map.97.refs_0_, bf16[272,256]{1,0:T(8,128)(2,1)S(1)} %collective-permute-done.3.refs_1_, bf16[272,256]{1,0:T(8,128)(2,1)S(1)} %collective-permute-done.5.refs_2_, ...), custom_call_target="tpu_custom_call" | custom-call | flops 3145728 | bytes 2097152 | tf_op jit(solution)/shard_map/pallas_call | solution.py:365
  (9 shorter events, 0.0 us)
Async XLA Ops:
  0.6 22.4 %copy-start = (bf16[1,8,256,256]{3,2,1,0:T(8,128)(2,1)S(1)}, bf16[1,8,256,256]{3,2,1,0:T(8,128)(2,1)}, u32[]{:S(2)}) copy-start(bf16[1,8,256,256]{3,2,1,0:T(8,128)(2,1)} %left_ref.15) | copy-start | bytes 3145732
  0.6 22.4 %copy-start.1 = (bf16[1,8,256,256]{3,2,1,0:T(8,128)(2,1)S(1)}, bf16[1,8,256,256]{3,2,1,0:T(8,128)(2,1)}, u32[]{:S(2)}) copy-start(bf16[1,8,256,256]{3,2,1,0:T(8,128)(2,1)} %right_ref.15) | copy-start | bytes 3145732
  2.1 18.2 %collective-permute-start.14 = (bf16[256,256]{1,0:T(8,128)(2,1)S(1)}, bf16[256,256]{1,0:T(8,128)(2,1)S(1)}, u32[]{:S(2)}, u32[]{:S(2)}) collective-permute-start(bf16[256,256]{1,0:T(8,128)(2,1)S(1)} %get-tuple-element.23), channel_id=1, source_target_pairs={{0,28},{1,29},{2,30},{3,31},{4,24},{5,25},{6,26},{7,27},{8,20},{9,... | collective-permute-start | bytes 393224 | tf_op jit(solution)/shard_map/ppermute | solution.py:407
  8.2 15.2 %collective-permute-start.12 = (bf16[256,256]{1,0:T(8,128)(2,1)S(1)}, bf16[256,256]{1,0:T(8,128)(2,1)S(1)}, u32[]{:S(2)}, u32[]{:S(2)}) collective-permute-start(bf16[256,256]{1,0:T(8,128)(2,1)S(1)} %get-tuple-element.22), channel_id=1, source_target_pairs={{0,24},{1,25},{2,26},{3,27},{4,28},{5,29},{6,30},{7,31},{8,16},{9,... | collective-permute-start | bytes 393224 | tf_op jit(solution)/shard_map/ppermute | solution.py:407
  8.4 18.1 %collective-permute-start.2 = (bf16[256,256]{1,0:T(8,128)(2,1)S(1)}, bf16[256,256]{1,0:T(8,128)(2,1)S(1)}, u32[]{:S(2)}, u32[]{:S(2)}) collective-permute-start(bf16[256,256]{1,0:T(8,128)(2,1)S(1)} %get-tuple-element.17), channel_id=1, source_target_pairs={{0,4},{1,17},{2,6},{3,19},{4,0},{5,21},{6,2},{7,23},{8,24},{9,13},... | collective-permute-start | bytes 393224 | tf_op jit(solution)/shard_map/ppermute | solution.py:407
  8.8 27.1 %collective-permute-start.10 = (bf16[256,256]{1,0:T(8,128)(2,1)S(1)}, bf16[256,256]{1,0:T(8,128)(2,1)S(1)}, u32[]{:S(2)}, u32[]{:S(2)}) collective-permute-start(bf16[256,256]{1,0:T(8,128)(2,1)S(1)} %get-tuple-element.21), channel_id=1, source_target_pairs={{0,20},{1,21},{2,22},{3,23},{4,16},{5,17},{6,18},{7,19},{8,28},{9,... | collective-permute-start | bytes 393224 | tf_op jit(solution)/shard_map/ppermute | solution.py:407
  13.2 1.2 %collective-permute-start = (f32[8,128]{1,0:T(8,128)S(1)}, f32[8,128]{1,0:T(8,128)S(1)}, u32[]{:S(2)}, u32[]{:S(2)}) collective-permute-start(f32[8,128]{1,0:T(8,128)S(1)} %get-tuple-element.16), channel_id=1, source_target_pairs={{0,1},{1,0},{2,3},{3,2},{4,5},{5,4},{6,7},{7,6},{8,9},{9,8},{10,11... | collective-permute-start | bytes 12296 | tf_op jit(solution)/shard_map/ppermute | solution.py:413
  14.4 3.6 %collective-permute-start.1 = (f32[8,128]{1,0:T(8,128)S(1)}, f32[8,128]{1,0:T(8,128)S(1)}, u32[]{:S(2)}, u32[]{:S(2)}) collective-permute-start(f32[8,128]{1,0:T(8,128)S(1)} %add.10), channel_id=1, source_target_pairs={{0,2},{1,3},{2,0},{3,1},{4,6},{5,7},{6,4},{7,5},{8,10},{9,11},{10,... | collective-permute-start | bytes 12296 | tf_op jit(solution)/shard_map/ppermute | solution.py:413
  18.0 23.1 %collective-permute-start.6 = (bf16[256,256]{1,0:T(8,128)(2,1)S(1)}, bf16[256,256]{1,0:T(8,128)(2,1)S(1)}, u32[]{:S(2)}, u32[]{:S(2)}) collective-permute-start(bf16[256,256]{1,0:T(8,128)(2,1)S(1)} %get-tuple-element.19), channel_id=1, source_target_pairs={{0,16},{1,5},{2,18},{3,7},{4,20},{5,1},{6,22},{7,3},{8,12},{9,25},... | collective-permute-start | bytes 393224 | tf_op jit(solution)/shard_map/ppermute | solution.py:407
  20.3 16.2 %collective-permute-start.8 = (bf16[256,256]{1,0:T(8,128)(2,1)S(1)}, bf16[256,256]{1,0:T(8,128)(2,1)S(1)}, u32[]{:S(2)}, u32[]{:S(2)}) collective-permute-start(bf16[256,256]{1,0:T(8,128)(2,1)S(1)} %get-tuple-element.20), channel_id=1, source_target_pairs={{0,12},{1,13},{2,14},{3,15},{4,8},{5,9},{6,10},{7,11},{8,4},{9,5},... | collective-permute-start | bytes 393224 | tf_op jit(solution)/shard_map/ppermute | solution.py:407
  23.4 20.9 %collective-permute-start.15 = (bf16[272,256]{1,0:T(8,128)(2,1)S(1)}, bf16[272,256]{1,0:T(8,128)(2,1)S(1)}, u32[]{:S(2)}, u32[]{:S(2)}) collective-permute-start(bf16[272,256]{1,0:T(8,128)(2,1)S(1)} %shard_map.104), channel_id=1, source_target_pairs={{0,28},{1,29},{2,30},{3,31},{4,24},{5,25},{6,26},{7,27},{8,20},{9,... | collective-permute-start | bytes 417800 | tf_op jit(solution)/shard_map/ppermute | solution.py:407
  26.5 19.8 %collective-permute-start.13 = (bf16[272,256]{1,0:T(8,128)(2,1)S(1)}, bf16[272,256]{1,0:T(8,128)(2,1)S(1)}, u32[]{:S(2)}, u32[]{:S(2)}) collective-permute-start(bf16[272,256]{1,0:T(8,128)(2,1)S(1)} %shard_map.103), channel_id=1, source_target_pairs={{0,24},{1,25},{2,26},{3,27},{4,28},{5,29},{6,30},{7,31},{8,16},{9,... | collective-permute-start | bytes 417800 | tf_op jit(solution)/shard_map/ppermute | solution.py:407
  35.9 6.5 %collective-permute-start.4 = (bf16[256,256]{1,0:T(8,128)(2,1)S(1)}, bf16[256,256]{1,0:T(8,128)(2,1)S(1)}, u32[]{:S(2)}, u32[]{:S(2)}) collective-permute-start(bf16[256,256]{1,0:T(8,128)(2,1)S(1)} %get-tuple-element.18), channel_id=1, source_target_pairs={{0,8},{1,9},{2,10},{3,11},{4,12},{5,13},{6,14},{7,15},{8,0},{9,1},... | collective-permute-start | bytes 393224 | tf_op jit(solution)/shard_map/ppermute | solution.py:407
  36.6 15.1 %collective-permute-start.11 = (bf16[272,256]{1,0:T(8,128)(2,1)S(1)}, bf16[272,256]{1,0:T(8,128)(2,1)S(1)}, u32[]{:S(2)}, u32[]{:S(2)}) collective-permute-start(bf16[272,256]{1,0:T(8,128)(2,1)S(1)} %shard_map.102), channel_id=1, source_target_pairs={{0,20},{1,21},{2,22},{3,23},{4,16},{5,17},{6,18},{7,19},{8,28},{9,... | collective-permute-start | bytes 417800 | tf_op jit(solution)/shard_map/ppermute | solution.py:407
  41.2 10.5 %collective-permute-start.9 = (bf16[272,256]{1,0:T(8,128)(2,1)S(1)}, bf16[272,256]{1,0:T(8,128)(2,1)S(1)}, u32[]{:S(2)}, u32[]{:S(2)}) collective-permute-start(bf16[272,256]{1,0:T(8,128)(2,1)S(1)} %shard_map.101), channel_id=1, source_target_pairs={{0,12},{1,13},{2,14},{3,15},{4,8},{5,9},{6,10},{7,11},{8,4},{9,5},... | collective-permute-start | bytes 417800 | tf_op jit(solution)/shard_map/ppermute | solution.py:407
  42.3 4.5 %copy-start.2 = (f32[1,8,256,256]{3,2,1,0:T(8,128)S(1)}, f32[1,8,256,256]{3,2,1,0:T(8,128)}, u32[]{:S(2)}) copy-start(f32[1,8,256,256]{3,2,1,0:T(8,128)} %refs_8_.1) | copy-start | bytes 6291460
  42.3 4.5 %copy-start.3 = (f32[1,8,256,256]{3,2,1,0:T(8,128)S(1)}, f32[1,8,256,256]{3,2,1,0:T(8,128)}, u32[]{:S(2)}) copy-start(f32[1,8,256,256]{3,2,1,0:T(8,128)} %refs_9_.1) | copy-start | bytes 6291460
  42.3 12.2 %collective-permute-start.7 = (bf16[272,256]{1,0:T(8,128)(2,1)S(1)}, bf16[272,256]{1,0:T(8,128)(2,1)S(1)}, u32[]{:S(2)}, u32[]{:S(2)}) collective-permute-start(bf16[272,256]{1,0:T(8,128)(2,1)S(1)} %shard_map.100), channel_id=1, source_target_pairs={{0,16},{1,5},{2,18},{3,7},{4,20},{5,1},{6,22},{7,3},{8,12},{9,25},... | collective-permute-start | bytes 417800 | tf_op jit(solution)/shard_map/ppermute | solution.py:407
  44.3 10.5 %collective-permute-start.5 = (bf16[272,256]{1,0:T(8,128)(2,1)S(1)}, bf16[272,256]{1,0:T(8,128)(2,1)S(1)}, u32[]{:S(2)}, u32[]{:S(2)}) collective-permute-start(bf16[272,256]{1,0:T(8,128)(2,1)S(1)} %shard_map.99), channel_id=1, source_target_pairs={{0,8},{1,9},{2,10},{3,11},{4,12},{5,13},{6,14},{7,15},{8,0},{9,1},... | collective-permute-start | bytes 417800 | tf_op jit(solution)/shard_map/ppermute | solution.py:407
  46.3 8.5 %collective-permute-start.3 = (bf16[272,256]{1,0:T(8,128)(2,1)S(1)}, bf16[272,256]{1,0:T(8,128)(2,1)S(1)}, u32[]{:S(2)}, u32[]{:S(2)}) collective-permute-start(bf16[272,256]{1,0:T(8,128)(2,1)S(1)} %shard_map.98), channel_id=1, source_target_pairs={{0,4},{1,17},{2,6},{3,19},{4,0},{5,21},{6,2},{7,23},{8,24},{9,13},... | collective-permute-start | bytes 417800 | tf_op jit(solution)/shard_map/ppermute | solution.py:407
  46.9 7.9 %copy-start.4 = (s32[1,64,1]{1,2,0:T(1,128)S(1)}, s32[1,64,1]{1,2,0:T(1,128)}, u32[]{:S(2)}) copy-start(s32[1,64,1]{1,2,0:T(1,128)} %param.9) | copy-start | bytes 772

commit v13 on v11

--- a/solution.py
+++ b/solution.py
@@ -378,7 +378,8 @@
     me = lax.axis_index("fsdp").astype(jnp.int32).reshape(1)
     owner_list = owners[0, :, 0]
     half = count // 2
-    order = [0, *range(half - 2, 0, -1), half, half - 1, *range(half + 1, count)]
+    order = [*range(half - 1), half + 1, half - 1, half, *range(half + 2, count - 2)]
+    order += [count - 1, count - 2]
 
     def swap(value, m, axis="fsdp"):
         if m == 0:

time: 57.7 us -> 56.3 us (0.976)
  starting transfers between devices: 34.7 us -> 33.7 us
    ppermute x16, starting transfers between devices: 34.7 us -> 33.7 us  [swap(): lax.ppermute(value, axis, [(i, i ^ m) for i in range(lax.axis_size(axis))])]
where the time goes in v13:
time: 56.3 us; the launch traced here: 56.1 us
  starting transfers between devices  33.7 us (60%)
  Pallas kernels  13.4 us (24%)
  waiting for transfers between devices  8.22 us (15%)
  between operations  0.84 us (1%)
    ppermute x16, starting transfers between devices, swap(): lax.ppermute(value, axis, [(i, i ^ m) for i in range(lax.axis_size(axis))])  33.7 us
    ppermute x16, waiting for transfers between devices, swap(): lax.ppermute(value, axis, [(i, i ^ m) for i in range(lax.axis_size(axis))])  8.22 us
    pallas_call x1, Pallas kernels, gram_update(): pl.pallas_call(functools.partial(gram_kernel, order), grid_spec=pltpu.Pre...  4.68 us
    pallas_call x8, Pallas kernels, precondition(): pl.pallas_call(functools.partial(precondition_kernel, m), grid_spec=pltpu...  2.8 us
    pallas_call x1, Pallas kernels, adam_squares(): pl.pallas_call(adam_kernel, in_specs=[hbm, hbm], out_specs=[pl.BlockSpec(...  2.53 us
    pallas_call x1, Pallas kernels, finish(): pl.pallas_call(functools.partial(finish_kernel, order, entries), grid_spe...  1.76 us
    pallas_call x1, Pallas kernels, route(): pl.pallas_call(functools.partial(route_kernel, order), in_specs=[hbm, pl....  1.46 us
  transfers between devices with their start and end apart: 16, of which 6 were waited for; matrix products, arithmetic and copies ran while one was open for 0% of the time, Pallas kernels for 18%

profile of v13, /device:TPU:0, one launch (start us, length us, event | category | flops | bytes accessed | tf_op | source)
XLA Modules:
  0.0 56.1 jit_solution(17716540105022233604)
XLA Ops:
  0.7 1.5 %shard_map.94 = (bf16[256,256]{1,0:T(8,128)(2,1)S(1)}, bf16[256,256]{1,0:T(8,128)(2,1)S(1)}, bf16[256,256]{1,0:T(8,128)(2,1)S(1)}, bf16[256,256]{1,0:T(8,128)(2,...) custom-call(s32[64]{0:T(128)} %bitcast.2, ...), custom_call_target="tpu_custom_call" | custom-call | bytes 2097152 | tf_op jit(solution)/shard_map/pallas_call | solution.py:128
  2.1 5.1 %collective-permute-start.14 = (bf16[256,256]{1,0:T(8,128)(2,1)S(1)}, bf16[256,256]{1,0:T(8,128)(2,1)S(1)}, u32[]{:S(2)}, u32[]{:S(2)}) collective-permute-start(bf16[256,256]{1,0:T(8,128)(2,1)S(1)} %get-tuple-element.23), channel_id=1, source_target_pairs={{0,24},{4,28},{8,16},{12,20},{16,8},{20,12},{24,0},{28,4},{1,25},{... | collective-permute-start | bytes 393224 | tf_op jit(solution)/shard_map/ppermute | solution.py:387
  7.2 1.1 %collective-permute-start.12 = (bf16[256,256]{1,0:T(8,128)(2,1)S(1)}, bf16[256,256]{1,0:T(8,128)(2,1)S(1)}, u32[]{:S(2)}, u32[]{:S(2)}) collective-permute-start(bf16[256,256]{1,0:T(8,128)(2,1)S(1)} %get-tuple-element.22), channel_id=1, source_target_pairs={{0,28},{4,24},{8,20},{12,16},{16,12},{20,8},{24,4},{28,0},{1,29},{... | collective-permute-start | bytes 393224 | tf_op jit(solution)/shard_map/ppermute | solution.py:387
  8.4 0.4 collective-permute-start.2
  8.8 0.9 %collective-permute-start.10 = (bf16[256,256]{1,0:T(8,128)(2,1)S(1)}, bf16[256,256]{1,0:T(8,128)(2,1)S(1)}, u32[]{:S(2)}, u32[]{:S(2)}) collective-permute-start(bf16[256,256]{1,0:T(8,128)(2,1)S(1)} %get-tuple-element.21), channel_id=1, source_target_pairs={{0,16},{4,20},{8,24},{12,28},{16,0},{20,4},{24,8},{28,12},{1,17},{... | collective-permute-start | bytes 393224 | tf_op jit(solution)/shard_map/ppermute | solution.py:387
  9.7 2.5 %shard_map.95 = (f32[8,128]{1,0:T(8,128)S(1)}, f32[8,128]{1,0:T(8,128)S(1)}) custom-call(bf16[1,8,256,256]{3,2,1,0:T(8,128)(2,1)} %grad_hbm.3, f32[1,8,256,256]{3,2,1,0:T(8,128)} %moment_hbm.1), custom_call_target="tpu_custom_call" | custom-call | flops 4194304 | bytes 3145728 | tf_op jit(solution)/shard_map/pallas_call | solution.py:179
  12.3 0.1 collective-permute-start
  12.3 1.2 %collective-permute-done = f32[8,128]{1,0:T(8,128)S(1)} collective-permute-done((f32[8,128]{1,0:T(8,128)S(1)}, f32[8,128]{1,0:T(8,128)S(1)}, u32[]{:S(2)}, u32[]{:S(2)}) %collective-permute-start) | collective-permute-done | bytes 4128 | tf_op jit(solution)/shard_map/ppermute | solution.py:387
  13.5 1.5 %collective-permute-start.1 = (f32[8,128]{1,0:T(8,128)S(1)}, f32[8,128]{1,0:T(8,128)S(1)}, u32[]{:S(2)}, u32[]{:S(2)}) collective-permute-start(f32[8,128]{1,0:T(8,128)S(1)} %add.6), channel_id=1, source_target_pairs={{0,2},{1,3},{2,0},{3,1},{4,6},{5,7},{6,4},{7,5},{8,10},{9,11},{10,... | collective-permute-start | bytes 12296 | tf_op jit(solution)/shard_map/ppermute | solution.py:387
  15.0 2.1 %collective-permute-done.1 = f32[8,128]{1,0:T(8,128)S(1)} collective-permute-done((f32[8,128]{1,0:T(8,128)S(1)}, f32[8,128]{1,0:T(8,128)S(1)}, u32[]{:S(2)}, u32[]{:S(2)}) %collective-permute-start.1) | collective-permute-done | bytes 4128 | tf_op jit(solution)/shard_map/ppermute | solution.py:387
  17.1 3.1 %collective-permute-start.6 = (bf16[256,256]{1,0:T(8,128)(2,1)S(1)}, bf16[256,256]{1,0:T(8,128)(2,1)S(1)}, u32[]{:S(2)}, u32[]{:S(2)}) collective-permute-start(bf16[256,256]{1,0:T(8,128)(2,1)S(1)} %get-tuple-element.19), channel_id=1, source_target_pairs={{0,20},{4,16},{8,28},{12,24},{16,4},{20,0},{24,12},{28,8},{1,21},{... | collective-permute-start | bytes 393224 | tf_op jit(solution)/shard_map/ppermute | solution.py:387
  20.2 0.1 shard_map.96.tail_ref
  20.3 0.0 collective-permute-done.14.grad_ref.refs_7_
  20.3 1.3 %collective-permute-start.8 = (bf16[256,256]{1,0:T(8,128)(2,1)S(1)}, bf16[256,256]{1,0:T(8,128)(2,1)S(1)}, u32[]{:S(2)}, u32[]{:S(2)}) collective-permute-start(bf16[256,256]{1,0:T(8,128)(2,1)S(1)} %get-tuple-element.20), channel_id=1, source_target_pairs={{0,12},{4,8},{8,4},{12,0},{16,28},{20,24},{24,20},{28,16},{1,13},{... | collective-permute-start | bytes 393224 | tf_op jit(solution)/shard_map/ppermute | solution.py:387
  21.6 0.4 shard_map.104
  22.0 0.0 collective-permute-done.12.grad_ref.refs_6_
  22.0 2.5 %collective-permute-start.15 = (bf16[272,256]{1,0:T(8,128)(2,1)S(1)}, bf16[272,256]{1,0:T(8,128)(2,1)S(1)}, u32[]{:S(2)}, u32[]{:S(2)}) collective-permute-start(bf16[272,256]{1,0:T(8,128)(2,1)S(1)} %shard_map.104), channel_id=1, source_target_pairs={{0,24},{4,28},{8,16},{12,20},{16,8},{20,12},{24,0},{28,4},{1,25},{... | collective-permute-start | bytes 417800 | tf_op jit(solution)/shard_map/ppermute | solution.py:387
  24.4 0.3 shard_map.103
  24.8 0.0 collective-permute-done.2.grad_ref.refs_1_
  24.8 2.4 %collective-permute-start.13 = (bf16[272,256]{1,0:T(8,128)(2,1)S(1)}, bf16[272,256]{1,0:T(8,128)(2,1)S(1)}, u32[]{:S(2)}, u32[]{:S(2)}) collective-permute-start(bf16[272,256]{1,0:T(8,128)(2,1)S(1)} %shard_map.103), channel_id=1, source_target_pairs={{0,28},{4,24},{8,20},{12,16},{16,12},{20,8},{24,4},{28,0},{1,29},{... | collective-permute-start | bytes 417800 | tf_op jit(solution)/shard_map/ppermute | solution.py:387
  27.2 0.1 collective-permute-done.10.grad_ref.refs_5_
  27.3 5.0 %collective-permute-start.4 = (bf16[256,256]{1,0:T(8,128)(2,1)S(1)}, bf16[256,256]{1,0:T(8,128)(2,1)S(1)}, u32[]{:S(2)}, u32[]{:S(2)}) collective-permute-start(bf16[256,256]{1,0:T(8,128)(2,1)S(1)} %get-tuple-element.18), channel_id=1, source_target_pairs={{0,8},{4,12},{8,0},{12,4},{16,24},{20,28},{24,16},{28,20},{1,9},{5... | collective-permute-start | bytes 393224 | tf_op jit(solution)/shard_map/ppermute | solution.py:387
  32.3 0.3 shard_map.98
  32.7 0.4 shard_map.102
  33.1 0.0 collective-permute-done.8.grad_ref.refs_4_
  33.1 4.1 %collective-permute-start.11 = (bf16[272,256]{1,0:T(8,128)(2,1)S(1)}, bf16[272,256]{1,0:T(8,128)(2,1)S(1)}, u32[]{:S(2)}, u32[]{:S(2)}) collective-permute-start(bf16[272,256]{1,0:T(8,128)(2,1)S(1)} %shard_map.102), channel_id=1, source_target_pairs={{0,16},{4,20},{8,24},{12,28},{16,0},{20,4},{24,8},{28,12},{1,17},{... | collective-permute-start | bytes 417800 | tf_op jit(solution)/shard_map/ppermute | solution.py:387
  37.1 0.3 shard_map.101
  37.5 1.4 %collective-permute-done.6.grad_ref.refs_3_ = bf16[256,256]{1,0:T(8,128)(2,1)S(1)} collective-permute-done((bf16[256,256]{1,0:T(8,128)(2,1)S(1)}, bf16[256,256]{1,0:T(8,128)(2,1)S(1)}, u32[]{:S(2)}, u32[]{:S(2)}) %collective-permute-start.6) | collective-permute-done | bytes 131104 | tf_op jit(solution)/shard_map/ppermute | solution.py:387
  38.9 2.4 %collective-permute-start.9 = (bf16[272,256]{1,0:T(8,128)(2,1)S(1)}, bf16[272,256]{1,0:T(8,128)(2,1)S(1)}, u32[]{:S(2)}, u32[]{:S(2)}) collective-permute-start(bf16[272,256]{1,0:T(8,128)(2,1)S(1)} %shard_map.101), channel_id=1, source_target_pairs={{0,12},{4,8},{8,4},{12,0},{16,28},{20,24},{24,20},{28,16},{1,13},{... | collective-permute-start | bytes 417800 | tf_op jit(solution)/shard_map/ppermute | solution.py:387
  41.3 0.3 shard_map.100
  41.7 0.0 copy-start.2
  41.7 0.0 copy-start.3
  41.7 0.0 collective-permute-done.4.grad_ref.refs_2_
  41.7 2.4 %collective-permute-start.7 = (bf16[272,256]{1,0:T(8,128)(2,1)S(1)}, bf16[272,256]{1,0:T(8,128)(2,1)S(1)}, u32[]{:S(2)}, u32[]{:S(2)}) collective-permute-start(bf16[272,256]{1,0:T(8,128)(2,1)S(1)} %shard_map.100), channel_id=1, source_target_pairs={{0,20},{4,16},{8,28},{12,24},{16,4},{20,0},{24,12},{28,8},{1,21},{... | collective-permute-start | bytes 417800 | tf_op jit(solution)/shard_map/ppermute | solution.py:387
  44.1 0.4 shard_map.99
  44.5 0.0 collective-permute-done.15.refs_7_
  44.5 1.3 %collective-permute-start.5 = (bf16[272,256]{1,0:T(8,128)(2,1)S(1)}, bf16[272,256]{1,0:T(8,128)(2,1)S(1)}, u32[]{:S(2)}, u32[]{:S(2)}) collective-permute-start(bf16[272,256]{1,0:T(8,128)(2,1)S(1)} %shard_map.99), channel_id=1, source_target_pairs={{0,8},{4,12},{8,0},{12,4},{16,24},{20,28},{24,16},{28,20},{1,9},{5... | collective-permute-start | bytes 417800 | tf_op jit(solution)/shard_map/ppermute | solution.py:387
  45.8 0.0 collective-permute-done.13.refs_6_
  45.8 0.0 collective-permute-start.3
  45.8 0.4 shard_map.97.refs_0_
  46.2 0.0 copy-start.4
  46.2 4.7 %shard_map.106 = (f32[1,8,256,256]{3,2,1,0:T(8,128)}, f32[1,8,256,256]{3,2,1,0:T(8,128)}) custom-call(s32[1]{0:T(128)} %bitcast.1.me_ref, bf16[256,256]{1,0:T(8,128)(2,1)S(1)} %get-tuple-element.15.grad_ref.refs_0_, bf16[256,256]{1,0:T(8,128)(2,1)S(1)} %collective-permute-done.2.grad_ref.refs_1_, ...), custom_call_target="tpu_custom_call" | custom-call | flops 536870912 | bytes 9437184 | tf_op jit(solution)/shard_map/pallas_call | solution.py:293
  50.9 0.6 %collective-permute-done.11.refs_5_ = bf16[272,256]{1,0:T(8,128)(2,1)S(1)} collective-permute-done((bf16[272,256]{1,0:T(8,128)(2,1)S(1)}, bf16[272,256]{1,0:T(8,128)(2,1)S(1)}, u32[]{:S(2)}, u32[]{:S(2)}) %collective-permute-start.11) | collective-permute-done | bytes 139296 | tf_op jit(solution)/shard_map/ppermute | solution.py:387
  51.6 0.0 collective-permute-done.9.refs_4_
  51.6 2.8 %collective-permute-done.7.refs_3_ = bf16[272,256]{1,0:T(8,128)(2,1)S(1)} collective-permute-done((bf16[272,256]{1,0:T(8,128)(2,1)S(1)}, bf16[272,256]{1,0:T(8,128)(2,1)S(1)}, u32[]{:S(2)}, u32[]{:S(2)}) %collective-permute-start.7) | collective-permute-done | bytes 139296 | tf_op jit(solution)/shard_map/ppermute | solution.py:387
  54.4 0.0 collective-permute-done.5.refs_2_
  54.4 0.0 collective-permute-done.3.refs_1_
  54.4 1.8 %shard_map.105 = bf16[1,8,256,256]{3,2,1,0:T(8,128)(2,1)} custom-call(s32[64]{0:T(128)S(1)} %bitcast.3, s32[1]{0:T(128)} %bitcast.1.me_ref, bf16[272,256]{1,0:T(8,128)(2,1)S(1)} %shard_map.97.refs_0_, bf16[272,256]{1,0:T(8,128)(2,1)S(1)} %collective-permute-done.3.refs_1_, bf16[272,256]{1,0:T(8,128)(2,1)S(1)} %collective-permute-done.5.refs_2_, ...), custom_call_target="tpu_custom_call" | custom-call | flops 3145728 | bytes 2097152 | tf_op jit(solution)/shard_map/pallas_call | solution.py:347
  (9 shorter events, 0.0 us)
Async XLA Ops:
  0.6 21.0 %copy-start = (bf16[1,8,256,256]{3,2,1,0:T(8,128)(2,1)S(1)}, bf16[1,8,256,256]{3,2,1,0:T(8,128)(2,1)}, u32[]{:S(2)}) copy-start(bf16[1,8,256,256]{3,2,1,0:T(8,128)(2,1)} %left_ref.15) | copy-start | bytes 3145732
  0.6 21.0 %copy-start.1 = (bf16[1,8,256,256]{3,2,1,0:T(8,128)(2,1)S(1)}, bf16[1,8,256,256]{3,2,1,0:T(8,128)(2,1)}, u32[]{:S(2)}) copy-start(bf16[1,8,256,256]{3,2,1,0:T(8,128)(2,1)} %right_ref.15) | copy-start | bytes 3145732
  2.1 18.2 %collective-permute-start.14 = (bf16[256,256]{1,0:T(8,128)(2,1)S(1)}, bf16[256,256]{1,0:T(8,128)(2,1)S(1)}, u32[]{:S(2)}, u32[]{:S(2)}) collective-permute-start(bf16[256,256]{1,0:T(8,128)(2,1)S(1)} %get-tuple-element.23), channel_id=1, source_target_pairs={{0,24},{4,28},{8,16},{12,20},{16,8},{20,12},{24,0},{28,4},{1,25},{... | collective-permute-start | bytes 393224 | tf_op jit(solution)/shard_map/ppermute | solution.py:387
  7.2 14.7 %collective-permute-start.12 = (bf16[256,256]{1,0:T(8,128)(2,1)S(1)}, bf16[256,256]{1,0:T(8,128)(2,1)S(1)}, u32[]{:S(2)}, u32[]{:S(2)}) collective-permute-start(bf16[256,256]{1,0:T(8,128)(2,1)S(1)} %get-tuple-element.22), channel_id=1, source_target_pairs={{0,28},{4,24},{8,20},{12,16},{16,12},{20,8},{24,4},{28,0},{1,29},{... | collective-permute-start | bytes 393224 | tf_op jit(solution)/shard_map/ppermute | solution.py:387
  8.4 16.4 %collective-permute-start.2 = (bf16[256,256]{1,0:T(8,128)(2,1)S(1)}, bf16[256,256]{1,0:T(8,128)(2,1)S(1)}, u32[]{:S(2)}, u32[]{:S(2)}) collective-permute-start(bf16[256,256]{1,0:T(8,128)(2,1)S(1)} %get-tuple-element.17), channel_id=1, source_target_pairs={{0,4},{4,0},{8,12},{12,8},{16,20},{20,16},{24,28},{28,24},{1,5},{5... | collective-permute-start | bytes 393224 | tf_op jit(solution)/shard_map/ppermute | solution.py:387
  8.8 18.5 %collective-permute-start.10 = (bf16[256,256]{1,0:T(8,128)(2,1)S(1)}, bf16[256,256]{1,0:T(8,128)(2,1)S(1)}, u32[]{:S(2)}, u32[]{:S(2)}) collective-permute-start(bf16[256,256]{1,0:T(8,128)(2,1)S(1)} %get-tuple-element.21), channel_id=1, source_target_pairs={{0,16},{4,20},{8,24},{12,28},{16,0},{20,4},{24,8},{28,12},{1,17},{... | collective-permute-start | bytes 393224 | tf_op jit(solution)/shard_map/ppermute | solution.py:387
  12.3 1.2 %collective-permute-start = (f32[8,128]{1,0:T(8,128)S(1)}, f32[8,128]{1,0:T(8,128)S(1)}, u32[]{:S(2)}, u32[]{:S(2)}) collective-permute-start(f32[8,128]{1,0:T(8,128)S(1)} %get-tuple-element.16), channel_id=1, source_target_pairs={{0,1},{1,0},{2,3},{3,2},{4,5},{5,4},{6,7},{7,6},{8,9},{9,8},{10,11... | collective-permute-start | bytes 12296 | tf_op jit(solution)/shard_map/ppermute | solution.py:387
  13.5 3.6 %collective-permute-start.1 = (f32[8,128]{1,0:T(8,128)S(1)}, f32[8,128]{1,0:T(8,128)S(1)}, u32[]{:S(2)}, u32[]{:S(2)}) collective-permute-start(f32[8,128]{1,0:T(8,128)S(1)} %add.6), channel_id=1, source_target_pairs={{0,2},{1,3},{2,0},{3,1},{4,6},{5,7},{6,4},{7,5},{8,10},{9,11},{10,... | collective-permute-start | bytes 12296 | tf_op jit(solution)/shard_map/ppermute | solution.py:387
  17.1 21.8 %collective-permute-start.6 = (bf16[256,256]{1,0:T(8,128)(2,1)S(1)}, bf16[256,256]{1,0:T(8,128)(2,1)S(1)}, u32[]{:S(2)}, u32[]{:S(2)}) collective-permute-start(bf16[256,256]{1,0:T(8,128)(2,1)S(1)} %get-tuple-element.19), channel_id=1, source_target_pairs={{0,20},{4,16},{8,28},{12,24},{16,4},{20,0},{24,12},{28,8},{1,21},{... | collective-permute-start | bytes 393224 | tf_op jit(solution)/shard_map/ppermute | solution.py:387
  20.3 12.8 %collective-permute-start.8 = (bf16[256,256]{1,0:T(8,128)(2,1)S(1)}, bf16[256,256]{1,0:T(8,128)(2,1)S(1)}, u32[]{:S(2)}, u32[]{:S(2)}) collective-permute-start(bf16[256,256]{1,0:T(8,128)(2,1)S(1)} %get-tuple-element.20), channel_id=1, source_target_pairs={{0,12},{4,8},{8,4},{12,0},{16,28},{20,24},{24,20},{28,16},{1,13},{... | collective-permute-start | bytes 393224 | tf_op jit(solution)/shard_map/ppermute | solution.py:387
  22.0 22.5 %collective-permute-start.15 = (bf16[272,256]{1,0:T(8,128)(2,1)S(1)}, bf16[272,256]{1,0:T(8,128)(2,1)S(1)}, u32[]{:S(2)}, u32[]{:S(2)}) collective-permute-start(bf16[272,256]{1,0:T(8,128)(2,1)S(1)} %shard_map.104), channel_id=1, source_target_pairs={{0,24},{4,28},{8,16},{12,20},{16,8},{20,12},{24,0},{28,4},{1,25},{... | collective-permute-start | bytes 417800 | tf_op jit(solution)/shard_map/ppermute | solution.py:387
  24.8 21.0 %collective-permute-start.13 = (bf16[272,256]{1,0:T(8,128)(2,1)S(1)}, bf16[272,256]{1,0:T(8,128)(2,1)S(1)}, u32[]{:S(2)}, u32[]{:S(2)}) collective-permute-start(bf16[272,256]{1,0:T(8,128)(2,1)S(1)} %shard_map.103), channel_id=1, source_target_pairs={{0,28},{4,24},{8,20},{12,16},{16,12},{20,8},{24,4},{28,0},{1,29},{... | collective-permute-start | bytes 417800 | tf_op jit(solution)/shard_map/ppermute | solution.py:387
  27.3 14.4 %collective-permute-start.4 = (bf16[256,256]{1,0:T(8,128)(2,1)S(1)}, bf16[256,256]{1,0:T(8,128)(2,1)S(1)}, u32[]{:S(2)}, u32[]{:S(2)}) collective-permute-start(bf16[256,256]{1,0:T(8,128)(2,1)S(1)} %get-tuple-element.18), channel_id=1, source_target_pairs={{0,8},{4,12},{8,0},{12,4},{16,24},{20,28},{24,16},{28,20},{1,9},{5... | collective-permute-start | bytes 393224 | tf_op jit(solution)/shard_map/ppermute | solution.py:387
  33.1 18.5 %collective-permute-start.11 = (bf16[272,256]{1,0:T(8,128)(2,1)S(1)}, bf16[272,256]{1,0:T(8,128)(2,1)S(1)}, u32[]{:S(2)}, u32[]{:S(2)}) collective-permute-start(bf16[272,256]{1,0:T(8,128)(2,1)S(1)} %shard_map.102), channel_id=1, source_target_pairs={{0,16},{4,20},{8,24},{12,28},{16,0},{20,4},{24,8},{28,12},{1,17},{... | collective-permute-start | bytes 417800 | tf_op jit(solution)/shard_map/ppermute | solution.py:387
  38.9 12.7 %collective-permute-start.9 = (bf16[272,256]{1,0:T(8,128)(2,1)S(1)}, bf16[272,256]{1,0:T(8,128)(2,1)S(1)}, u32[]{:S(2)}, u32[]{:S(2)}) collective-permute-start(bf16[272,256]{1,0:T(8,128)(2,1)S(1)} %shard_map.101), channel_id=1, source_target_pairs={{0,12},{4,8},{8,4},{12,0},{16,28},{20,24},{24,20},{28,16},{1,13},{... | collective-permute-start | bytes 417800 | tf_op jit(solution)/shard_map/ppermute | solution.py:387
  41.7 4.5 %copy-start.2 = (f32[1,8,256,256]{3,2,1,0:T(8,128)S(1)}, f32[1,8,256,256]{3,2,1,0:T(8,128)}, u32[]{:S(2)}) copy-start(f32[1,8,256,256]{3,2,1,0:T(8,128)} %refs_8_.1) | copy-start | bytes 6291460
  41.7 4.5 %copy-start.3 = (f32[1,8,256,256]{3,2,1,0:T(8,128)S(1)}, f32[1,8,256,256]{3,2,1,0:T(8,128)}, u32[]{:S(2)}) copy-start(f32[1,8,256,256]{3,2,1,0:T(8,128)} %refs_9_.1) | copy-start | bytes 6291460
  41.7 12.6 %collective-permute-start.7 = (bf16[272,256]{1,0:T(8,128)(2,1)S(1)}, bf16[272,256]{1,0:T(8,128)(2,1)S(1)}, u32[]{:S(2)}, u32[]{:S(2)}) collective-permute-start(bf16[272,256]{1,0:T(8,128)(2,1)S(1)} %shard_map.100), channel_id=1, source_target_pairs={{0,20},{4,16},{8,28},{12,24},{16,4},{20,0},{24,12},{28,8},{1,21},{... | collective-permute-start | bytes 417800 | tf_op jit(solution)/shard_map/ppermute | solution.py:387
  44.5 9.9 %collective-permute-start.5 = (bf16[272,256]{1,0:T(8,128)(2,1)S(1)}, bf16[272,256]{1,0:T(8,128)(2,1)S(1)}, u32[]{:S(2)}, u32[]{:S(2)}) collective-permute-start(bf16[272,256]{1,0:T(8,128)(2,1)S(1)} %shard_map.99), channel_id=1, source_target_pairs={{0,8},{4,12},{8,0},{12,4},{16,24},{20,28},{24,16},{28,20},{1,9},{5... | collective-permute-start | bytes 417800 | tf_op jit(solution)/shard_map/ppermute | solution.py:387
  45.8 8.5 %collective-permute-start.3 = (bf16[272,256]{1,0:T(8,128)(2,1)S(1)}, bf16[272,256]{1,0:T(8,128)(2,1)S(1)}, u32[]{:S(2)}, u32[]{:S(2)}) collective-permute-start(bf16[272,256]{1,0:T(8,128)(2,1)S(1)} %shard_map.98), channel_id=1, source_target_pairs={{0,4},{4,0},{8,12},{12,8},{16,20},{20,16},{24,28},{28,24},{1,5},{5... | collective-permute-start | bytes 417800 | tf_op jit(solution)/shard_map/ppermute | solution.py:387
  46.2 8.1 %copy-start.4 = (s32[1,64,1]{1,2,0:T(1,128)S(1)}, s32[1,64,1]{1,2,0:T(1,128)}, u32[]{:S(2)}) copy-start(s32[1,64,1]{1,2,0:T(1,128)} %param.9) | copy-start | bytes 772
